TPU v7x, 32 devices: a whole 2x2x4 slice. The times are simulated.
32 devices in a mesh: section: 2 (over y), dp: 4 (over x, core), tensor: 4 (over z).
Axes of the slice: x: 2, y: 2, z: 4, core: 2. Of those that a mesh axis runs over, the one named last changes fastest.
Arguments:
- inputs: bfloat16 [4, 4096, 1536], P(None, ('dp', 'tensor')), may hold values from -6 to 6
- cotangent: bfloat16 [4, 4096, 1536], P(None, ('dp', 'tensor')), may hold values from -6 to 6
- attn_gain: float32 [2, 1536], P('section'), may hold values from 0.1 to 1.9
- w_query: bfloat16 [2, 1536, 1536], P('section', 'dp', 'tensor'), may hold values from -0.15625 to 0.15625
- w_key: bfloat16 [2, 1536, 768], P('section', 'dp'), may hold values from -0.15625 to 0.15625
- w_value: bfloat16 [2, 1536, 768], P('section', 'dp'), may hold values from -0.15625 to 0.15625
- w_out: bfloat16 [2, 1536, 1536], P('section', 'tensor', 'dp'), may hold values from -0.875 to 0.875
- mlp_gain: float32 [2, 1536], P('section'), may hold values from 0.1 to 1.9
- w_gate: bfloat16 [2, 1536, 4096], P('section', 'dp', 'tensor'), may hold values from -0.15625 to 0.15625
- w_up: bfloat16 [2, 1536, 4096], P('section', 'dp', 'tensor'), may hold values from -0.15625 to 0.15625
- w_down: bfloat16 [2, 4096, 1536], P('section', 'tensor', 'dp'), may hold values from -0.09375 to 0.09375
Outputs:
- outputs: bfloat16 [2, 4, 4096, 1536], P('section', None, ('dp', 'tensor'))
- input_grads: bfloat16 [2, 4, 4096, 1536], P('section', None, ('dp', 'tensor'))
- attn_gain_grad: float32 [2, 1536], P('section')
- w_query_grad: float32 [2, 1536, 1536], P('section', 'dp', 'tensor')
- w_key_grad: float32 [2, 1536, 768], P('section', 'dp')
- w_value_grad: float32 [2, 1536, 768], P('section', 'dp')
- w_out_grad: float32 [2, 1536, 1536], P('section', 'tensor', 'dp')
- mlp_gain_grad: float32 [2, 1536], P('section')
- w_gate_grad: float32 [2, 1536, 4096], P('section', 'dp', 'tensor')
- w_up_grad: float32 [2, 1536, 4096], P('section', 'dp', 'tensor')
- w_down_grad: float32 [2, 4096, 1536], P('section', 'tensor', 'dp')
All inputs are finite; a program needn't handle non-finite values.
Results may differ from a plain program's by a relative error of at most 0.04.
Values may be sent and summed in bfloat16 or wider, within the bound.
No kernel may reach another device: no remote copies, remote signals or barrier semaphores. Data moves between devices by JAX's collectives and lax.ppermute only.
A program may use at most 448 MiB of HBM per device.

v0:
```python
import jax
import jax.numpy as jnp
from jax import lax
from jax.sharding import PartitionSpec as P

HEADS = 16
KV_HEADS = 8
HD = 96
L = 1024


epsilon = 1e-05
rope_base = 100000.0


def shifted(array, axis, by):
    size = lax.axis_size(axis)
    pairs = [(i, i + by) for i in range(size) if 0 <= i + by < size]
    return lax.ppermute(array, axis, pairs)


def rotate(values, positions, sign):
    half = values.shape[-1] // 2
    freqs = rope_base ** (-jnp.arange(half, dtype=jnp.float32) / half)
    angles = positions.astype(jnp.float32)[:, None] * freqs[None, :]
    cosine = jnp.cos(angles)[:, None, :]
    sine = sign * jnp.sin(angles)[:, None, :]
    first = values[..., :half]
    second = values[..., half:]
    return jnp.concatenate(
        [first * cosine - second * sine, second * cosine + first * sine], axis=-1
    )


def dot_rows(left, right):
    return jnp.dot(left, right, preferred_element_type=jnp.float32)


def dot_across(left, right):
    return lax.dot_general(
        left, right, (((1,), (1,)), ((), ())), preferred_element_type=jnp.float32
    )


def dot_inner(left, right):
    return lax.dot_general(
        left, right, (((0,), (0,)), ((), ())), preferred_element_type=jnp.float32
    )


def norm_forward(rows, gain):
    inverse = lax.rsqrt(jnp.mean(rows * rows, axis=-1, keepdims=True) + epsilon)
    return (rows * inverse * gain, inverse)


def norm_backward(rows, inverse, gain, grad):
    scaled = grad * gain
    gain_grad = jnp.sum(grad * rows * inverse, axis=0)
    mean_term = jnp.mean(scaled * rows, axis=-1, keepdims=True)
    return (scaled * inverse - rows * inverse * inverse * inverse * mean_term, gain_grad)


def gather_rows(rows):
    return lax.all_gather(rows, "tensor", axis=0, tiled=True)


def reduce_rows(left, right, across):
    share = left.shape[0] // lax.axis_size("tensor")

    def term(start, count):
        return dot_across(left, right) if across else dot_rows(left, right)

    return lax.psum_scatter(
        term(jnp.int32(0), lax.axis_size("tensor") * share).astype(jnp.bfloat16),
        "tensor",
        scatter_dimension=0,
        tiled=True,
    ).astype(jnp.float32)


def causal_mask():
    places = jnp.arange(L)
    return places[:, None] >= places[None, :]


def attention_forward(queries, keys, values):
    total, heads, size = queries.shape
    shape = (total // L, L, heads, size)
    scale = HD ** (-0.5)
    causal = causal_mask()

    def per_sequence(items):
        query_block, key_block, value_block = items
        scores = (
            jnp.einsum("qhd,khd->hqk", query_block, key_block, preferred_element_type=jnp.float32)
            * scale
        )
        scores = jnp.where(causal[None], scores, -1000000000.0)
        top = jnp.max(scores, axis=-1, keepdims=True)
        weights = jnp.exp(scores - top)
        totals = jnp.sum(weights, axis=-1, keepdims=True)
        probs = (weights / totals).astype(jnp.bfloat16)
        mixed = jnp.einsum("hqk,khd->qhd", probs, value_block, preferred_element_type=jnp.float32)
        return (mixed, (top + jnp.log(totals))[..., 0])

    mixed, log_totals = lax.map(
        per_sequence, (queries.reshape(shape), keys.reshape(shape), values.reshape(shape))
    )
    return (mixed.reshape(total, heads * size), log_totals)


def attention_backward(queries, keys, values, mixed_grad, log_totals):
    total, heads, size = queries.shape
    shape = (total // L, L, heads, size)
    scale = HD ** (-0.5)
    causal = causal_mask()

    def per_sequence(items):
        query_block, key_block, value_block, grad_block, log_block = items
        scores = (
            jnp.einsum("qhd,khd->hqk", query_block, key_block, preferred_element_type=jnp.float32)
            * scale
        )
        scores = jnp.where(causal[None], scores, -1000000000.0)
        probs = jnp.exp(scores - log_block[..., None])
        prob_grad = jnp.einsum(
            "qhd,khd->hqk", grad_block, value_block, preferred_element_type=jnp.float32
        )
        centre = jnp.sum(probs * prob_grad, axis=-1, keepdims=True)
        score_grad = (probs * (prob_grad - centre)).astype(jnp.bfloat16)
        query_grad = (
            jnp.einsum("hqk,khd->qhd", score_grad, key_block, preferred_element_type=jnp.float32)
            * scale
        )
        key_grad = (
            jnp.einsum("hqk,qhd->khd", score_grad, query_block, preferred_element_type=jnp.float32)
            * scale
        )
        value_grad = jnp.einsum(
            "hqk,qhd->khd",
            probs.astype(jnp.bfloat16),
            grad_block,
            preferred_element_type=jnp.float32,
        )
        return (query_grad, key_grad, value_grad)

    grads = lax.map(
        per_sequence,
        (
            queries.reshape(shape),
            keys.reshape(shape),
            values.reshape(shape),
            mixed_grad.reshape(shape),
            log_totals,
        ),
    )
    return tuple((block.reshape(total, heads, size) for block in grads))


def weight_terms(operands):
    return tuple((dot_inner(left, right) for left, right in operands))


def local(
    inputs, cotangent, attn_gain, w_query, w_key, w_value, w_out, mlp_gain, w_gate, w_up, w_down
):
    micro = inputs.shape[0]
    width = inputs.shape[2]
    section = lax.axis_index("section")
    first_section = section == 0
    heads_dev = w_query.shape[2] // HD
    groups = HEADS // KV_HEADS
    kv_dev = max(1, heads_dev // groups)
    copies = heads_dev // kv_dev
    kv_start = lax.axis_index("tensor") * heads_dev // groups
    query_width = heads_dev * HD
    kv_width = kv_dev * HD
    key_cols = lax.dynamic_slice_in_dim(w_key[0], kv_start * HD, kv_width, 1)
    value_cols = lax.dynamic_slice_in_dim(w_value[0], kv_start * HD, kv_width, 1)
    full_query, full_key, full_value, full_out, full_gate, full_up, full_down = (
        lax.all_gather(w_query[0], "dp", axis=0, tiled=True),
        lax.all_gather(key_cols, "dp", axis=0, tiled=True),
        lax.all_gather(value_cols, "dp", axis=0, tiled=True),
        lax.all_gather(w_out[0], "dp", axis=1, tiled=True),
        lax.all_gather(w_gate[0], "dp", axis=0, tiled=True),
        lax.all_gather(w_up[0], "dp", axis=0, tiled=True),
        lax.all_gather(w_down[0], "dp", axis=1, tiled=True),
    )
    ff_cols = full_gate.shape[1]
    attn_scale = attn_gain[0]
    mlp_scale = mlp_gain[0]

    def spread(columns):
        return jnp.repeat(columns.reshape(width, kv_dev, HD), copies, axis=1).reshape(
            width, query_width
        )

    w_projections = jnp.concatenate([full_query, full_key, full_value], axis=1)
    w_repeated = jnp.concatenate([full_query, spread(full_key), spread(full_value)], axis=1)
    w_gate_up = jnp.concatenate([full_gate, full_up], axis=1)

    def layer_backward(incoming_grad, kept):
        (
            rows,
            inverse,
            normed_bf,
            gathered,
            queries,
            keys,
            values,
            log_totals,
            mixed_bf,
            middle,
            inverse_mlp,
            normed_mlp_bf,
            mlp_rows,
            gate,
            upward,
            hidden,
        ) = kept
        out_grad = incoming_grad.astype(jnp.float32)
        grad_rows = gather_rows(incoming_grad)
        mlp_input = gather_rows(normed_mlp_bf)
        hidden_grad = dot_across(grad_rows, full_down)
        sigma = jax.nn.sigmoid(gate)
        gate_grad = hidden_grad * upward * (sigma * (1.0 + gate * (1.0 - sigma)))
        up_grad = hidden_grad * gate * sigma
        both_grad = jnp.concatenate([gate_grad, up_grad], axis=1).astype(jnp.bfloat16)
        mlp_back = reduce_rows(both_grad, w_gate_up, True)
        branch_grad, mlp_gain_grad = norm_backward(middle, inverse_mlp, mlp_scale, mlp_back)
        middle_grad = out_grad + branch_grad
        middle_rows = gather_rows(middle_grad.astype(jnp.bfloat16))
        mixed_grad = dot_across(middle_rows, full_out).astype(jnp.bfloat16)
        total = mixed_grad.shape[0]
        positions = jnp.arange(total) % L
        query_grad, key_grad, value_grad = attention_backward(
            queries, keys, values, mixed_grad.reshape(total, heads_dev, HD), log_totals
        )
        query_grad = rotate(query_grad, positions, -1.0).reshape(total, query_width)
        key_grad = rotate(key_grad, positions, -1.0).reshape(total, query_width)
        proj_grad = jnp.concatenate(
            [query_grad, key_grad, value_grad.reshape(total, query_width)], axis=1
        ).astype(jnp.bfloat16)
        attn_input = gather_rows(normed_bf)
        attn_back = reduce_rows(proj_grad, w_repeated, True)
        rows_grad, attn_gain_grad = norm_backward(rows, inverse, attn_scale, attn_back)
        outgoing = (middle_grad + rows_grad).astype(jnp.bfloat16)
        operands = (
            (attn_input, proj_grad),
            (mixed_bf, middle_rows),
            (mlp_input, both_grad),
            (hidden, grad_rows),
        )
        return (outgoing, operands, (attn_gain_grad, mlp_gain_grad))

    received = jnp.zeros(inputs.shape[1:], jnp.bfloat16)
    produced = []
    stored = []
    for tick_index in range(micro + 1):
        source = inputs[min(tick_index, micro - 1)]
        incoming = jnp.where(first_section, source, received)
        layer_rows = incoming.astype(jnp.float32)
        normed, layer_inverse = norm_forward(layer_rows, attn_scale)
        layer_normed_bf = normed.astype(jnp.bfloat16)
        layer_gathered = gather_rows(layer_normed_bf)
        layer_total = layer_gathered.shape[0]
        layer_positions = jnp.arange(layer_total) % L
        projected = dot_rows(layer_gathered, w_projections)
        layer_queries = rotate(
            projected[:, :query_width].reshape(layer_total, heads_dev, HD), layer_positions, 1.0
        ).astype(jnp.bfloat16)
        layer_keys = jnp.repeat(
            projected[:, query_width : query_width + kv_width].reshape(layer_total, kv_dev, HD),
            copies,
            axis=1,
        )
        layer_keys = rotate(layer_keys, layer_positions, 1.0).astype(jnp.bfloat16)
        layer_values = jnp.repeat(
            projected[:, query_width + kv_width :].reshape(layer_total, kv_dev, HD), copies, axis=1
        ).astype(jnp.bfloat16)
        mixed, layer_log_totals = attention_forward(layer_queries, layer_keys, layer_values)
        layer_mixed_bf = mixed.astype(jnp.bfloat16)
        layer_middle = layer_rows + reduce_rows(layer_mixed_bf, full_out, False)
        normed_mlp, layer_inverse_mlp = norm_forward(layer_middle, mlp_scale)
        layer_normed_mlp_bf = normed_mlp.astype(jnp.bfloat16)
        layer_mlp_rows = gather_rows(layer_normed_mlp_bf)
        both = dot_rows(layer_mlp_rows, w_gate_up)
        layer_gate = both[:, :ff_cols]
        layer_upward = both[:, ff_cols:]
        layer_hidden = (jax.nn.silu(layer_gate) * layer_upward).astype(jnp.bfloat16)
        branch = reduce_rows(layer_hidden, full_down, False)
        layer_outgoing = (layer_middle + branch).astype(jnp.bfloat16)
        kept_gathered = None
        kept_mlp = None
        layer_kept = (
            layer_rows,
            layer_inverse,
            layer_normed_bf,
            kept_gathered,
            layer_queries,
            layer_keys,
            layer_values,
            layer_log_totals,
            layer_mixed_bf,
            layer_middle,
            layer_inverse_mlp,
            layer_normed_mlp_bf,
            kept_mlp,
            layer_gate,
            layer_upward,
            layer_hidden,
        )
        outgoing = layer_outgoing
        kept = layer_kept
        produced.append(outgoing)
        stored.append(kept)
        if tick_index < micro:
            received = shifted(outgoing, "section", 1)
    returned = jnp.zeros(inputs.shape[1:], jnp.bfloat16)
    sent_back = []
    totals = None
    for tick_index in range(micro + 1):
        incoming_grad = jnp.where(
            first_section, returned, cotangent[max(micro - 1 - tick_index, 0)]
        )
        valid = jnp.where(
            first_section, jnp.float32(tick_index >= 1), jnp.float32(tick_index <= micro - 1)
        )
        kept = stored[micro - tick_index]
        outgoing_grad, operands, gains = layer_backward(incoming_grad, kept)
        terms = tuple((valid * term for term in weight_terms(operands) + gains))
        totals = (
            terms
            if totals is None
            else jax.tree.map(lambda earlier, later: earlier + later, totals, terms)
        )
        sent_back.append(outgoing_grad)
        if tick_index < micro:
            returned = shifted(outgoing_grad, "section", -1)
    input_grads = lax.dynamic_slice_in_dim(jnp.stack(sent_back[::-1]), section, micro, 0)[None]
    outputs = lax.dynamic_slice_in_dim(jnp.stack(produced), section, micro, 0)[None]
    proj_total, out_total, gate_up_total, down_total, attn_gain_total, mlp_gain_total = totals
    query_total = proj_total[:, :query_width]

    def fold(block):
        folded = block.reshape(width, kv_dev, copies, HD).sum(axis=2).reshape(width, kv_width)
        empty = jnp.zeros((width, KV_HEADS * HD), jnp.float32)
        return lax.dynamic_update_slice_in_dim(empty, folded, kv_start * HD, 1)

    key_total = fold(proj_total[:, query_width : 2 * query_width])
    value_total = fold(proj_total[:, 2 * query_width :])
    gate_total = gate_up_total[:, :ff_cols]
    up_total = gate_up_total[:, ff_cols:]
    query_part, out_part, gate_part, up_part, down_part = (
        lax.psum_scatter(
            query_total.astype(jnp.bfloat16), "dp", scatter_dimension=0, tiled=True
        ).astype(jnp.float32),
        lax.psum_scatter(
            out_total.astype(jnp.bfloat16), "dp", scatter_dimension=1, tiled=True
        ).astype(jnp.float32),
        lax.psum_scatter(
            gate_total.astype(jnp.bfloat16), "dp", scatter_dimension=0, tiled=True
        ).astype(jnp.float32),
        lax.psum_scatter(
            up_total.astype(jnp.bfloat16), "dp", scatter_dimension=0, tiled=True
        ).astype(jnp.float32),
        lax.psum_scatter(
            down_total.astype(jnp.bfloat16), "dp", scatter_dimension=1, tiled=True
        ).astype(jnp.float32),
    )
    key_sum, value_sum, attn_gain_sum, mlp_gain_sum = lax.psum(
        (key_total, value_total, attn_gain_total, mlp_gain_total), ("dp", "tensor")
    )
    share = width // lax.axis_size("dp")
    key_part = lax.dynamic_slice_in_dim(key_sum, lax.axis_index("dp") * share, share, 0)
    value_part = lax.dynamic_slice_in_dim(value_sum, lax.axis_index("dp") * share, share, 0)
    return (
        outputs,
        input_grads,
        attn_gain_sum[None],
        query_part[None],
        key_part[None],
        value_part[None],
        out_part[None],
        mlp_gain_sum[None],
        gate_part[None],
        up_part[None],
        down_part[None],
    )


def solution(mesh):
    in_specs = (
        P(None, ("dp", "tensor"), None),
        P(None, ("dp", "tensor"), None),
        P("section", None),
        P("section", "dp", "tensor"),
        P("section", "dp", None),
        P("section", "dp", None),
        P("section", "tensor", "dp"),
        P("section", None),
        P("section", "dp", "tensor"),
        P("section", "dp", "tensor"),
        P("section", "tensor", "dp"),
    )
    out_specs = (
        P("section", None, ("dp", "tensor"), None),
        P("section", None, ("dp", "tensor"), None),
        P("section", None),
        P("section", "dp", "tensor"),
        P("section", "dp", None),
        P("section", "dp", None),
        P("section", "tensor", "dp"),
        P("section", None),
        P("section", "dp", "tensor"),
        P("section", "dp", "tensor"),
        P("section", "tensor", "dp"),
    )
    return jax.shard_map(local, mesh=mesh, in_specs=in_specs, out_specs=out_specs, check_vma=False)
```

profile of v0, /device:TPU:0, one launch (start us, length us, event | category | flops | bytes accessed | tf_op | source)
XLA Modules:
  0.0 3844.1 jit_solution(15774168528636658373)
XLA Ops:
  39.0 60.0 %all-gather.34.cloned.1.call-done = bf16[1024,1536]{1,0:T(8,128)(2,1)} async-done(((bf16[256,1536]{1,0:T(8,128)(2,1)}), bf16[1024,1536]{1,0:T(8,128)(2,1)}) %all-gather.34.cloned.1.call-update) | async-done | bytes 3145744 | tf_op jit(solution)/shard_map/all_gather | solution.py:64
  253.9 65.7 %all-gather.36.cloned.1.call-done = bf16[1024,1536]{1,0:T(8,128)(2,1)} async-done(((bf16[256,1536]{1,0:T(8,128)(2,1)}), bf16[1024,1536]{1,0:T(8,128)(2,1)}) %all-gather.36.cloned.1.call-update) | async-done | bytes 3145744 | tf_op jit(solution)/shard_map/all_gather | solution.py:64
  355.0 60.4 %reduce-scatter.34.cloned.1.call-done = bf16[256,1536]{1,0:T(8,128)(2,1)} async-done(((bf16[1024,1536]{1,0:T(8,128)(2,1)}), bf16[256,1536]{1,0:T(8,128)(2,1)}) %reduce-scatter.34.cloned.1.call-update) | async-done | bytes 786448 | tf_op jit(solution)/shard_map/reduce_scatter | solution.py:73
  441.2 64.5 %all-gather.38.cloned.1.call-done = bf16[1024,1536]{1,0:T(8,128)(2,1)} async-done(((bf16[256,1536]{1,0:T(8,128)(2,1)}), bf16[1024,1536]{1,0:T(8,128)(2,1)}) %all-gather.38.cloned.1.call-update) | async-done | bytes 3145744 | tf_op jit(solution)/shard_map/all_gather | solution.py:64
  540.3 59.0 %reduce-scatter.36.cloned.1.call-done = bf16[256,1536]{1,0:T(8,128)(2,1)} async-done(((bf16[1024,1536]{1,0:T(8,128)(2,1)}), bf16[256,1536]{1,0:T(8,128)(2,1)}) %reduce-scatter.36.cloned.1.call-update) | async-done | bytes 786448 | tf_op jit(solution)/shard_map/reduce_scatter | solution.py:73
  603.4 63.5 %all-gather.40.cloned.1.call-done = bf16[1024,1536]{1,0:T(8,128)(2,1)} async-done(((bf16[256,1536]{1,0:T(8,128)(2,1)}), bf16[1024,1536]{1,0:T(8,128)(2,1)}) %all-gather.40.cloned.1.call-update) | async-done | bytes 3145744 | tf_op jit(solution)/shard_map/all_gather | solution.py:64
  686.8 59.0 %reduce-scatter.38.cloned.1.call-done = bf16[256,1536]{1,0:T(8,128)(2,1)} async-done(((bf16[1024,1536]{1,0:T(8,128)(2,1)}), bf16[256,1536]{1,0:T(8,128)(2,1)}) %reduce-scatter.38.cloned.1.call-update) | async-done | bytes 786448 | tf_op jit(solution)/shard_map/reduce_scatter | solution.py:73
  771.2 64.7 %all-gather.42.cloned.1.call-done = bf16[1024,1536]{1,0:T(8,128)(2,1)} async-done(((bf16[256,1536]{1,0:T(8,128)(2,1)}), bf16[1024,1536]{1,0:T(8,128)(2,1)}) %all-gather.42.cloned.1.call-update) | async-done | bytes 3145744 | tf_op jit(solution)/shard_map/all_gather | solution.py:64
  870.4 59.0 %reduce-scatter.40.cloned.1.call-done = bf16[256,1536]{1,0:T(8,128)(2,1)} async-done(((bf16[1024,1536]{1,0:T(8,128)(2,1)}), bf16[256,1536]{1,0:T(8,128)(2,1)}) %reduce-scatter.40.cloned.1.call-update) | async-done | bytes 786448 | tf_op jit(solution)/shard_map/reduce_scatter | solution.py:73
  933.5 63.4 %all-gather.44.cloned.1.call-done = bf16[1024,1536]{1,0:T(8,128)(2,1)} async-done(((bf16[256,1536]{1,0:T(8,128)(2,1)}), bf16[1024,1536]{1,0:T(8,128)(2,1)}) %all-gather.44.cloned.1.call-update) | async-done | bytes 3145744 | tf_op jit(solution)/shard_map/all_gather | solution.py:64
  1016.8 59.0 %reduce-scatter.42.cloned.1.call-done = bf16[256,1536]{1,0:T(8,128)(2,1)} async-done(((bf16[1024,1536]{1,0:T(8,128)(2,1)}), bf16[256,1536]{1,0:T(8,128)(2,1)}) %reduce-scatter.42.cloned.1.call-update) | async-done | bytes 786448 | tf_op jit(solution)/shard_map/reduce_scatter | solution.py:73
  1101.5 64.4 %all-gather.46.cloned.1.call-done = bf16[1024,1536]{1,0:T(8,128)(2,1)} async-done(((bf16[256,1536]{1,0:T(8,128)(2,1)}), bf16[1024,1536]{1,0:T(8,128)(2,1)}) %all-gather.46.cloned.1.call-update) | async-done | bytes 3145744 | tf_op jit(solution)/shard_map/all_gather | solution.py:64
  1200.5 59.0 %reduce-scatter.44.cloned.1.call-done = bf16[256,1536]{1,0:T(8,128)(2,1)} async-done(((bf16[1024,1536]{1,0:T(8,128)(2,1)}), bf16[256,1536]{1,0:T(8,128)(2,1)}) %reduce-scatter.44.cloned.1.call-update) | async-done | bytes 786448 | tf_op jit(solution)/shard_map/reduce_scatter | solution.py:73
  1263.5 63.5 %all-gather.48.cloned.1.call-done = bf16[1024,1536]{1,0:T(8,128)(2,1)} async-done(((bf16[256,1536]{1,0:T(8,128)(2,1)}), bf16[1024,1536]{1,0:T(8,128)(2,1)}) %all-gather.48.cloned.1.call-update) | async-done | bytes 3145744 | tf_op jit(solution)/shard_map/all_gather | solution.py:64
  1347.0 59.0 %reduce-scatter.46.cloned.1.call-done = bf16[256,1536]{1,0:T(8,128)(2,1)} async-done(((bf16[1024,1536]{1,0:T(8,128)(2,1)}), bf16[256,1536]{1,0:T(8,128)(2,1)}) %reduce-scatter.46.cloned.1.call-update) | async-done | bytes 786448 | tf_op jit(solution)/shard_map/reduce_scatter | solution.py:73
  1431.4 64.6 %all-gather.50.cloned.1.call-done = bf16[1024,1536]{1,0:T(8,128)(2,1)} async-done(((bf16[256,1536]{1,0:T(8,128)(2,1)}), bf16[1024,1536]{1,0:T(8,128)(2,1)}) %all-gather.50.cloned.1.call-update) | async-done | bytes 3145744 | tf_op jit(solution)/shard_map/all_gather | solution.py:64
  1595.8 61.2 %all-gather.52.cloned.1.call-done = bf16[1024,1536]{1,0:T(8,128)(2,1)} async-done(((bf16[256,1536]{1,0:T(8,128)(2,1)}), bf16[1024,1536]{1,0:T(8,128)(2,1)}) %all-gather.52.cloned.1.call-update) | async-done | bytes 3145744 | tf_op jit(solution)/shard_map/all_gather | solution.py:64
  1808.0 63.1 %all-gather.54.cloned.1.call-done = bf16[1024,1536]{1,0:T(8,128)(2,1)} async-done(((bf16[256,1536]{1,0:T(8,128)(2,1)}), bf16[1024,1536]{1,0:T(8,128)(2,1)}) %all-gather.54.cloned.1.call-update) | async-done | bytes 3145744 | tf_op jit(solution)/shard_map/all_gather | solution.py:64
  1922.6 59.0 %reduce-scatter.54.cloned.1.call-done = bf16[256,1536]{1,0:T(8,128)(2,1)} async-done(((bf16[1024,1536]{1,0:T(8,128)(2,1)}), bf16[256,1536]{1,0:T(8,128)(2,1)}) %reduce-scatter.54.cloned.1.call-update) | async-done | bytes 786448 | tf_op jit(solution)/shard_map/reduce_scatter | solution.py:73
  2010.8 62.7 %all-gather.56.cloned.1.call-done = bf16[1024,1536]{1,0:T(8,128)(2,1)} async-done(((bf16[256,1536]{1,0:T(8,128)(2,1)}), bf16[1024,1536]{1,0:T(8,128)(2,1)}) %all-gather.56.cloned.1.call-update) | async-done | bytes 3145744 | tf_op jit(solution)/shard_map/all_gather | solution.py:64
  2159.8 63.3 %all-gather.58.cloned.1.call-done = bf16[1024,1536]{1,0:T(8,128)(2,1)} async-done(((bf16[256,1536]{1,0:T(8,128)(2,1)}), bf16[1024,1536]{1,0:T(8,128)(2,1)}) %all-gather.58.cloned.1.call-update) | async-done | bytes 3145744 | tf_op jit(solution)/shard_map/all_gather | solution.py:64
  2274.0 59.0 %reduce-scatter.58.cloned.1.call-done = bf16[256,1536]{1,0:T(8,128)(2,1)} async-done(((bf16[1024,1536]{1,0:T(8,128)(2,1)}), bf16[256,1536]{1,0:T(8,128)(2,1)}) %reduce-scatter.58.cloned.1.call-update) | async-done | bytes 786448 | tf_op jit(solution)/shard_map/reduce_scatter | solution.py:73
  2362.1 62.8 %all-gather.60.cloned.1.call-done = bf16[1024,1536]{1,0:T(8,128)(2,1)} async-done(((bf16[256,1536]{1,0:T(8,128)(2,1)}), bf16[1024,1536]{1,0:T(8,128)(2,1)}) %all-gather.60.cloned.1.call-update) | async-done | bytes 3145744 | tf_op jit(solution)/shard_map/all_gather | solution.py:64
  2511.0 63.4 %all-gather.62.cloned.1.call-done = bf16[1024,1536]{1,0:T(8,128)(2,1)} async-done(((bf16[256,1536]{1,0:T(8,128)(2,1)}), bf16[1024,1536]{1,0:T(8,128)(2,1)}) %all-gather.62.cloned.1.call-update) | async-done | bytes 3145744 | tf_op jit(solution)/shard_map/all_gather | solution.py:64
  2625.0 59.0 %reduce-scatter.62.cloned.1.call-done = bf16[256,1536]{1,0:T(8,128)(2,1)} async-done(((bf16[1024,1536]{1,0:T(8,128)(2,1)}), bf16[256,1536]{1,0:T(8,128)(2,1)}) %reduce-scatter.62.cloned.1.call-update) | async-done | bytes 786448 | tf_op jit(solution)/shard_map/reduce_scatter | solution.py:73
  2713.4 62.5 %all-gather.64.cloned.1.call-done = bf16[1024,1536]{1,0:T(8,128)(2,1)} async-done(((bf16[256,1536]{1,0:T(8,128)(2,1)}), bf16[1024,1536]{1,0:T(8,128)(2,1)}) %all-gather.64.cloned.1.call-update) | async-done | bytes 3145744 | tf_op jit(solution)/shard_map/all_gather | solution.py:64
  2862.0 63.4 %all-gather.66.cloned.1.call-done = bf16[1024,1536]{1,0:T(8,128)(2,1)} async-done(((bf16[256,1536]{1,0:T(8,128)(2,1)}), bf16[1024,1536]{1,0:T(8,128)(2,1)}) %all-gather.66.cloned.1.call-update) | async-done | bytes 3145744 | tf_op jit(solution)/shard_map/all_gather | solution.py:64
  2976.0 59.0 %reduce-scatter.66.cloned.1.call-done = bf16[256,1536]{1,0:T(8,128)(2,1)} async-done(((bf16[1024,1536]{1,0:T(8,128)(2,1)}), bf16[256,1536]{1,0:T(8,128)(2,1)}) %reduce-scatter.66.cloned.1.call-update) | async-done | bytes 786448 | tf_op jit(solution)/shard_map/reduce_scatter | solution.py:73
  3064.4 62.5 %all-gather.68.cloned.1.call-done = bf16[1024,1536]{1,0:T(8,128)(2,1)} async-done(((bf16[256,1536]{1,0:T(8,128)(2,1)}), bf16[1024,1536]{1,0:T(8,128)(2,1)}) %all-gather.68.cloned.1.call-update) | async-done | bytes 3145744 | tf_op jit(solution)/shard_map/all_gather | solution.py:64
  3148.8 59.0 %reduce-scatter.68.cloned.1.call-done = bf16[256,1536]{1,0:T(8,128)(2,1)} async-done(((bf16[1024,1536]{1,0:T(8,128)(2,1)}), bf16[256,1536]{1,0:T(8,128)(2,1)}) %reduce-scatter.68.cloned.1.call-update) | async-done | bytes 786448 | tf_op jit(solution)/shard_map/reduce_scatter | solution.py:73
  3518.8 187.3 %all-reduce.4.cloned.1.call-done = (f32[1536,768]{0,1:T(8,128)}, f32[1536,768]{0,1:T(8,128)}) async-done(((f32[1536,768]{0,1:T(8,128)}, f32[1536,768]{0,1:T(8,128)}), (f32[1536,768]{0,1:T(8,128)}, f32[1536,768]{0,1:T(8,128)})) %all-reduce.4.cloned.1.call-update) | async-done | bytes 9437200 | tf_op jit(solution)/shard_map/psum | solution.py:371
  3776.5 60.6 %all-reduce = (f32[1,1536]{1,0:T(1,128)}, f32[1,1536]{1,0:T(1,128)}) all-reduce(f32[1,1536]{1,0:T(1,128)S(1)} %broadcast_in_dim.428, f32[1,1536]{1,0:T(1,128)S(1)} %broadcast_in_dim.435), channel_id=1, replica_groups=mesh['section'=2,'dp'=4,'tensor'=4] {'dp','tensor'}, use_global_device_ids=true, to_apply=%region_60.61 | all-reduce | flops 3072 | bytes 24576 | tf_op jit(solution)/shard_map/psum | solution.py:371
  (988 shorter events, 1729.0 us)
Async XLA Ops:
  14.9 178.9 %reduce-scatter.32.cloned.1.call-start = ((), (), s32[]{:S(2)}) async-start(), calls=%async_computation.26 | async-start | bytes 3932160 | tf_op jit(solution)/shard_map/reduce_scatter | solution.py:73
  136.0 183.5 %all-gather.36.cloned.1.call-start = ((), (), s32[]{:S(2)}) async-start(), calls=%async_computation.27 | async-start | bytes 3932160 | tf_op jit(solution)/shard_map/all_gather | solution.py:64
  198.3 150.0 %all-gather.80.cloned.1.call-start = ((), (), s32[]{:S(2)}) async-start(), calls=%async_computation.70 | async-start | bytes 3932160 | tf_op jit(solution)/shard_map/all_gather | solution.py:187
  199.0 216.3 %reduce-scatter.34.cloned.1.call-start = ((), (), s32[]{:S(2)}) async-start(), calls=%async_computation.28 | async-start | bytes 3932160 | tf_op jit(solution)/shard_map/reduce_scatter | solution.py:73
  354.9 150.8 %all-gather.38.cloned.1.call-start = ((), (), s32[]{:S(2)}) async-start(), calls=%async_computation.29 | async-start | bytes 3932160 | tf_op jit(solution)/shard_map/all_gather | solution.py:64
  440.8 158.5 %reduce-scatter.36.cloned.1.call-start = ((), (), s32[]{:S(2)}) async-start(), calls=%async_computation.30 | async-start | bytes 3932160 | tf_op jit(solution)/shard_map/reduce_scatter | solution.py:73
  686.8 149.1 %all-gather.42.cloned.1.call-start = ((), (), s32[]{:S(2)}) async-start(), calls=%async_computation.33 | async-start | bytes 3932160 | tf_op jit(solution)/shard_map/all_gather | solution.py:64
  770.9 158.4 %reduce-scatter.40.cloned.1.call-start = ((), (), s32[]{:S(2)}) async-start(), calls=%async_computation.34 | async-start | bytes 3932160 | tf_op jit(solution)/shard_map/reduce_scatter | solution.py:73
  1016.8 149.1 %all-gather.46.cloned.1.call-start = ((), (), s32[]{:S(2)}) async-start(), calls=%async_computation.37 | async-start | bytes 3932160 | tf_op jit(solution)/shard_map/all_gather | solution.py:64
  1100.9 158.6 %reduce-scatter.44.cloned.1.call-start = ((), (), s32[]{:S(2)}) async-start(), calls=%async_computation.38 | async-start | bytes 3932160 | tf_op jit(solution)/shard_map/reduce_scatter | solution.py:73
  1263.3 142.7 %reduce-scatter.46.cloned.1.call-start = ((), (), s32[]{:S(2)}) async-start(), calls=%async_computation.40 | async-start | bytes 3932160 | tf_op jit(solution)/shard_map/reduce_scatter | solution.py:73
  1347.0 149.1 %all-gather.50.cloned.1.call-start = ((), (), s32[]{:S(2)}) async-start(), calls=%async_computation.41 | async-start | bytes 3932160 | tf_op jit(solution)/shard_map/all_gather | solution.py:64
  1431.1 158.4 %reduce-scatter.48.cloned.1.call-start = ((), (), s32[]{:S(2)}) async-start(), calls=%async_computation.42 | async-start | bytes 3932160 | tf_op jit(solution)/shard_map/reduce_scatter | solution.py:73
  1595.5 206.6 %reduce-scatter.52.cloned.1.call-start = ((), (), s32[]{:S(2)}) async-start(), calls=%async_computation.45 | async-start | bytes 3932160 | tf_op jit(solution)/shard_map/reduce_scatter | solution.py:73
  1807.4 174.2 %reduce-scatter.54.cloned.1.call-start = ((), (), s32[]{:S(2)}) async-start(), calls=%async_computation.47 | async-start | bytes 3932160 | tf_op jit(solution)/shard_map/reduce_scatter | solution.py:73
  1922.5 151.0 %all-gather.56.cloned.1.call-start = ((), (), s32[]{:S(2)}) async-start(), calls=%async_computation.48 | async-start | bytes 3932160 | tf_op jit(solution)/shard_map/all_gather | solution.py:64
  2010.5 143.8 %reduce-scatter.56.cloned.1.call-start = ((), (), s32[]{:S(2)}) async-start(), calls=%async_computation.49 | async-start | bytes 3932160 | tf_op jit(solution)/shard_map/reduce_scatter | solution.py:73
  2159.4 173.6 %reduce-scatter.58.cloned.1.call-start = ((), (), s32[]{:S(2)}) async-start(), calls=%async_computation.51 | async-start | bytes 3932160 | tf_op jit(solution)/shard_map/reduce_scatter | solution.py:73
  2273.9 150.9 %all-gather.60.cloned.1.call-start = ((), (), s32[]{:S(2)}) async-start(), calls=%async_computation.52 | async-start | bytes 3932160 | tf_op jit(solution)/shard_map/all_gather | solution.py:64
  2361.9 143.8 %reduce-scatter.60.cloned.1.call-start = ((), (), s32[]{:S(2)}) async-start(), calls=%async_computation.53 | async-start | bytes 3932160 | tf_op jit(solution)/shard_map/reduce_scatter | solution.py:73
  2510.7 173.3 %reduce-scatter.62.cloned.1.call-start = ((), (), s32[]{:S(2)}) async-start(), calls=%async_computation.55 | async-start | bytes 3932160 | tf_op jit(solution)/shard_map/reduce_scatter | solution.py:73
  2624.9 150.9 %all-gather.64.cloned.1.call-start = ((), (), s32[]{:S(2)}) async-start(), calls=%async_computation.56 | async-start | bytes 3932160 | tf_op jit(solution)/shard_map/all_gather | solution.py:64
  2712.9 143.8 %reduce-scatter.64.cloned.1.call-start = ((), (), s32[]{:S(2)}) async-start(), calls=%async_computation.57 | async-start | bytes 3932160 | tf_op jit(solution)/shard_map/reduce_scatter | solution.py:73
  2861.7 173.4 %reduce-scatter.66.cloned.1.call-start = ((), (), s32[]{:S(2)}) async-start(), calls=%async_computation.59 | async-start | bytes 3932160 | tf_op jit(solution)/shard_map/reduce_scatter | solution.py:73
  2976.0 151.0 %all-gather.68.cloned.1.call-start = ((), (), s32[]{:S(2)}) async-start(), calls=%async_computation.60 | async-start | bytes 3932160 | tf_op jit(solution)/shard_map/all_gather | solution.py:64
  3064.0 143.8 %reduce-scatter.68.cloned.1.call-start = ((), (), s32[]{:S(2)}) async-start(), calls=%async_computation.61 | async-start | bytes 3932160 | tf_op jit(solution)/shard_map/reduce_scatter | solution.py:73
  3148.7 211.9 %all-gather.70.cloned.1.call-start = ((), (), s32[]{:S(2)}) async-start(), calls=%async_computation.62 | async-start | bytes 3932160 | tf_op jit(solution)/shard_map/all_gather | solution.py:64
  3213.4 243.8 %reduce-scatter.50.cloned.1.call-start = ((), (), s32[]{:S(2)}) async-start(), calls=%async_computation.44 | async-start | bytes 3932160 | tf_op jit(solution)/shard_map/reduce_scatter | solution.py:73
  3221.1 243.7 %reduce-scatter.80.cloned.1.call-start = ((), (), s32[]{:S(2)}) async-start(), calls=%async_computation.74 | async-start | bytes 3932160
  3277.1 190.4 %reduce-scatter.72.cloned.1.call-start = ((), (), s32[]{:S(2)}) async-start(), calls=%async_computation.64 | async-start | bytes 3932160 | tf_op jit(solution)/shard_map/reduce_scatter | solution.py:361
  3431.4 274.7 %all-reduce.4.cloned.1.call-start = ((), (), s32[]{:S(2)}) async-start(), calls=%async_computation.75 | async-start | bytes 18874368 | tf_op jit(solution)/shard_map/psum | solution.py:371
  3447.7 321.0 %reduce-scatter.70.cloned.1.call-start = ((), (), s32[]{:S(2)}) async-start(), calls=%async_computation.63 | async-start | bytes 3932160 | tf_op jit(solution)/shard_map/reduce_scatter | solution.py:73
  (313 other events, 19482.9 us)
Sparse Core Ops, SparseCore 0:
  34.6 64.3 all-gather.33
  256.0 63.4 all-gather.35
  355.0 60.2 reduce-scatter.33
  440.9 64.7 all-gather.37
  603.2 63.5 all-gather.39
  771.1 64.7 all-gather.41
  870.4 58.8 reduce-scatter.39
  933.3 63.5 all-gather.43
  1016.9 58.8 reduce-scatter.41
  1101.1 64.7 all-gather.45
  1200.6 58.8 reduce-scatter.43
  1263.4 63.5 all-gather.47
  1431.3 64.7 all-gather.49
  1593.5 63.5 all-gather.51
  1659.2 62.1 all-gather.81
  1807.5 63.5 all-gather.53
  1922.6 58.8 reduce-scatter.53
  2010.6 62.8 all-gather.55
  2095.4 58.8 reduce-scatter.55
  2159.5 63.5 all-gather.57
  2274.0 58.8 reduce-scatter.57
  2362.0 62.8 all-gather.59
  2510.8 63.5 all-gather.61
  2625.0 58.8 reduce-scatter.61
  2713.0 62.8 all-gather.63
  2861.8 63.5 all-gather.65
  2976.1 58.8 reduce-scatter.65
  3064.1 62.8 all-gather.67
  3148.8 58.8 reduce-scatter.67
  3213.5 63.5 all-gather.69
  3520.9 185.1 all-reduce.3
  3708.3 60.3 reduce-scatter.69
  (19 shorter events, 816.9 us)
where the time goes:
time: 3860 us; the launch traced here: 3840 us
  waiting for transfers between devices  2750 us (71%)
  matrix products  633 us (16%)
  other arithmetic  217 us (6%)
  local copies, waits for them, and re-layouts  113 us (3%)
  blocking collectives  80.1 us (2%)
    all_gather x20, waiting for transfers between devices, gather_rows(): return lax.all_gather(rows, 'tensor', axis=0, tiled=True)  1190 us
    reduce_scatter x20, waiting for transfers between devices, reduce_rows(): lax.psum_scatter(term(jnp.int32(0), lax.axis_size('tensor') * share).asty...  1120 us
    psum x1, waiting for transfers between devices, local(): lax.psum((key_total, value_total, attn_gain_total, mlp_gain_total), ('dp'...  187 us
    dot_general x20, matrix products, dot_across(): lax.dot_general(left, right, (((1,), (1,)), ((), ())), preferred_element_...  148 us
    ppermute x8, waiting for transfers between devices, shifted(): return lax.ppermute(array, axis, pairs)  145 us
    dot_general x20, matrix products, dot_inner(): lax.dot_general(left, right, (((0,), (0,)), ((), ())), preferred_element_...  142 us
    dot_general x20, matrix products, dot_rows(): return jnp.dot(left, right, preferred_element_type=jnp.float32)  123 us
    unnamed x585, local copies, waits for them, and re-layouts  77.5 us
  transfers between devices with their start and end apart: 59, of which 52 were waited for; matrix products, arithmetic and copies ran while one was open for 8% of the time, Pallas kernels for 0%

commit v1 on v0

v1 whole, which is shorter than its diff:
```python
import jax
import jax.numpy as jnp
from jax import lax
from jax.sharding import PartitionSpec as P

HEADS = 16
KV_HEADS = 8
HD = 96
L = 1024

epsilon = 1e-05
rope_base = 100000.0
bf16 = jnp.bfloat16
f32 = jnp.float32


def shifted(array, axis, by):
    size = lax.axis_size(axis)
    pairs = [(i, i + by) for i in range(size) if 0 <= i + by < size]
    return lax.ppermute(array, axis, pairs)


def swapped(array, axis, bit):
    return lax.ppermute(array, axis, [(i, i ^ bit) for i in range(lax.axis_size(axis))])


def bits_of(size):
    return [1 << k for k in range(size.bit_length() - 1)]


def rotate(values, cosine, sine):
    half = values.shape[-1] // 2
    first = values[..., :half]
    second = values[..., half:]
    return jnp.concatenate(
        [first * cosine - second * sine, second * cosine + first * sine], axis=-1
    )


def mm(left, right):
    return jnp.dot(left, right, preferred_element_type=f32)


def mm_nt(left, right):
    return lax.dot_general(
        left, right, (((1,), (1,)), ((), ())), preferred_element_type=f32
    )


def mm_tn(left, right):
    return lax.dot_general(
        left, right, (((0,), (0,)), ((), ())), preferred_element_type=f32
    )


def norm_forward(rows, gain):
    inverse = lax.rsqrt(jnp.mean(rows * rows, axis=-1, keepdims=True) + epsilon)
    return (rows * inverse * gain, inverse)


def norm_backward(rows, inverse, gain, grad):
    scaled = grad * gain
    mean_term = jnp.mean(scaled * rows, axis=-1, keepdims=True)
    return scaled * inverse - rows * inverse * inverse * inverse * mean_term


def gain_sum(rows, inverse, grad):
    return jnp.sum(grad * rows * inverse, axis=0)


def attention_forward(queries, keys, values, causal):
    scale = HD ** (-0.5)

    def per_head(items):
        q, k, v = items
        scores = jnp.einsum("cqd,kd->cqk", q, k, preferred_element_type=f32) * scale
        scores = jnp.where(causal[None], scores, -1000000000.0)
        top = jnp.max(scores, axis=-1, keepdims=True)
        weights = jnp.exp(scores - top)
        totals = jnp.sum(weights, axis=-1, keepdims=True)
        probs = (weights / totals).astype(bf16)
        mixed = jnp.einsum("cqk,kd->cqd", probs, v, preferred_element_type=f32)
        return (mixed.astype(bf16), top + jnp.log(totals))

    return lax.map(per_head, (queries, keys, values))


def attention_backward(queries, keys, values, mixed_grad, log_totals, causal):
    scale = HD ** (-0.5)

    def per_head(items):
        q, k, v, g, lse = items
        scores = jnp.einsum("cqd,kd->cqk", q, k, preferred_element_type=f32) * scale
        scores = jnp.where(causal[None], scores, -1000000000.0)
        probs = jnp.exp(scores - lse)
        prob_grad = jnp.einsum("cqd,kd->cqk", g, v, preferred_element_type=f32)
        centre = jnp.sum(probs * prob_grad, axis=-1, keepdims=True)
        score_grad = (probs * (prob_grad - centre)).astype(bf16)
        query_grad = jnp.einsum("cqk,kd->cqd", score_grad, k, preferred_element_type=f32) * scale
        key_grad = jnp.einsum("cqk,cqd->kd", score_grad, q, preferred_element_type=f32) * scale
        value_grad = jnp.einsum("cqk,cqd->kd", probs.astype(bf16), g, preferred_element_type=f32)
        return (query_grad, key_grad, value_grad)

    return lax.map(per_head, (queries, keys, values, mixed_grad, log_totals))


def local(
    inputs, cotangent, attn_gain, w_query, w_key, w_value, w_out, mlp_gain, w_gate, w_up, w_down
):
    micro, nloc, width = inputs.shape
    tsize = lax.axis_size("tensor")
    dsize = lax.axis_size("dp")
    ranks = tsize // micro
    n = nloc * micro
    share = width // dsize
    first_section = lax.axis_index("section") == 0
    t = lax.axis_index("tensor")
    d = lax.axis_index("dp")
    seq = t % micro
    seg = t // micro
    copies = HEADS // KV_HEADS
    dims = KV_HEADS * HD
    same_seq = [[g + micro * r for r in range(ranks)] for g in range(micro)]

    def exchange(blocks):
        out = blocks
        for j in range(1, micro):
            sent = lax.dynamic_index_in_dim(blocks, seq ^ j, 0, keepdims=True)
            got = swapped(sent, "tensor", j)
            out = lax.dynamic_update_slice_in_dim(out, got, seq ^ j, 0)
        return out

    def reorder(array, axis):
        return jnp.concatenate(
            [lax.dynamic_slice_in_dim(array, (d ^ m) * share, share, axis) for m in range(dsize)],
            axis=axis,
        )

    def spread_rows(block):
        parts = {0: block}
        for bit in reversed(bits_of(dsize)):
            for m in sorted(parts):
                parts[m ^ bit] = swapped(parts[m], "dp", bit)
        return jnp.concatenate([parts[m] for m in range(dsize)], axis=0)

    def gather_weight(shard):
        whole = lax.all_gather(shard, "tensor", axis=0)
        whole = whole.transpose(1, 0, 2).reshape(share, tsize * shard.shape[1])
        return spread_rows(whole)

    def sum_rows(grad):
        parts = {m: grad[m * share : (m + 1) * share].astype(bf16) for m in range(dsize)}
        for bit in bits_of(dsize):
            for m in sorted(parts):
                if m & bit:
                    continue
                got = swapped(parts[m ^ bit], "dp", bit)
                parts[m] = (parts[m].astype(f32) + got.astype(f32)).astype(bf16)
            parts = {m: part for m, part in parts.items() if not m & bit}
        return parts[0]

    def scatter_weight(grad):
        part = sum_rows(grad)
        part = part.reshape(share, tsize, -1).transpose(1, 0, 2)
        return lax.psum_scatter(part, "tensor", scatter_dimension=0)

    rows_in = reorder(exchange(inputs).reshape(n, width), 1)
    attn_scale = reorder(attn_gain[0], 0)
    mlp_scale = reorder(mlp_gain[0], 0)

    wq = gather_weight(w_query[0])
    wkv = spread_rows(jnp.concatenate([w_key[0], w_value[0]], axis=1))
    wo = gather_weight(w_out[0].T)
    wg = gather_weight(w_gate[0])
    wu = gather_weight(w_up[0])
    wd = gather_weight(w_down[0].T)
    cot = reorder(exchange(cotangent).reshape(n, width), 1)

    places = seg * n + jnp.arange(n)
    half = HD // 2
    freqs = rope_base ** (-jnp.arange(half, dtype=f32) / half)
    angles = places.astype(f32)[:, None] * freqs[None, :]
    cosine = jnp.cos(angles)
    sine = jnp.sin(angles)
    causal = places[:, None] >= jnp.arange(L)[None, :]

    def all_keys(array):
        if ranks == 1:
            return array
        return lax.all_gather(
            array, "tensor", axis=1, tiled=True, axis_index_groups=same_seq
        )

    def own_keys(array):
        if ranks == 1:
            return array
        return lax.psum_scatter(
            array.astype(bf16),
            "tensor",
            scatter_dimension=1,
            tiled=True,
            axis_index_groups=same_seq,
        ).astype(f32)

    def forward(rows_bf):
        rows = rows_bf.astype(f32)
        normed, inverse = norm_forward(rows, attn_scale)
        normed = normed.astype(bf16)
        queries = mm(normed, wq).reshape(n, KV_HEADS, copies, HD).transpose(1, 2, 0, 3)
        queries = rotate(queries, cosine, sine).astype(bf16)
        both = mm(normed, wkv)
        keys = both[:, :dims].reshape(n, KV_HEADS, HD).transpose(1, 0, 2)
        keys = all_keys(rotate(keys, cosine, sine).astype(bf16))
        values = both[:, dims:].reshape(n, KV_HEADS, HD).transpose(1, 0, 2)
        values = all_keys(values.astype(bf16))
        mixed, log_totals = attention_forward(queries, keys, values, causal)
        mixed = mixed.transpose(2, 0, 1, 3).reshape(n, HEADS * HD)
        middle = rows + mm_nt(mixed, wo)
        normed_mlp, inverse_mlp = norm_forward(middle, mlp_scale)
        normed_mlp = normed_mlp.astype(bf16)
        gate = mm(normed_mlp, wg)
        upward = mm(normed_mlp, wu)
        hidden = (jax.nn.silu(gate) * upward).astype(bf16)
        outgoing = (middle + mm_nt(hidden, wd)).astype(bf16)
        kept = (
            rows_bf, inverse, normed, queries, keys, values, log_totals, mixed,
            middle, inverse_mlp, normed_mlp, gate.astype(bf16), upward.astype(bf16), hidden,
        )
        return outgoing, kept

    def backward(grad, kept, weights_too):
        (
            rows_bf, inverse, normed, queries, keys, values, log_totals, mixed,
            middle, inverse_mlp, normed_mlp, gate, upward, hidden,
        ) = kept
        rows = rows_bf.astype(f32)
        gate = gate.astype(f32)
        upward = upward.astype(f32)
        done = []
        if weights_too:
            done.append(scatter_weight(mm_tn(grad, hidden)))
        hidden_grad = mm(grad, wd)
        sigma = jax.nn.sigmoid(gate)
        gate_grad = (hidden_grad * upward * (sigma * (1.0 + gate * (1.0 - sigma)))).astype(bf16)
        up_grad = (hidden_grad * gate * sigma).astype(bf16)
        if weights_too:
            done.append(scatter_weight(mm_tn(normed_mlp, gate_grad)))
            done.append(scatter_weight(mm_tn(normed_mlp, up_grad)))
        mlp_back = mm_nt(gate_grad, wg) + mm_nt(up_grad, wu)
        middle_grad = grad.astype(f32) + norm_backward(middle, inverse_mlp, mlp_scale, mlp_back)
        middle_bf = middle_grad.astype(bf16)
        if weights_too:
            done.append(scatter_weight(mm_tn(middle_bf, mixed)))
        mixed_grad = mm(middle_bf, wo).astype(bf16)
        mixed_grad = mixed_grad.reshape(n, KV_HEADS, copies, HD).transpose(1, 2, 0, 3)
        dq, dk, dv = attention_backward(queries, keys, values, mixed_grad, log_totals, causal)
        dk = own_keys(dk)
        dv = own_keys(dv)
        dq = rotate(dq, cosine, -sine).transpose(2, 0, 1, 3).reshape(n, HEADS * HD).astype(bf16)
        dk = rotate(dk, cosine, -sine).transpose(1, 0, 2).reshape(n, dims)
        dkv = jnp.concatenate([dk, dv.transpose(1, 0, 2).reshape(n, dims)], axis=1).astype(bf16)
        if weights_too:
            done.append(scatter_weight(mm_tn(normed, dq)))
            done.append(scatter_weight(mm_tn(normed, dkv)))
        attn_back = mm_nt(dq, wq) + mm_nt(dkv, wkv)
        outgoing = middle_grad + norm_backward(rows, inverse, attn_scale, attn_back)
        if weights_too:
            done.append(gain_sum(rows, inverse, attn_back))
            done.append(gain_sum(middle, inverse_mlp, mlp_back))
        return outgoing.astype(bf16), done

    first_out, _ = forward(rows_in)
    received = shifted(first_out, "section", 1)
    second_out, kept = forward(jnp.where(first_section, rows_in, received))
    first_grad, _ = backward(cot, kept, False)
    returned = shifted(first_grad, "section", -1)
    second_grad, done = backward(jnp.where(first_section, returned, cot), kept, True)

    def to_places(rows):
        return exchange(reorder(rows, 1).reshape(micro, nloc, width))[None]

    outputs = to_places(second_out)
    input_grads = to_places(second_grad)
    down, gate, up, out, query, kv, attn_sum, mlp_sum = done
    kv = lax.all_gather(kv, "tensor", axis=0).transpose(1, 0, 2).reshape(share, 2 * dims)
    gains = jnp.stack([reorder(attn_sum, 0), reorder(mlp_sum, 0)])
    gains = lax.psum(gains, ("dp", "tensor"))
    return (
        outputs,
        input_grads,
        gains[:1],
        query.astype(f32)[None],
        kv[:, :dims].astype(f32)[None],
        kv[:, dims:].astype(f32)[None],
        out.astype(f32).T[None],
        gains[1:],
        gate.astype(f32)[None],
        up.astype(f32)[None],
        down.astype(f32).T[None],
    )


def solution(mesh):
    in_specs = (
        P(None, ("dp", "tensor"), None),
        P(None, ("dp", "tensor"), None),
        P("section", None),
        P("section", "dp", "tensor"),
        P("section", "dp", None),
        P("section", "dp", None),
        P("section", "tensor", "dp"),
        P("section", None),
        P("section", "dp", "tensor"),
        P("section", "dp", "tensor"),
        P("section", "tensor", "dp"),
    )
    out_specs = (
        P("section", None, ("dp", "tensor"), None),
        P("section", None, ("dp", "tensor"), None),
        P("section", None),
        P("section", "dp", "tensor"),
        P("section", "dp", None),
        P("section", "dp", None),
        P("section", "tensor", "dp"),
        P("section", None),
        P("section", "dp", "tensor"),
        P("section", "dp", "tensor"),
        P("section", "tensor", "dp"),
    )
    return jax.shard_map(local, mesh=mesh, in_specs=in_specs, out_specs=out_specs, check_vma=False)
```

time: 3860 us -> 2060 us (0.53)
  waiting for transfers between devices: 2750 us -> 579 us
  matrix products: 633 us -> 873 us
  blocking collectives: 80.1 us -> 148 us
  local copies, waits for them, and re-layouts: 113 us -> 171 us
    all_gather x25 -> x6, waiting for transfers between devices: 1260 us -> 75 us  [the longest x5 75 us: gather_weight(): whole = lax.all_gather(shard, 'tensor', axis=0)]
    reduce_scatter x22 -> x6, waiting for transfers between devices: 1120 us -> 0.01 us  [scatter_weight(): return lax.psum_scatter(part, 'tensor', scatter_dimension=0)]
    ppermute x0 -> x48, waiting for transfers between devices: none -> 386 us  [swapped(): lax.ppermute(array, axis, [(i, i ^ bit) for i in range(lax.axis_size(axis...]
    psum x1 -> x0, waiting for transfers between devices: 187 us -> none  [local(): lax.psum((key_total, value_total, attn_gain_total, mlp_gain_total), ('dp'...]
    dot_general x90 -> x134, matrix products: 633 us -> 814 us  [the longest x12 206 us: mm_nt(): lax.dot_general(left, right, (((1,), (1,)), ((), ())), preferred_element_...]
    psum x1, blocking collectives: 60.6 us -> 148 us  [local(): gains = lax.psum(gains, ('dp', 'tensor'))]
    sub x0 -> x8, matrix products: none -> 59.8 us  [per_head(): weights = jnp.exp(scores - top)]
    reduce_sum x17 -> x8, other arithmetic: 66.6 us -> 16 us  [per_head(): totals = jnp.sum(weights, axis=-1, keepdims=True)]
  transfers between devices with their start and end apart: 59 -> 62, of which waited for: 52 -> 16; matrix products, arithmetic and copies ran while one was open for 8% -> 23% of each run, Pallas kernels for 0% -> 0%
where the time goes in v1:
time: 2060 us; the launch traced here: 2030 us
  matrix products  873 us (42%)
  waiting for transfers between devices  579 us (28%)
  other arithmetic  203 us (10%)
  local copies, waits for them, and re-layouts  171 us (8%)
  blocking collectives  148 us (7%)
  starting transfers between devices  41.9 us (2%)
    ppermute x48, waiting for transfers between devices, swapped(): lax.ppermute(array, axis, [(i, i ^ bit) for i in range(lax.axis_size(axis...  386 us
    dot_general x12, matrix products, mm_nt(): lax.dot_general(left, right, (((1,), (1,)), ((), ())), preferred_element_...  206 us
    dot_general x12, matrix products, mm(): return jnp.dot(left, right, preferred_element_type=f32)  195 us
    psum x1, blocking collectives, local(): gains = lax.psum(gains, ('dp', 'tensor'))  148 us
    ppermute x2, waiting for transfers between devices, shifted(): return lax.ppermute(array, axis, pairs)  118 us
    dot_general x16, matrix products, per_head(): mixed = jnp.einsum('cqk,kd->cqd', probs, v, preferred_element_type=f32)  76.7 us
    dot_general x6, matrix products, mm_tn(): lax.dot_general(left, right, (((0,), (0,)), ((), ())), preferred_element_...  75.2 us
    all_gather x5, waiting for transfers between devices, gather_weight(): whole = lax.all_gather(shard, 'tensor', axis=0)  75 us
  transfers between devices with their start and end apart: 62, of which 16 were waited for; matrix products, arithmetic and copies ran while one was open for 23% of the time, Pallas kernels for 0%

profile of v1, /device:TPU:0, one launch (start us, length us, event | category | flops | bytes accessed | tf_op | source)
XLA Modules:
  0.0 2033.6 jit_solution(16298960541261938382)
XLA Ops:
  28.1 30.8 %collective-permute-done.25 = bf16[1,256,1536]{2,1,0:T(8,128)(2,1)} collective-permute-done((bf16[1,256,1536]{2,1,0:T(8,128)(2,1)}, bf16[1,256,1536]{2,1,0:T(8,128)(2,1)}, u32[]{:S(2)}, u32[]{:S(2)}) %collective-permute-start.25) | collective-permute-done | bytes 786464 | tf_op jit(solution)/shard_map/ppermute | solution.py:24
  66.5 35.2 %collective-permute-done = bf16[1,256,1536]{2,1,0:T(8,128)(2,1)} collective-permute-done((bf16[1,256,1536]{2,1,0:T(8,128)(2,1)}, bf16[1,256,1536]{2,1,0:T(8,128)(2,1)}, u32[]{:S(2)}, u32[]{:S(2)}) %collective-permute-start) | collective-permute-done | bytes 786464 | tf_op jit(solution)/shard_map/ppermute | solution.py:24
  111.7 56.3 %collective-permute-done.26 = bf16[1,256,1536]{2,1,0:T(8,128)(2,1)} collective-permute-done((bf16[1,256,1536]{2,1,0:T(8,128)(2,1)}, bf16[1,256,1536]{2,1,0:T(8,128)(2,1)}, u32[]{:S(2)}, u32[]{:S(2)}) %collective-permute-start.26) | collective-permute-done | bytes 786464 | tf_op jit(solution)/shard_map/ppermute | solution.py:24
  172.2 75.6 %collective-permute-done.1 = bf16[1,256,1536]{2,1,0:T(8,128)(2,1)} collective-permute-done((bf16[1,256,1536]{2,1,0:T(8,128)(2,1)}, bf16[1,256,1536]{2,1,0:T(8,128)(2,1)}, u32[]{:S(2)}, u32[]{:S(2)}) %collective-permute-start.1) | collective-permute-done | bytes 786464 | tf_op jit(solution)/shard_map/ppermute | solution.py:24
  307.9 17.5 all-gather.19.cloned.1.call-done
  331.5 57.5 %all-gather.11.cloned.1.call-done = bf16[4,384,1024]{2,1,0:T(8,128)(2,1)} async-done(((bf16[1,384,1024]{2,1,0:T(8,128)(2,1)}), bf16[4,384,1024]{2,1,0:T(8,128)(2,1)}) %all-gather.11.cloned.1.call-update) | async-done | bytes 3145744 | tf_op jit(solution)/shard_map/all_gather | solution.py:147
  397.2 106.7 %while.54 = (s32[]{:T(128)}, bf16[8,2,1024,96]{2,3,1,0:T(8,128)(2,1)}, bf16[8,2,1024,96]{2,3,1,0:T(8,128)(2,1)}, bf16[8,1024,96]{1,2,0:T(8,128)(2,1)}, bf16[8,10...) while((s32[]{:T(128)}, bf16[8,2,1024,96]{2,3,1,0:T(8,128)(2,1)}, ...), condition=%wide.region_4.5_spmd.clone, body=%wide.region_1.4_spmd.clone.sunk | while | flops 819135488 | bytes 20076620 | solution.py:85
  517.2 21.8 %fusion.212 = f32[1024,4096]{1,0:T(8,128)} fusion(f32[1024,1536]{1,0:T(8,128)} %get-tuple-element.452, f32[1536]{0:T(1024)S(1)} %pad_maximum_fusion.24, f32[1024]{0:T(1024)S(1)} %add_rsqrt_fusion.2, bf16[384,4096]{0,1:T(8,128)(2,1)} %collective-permute-done.17, bf16[384,4096]{0,1:T(8,128)(2,1)} %collective-permute-done.16, ...), kind=kOutput, calls=%fused_computation.371 | convolution fusion | flops 12939952128 | bytes 35661824 | tf_op jit(solution)/shard_map/dot_general | solution.py:41
  540.7 21.9 %multiply_convert_fusion.22 = bf16[1024,4096]{1,0:T(8,128)(2,1)} fusion(f32[1024,4096]{1,0:T(8,128)} %fusion.212, f32[1024,1536]{1,0:T(8,128)} %get-tuple-element.452, f32[1536]{0:T(1024)S(1)} %pad_maximum_fusion.24, f32[1024]{0:T(1024)S(1)} %add_rsqrt_fusion.2, bf16[384,4096]{0,1:T(8,128)(2,1)} %collective-permute-done.14, ...), kind=kOutput, calls=%fused_computation.156.clone.clone.clone.clone.2 | convolution fusion | flops 12965117952 | bytes 44050432 | tf_op jit(solution)/shard_map/dot_general | solution.py:41
  562.7 20.5 %add_convert_fusion.10 = bf16[1024,1536]{1,0:T(8,128)(2,1)} fusion(f32[1024,1536]{1,0:T(8,128)} %get-tuple-element.452, bf16[384,4096]{0,1:T(8,128)(2,1)} %collective-permute-done.20, bf16[384,4096]{0,1:T(8,128)(2,1)} %collective-permute-done.19, bf16[384,4096]{0,1:T(8,128)(2,1)} %collective-permute-done.18, bf16[384,4096]{0,1:T(8,128)(2,1)} %bitcast.31, ...), kind=kOutput, calls=%fused_computation.218 | convolution fusion | flops 12938379264 | bytes 30408704 | tf_op jit(solution)/shard_map/dot_general | solution.py:45
  588.4 20.0 fusion.214
  608.4 46.4 %collective-permute-done.21 = bf16[1024,1536]{1,0:T(8,128)(2,1)} collective-permute-done((bf16[1024,1536]{1,0:T(8,128)(2,1)}, bf16[1024,1536]{1,0:T(8,128)(2,1)}, u32[]{:S(2)}, u32[]{:S(2)}) %collective-permute-start.21) | collective-permute-done | bytes 3145760 | tf_op jit(solution)/shard_map/ppermute | solution.py:20
  693.2 83.0 %while.55 = (s32[]{:T(128)}, bf16[8,2,1024,96]{2,3,1,0:T(8,128)(2,1)}, f32[8,2,1024,1]{2,1,3,0:T(2,128)}, bf16[8,2,1024,96]{2,3,1,0:T(8,128)(2,1)S(1)}, bf16[8,1...) while((s32[]{:T(128)}, ...), condition=%wide.region_10.11_spmd.clone, body=%wide.region_7.10_spmd.clone.sunk | while | flops 831715328 | bytes 30612052 | solution.py:85
  790.3 21.9 %fusion.244 = (bf16[1024,4096]{1,0:T(8,128)(2,1)}, f32[1024,4096]{1,0:T(8,128)}) fusion(bf16[1024,1536]{1,0:T(8,128)(2,1)S(1)} %multiply_convert_fusion.5, bf16[384,4096]{0,1:T(8,128)(2,1)} %collective-permute-done.14, bf16[384,4096]{0,1:T(8,128)(2,1)} %collective-permute-done.13, bf16[384,4096]{0,1:T(8,128)(2,1)} %copy-done.87, bf16[384,4096]{0,1:T(8,128)(2,1)} %bitcast.22), kind=kOutput, calls=%fused_computation.391 | convolution fusion | flops 12939427840 | bytes 40894464 | tf_op jit(solution)/shard_map/dot_general | solution.py:41
  812.2 19.9 fusion.224
  832.1 21.1 %fusion.156 = f32[1024,1536]{1,0:T(8,128)} fusion(f32[1024,4096]{1,0:T(8,128)} %fusion.214, bf16[1024,4096]{1,0:T(8,128)(2,1)} %get-tuple-element.455, bf16[384,4096]{0,1:T(8,128)(2,1)} %collective-permute-done.17, bf16[384,4096]{0,1:T(8,128)(2,1)} %collective-permute-done.16, bf16[384,4096]{0,1:T(8,128)(2,1)} %collective-permute-done.15, ...), kind=kOutput, calls=%fused_computation.174 | convolution fusion | flops 12964593664 | bytes 44040192 | tf_op jit(solution)/shard_map/dot_general | solution.py:45
  853.2 30.0 %multiply_reduce_fusion.4 = (f32[1024]{0:T(1024)S(1)}, f32[1024,1536]{1,0:T(8,128)}) fusion(f32[1024,1536]{1,0:T(8,128)} %copy-done, f32[1536]{0:T(1024)S(1)} %copy-done.69, f32[1024,1536]{1,0:T(8,128)} %fusion.156, bf16[384,4096]{0,1:T(8,128)(2,1)} %collective-permute-done.14, bf16[384,4096]{0,1:T(8,128)(2,1)} %collective-permute-done.13, ...), kind=kOutput, calls=%fused_computation.212 | convolution fusion | flops 12996049920 | bytes 73410560 | tf_op jit(solution)/shard_map/dot_general | solution.py:45
  904.7 157.4 %while.56 = (s32[]{:T(128)}, f32[8,2,1024,96]{2,3,1,0:T(8,128)}, f32[8,1024,96]{1,2,0:T(8,128)S(1)}, bf16[8,1024,96]{1,2,0:T(8,128)(2,1)}, bf16[8,2,1024,96]{2,3...) while((s32[]{:T(128)}, f32[8,2,1024,96]{2,3,1,0:T(8,128)}, ...), condition=%wide.region_15.16_spmd.clone, body=%wide.region_13.15_spmd.clone.sunk | while | flops 2046064640 | bytes 70911088 | solution.py:104
  1101.6 71.2 %collective-permute-done.28 = bf16[1024,1536]{1,0:T(8,128)(2,1)S(1)} collective-permute-done((bf16[1024,1536]{1,0:T(8,128)(2,1)S(1)}, bf16[1024,1536]{1,0:T(8,128)(2,1)S(1)}, u32[]{:S(2)}, u32[]{:S(2)}) %collective-permute-start.28) | collective-permute-done | bytes 3145760 | tf_op jit(solution)/shard_map/ppermute | solution.py:20
  1173.9 35.3 %fusion.143 = (bf16[1024,4096]{1,0:T(8,128)(2,1)}, bf16[1024,4096]{1,0:T(8,128)(2,1)}, bf16[1024,4096]{1,0:T(8,128)(2,1)}) fusion(f32[1024,4096]{1,0:T(8,128)} %fusion.224, bf16[1024,4096]{1,0:T(8,128)(2,1)} %get-tuple-element.455, f32[1024,4096]{1,0:T(8,128)} %get-tuple-element.456, bf16[1024,1536]{1,0:T(8,128)(2,1)S(1)} %broadcast_select_fusion, ...), kind=kOutput, calls=%fused_computation.145 | convolution fusion | flops 13027508224 | bytes 82837504 | tf_op jit(solution)/shard_map/dot_general | solution.py:41
  1209.1 20.1 convolution_convert_fusion.1
  1229.2 21.1 %fusion.223 = f32[1024,1536]{1,0:T(8,128)} fusion(bf16[1024,4096]{1,0:T(8,128)(2,1)} %get-tuple-element.376, bf16[384,4096]{0,1:T(8,128)(2,1)} %collective-permute-done.17, bf16[384,4096]{0,1:T(8,128)(2,1)} %collective-permute-done.16, bf16[384,4096]{0,1:T(8,128)(2,1)} %collective-permute-done.15, bf16[384,4096]{0,1:T(8,128)(2,1)} %bitcast.25), kind=kOutput, calls=%fused_computation.378 | convolution fusion | flops 12935233536 | bytes 27262976 | tf_op jit(solution)/shard_map/dot_general | solution.py:45
  1250.4 23.0 %multiply_reduce_fusion.2 = (f32[1536]{0:T(1024)}, f32[1024]{0:T(1024)S(1)}, f32[1024,1536]{1,0:T(8,128)}) fusion(f32[1024,1536]{1,0:T(8,128)} %copy-done, f32[1024]{0:T(1024)S(1)} %copy-done.74, f32[1536]{0:T(1024)S(1)} %copy-done.70, f32[1024,1536]{1,0:T(8,128)} %fusion.223, bf16[1024,4096]{1,0:T(8,128)(2,1)} %get-tuple-element.375, ...), kind=kOutput, calls=%fused_computation.207 | convolution fusion | flops 12946240512 | bytes 39866368 | tf_op jit(solution)/shard_map/dot_general | solution.py:45
  1298.7 153.0 %while.57 = (s32[]{:T(128)}, f32[8,2,1024,96]{2,3,1,0:T(8,128)}, f32[8,1024,96]{1,2,0:T(8,128)}, bf16[8,1024,96]{1,2,0:T(8,128)(2,1)}, bf16[8,2,1024,96]{2,3,1,0...) while((s32[]{:T(128)}, f32[8,2,1024,96]{2,3,1,0:T(8,128)}, ...), condition=%wide.region_20.21_spmd.clone, body=%wide.region_18.20_spmd.clone.sunk | while | flops 2046064640 | bytes 70911088 | solution.py:104
  1484.0 17.7 collective-permute-done.37
  1519.7 17.0 collective-permute-done.34
  1583.6 63.1 %collective-permute-done.46 = bf16[384,4096]{1,0:T(8,128)(2,1)} collective-permute-done((bf16[384,4096]{1,0:T(8,128)(2,1)}, bf16[384,4096]{1,0:T(8,128)(2,1)}, u32[]{:S(2)}, u32[]{:S(2)}) %collective-permute-start.46) | collective-permute-done | bytes 3145760 | tf_op jit(solution)/shard_map/ppermute | solution.py:24
  1654.3 17.0 convolution_convert_fusion.2
  1690.5 22.7 %collective-permute-done.49 = bf16[384,4096]{1,0:T(8,128)(2,1)} collective-permute-done((bf16[384,4096]{1,0:T(8,128)(2,1)}, bf16[384,4096]{1,0:T(8,128)(2,1)}, u32[]{:S(2)}, u32[]{:S(2)}) %collective-permute-start.49) | collective-permute-done | bytes 3145760 | tf_op jit(solution)/shard_map/ppermute | solution.py:24
  1751.1 49.6 %collective-permute-done.43 = bf16[384,4096]{1,0:T(8,128)(2,1)} collective-permute-done((bf16[384,4096]{1,0:T(8,128)(2,1)}, bf16[384,4096]{1,0:T(8,128)(2,1)}, u32[]{:S(2)}, u32[]{:S(2)}) %collective-permute-start.43) | collective-permute-done | bytes 3145760 | tf_op jit(solution)/shard_map/ppermute | solution.py:24
  1808.3 20.6 %add_convert_fusion.9 = bf16[1024,1536]{1,0:T(8,128)(2,1)} fusion(f32[1024,1536]{1,0:T(8,128)} %copy-done, bf16[1024,4096]{1,0:T(8,128)(2,1)} %get-tuple-element.377, bf16[384,4096]{0,1:T(8,128)(2,1)} %collective-permute-done.20, bf16[384,4096]{0,1:T(8,128)(2,1)} %collective-permute-done.19, bf16[384,4096]{0,1:T(8,128)(2,1)} %collective-permute-done.18, ...), kind=kOutput, calls=%fused_computation.215 | convolution fusion | flops 12938379264 | bytes 30408704 | tf_op jit(solution)/shard_map/dot_general | solution.py:45
  1837.3 147.9 %psum.7 = f32[2,1536]{1,0:T(2,128)S(1)} all-reduce(f32[2,1536]{1,0:T(2,128)S(1)} %pad_maximum_fusion.22), channel_id=1, replica_groups=mesh['section'=2,'dp'=4,'tensor'=4] {'dp','tensor'}, use_global_device_ids=true, to_apply=%region_24.25 | all-reduce | flops 3072 | bytes 24576 | tf_op jit(solution)/shard_map/psum | solution.py:287
  (660 shorter events, 993.5 us)
Async XLA Ops:
  7.2 241.8 %all-gather.9.cloned.1.call-start = ((), (), s32[]{:S(2)}) async-start(), calls=%async_computation.6 | async-start | bytes 1474560 | tf_op jit(solution)/shard_map/all_gather | solution.py:147
  11.4 249.5 %all-gather.17.cloned.1.call-start = ((), (), s32[]{:S(2)}) async-start(), calls=%async_computation.16 | async-start | bytes 1474560 | tf_op jit(solution)/shard_map/all_gather | solution.py:147
  13.1 250.3 %all-gather.13.cloned.1.call-start = ((), (), s32[]{:S(2)}) async-start(), calls=%async_computation.8 | async-start | bytes 3932160 | tf_op jit(solution)/shard_map/all_gather | solution.py:147
  13.8 311.6 %all-gather.19.cloned.1.call-start = ((), (), s32[]{:S(2)}) async-start(), calls=%async_computation.17 | async-start | bytes 3932160 | tf_op jit(solution)/shard_map/all_gather | solution.py:147
  16.2 372.8 %all-gather.11.cloned.1.call-start = ((), (), s32[]{:S(2)}) async-start(), calls=%async_computation.7 | async-start | bytes 3932160 | tf_op jit(solution)/shard_map/all_gather | solution.py:147
  25.2 242.8 %collective-permute-start.6 = (bf16[384,1536]{1,0:T(8,128)(2,1)}, bf16[384,1536]{1,0:T(8,128)(2,1)}, u32[]{:S(2)}, u32[]{:S(2)}) collective-permute-start(bf16[384,1536]{1,0:T(8,128)(2,1)} %pad_maximum_fusion.21), channel_id=1, source_target_pairs={{0,4},{4,0},{8,12},{12,8},{1,5},{5,1},{9,13},{13,9},{2,6},{6,2},{1... | collective-permute-start | bytes 3538952 | tf_op jit(solution)/shard_map/ppermute | solution.py:24
  26.6 1549.3 %reduce-scatter.9.cloned.1.call-start = ((), (), s32[]{:S(2)}) async-start(), calls=%async_computation.10 | async-start | bytes 1474560 | tf_op jit(solution)/shard_map/reduce_scatter | solution.py:165
  62.0 106.0 %collective-permute-start.26 = (bf16[1,256,1536]{2,1,0:T(8,128)(2,1)}, bf16[1,256,1536]{2,1,0:T(8,128)(2,1)}, u32[]{:S(2)}, u32[]{:S(2)}) collective-permute-start(bf16[1,256,1536]{2,1,0:T(8,128)(2,1)} %get-tuple-element.421), channel_id=1, source_target_pairs={{0,2},{1,3},{2,0},{3,1},{4,6},{5,7},{6,4},{7,5},{8,10},{9,11},{10,... | collective-permute-start | bytes 2359304 | tf_op jit(solution)/shard_map/ppermute | solution.py:24
  64.5 105.6 %collective-permute-start.27 = (bf16[1,256,1536]{2,1,0:T(8,128)(2,1)}, bf16[1,256,1536]{2,1,0:T(8,128)(2,1)}, u32[]{:S(2)}, u32[]{:S(2)}) collective-permute-start(bf16[1,256,1536]{2,1,0:T(8,128)(2,1)} %get-tuple-element.419), channel_id=1, source_target_pairs={{0,3},{1,2},{2,1},{3,0},{4,7},{5,6},{6,5},{7,4},{8,11},{9,10},{10,... | collective-permute-start | bytes 2359304 | tf_op jit(solution)/shard_map/ppermute | solution.py:24
  104.1 143.6 %collective-permute-start.1 = (bf16[1,256,1536]{2,1,0:T(8,128)(2,1)}, bf16[1,256,1536]{2,1,0:T(8,128)(2,1)}, u32[]{:S(2)}, u32[]{:S(2)}) collective-permute-start(bf16[1,256,1536]{2,1,0:T(8,128)(2,1)} %get-tuple-element.435), channel_id=1, source_target_pairs={{0,2},{1,3},{2,0},{3,1},{4,6},{5,7},{6,4},{7,5},{8,10},{9,11},{10,... | collective-permute-start | bytes 2359304 | tf_op jit(solution)/shard_map/ppermute | solution.py:24
  109.7 147.7 %collective-permute-start.2 = (bf16[1,256,1536]{2,1,0:T(8,128)(2,1)}, bf16[1,256,1536]{2,1,0:T(8,128)(2,1)}, u32[]{:S(2)}, u32[]{:S(2)}) collective-permute-start(bf16[1,256,1536]{2,1,0:T(8,128)(2,1)} %get-tuple-element.433), channel_id=1, source_target_pairs={{0,3},{1,2},{2,1},{3,0},{4,7},{5,6},{6,5},{7,4},{8,11},{9,10},{10,... | collective-permute-start | bytes 2359304 | tf_op jit(solution)/shard_map/ppermute | solution.py:24
  168.0 103.1 %collective-permute-start.8 = (bf16[384,1536]{1,0:T(8,128)(2,1)}, bf16[384,1536]{1,0:T(8,128)(2,1)}, u32[]{:S(2)}, u32[]{:S(2)}) collective-permute-start(bf16[384,1536]{1,0:T(8,128)(2,1)} %collective-permute-done.7), channel_id=1, source_target_pairs={{0,4},{4,0},{8,12},{12,8},{1,5},{5,1},{9,13},{13,9},{2,6},{6,2},{1... | collective-permute-start | bytes 3538952 | tf_op jit(solution)/shard_map/ppermute | solution.py:24
  268.0 125.6 %collective-permute-start.9 = (bf16[384,1536]{0,1:T(8,128)(2,1)}, bf16[384,1536]{0,1:T(8,128)(2,1)}, u32[]{:S(2)}, u32[]{:S(2)}) collective-permute-start(bf16[384,1536]{0,1:T(8,128)(2,1)} %bitcast.431), channel_id=1, source_target_pairs={{0,4},{4,0},{8,12},{12,8},{1,5},{5,1},{9,13},{13,9},{2,6},{6,2},{1... | collective-permute-start | bytes 3538952 | tf_op jit(solution)/shard_map/ppermute | solution.py:24
  271.2 123.9 %collective-permute-start.16 = (bf16[384,4096]{0,1:T(8,128)(2,1)}, bf16[384,4096]{0,1:T(8,128)(2,1)}, u32[]{:S(2)}, u32[]{:S(2)}) collective-permute-start(bf16[384,4096]{0,1:T(8,128)(2,1)} %bitcast.25), channel_id=1, source_target_pairs={{0,8},{4,12},{8,0},{12,4},{1,9},{5,13},{9,1},{13,5},{2,10},{6,14},... | collective-permute-start | bytes 9437192 | tf_op jit(solution)/shard_map/ppermute | solution.py:24
  296.5 207.5 %collective-permute-start.11 = (bf16[384,1536]{0,1:T(8,128)(2,1)}, bf16[384,1536]{0,1:T(8,128)(2,1)}, u32[]{:S(2)}, u32[]{:S(2)}) collective-permute-start(bf16[384,1536]{0,1:T(8,128)(2,1)} %collective-permute-done.10), channel_id=1, source_target_pairs={{0,4},{4,0},{8,12},{12,8},{1,5},{5,1},{9,13},{13,9},{2,6},{6,2},{1... | collective-permute-start | bytes 3538952 | tf_op jit(solution)/shard_map/ppermute | solution.py:24
  307.4 209.2 %collective-permute-start.15 = (bf16[384,4096]{0,1:T(8,128)(2,1)}, bf16[384,4096]{0,1:T(8,128)(2,1)}, u32[]{:S(2)}, u32[]{:S(2)}) collective-permute-start(bf16[384,4096]{0,1:T(8,128)(2,1)} %bitcast.25), channel_id=1, source_target_pairs={{0,4},{4,0},{8,12},{12,8},{1,5},{5,1},{9,13},{13,9},{2,6},{6,2},{1... | collective-permute-start | bytes 9437192 | tf_op jit(solution)/shard_map/ppermute | solution.py:24
  330.1 186.5 %collective-permute-start.19 = (bf16[384,4096]{0,1:T(8,128)(2,1)}, bf16[384,4096]{0,1:T(8,128)(2,1)}, u32[]{:S(2)}, u32[]{:S(2)}) collective-permute-start(bf16[384,4096]{0,1:T(8,128)(2,1)} %bitcast.31), channel_id=1, source_target_pairs={{0,8},{4,12},{8,0},{12,4},{1,9},{5,13},{9,1},{13,5},{2,10},{6,14},... | collective-permute-start | bytes 9437192 | tf_op jit(solution)/shard_map/ppermute | solution.py:24
  393.7 123.4 %collective-permute-start.13 = (bf16[384,4096]{0,1:T(8,128)(2,1)}, bf16[384,4096]{0,1:T(8,128)(2,1)}, u32[]{:S(2)}, u32[]{:S(2)}) collective-permute-start(bf16[384,4096]{0,1:T(8,128)(2,1)} %bitcast.22), channel_id=1, source_target_pairs={{0,8},{4,12},{8,0},{12,4},{1,9},{5,13},{9,1},{13,5},{2,10},{6,14},... | collective-permute-start | bytes 9437192 | tf_op jit(solution)/shard_map/ppermute | solution.py:24
  395.1 122.1 %collective-permute-start.17 = (bf16[384,4096]{0,1:T(8,128)(2,1)}, bf16[384,4096]{0,1:T(8,128)(2,1)}, u32[]{:S(2)}, u32[]{:S(2)}) collective-permute-start(bf16[384,4096]{0,1:T(8,128)(2,1)} %collective-permute-done.16), channel_id=1, source_target_pairs={{0,4},{4,0},{8,12},{12,8},{1,5},{5,1},{9,13},{13,9},{2,6},{6,2},{1... | collective-permute-start | bytes 9437192 | tf_op jit(solution)/shard_map/ppermute | solution.py:24
  1505.6 499.6 %reduce-scatter.7.cloned.1.call-start = ((), (), s32[]{:S(2)}) async-start(), calls=%async_computation.9 | async-start | bytes 1474560 | tf_op jit(solution)/shard_map/reduce_scatter | solution.py:165
  1542.2 464.8 %reduce-scatter.11.cloned.1.call-start = ((), (), s32[]{:S(2)}) async-start(), calls=%async_computation.12 | async-start | bytes 1474560 | tf_op jit(solution)/shard_map/reduce_scatter | solution.py:165
  1569.6 439.2 %all-gather.15.cloned.1.call-start = ((), (), s32[]{:S(2)}) async-start(), calls=%async_computation.11 | async-start | bytes 1474560 | tf_op jit(solution)/shard_map/all_gather | solution.py:285
  1575.9 114.6 %collective-permute-start.47 = (bf16[384,4096]{1,0:T(8,128)(2,1)}, bf16[384,4096]{1,0:T(8,128)(2,1)}, u32[]{:S(2)}, u32[]{:S(2)}) collective-permute-start(bf16[384,4096]{1,0:T(8,128)(2,1)} %get-tuple-element.378), channel_id=1, source_target_pairs={{0,4},{4,0},{8,12},{12,8},{1,5},{5,1},{9,13},{13,9},{2,6},{6,2},{1... | collective-permute-start | bytes 9437192 | tf_op jit(solution)/shard_map/ppermute | solution.py:24
  1575.9 443.3 %reduce-scatter.15.cloned.1.call-start = ((), (), s32[]{:S(2)}) async-start(), calls=%async_computation.14 | async-start | bytes 3932160 | tf_op jit(solution)/shard_map/reduce_scatter | solution.py:165
  1582.0 131.2 %collective-permute-start.49 = (bf16[384,4096]{1,0:T(8,128)(2,1)}, bf16[384,4096]{1,0:T(8,128)(2,1)}, u32[]{:S(2)}, u32[]{:S(2)}) collective-permute-start(bf16[384,4096]{1,0:T(8,128)(2,1)} %add_convert_fusion.1), channel_id=1, source_target_pairs={{0,8},{4,12},{8,0},{12,4},{1,9},{5,13},{9,1},{13,5},{2,10},{6,14},... | collective-permute-start | bytes 9437192 | tf_op jit(solution)/shard_map/ppermute | solution.py:24
  1654.2 367.5 %reduce-scatter.17.cloned.1.call-start = ((), (), s32[]{:S(2)}) async-start(), calls=%async_computation.15 | async-start | bytes 3932160 | tf_op jit(solution)/shard_map/reduce_scatter | solution.py:165
  1725.2 299.0 %reduce-scatter.13.cloned.1.call-start = ((), (), s32[]{:S(2)}) async-start(), calls=%async_computation.13 | async-start | bytes 3932160 | tf_op jit(solution)/shard_map/reduce_scatter | solution.py:165
  1746.7 239.1 %collective-permute-start.29 = (bf16[1,256,1536]{2,1,0:T(8,128)(2,1)}, bf16[1,256,1536]{2,1,0:T(8,128)(2,1)}, u32[]{:S(2)}, u32[]{:S(2)}) collective-permute-start(bf16[1,256,1536]{2,1,0:T(8,128)(2,1)} %get-tuple-element.408), channel_id=1, source_target_pairs={{0,1},{1,0},{2,3},{3,2},{4,5},{5,4},{6,7},{7,6},{8,9},{9,8},{10,11... | collective-permute-start | bytes 2359304 | tf_op jit(solution)/shard_map/ppermute | solution.py:24
  1746.7 240.3 %collective-permute-start.30 = (bf16[1,256,1536]{2,1,0:T(8,128)(2,1)}, bf16[1,256,1536]{2,1,0:T(8,128)(2,1)}, u32[]{:S(2)}, u32[]{:S(2)}) collective-permute-start(bf16[1,256,1536]{2,1,0:T(8,128)(2,1)} %get-tuple-element.407), channel_id=1, source_target_pairs={{0,2},{1,3},{2,0},{3,1},{4,6},{5,7},{6,4},{7,5},{8,10},{9,11},{10,... | collective-permute-start | bytes 2359304 | tf_op jit(solution)/shard_map/ppermute | solution.py:24
  1748.1 240.1 %collective-permute-start.31 = (bf16[1,256,1536]{2,1,0:T(8,128)(2,1)}, bf16[1,256,1536]{2,1,0:T(8,128)(2,1)}, u32[]{:S(2)}, u32[]{:S(2)}) collective-permute-start(bf16[1,256,1536]{2,1,0:T(8,128)(2,1)} %get-tuple-element.406), channel_id=1, source_target_pairs={{0,3},{1,2},{2,1},{3,0},{4,7},{5,6},{6,5},{7,4},{8,11},{9,10},{10,... | collective-permute-start | bytes 2359304 | tf_op jit(solution)/shard_map/ppermute | solution.py:24
  1835.9 153.5 %collective-permute-start.22 = (bf16[1,256,1536]{2,1,0:T(8,128)(2,1)}, bf16[1,256,1536]{2,1,0:T(8,128)(2,1)}, u32[]{:S(2)}, u32[]{:S(2)}) collective-permute-start(bf16[1,256,1536]{2,1,0:T(8,128)(2,1)} %get-tuple-element.424), channel_id=1, source_target_pairs={{0,1},{1,0},{2,3},{3,2},{4,5},{5,4},{6,7},{7,6},{8,9},{9,8},{10,11... | collective-permute-start | bytes 2359304 | tf_op jit(solution)/shard_map/ppermute | solution.py:24
  1835.9 156.2 %collective-permute-start.23 = (bf16[1,256,1536]{2,1,0:T(8,128)(2,1)}, bf16[1,256,1536]{2,1,0:T(8,128)(2,1)}, u32[]{:S(2)}, u32[]{:S(2)}) collective-permute-start(bf16[1,256,1536]{2,1,0:T(8,128)(2,1)} %get-tuple-element.423), channel_id=1, source_target_pairs={{0,2},{1,3},{2,0},{3,1},{4,6},{5,7},{6,4},{7,5},{8,10},{9,11},{10,... | collective-permute-start | bytes 2359304 | tf_op jit(solution)/shard_map/ppermute | solution.py:24
  (128 other events, 4297.5 us)
Sparse Core Ops, SparseCore 0:
  11.5 48.7 all-gather.8
  62.4 109.9 all-gather.16
  174.0 87.9 all-gather.12
  263.4 61.9 all-gather.18
  326.8 62.1 all-gather.10
  1505.7 26.0 reduce-scatter.8
  1542.3 26.0 reduce-scatter.6
  1571.2 27.8 reduce-scatter.10
  1600.7 29.1 all-gather.14
  1654.4 56.9 reduce-scatter.14
  1725.3 87.8 reduce-scatter.16
  1815.3 101.7 reduce-scatter.12

commit v2 on v1

--- a/solution.py
+++ b/solution.py
@@ -1,6 +1,10 @@
+import functools
+
 import jax
 import jax.numpy as jnp
 from jax import lax
+from jax.experimental import pallas as pl
+from jax.experimental.pallas import tpu as pltpu
 from jax.sharding import PartitionSpec as P
 
 HEADS = 16
@@ -68,40 +72,137 @@
     return jnp.sum(grad * rows * inverse, axis=0)
 
 
-def attention_forward(queries, keys, values, causal):
+QB = 256
+LOG2E = 1.4426950408889634
+
+
+def score_parts(offset_ref, k_ref, q, i, size, single):
+    cols = q.shape[0]
+    first = i * size if single else 0
+    count = size if single else k_ref.shape[1]
+    parts = []
+    if first:
+        parts.append((0, first, mm_nt(k_ref[0, :first], q)))
+    diagonal = mm_nt(k_ref[0, first : first + count], q)
+    key_at = first + lax.broadcasted_iota(jnp.int32, (count, cols), 0)
+    query_at = i * size + lax.rem(lax.broadcasted_iota(jnp.int32, (count, cols), 1), size)
+    if not single:
+        query_at = query_at + offset_ref[0]
+    diagonal = jnp.where(key_at <= query_at, diagonal, -1e30)
+    parts.append((first, count, diagonal))
+    return parts
+
+
+def attend_forward_kernel(offset_ref, q_ref, k_ref, vt_ref, o_ref, lse_ref, *, single):
+    copies, n, size_h = q_ref.shape[1:]
+    size = min(QB, n)
+    factor = HD ** (-0.5) * LOG2E
+    for i in range(n // size):
+        rows = slice(i * size, (i + 1) * size)
+        q = q_ref[0, :, rows, :].reshape(copies * size, size_h)
+        parts = score_parts(offset_ref, k_ref, q, i, size, single)
+        top = functools.reduce(
+            jnp.maximum, [jnp.max(part, axis=0, keepdims=True) for _, _, part in parts]
+        )
+        total = 0.0
+        mixed = 0.0
+        for first, count, part in parts:
+            weights = jnp.exp2((part - top) * factor)
+            total = total + jnp.sum(weights, axis=0, keepdims=True)
+            mixed = mixed + mm(vt_ref[0, :, first : first + count], weights.astype(bf16))
+        mixed = (mixed * (1.0 / total)).T.astype(bf16)
+        o_ref[0, :, rows, :] = mixed.reshape(copies, size, size_h)
+        lse_ref[0, i] = top * factor + jnp.log2(total)
+
+
+def attend_backward_kernel(
+    offset_ref, q_ref, k_ref, kt_ref, v_ref, g_ref, lse_ref, dq_ref, dk_ref, dv_ref,
+    dk_acc, dv_acc, *, single
+):
+    copies, n, size_h = q_ref.shape[1:]
+    size = min(QB, n)
     scale = HD ** (-0.5)
-
-    def per_head(items):
-        q, k, v = items
-        scores = jnp.einsum("cqd,kd->cqk", q, k, preferred_element_type=f32) * scale
-        scores = jnp.where(causal[None], scores, -1000000000.0)
-        top = jnp.max(scores, axis=-1, keepdims=True)
-        weights = jnp.exp(scores - top)
-        totals = jnp.sum(weights, axis=-1, keepdims=True)
-        probs = (weights / totals).astype(bf16)
-        mixed = jnp.einsum("cqk,kd->cqd", probs, v, preferred_element_type=f32)
-        return (mixed.astype(bf16), top + jnp.log(totals))
-
-    return lax.map(per_head, (queries, keys, values))
-
-
-def attention_backward(queries, keys, values, mixed_grad, log_totals, causal):
-    scale = HD ** (-0.5)
-
-    def per_head(items):
-        q, k, v, g, lse = items
-        scores = jnp.einsum("cqd,kd->cqk", q, k, preferred_element_type=f32) * scale
-        scores = jnp.where(causal[None], scores, -1000000000.0)
-        probs = jnp.exp(scores - lse)
-        prob_grad = jnp.einsum("cqd,kd->cqk", g, v, preferred_element_type=f32)
-        centre = jnp.sum(probs * prob_grad, axis=-1, keepdims=True)
-        score_grad = (probs * (prob_grad - centre)).astype(bf16)
-        query_grad = jnp.einsum("cqk,kd->cqd", score_grad, k, preferred_element_type=f32) * scale
-        key_grad = jnp.einsum("cqk,cqd->kd", score_grad, q, preferred_element_type=f32) * scale
-        value_grad = jnp.einsum("cqk,cqd->kd", probs.astype(bf16), g, preferred_element_type=f32)
-        return (query_grad, key_grad, value_grad)
-
-    return lax.map(per_head, (queries, keys, values, mixed_grad, log_totals))
+    factor = scale * LOG2E
+    dk_acc[...] = jnp.zeros_like(dk_acc)
+    dv_acc[...] = jnp.zeros_like(dv_acc)
+    for i in range(n // size):
+        rows = slice(i * size, (i + 1) * size)
+        q = q_ref[0, :, rows, :].reshape(copies * size, size_h)
+        g = g_ref[0, :, rows, :].reshape(copies * size, size_h)
+        lse = lse_ref[0, i]
+        kept = []
+        centre = 0.0
+        for first, count, part in score_parts(offset_ref, k_ref, q, i, size, single):
+            keys = slice(first, first + count)
+            probs = jnp.exp2(part * factor - lse)
+            prob_grad = mm_nt(v_ref[0, keys], g)
+            dv_acc[keys] += mm(probs.astype(bf16), g)
+            centre = centre + jnp.sum(probs * prob_grad, axis=0, keepdims=True)
+            kept.append((keys, probs, prob_grad))
+        dqt = 0.0
+        for keys, probs, prob_grad in kept:
+            score_grad = (probs * (prob_grad - centre)).astype(bf16)
+            dk_acc[keys] += mm(score_grad, q)
+            dqt = dqt + mm(kt_ref[0, :, keys], score_grad)
+        dq = (dqt * scale).T.astype(bf16)
+        dq_ref[0, :, rows, :] = dq.reshape(copies, size, size_h)
+    dk_ref[0] = (dk_acc[...] * scale).astype(dk_ref.dtype)
+    dv_ref[0] = dv_acc[...].astype(dv_ref.dtype)
+
+
+def block_of(shape):
+    rest = (0,) * (len(shape) - 1)
+    return pl.BlockSpec((1,) + tuple(shape[1:]), lambda h: (h,) + rest)
+
+
+def attention_forward(queries, keys, values_t, offset, single):
+    kv, copies, n, size_h = queries.shape
+    size = min(QB, n)
+    out_shape = (
+        jax.ShapeDtypeStruct(queries.shape, bf16),
+        jax.ShapeDtypeStruct((kv, n // size, 1, copies * size), f32),
+    )
+    operands = (queries, keys, values_t)
+    return pl.pallas_call(
+        functools.partial(attend_forward_kernel, single=single),
+        grid=(kv,),
+        in_specs=[pl.BlockSpec(memory_space=pltpu.SMEM)] + [block_of(a.shape) for a in operands],
+        out_specs=[block_of(a.shape) for a in out_shape],
+        out_shape=out_shape,
+        compiler_params=pltpu.CompilerParams(vmem_limit_bytes=40 * 2**20),
+        cost_estimate=pl.CostEstimate(
+            flops=8 * kv * copies * n * L * HD,
+            bytes_accessed=8 * kv * n * 128 * copies,
+            transcendentals=kv * copies * n * L,
+        ),
+        name="attend_forward",
+    )(offset, *operands)
+
+
+def attention_backward(queries, keys, values, mixed_grad, lse, offset, single):
+    kv, copies, n, size_h = queries.shape
+    count = keys.shape[1]
+    out_shape = (
+        jax.ShapeDtypeStruct(queries.shape, bf16),
+        jax.ShapeDtypeStruct(keys.shape, bf16),
+        jax.ShapeDtypeStruct(keys.shape, bf16),
+    )
+    operands = (queries, keys, keys.transpose(0, 2, 1), values, mixed_grad, lse)
+    return pl.pallas_call(
+        functools.partial(attend_backward_kernel, single=single),
+        grid=(kv,),
+        in_specs=[pl.BlockSpec(memory_space=pltpu.SMEM)] + [block_of(a.shape) for a in operands],
+        out_specs=[block_of(a.shape) for a in out_shape],
+        out_shape=out_shape,
+        scratch_shapes=[pltpu.VMEM((count, size_h), f32), pltpu.VMEM((count, size_h), f32)],
+        compiler_params=pltpu.CompilerParams(vmem_limit_bytes=40 * 2**20),
+        cost_estimate=pl.CostEstimate(
+            flops=20 * kv * copies * n * L * HD,
+            bytes_accessed=16 * kv * n * 128 * copies,
+            transcendentals=kv * copies * n * L,
+        ),
+        name="attend_backward",
+    )(offset, *operands)
 
 
 def local(
@@ -148,23 +249,36 @@
         whole = whole.transpose(1, 0, 2).reshape(share, tsize * shard.shape[1])
         return spread_rows(whole)
 
-    def sum_rows(grad):
-        parts = {m: grad[m * share : (m + 1) * share].astype(bf16) for m in range(dsize)}
-        for bit in bits_of(dsize):
-            for m in sorted(parts):
-                if m & bit:
-                    continue
+    def spread_inputs(array):
+        side = lax.axis_index("section")
+        mine = exchange(lax.dynamic_slice_in_dim(array, side * (width // 2), width // 2, 2))
+        other = swapped(mine, "section", 1)
+        whole = jnp.concatenate(
+            [jnp.where(first_section, mine, other), jnp.where(first_section, other, mine)], axis=2
+        )
+        return reorder(whole.reshape(n, width), 1)
+
+    def split_rows(grad):
+        return {m: grad[m * share : (m + 1) * share].astype(bf16) for m in range(dsize)}
+
+    def add_partner(parts, bit):
+        summed = {}
+        for m in sorted(parts):
+            if not m & bit:
                 got = swapped(parts[m ^ bit], "dp", bit)
-                parts[m] = (parts[m].astype(f32) + got.astype(f32)).astype(bf16)
-            parts = {m: part for m, part in parts.items() if not m & bit}
-        return parts[0]
-
-    def scatter_weight(grad):
-        part = sum_rows(grad)
+                summed[m] = (parts[m].astype(f32) + got.astype(f32)).astype(bf16)
+        return summed
+
+    def scatter_columns(part):
         part = part.reshape(share, tsize, -1).transpose(1, 0, 2)
         return lax.psum_scatter(part, "tensor", scatter_dimension=0)
 
-    rows_in = reorder(exchange(inputs).reshape(n, width), 1)
+    def finish_rows(parts, bits):
+        for bit in bits:
+            parts = add_partner(parts, bit)
+        return parts
+
+    rows_in = spread_inputs(inputs)
     attn_scale = reorder(attn_gain[0], 0)
     mlp_scale = reorder(mlp_gain[0], 0)
 
@@ -174,7 +288,6 @@
     wg = gather_weight(w_gate[0])
     wu = gather_weight(w_up[0])
     wd = gather_weight(w_down[0].T)
-    cot = reorder(exchange(cotangent).reshape(n, width), 1)
 
     places = seg * n + jnp.arange(n)
     half = HD // 2
@@ -182,25 +295,30 @@
     angles = places.astype(f32)[:, None] * freqs[None, :]
     cosine = jnp.cos(angles)
     sine = jnp.sin(angles)
-    causal = places[:, None] >= jnp.arange(L)[None, :]
+    single = ranks == 1
+    offset = (seg * n).astype(jnp.int32).reshape(1)
 
     def all_keys(array):
-        if ranks == 1:
+        if single:
             return array
         return lax.all_gather(
             array, "tensor", axis=1, tiled=True, axis_index_groups=same_seq
         )
 
     def own_keys(array):
-        if ranks == 1:
-            return array
+        if single:
+            return array.astype(f32)
         return lax.psum_scatter(
-            array.astype(bf16),
+            array,
             "tensor",
             scatter_dimension=1,
             tiled=True,
             axis_index_groups=same_seq,
         ).astype(f32)
+
+    def token_chunks(count):
+        step = n // count
+        return [slice(i * step, (i + 1) * step) for i in range(count)]
 
     def forward(rows_bf):
         rows = rows_bf.astype(f32)
@@ -213,7 +331,7 @@
         keys = all_keys(rotate(keys, cosine, sine).astype(bf16))
         values = both[:, dims:].reshape(n, KV_HEADS, HD).transpose(1, 0, 2)
         values = all_keys(values.astype(bf16))
-        mixed, log_totals = attention_forward(queries, keys, values, causal)
+        mixed, lse = attention_forward(queries, keys, values.transpose(0, 2, 1), offset, single)
         mixed = mixed.transpose(2, 0, 1, 3).reshape(n, HEADS * HD)
         middle = rows + mm_nt(mixed, wo)
         normed_mlp, inverse_mlp = norm_forward(middle, mlp_scale)
@@ -221,70 +339,113 @@
         gate = mm(normed_mlp, wg)
         upward = mm(normed_mlp, wu)
         hidden = (jax.nn.silu(gate) * upward).astype(bf16)
-        outgoing = (middle + mm_nt(hidden, wd)).astype(bf16)
         kept = (
-            rows_bf, inverse, normed, queries, keys, values, log_totals, mixed,
+            rows_bf, inverse, normed, queries, keys, values, lse, mixed,
             middle, inverse_mlp, normed_mlp, gate.astype(bf16), upward.astype(bf16), hidden,
         )
-        return outgoing, kept
+        return kept
+
+    def layer_output(kept, chunk):
+        middle, hidden = kept[8], kept[13]
+        return (middle[chunk] + mm_nt(hidden[chunk], wd)).astype(bf16)
 
     def backward(grad, kept, weights_too):
         (
-            rows_bf, inverse, normed, queries, keys, values, log_totals, mixed,
+            rows_bf, inverse, normed, queries, keys, values, lse, mixed,
             middle, inverse_mlp, normed_mlp, gate, upward, hidden,
         ) = kept
         rows = rows_bf.astype(f32)
         gate = gate.astype(f32)
         upward = upward.astype(f32)
-        done = []
+        done = None
+        low_bits = bits_of(dsize)[:1]
+        high_bits = bits_of(dsize)[1:]
         if weights_too:
-            done.append(scatter_weight(mm_tn(grad, hidden)))
+            down = mm_tn(grad, hidden).astype(bf16)
+            grad, down = lax.optimization_barrier((grad, down))
+            down = split_rows(down)
         hidden_grad = mm(grad, wd)
         sigma = jax.nn.sigmoid(gate)
         gate_grad = (hidden_grad * upward * (sigma * (1.0 + gate * (1.0 - sigma)))).astype(bf16)
         up_grad = (hidden_grad * gate * sigma).astype(bf16)
         if weights_too:
-            done.append(scatter_weight(mm_tn(normed_mlp, gate_grad)))
-            done.append(scatter_weight(mm_tn(normed_mlp, up_grad)))
+            down = finish_rows(down, low_bits)
+            gate_up = mm_tn(normed_mlp, gate_grad).astype(bf16)
+            up_up = mm_tn(normed_mlp, up_grad).astype(bf16)
+            gate_grad, up_grad, gate_up, up_up, down = lax.optimization_barrier(
+                (gate_grad, up_grad, gate_up, up_up, down)
+            )
+            gate_up = split_rows(gate_up)
+            up_up = split_rows(up_up)
         mlp_back = mm_nt(gate_grad, wg) + mm_nt(up_grad, wu)
         middle_grad = grad.astype(f32) + norm_backward(middle, inverse_mlp, mlp_scale, mlp_back)
         middle_bf = middle_grad.astype(bf16)
         if weights_too:
-            done.append(scatter_weight(mm_tn(middle_bf, mixed)))
+            out_up = mm_tn(middle_bf, mixed).astype(bf16)
+            gate_up = finish_rows(gate_up, low_bits)
+            up_up = finish_rows(up_up, low_bits)
+            middle_bf, out_up, gate_up, up_up = lax.optimization_barrier(
+                (middle_bf, out_up, gate_up, up_up)
+            )
+            out_up = split_rows(out_up)
         mixed_grad = mm(middle_bf, wo).astype(bf16)
         mixed_grad = mixed_grad.reshape(n, KV_HEADS, copies, HD).transpose(1, 2, 0, 3)
-        dq, dk, dv = attention_backward(queries, keys, values, mixed_grad, log_totals, causal)
+        dq, dk, dv = attention_backward(queries, keys, values, mixed_grad, lse, offset, single)
         dk = own_keys(dk)
         dv = own_keys(dv)
-        dq = rotate(dq, cosine, -sine).transpose(2, 0, 1, 3).reshape(n, HEADS * HD).astype(bf16)
+        dq = rotate(dq.astype(f32), cosine, -sine)
+        dq = dq.transpose(2, 0, 1, 3).reshape(n, HEADS * HD).astype(bf16)
         dk = rotate(dk, cosine, -sine).transpose(1, 0, 2).reshape(n, dims)
         dkv = jnp.concatenate([dk, dv.transpose(1, 0, 2).reshape(n, dims)], axis=1).astype(bf16)
-        if weights_too:
-            done.append(scatter_weight(mm_tn(normed, dq)))
-            done.append(scatter_weight(mm_tn(normed, dkv)))
+        if not weights_too:
+            outgoing = []
+            for chunk in token_chunks(4):
+                attn_back = mm_nt(dq[chunk], wq) + mm_nt(dkv[chunk], wkv)
+                branch = norm_backward(rows[chunk], inverse[chunk], attn_scale, attn_back)
+                outgoing.append((middle_grad[chunk] + branch).astype(bf16))
+            return outgoing
+        query_up = mm_tn(normed, dq).astype(bf16)
+        kv_up = mm_tn(normed, dkv).astype(bf16)
+        dq, dkv, query_up, kv_up = lax.optimization_barrier((dq, dkv, query_up, kv_up))
         attn_back = mm_nt(dq, wq) + mm_nt(dkv, wkv)
         outgoing = middle_grad + norm_backward(rows, inverse, attn_scale, attn_back)
-        if weights_too:
-            done.append(gain_sum(rows, inverse, attn_back))
-            done.append(gain_sum(middle, inverse_mlp, mlp_back))
-        return outgoing.astype(bf16), done
-
-    first_out, _ = forward(rows_in)
-    received = shifted(first_out, "section", 1)
-    second_out, kept = forward(jnp.where(first_section, rows_in, received))
-    first_grad, _ = backward(cot, kept, False)
-    returned = shifted(first_grad, "section", -1)
-    second_grad, done = backward(jnp.where(first_section, returned, cot), kept, True)
+        sums = [
+            scatter_columns(finish_rows(parts, bits)[0])
+            for parts, bits in (
+                (down, high_bits), (gate_up, high_bits), (up_up, high_bits),
+                (out_up, bits_of(dsize)),
+                (split_rows(query_up), bits_of(dsize)),
+                (split_rows(kv_up), bits_of(dsize)),
+            )
+        ]
+        gains = jnp.stack(
+            [gain_sum(rows, inverse, attn_back), gain_sum(middle, inverse_mlp, mlp_back)]
+        )
+        return outgoing.astype(bf16), sums, gains
 
     def to_places(rows):
         return exchange(reorder(rows, 1).reshape(micro, nloc, width))[None]
 
+    kept = forward(rows_in)
+    received = jnp.concatenate(
+        [shifted(layer_output(kept, chunk), "section", 1) for chunk in token_chunks(4)], axis=0
+    )
+    received, late_cotangent = lax.optimization_barrier((received, cotangent))
+    kept = forward(jnp.where(first_section, rows_in, received))
+    second_out = layer_output(kept, slice(0, n))
+    cot = spread_inputs(late_cotangent)
+    first_grad = backward(cot, kept, False)
     outputs = to_places(second_out)
+    returned = jnp.concatenate([shifted(part, "section", -1) for part in first_grad], axis=0)
+    returned, outputs = lax.optimization_barrier((returned, outputs))
+    second_grad, sums, gains = backward(jnp.where(first_section, returned, cot), kept, True)
     input_grads = to_places(second_grad)
-    down, gate, up, out, query, kv, attn_sum, mlp_sum = done
+    down, gate, up, out, query, kv = sums
     kv = lax.all_gather(kv, "tensor", axis=0).transpose(1, 0, 2).reshape(share, 2 * dims)
-    gains = jnp.stack([reorder(attn_sum, 0), reorder(mlp_sum, 0)])
-    gains = lax.psum(gains, ("dp", "tensor"))
+    gains = reorder(gains, 1)
+    for axis, size in (("dp", dsize), ("tensor", tsize)):
+        for bit in bits_of(size):
+            gains = gains + swapped(gains, axis, bit)
     return (
         outputs,
         input_grads,

time: 2060 us -> 1860 us (0.903)
  matrix products: 873 us -> 512 us
  waiting for transfers between devices: 579 us -> 736 us
  blocking collectives: 148 us -> 0 us
  Pallas kernels: 0 us -> 116 us
  local copies, waits for them, and re-layouts: 171 us -> 225 us
  other arithmetic: 203 us -> 159 us
  starting transfers between devices: 41.9 us -> 67.7 us
    dot_general x104 -> x0, matrix products: 338 us -> none  [the longest x16 76.7 us: per_head(): mixed = jnp.einsum('cqk,kd->cqd', probs, v, preferred_element_type=f32)]
    psum x1 -> x0, blocking collectives: 148 us -> none  [local(): gains = lax.psum(gains, ('dp', 'tensor'))]
    ppermute x48 -> x54, waiting for transfers between devices: 386 us -> 513 us  [swapped(): lax.ppermute(array, axis, [(i, i ^ bit) for i in range(lax.axis_size(axis...]
    pallas_call x0 -> x4, Pallas kernels: none -> 116 us  [the longest x2 74.9 us: attention_backward(): pl.pallas_call(functools.partial(attend_backward_kernel, single=single),...]
    sub x8 -> x0, matrix products: 59.8 us -> none  [per_head(): weights = jnp.exp(scores - top)]
    all_gather x5, waiting for transfers between devices: 75 us -> 121 us  [gather_weight(): whole = lax.all_gather(shard, 'tensor', axis=0)]
    dot_general x12 -> x21, matrix products: 206 us -> 238 us  [mm_nt(): lax.dot_general(left, right, (((1,), (1,)), ((), ())), preferred_element_...]
    reshape x5 -> x10, local copies, waits for them, and re-layouts: 13.7 us -> 43 us  [the longest x2 17.4 us: forward(): mm(normed, wq).reshape(n, KV_HEADS, copies, HD).transpose(1, 2, 0, 3)]
  transfers between devices with their start and end apart: 62 -> 74, of which waited for: 16 -> 29; matrix products, arithmetic and copies ran while one was open for 23% -> 32% of each run, Pallas kernels for 0% -> 3%
where the time goes in v2:
time: 1860 us; the launch traced here: 1830 us
  waiting for transfers between devices  736 us (40%)
  matrix products  512 us (28%)
  local copies, waits for them, and re-layouts  225 us (12%)
  other arithmetic  159 us (9%)
  Pallas kernels  116 us (6%)
  starting transfers between devices  67.7 us (4%)
    ppermute x54, waiting for transfers between devices, swapped(): lax.ppermute(array, axis, [(i, i ^ bit) for i in range(lax.axis_size(axis...  513 us
    dot_general x21, matrix products, mm_nt(): lax.dot_general(left, right, (((1,), (1,)), ((), ())), preferred_element_...  238 us
    dot_general x12, matrix products, mm(): return jnp.dot(left, right, preferred_element_type=f32)  194 us
    all_gather x5, waiting for transfers between devices, gather_weight(): whole = lax.all_gather(shard, 'tensor', axis=0)  121 us
    ppermute x8, waiting for transfers between devices, shifted(): return lax.ppermute(array, axis, pairs)  100 us
    dot_general x6, matrix products, mm_tn(): lax.dot_general(left, right, (((0,), (0,)), ((), ())), preferred_element_...  80.5 us
    pallas_call x2, Pallas kernels, attention_backward(): pl.pallas_call(functools.partial(attend_backward_kernel, single=single),...  74.9 us
    ppermute x54, starting transfers between devices, swapped(): lax.ppermute(array, axis, [(i, i ^ bit) for i in range(lax.axis_size(axis...  54.4 us
  transfers between devices with their start and end apart: 74, of which 29 were waited for; matrix products, arithmetic and copies ran while one was open for 32% of the time, Pallas kernels for 3%

profile of v2, /device:TPU:0, one launch (start us, length us, event | category | flops | bytes accessed | tf_op | source)
XLA Modules:
  0.0 1833.8 jit_solution(16693012707988724589)
XLA Ops:
  20.4 23.7 %collective-permute-done = bf16[1,256,768]{2,1,0:T(8,128)(2,1)S(1)} collective-permute-done((bf16[1,256,768]{2,1,0:T(8,128)(2,1)S(1)}, bf16[1,256,768]{2,1,0:T(8,128)(2,1)S(1)}, u32[]{:S(2)}, u32[]{:S(2)}) %collective-permute-start) | collective-permute-done | bytes 393248 | tf_op jit(solution)/shard_map/ppermute | solution.py:28
  71.8 21.3 %collective-permute-done.8 = bf16[384,1536]{1,0:T(8,128)(2,1)} collective-permute-done((bf16[384,1536]{1,0:T(8,128)(2,1)}, bf16[384,1536]{1,0:T(8,128)(2,1)}, u32[]{:S(2)}, u32[]{:S(2)}) %collective-permute-start.8) | collective-permute-done | bytes 1179680 | tf_op jit(solution)/shard_map/ppermute | solution.py:28
  108.8 56.4 %all-gather.11.cloned.1.call-done = bf16[4,384,1024]{2,1,0:T(8,128)(2,1)} async-done(((bf16[1,384,1024]{2,1,0:T(8,128)(2,1)}), bf16[4,384,1024]{2,1,0:T(8,128)(2,1)}) %all-gather.11.cloned.1.call-update) | async-done | bytes 3145744 | tf_op jit(solution)/shard_map/all_gather | solution.py:248
  235.0 57.4 %all-gather.19.cloned.1.call-done = bf16[1536,1024]{1,0:T(8,128)(2,1)} async-done(((bf16[384,1024]{1,0:T(8,128)(2,1)}), bf16[1536,1024]{1,0:T(8,128)(2,1)}) %all-gather.19.cloned.1.call-update) | async-done | bytes 3145744 | tf_op jit(solution)/shard_map/all_gather | solution.py:248
  304.0 20.4 %attend_forward.2 = (bf16[8,2,1024,96]{3,2,1,0:T(8,128)(2,1)S(1)}, f32[8,4,1,512]{3,2,1,0:T(1,128)}) custom-call(s32[1]{0:T(128)} %bitcast.1.offset_ref, bf16[8,2,1024,96]{3,2,1,0:T(8,128)(2,1)S(1)} %pad_maximum_fusion.6.q_ref, bf16[8,1024,96]{2,1,0:T(8,128)(2,1)S(1)} %copy.173.k_ref, bf16[8,96,1024]{2,1,0:T(8,128)(2,1)S(1)} %bitcast.183), custom_call_target="tpu_custom_call" | custom-call | flops 12884901888 | bytes 16777216 | tf_op jit(solution)/shard_map/attend_forward/pallas_call | solution.py:166
  345.0 30.7 %collective-permute-done.20 = bf16[384,4096]{0,1:T(8,128)(2,1)} collective-permute-done((bf16[384,4096]{0,1:T(8,128)(2,1)}, bf16[384,4096]{0,1:T(8,128)(2,1)}, u32[]{:S(2)}, u32[]{:S(2)}) %collective-permute-start.20) | collective-permute-done | bytes 3145760 | tf_op jit(solution)/shard_map/ppermute | solution.py:28
  375.7 22.0 %fusion.95 = f32[1024,4096]{1,0:T(8,128)} fusion(f32[1024,1536]{1,0:T(8,128)} %get-tuple-element.197, f32[1536]{0:T(1024)S(1)} %pad_maximum_fusion.26, f32[1024]{0:T(1024)S(1)} %add_rsqrt_fusion.2, bf16[384,4096]{0,1:T(8,128)(2,1)} %collective-permute-done.15, bf16[384,4096]{0,1:T(8,128)(2,1)} %collective-permute-done.14, ...), kind=kOutput, calls=%fused_computation.296 | convolution fusion | flops 12939952128 | bytes 35661824 | tf_op jit(solution)/shard_map/dot_general | solution.py:45
  397.7 22.5 %multiply_convert_fusion.1 = bf16[1024,4096]{1,0:T(8,128)(2,1)} fusion(f32[1024,4096]{1,0:T(8,128)} %fusion.95, f32[1024,1536]{1,0:T(8,128)} %get-tuple-element.197, f32[1536]{0:T(1024)S(1)} %pad_maximum_fusion.26, f32[1024]{0:T(1024)S(1)} %add_rsqrt_fusion.2, bf16[384,4096]{0,1:T(8,128)(2,1)} %collective-permute-done.18, ...), kind=kOutput, calls=%fused_computation.20 | convolution fusion | flops 12965117952 | bytes 44050432 | tf_op jit(solution)/shard_map/dot_general | solution.py:45
  466.1 16.9 collective-permute-done.24
  553.8 20.7 %attend_forward.3 = (bf16[8,2,1024,96]{3,2,1,0:T(8,128)(2,1)S(1)}, f32[8,4,1,512]{3,2,1,0:T(1,128)S(1)}) custom-call(s32[1]{0:T(128)} %bitcast.1.offset_ref, bf16[8,2,1024,96]{3,2,1,0:T(8,128)(2,1)S(1)} %pad_maximum_fusion.7.q_ref, bf16[8,1024,96]{2,1,0:T(8,128)(2,1)S(1)} %copy-done.6, bf16[8,96,1024]{2,1,0:T(8,128)(2,1)S(1)} %bitcast.175), custom_call_target="tpu_custom_call" | custom-call | flops 12884901888 | bytes 16777216 | tf_op jit(solution)/shard_map/attend_forward/pallas_call | solution.py:166
  597.1 20.0 %fusion.104 = f32[1024,4096]{1,0:T(8,128)} fusion(bf16[1024,1536]{1,0:T(8,128)(2,1)S(1)} %multiply_convert_fusion.2, bf16[384,4096]{0,1:T(8,128)(2,1)} %collective-permute-done.15, bf16[384,4096]{0,1:T(8,128)(2,1)} %collective-permute-done.14, bf16[384,4096]{0,1:T(8,128)(2,1)} %collective-permute-done.13, bf16[384,4096]{0,1:T(8,128)(2,1)} %bitcast.22), kind=kOutput, calls=%fused_computation.301 | convolution fusion | flops 12935233536 | bytes 32505856 | tf_op jit(solution)/shard_map/dot_general | solution.py:45
  617.1 28.8 %multiply_convert_fusion = (bf16[1024,4096]{1,0:T(8,128)(2,1)}, bf16[1024,4096]{1,0:T(8,128)(2,1)}, bf16[1024,4096]{1,0:T(8,128)(2,1)}) fusion(f32[1024,4096]{1,0:T(8,128)} %fusion.104, bf16[1024,1536]{1,0:T(8,128)(2,1)} %copy-done.63, bf16[384,4096]{0,1:T(8,128)(2,1)} %collective-permute-done.18, bf16[384,4096]{0,1:T(8,128)(2,1)} %collective-permute-done.17, ...), kind=kOutput, calls=%fused_computation.19 | convolution fusion | flops 12968787968 | bytes 57671680 | tf_op jit(solution)/shard_map/dot_general | solution.py:45
  646.0 20.3 %add_convert_fusion.13 = bf16[1024,1536]{1,0:T(8,128)(2,1)} fusion(f32[1024,1536]{1,0:T(8,128)} %copy-done.18, bf16[1024,4096]{1,0:T(8,128)(2,1)} %get-tuple-element.104, bf16[384,4096]{0,1:T(8,128)(2,1)} %collective-permute-done.21, bf16[384,4096]{0,1:T(8,128)(2,1)} %collective-permute-done.20, bf16[384,4096]{0,1:T(8,128)(2,1)} %collective-permute-done.19, ...), kind=kOutput, calls=%fused_computation.75 | convolution fusion | flops 12938379264 | bytes 30408704 | tf_op jit(solution)/shard_map/dot_general | solution.py:49
  718.5 24.8 %collective-permute-done.34 = bf16[1,256,1536]{2,1,0:T(8,128)(2,1)S(1)} collective-permute-done((bf16[1,256,1536]{2,1,0:T(8,128)(2,1)}, bf16[1,256,1536]{2,1,0:T(8,128)(2,1)S(1)}, u32[]{:S(2)}, u32[]{:S(2)}) %collective-permute-start.34) | collective-permute-done | bytes 786464 | tf_op jit(solution)/shard_map/ppermute | solution.py:28
  747.8 20.6 %fusion.96 = f32[1024,4096]{1,0:T(8,128)} fusion(bf16[1024,384]{1,0:T(8,128)(2,1)S(1)} %get-tuple-element.162, bf16[1024,384]{1,0:T(8,128)(2,1)S(1)} %get-tuple-element.163, bf16[1024,384]{1,0:T(8,128)(2,1)} %get-tuple-element.164, bf16[1024,384]{1,0:T(8,128)(2,1)S(1)} %get-tuple-element.161, bf16[384,4096]{0,1:T(8,128)(2,1)} %collective-permute-done.21, ...), kind=kOutput, calls=%fused_computation.297 | convolution fusion | flops 12947816448 | bytes 32505856 | tf_op jit(solution)/shard_map/dot_general | solution.py:45
  768.4 20.7 %fusion.15 = f32[1024,1536]{1,0:T(8,128)} fusion(f32[1024,4096]{1,0:T(8,128)} %fusion.96, bf16[1024,4096]{1,0:T(8,128)(2,1)} %get-tuple-element.105, bf16[384,4096]{0,1:T(8,128)(2,1)} %collective-permute-done.18, bf16[384,4096]{0,1:T(8,128)(2,1)} %collective-permute-done.17, bf16[384,4096]{0,1:T(8,128)(2,1)} %copy-done.106, bf16[384,4096]{0,1:T(8,128)(2,1)} %bitcast.25), kind=kOutput, calls=%fused_computation.39 | convolution fusion | flops 12964593664 | bytes 44040192 | tf_op jit(solution)/shard_map/dot_general | solution.py:49
  789.1 28.9 %multiply_reduce_fusion.2 = (f32[1024]{0:T(1024)S(1)}, f32[1024,1536]{1,0:T(8,128)}) fusion(f32[1024,1536]{1,0:T(8,128)} %copy-done.18, f32[1536]{0:T(1024)S(1)} %copy-done.84, f32[1024,1536]{1,0:T(8,128)} %fusion.15, bf16[384,4096]{0,1:T(8,128)(2,1)} %collective-permute-done.15, bf16[384,4096]{0,1:T(8,128)(2,1)} %collective-permute-done.14, ...), kind=kOutput, calls=%fused_computation.77 | convolution fusion | flops 12991855616 | bytes 65021952 | tf_op jit(solution)/shard_map/dot_general | solution.py:49
  848.6 37.4 %attend_backward.2 = (bf16[8,2,1024,96]{3,2,1,0:T(8,128)(2,1)S(1)}, bf16[8,1024,96]{2,1,0:T(8,128)(2,1)S(1)}, bf16[8,1024,96]{2,1,0:T(8,128)(2,1)S(1)}) custom-call(s32[1]{0:T(128)} %bitcast.1.offset_ref, bf16[8,2,1024,96]{3,2,1,0:T(8,128)(2,1)} %copy-done, bf16[8,1024,96]{2,1,0:T(8,128)(2,1)S(1)} %copy-done.7, bf16[8,96,1024]{2,1,0:T(8,128)(2,1)S(1)} %copy-done.16, ...), custom_call_target="tpu_custom_call" | custom-call | flops 32212254720 | bytes 33554432 | tf_op jit(solution)/shard_map/attend_backward/pallas_call | solution.py:191
  996.7 16.9 collective-permute-done.30
  1045.8 20.2 %convolution_convert_fusion.2 = bf16[1536,4096]{1,0:T(8,128)(2,1)} fusion(bf16[1024,1536]{1,0:T(8,128)(2,1)S(1)} %broadcast_select_fusion, bf16[1024,4096]{1,0:T(8,128)(2,1)} %get-tuple-element.104), kind=kOutput, calls=%fused_computation.23 | convolution fusion | flops 12891193344 | bytes 24117248 | tf_op jit(solution)/shard_map/dot_general | solution.py:55
  1072.8 24.7 %fusion.12 = (bf16[1024,4096]{1,0:T(8,128)(2,1)}, bf16[1024,4096]{1,0:T(8,128)(2,1)}) fusion(bf16[1024,4096]{1,0:T(8,128)(2,1)} %get-tuple-element.105, bf16[1024,4096]{1,0:T(8,128)(2,1)} %get-tuple-element.200, bf16[1024,1536]{1,0:T(8,128)(2,1)S(1)} %broadcast_select_fusion, bf16[384,4096]{0,1:T(8,128)(2,1)} %collective-permute-done.21, ...), kind=kOutput, calls=%fused_computation.18 | convolution fusion | flops 12998148096 | bytes 49283072 | tf_op jit(solution)/shard_map/dot_general | solution.py:45
  1097.5 19.1 %convolution_convert_fusion = bf16[1536,4096]{1,0:T(8,128)(2,1)} fusion(bf16[1024,1536]{1,0:T(8,128)(2,1)S(1)} %copy-done.64, bf16[1024,4096]{1,0:T(8,128)(2,1)} %get-tuple-element.55), kind=kOutput, calls=%fused_computation.21 | convolution fusion | flops 12891193344 | bytes 24117248 | tf_op jit(solution)/shard_map/dot_general | solution.py:55
  1156.0 20.9 %fusion.105 = f32[1024,1536]{1,0:T(8,128)} fusion(bf16[1024,4096]{1,0:T(8,128)(2,1)} %get-tuple-element.55, bf16[384,4096]{0,1:T(8,128)(2,1)} %collective-permute-done.18, bf16[384,4096]{0,1:T(8,128)(2,1)} %collective-permute-done.17, bf16[384,4096]{0,1:T(8,128)(2,1)} %copy-done.106, bf16[384,4096]{0,1:T(8,128)(2,1)} %bitcast.25), kind=kOutput, calls=%fused_computation.302 | convolution fusion | flops 12935233536 | bytes 27262976 | tf_op jit(solution)/shard_map/dot_general | solution.py:49
  1176.9 22.3 %multiply_reduce_fusion = (f32[1536]{0:T(1024)S(1)}, f32[1024]{0:T(1024)S(1)}, f32[1024,1536]{1,0:T(8,128)}) fusion(f32[1024,1536]{1,0:T(8,128)} %copy-done.18, f32[1024]{0:T(1024)S(1)} %copy-done.89, f32[1536]{0:T(1024)S(1)} %copy-done.85, f32[1024,1536]{1,0:T(8,128)} %fusion.105, bf16[1024,4096]{1,0:T(8,128)(2,1)} %get-tuple-element.54, ...), kind=kOutput, calls=%fused_computation.66 | convolution fusion | flops 12946240512 | bytes 39866368 | tf_op jit(solution)/shard_map/dot_general | solution.py:49
  1247.5 37.4 %attend_backward.3 = (bf16[8,2,1024,96]{3,2,1,0:T(8,128)(2,1)S(1)}, bf16[8,1024,96]{2,1,0:T(8,128)(2,1)S(1)}, bf16[8,1024,96]{2,1,0:T(8,128)(2,1)S(1)}) custom-call(s32[1]{0:T(128)} %bitcast.1.offset_ref, bf16[8,2,1024,96]{3,2,1,0:T(8,128)(2,1)} %copy-done, bf16[8,1024,96]{2,1,0:T(8,128)(2,1)S(1)} %copy-done.7, bf16[8,96,1024]{2,1,0:T(8,128)(2,1)S(1)} %copy-done.17, ...), custom_call_target="tpu_custom_call" | custom-call | flops 32212254720 | bytes 33554432 | tf_op jit(solution)/shard_map/attend_backward/pallas_call | solution.py:191
  1346.8 24.9 %collective-permute-done.55 = bf16[384,1536]{1,0:T(8,128)(2,1)S(1)} collective-permute-done((bf16[384,1536]{1,0:T(8,128)(2,1)S(1)}, bf16[384,1536]{1,0:T(8,128)(2,1)S(1)}, u32[]{:S(2)}, u32[]{:S(2)}) %collective-permute-start.55) | collective-permute-done | bytes 1179680 | tf_op jit(solution)/shard_map/ppermute | solution.py:28
  1381.8 23.3 %collective-permute-done.52 = bf16[384,1536]{1,0:T(8,128)(2,1)S(1)} collective-permute-done((bf16[384,1536]{1,0:T(8,128)(2,1)S(1)}, bf16[384,1536]{1,0:T(8,128)(2,1)S(1)}, u32[]{:S(2)}, u32[]{:S(2)}) %collective-permute-start.52) | collective-permute-done | bytes 1179680 | tf_op jit(solution)/shard_map/ppermute | solution.py:28
  1412.6 90.6 %collective-permute-done.58 = bf16[384,1536]{1,0:T(8,128)(2,1)S(1)} collective-permute-done((bf16[384,1536]{1,0:T(8,128)(2,1)S(1)}, bf16[384,1536]{1,0:T(8,128)(2,1)S(1)}, u32[]{:S(2)}, u32[]{:S(2)}) %collective-permute-start.58) | collective-permute-done | bytes 1179680 | tf_op jit(solution)/shard_map/ppermute | solution.py:28
  1520.6 67.6 %collective-permute-done.60 = bf16[384,4096]{1,0:T(8,128)(2,1)} collective-permute-done((bf16[384,4096]{1,0:T(8,128)(2,1)}, bf16[384,4096]{1,0:T(8,128)(2,1)}, u32[]{:S(2)}, u32[]{:S(2)}) %collective-permute-start.60) | collective-permute-done | bytes 3145760 | tf_op jit(solution)/shard_map/ppermute | solution.py:28
  1618.8 43.7 %collective-permute-done.59 = bf16[384,4096]{1,0:T(8,128)(2,1)S(1)} collective-permute-done((bf16[384,4096]{1,0:T(8,128)(2,1)}, bf16[384,4096]{1,0:T(8,128)(2,1)S(1)}, u32[]{:S(2)}, u32[]{:S(2)}) %collective-permute-start.59) | collective-permute-done | bytes 3145760 | tf_op jit(solution)/shard_map/ppermute | solution.py:28
  1682.4 23.8 %collective-permute-done.48 = f32[2,1536]{1,0:T(2,128)S(1)} collective-permute-done((f32[2,1536]{1,0:T(2,128)S(1)}, f32[2,1536]{1,0:T(2,128)S(1)}, u32[]{:S(2)}, u32[]{:S(2)}) %collective-permute-start.48) | collective-permute-done | bytes 12320 | tf_op jit(solution)/shard_map/ppermute | solution.py:28
  1712.3 92.4 %collective-permute-done.44 = bf16[1,256,1536]{2,1,0:T(8,128)(2,1)S(1)} collective-permute-done((bf16[1,256,1536]{2,1,0:T(8,128)(2,1)S(1)}, bf16[1,256,1536]{2,1,0:T(8,128)(2,1)S(1)}, u32[]{:S(2)}, u32[]{:S(2)}) %collective-permute-start.44) | collective-permute-done | bytes 786464 | tf_op jit(solution)/shard_map/ppermute | solution.py:28
  (572 shorter events, 795.8 us)
Async XLA Ops:
  7.2 85.9 %all-gather.9.cloned.1.call-start = ((), (), s32[]{:S(2)}) async-start(), calls=%async_computation.6 | async-start | bytes 1474560 | tf_op jit(solution)/shard_map/all_gather | solution.py:248
  7.9 93.1 %all-gather.17.cloned.1.call-start = ((), (), s32[]{:S(2)}) async-start(), calls=%async_computation.16 | async-start | bytes 1474560 | tf_op jit(solution)/shard_map/all_gather | solution.py:248
  9.8 155.4 %all-gather.11.cloned.1.call-start = ((), (), s32[]{:S(2)}) async-start(), calls=%async_computation.7 | async-start | bytes 3932160 | tf_op jit(solution)/shard_map/all_gather | solution.py:248
  10.6 218.3 %all-gather.13.cloned.1.call-start = ((), (), s32[]{:S(2)}) async-start(), calls=%async_computation.8 | async-start | bytes 3932160 | tf_op jit(solution)/shard_map/all_gather | solution.py:248
  11.2 281.3 %all-gather.19.cloned.1.call-start = ((), (), s32[]{:S(2)}) async-start(), calls=%async_computation.17 | async-start | bytes 3932160 | tf_op jit(solution)/shard_map/all_gather | solution.py:248
  67.7 102.2 %collective-permute-start.7 = (bf16[384,1536]{1,0:T(8,128)(2,1)}, bf16[384,1536]{1,0:T(8,128)(2,1)}, u32[]{:S(2)}, u32[]{:S(2)}) collective-permute-start(bf16[384,1536]{1,0:T(8,128)(2,1)} %pad_maximum_fusion.21), channel_id=1, source_target_pairs={{0,4},{4,0},{8,12},{12,8},{1,5},{5,1},{9,13},{13,9},{2,6},{6,2},{1... | collective-permute-start | bytes 3538952 | tf_op jit(solution)/shard_map/ppermute | solution.py:28
  68.9 1451.6 %reduce-scatter.9.cloned.1.call-start = ((), (), s32[]{:S(2)}) async-start(), calls=%async_computation.10 | async-start | bytes 1474560 | tf_op jit(solution)/shard_map/reduce_scatter | solution.py:274
  93.1 77.3 %collective-permute-start.9 = (bf16[384,1536]{1,0:T(8,128)(2,1)}, bf16[384,1536]{1,0:T(8,128)(2,1)}, u32[]{:S(2)}, u32[]{:S(2)}) collective-permute-start(bf16[384,1536]{1,0:T(8,128)(2,1)} %collective-permute-done.8), channel_id=1, source_target_pairs={{0,4},{4,0},{8,12},{12,8},{1,5},{5,1},{9,13},{13,9},{2,6},{6,2},{1... | collective-permute-start | bytes 3538952 | tf_op jit(solution)/shard_map/ppermute | solution.py:28
  95.7 74.2 %collective-permute-start.5 = (bf16[384,1536]{0,1:T(8,128)(2,1)}, bf16[384,1536]{0,1:T(8,128)(2,1)}, u32[]{:S(2)}, u32[]{:S(2)}) collective-permute-start(bf16[384,1536]{0,1:T(8,128)(2,1)} %bitcast.238), channel_id=1, source_target_pairs={{0,8},{4,12},{8,0},{12,4},{1,9},{5,13},{9,1},{13,5},{2,10},{6,14},... | collective-permute-start | bytes 3538952 | tf_op jit(solution)/shard_map/ppermute | solution.py:28
  97.2 98.8 %collective-permute-start.4 = (bf16[384,1536]{0,1:T(8,128)(2,1)}, bf16[384,1536]{0,1:T(8,128)(2,1)}, u32[]{:S(2)}, u32[]{:S(2)}) collective-permute-start(bf16[384,1536]{0,1:T(8,128)(2,1)} %bitcast.239), channel_id=1, source_target_pairs={{0,4},{4,0},{8,12},{12,8},{1,5},{5,1},{9,13},{13,9},{2,6},{6,2},{1... | collective-permute-start | bytes 3538952 | tf_op jit(solution)/shard_map/ppermute | solution.py:28
  103.4 193.7 %collective-permute-start.11 = (bf16[384,1536]{0,1:T(8,128)(2,1)}, bf16[384,1536]{0,1:T(8,128)(2,1)}, u32[]{:S(2)}, u32[]{:S(2)}) collective-permute-start(bf16[384,1536]{0,1:T(8,128)(2,1)} %bitcast.247), channel_id=1, source_target_pairs={{0,8},{4,12},{8,0},{12,4},{1,9},{5,13},{9,1},{13,5},{2,10},{6,14},... | collective-permute-start | bytes 3538952 | tf_op jit(solution)/shard_map/ppermute | solution.py:28
  169.9 133.4 %collective-permute-start.10 = (bf16[384,1536]{0,1:T(8,128)(2,1)}, bf16[384,1536]{0,1:T(8,128)(2,1)}, u32[]{:S(2)}, u32[]{:S(2)}) collective-permute-start(bf16[384,1536]{0,1:T(8,128)(2,1)} %bitcast.248), channel_id=1, source_target_pairs={{0,4},{4,0},{8,12},{12,8},{1,5},{5,1},{9,13},{13,9},{2,6},{6,2},{1... | collective-permute-start | bytes 3538952 | tf_op jit(solution)/shard_map/ppermute | solution.py:28
  170.5 128.2 %collective-permute-start.14 = (bf16[384,4096]{0,1:T(8,128)(2,1)}, bf16[384,4096]{0,1:T(8,128)(2,1)}, u32[]{:S(2)}, u32[]{:S(2)}) collective-permute-start(bf16[384,4096]{0,1:T(8,128)(2,1)} %bitcast.22), channel_id=1, source_target_pairs={{0,8},{4,12},{8,0},{12,4},{1,9},{5,13},{9,1},{13,5},{2,10},{6,14},... | collective-permute-start | bytes 9437192 | tf_op jit(solution)/shard_map/ppermute | solution.py:28
  225.4 119.1 %collective-permute-start.13 = (bf16[384,4096]{0,1:T(8,128)(2,1)}, bf16[384,4096]{0,1:T(8,128)(2,1)}, u32[]{:S(2)}, u32[]{:S(2)}) collective-permute-start(bf16[384,4096]{0,1:T(8,128)(2,1)} %bitcast.22), channel_id=1, source_target_pairs={{0,4},{4,0},{8,12},{12,8},{1,5},{5,1},{9,13},{13,9},{2,6},{6,2},{1... | collective-permute-start | bytes 9437192 | tf_op jit(solution)/shard_map/ppermute | solution.py:28
  233.6 111.4 %collective-permute-start.17 = (bf16[384,4096]{0,1:T(8,128)(2,1)}, bf16[384,4096]{0,1:T(8,128)(2,1)}, u32[]{:S(2)}, u32[]{:S(2)}) collective-permute-start(bf16[384,4096]{0,1:T(8,128)(2,1)} %bitcast.25), channel_id=1, source_target_pairs={{0,8},{4,12},{8,0},{12,4},{1,9},{5,13},{9,1},{13,5},{2,10},{6,14},... | collective-permute-start | bytes 9437192 | tf_op jit(solution)/shard_map/ppermute | solution.py:28
  297.1 78.5 %collective-permute-start.20 = (bf16[384,4096]{0,1:T(8,128)(2,1)}, bf16[384,4096]{0,1:T(8,128)(2,1)}, u32[]{:S(2)}, u32[]{:S(2)}) collective-permute-start(bf16[384,4096]{0,1:T(8,128)(2,1)} %bitcast.31), channel_id=1, source_target_pairs={{0,8},{4,12},{8,0},{12,4},{1,9},{5,13},{9,1},{13,5},{2,10},{6,14},... | collective-permute-start | bytes 9437192 | tf_op jit(solution)/shard_map/ppermute | solution.py:28
  298.6 77.1 %collective-permute-start.15 = (bf16[384,4096]{0,1:T(8,128)(2,1)}, bf16[384,4096]{0,1:T(8,128)(2,1)}, u32[]{:S(2)}, u32[]{:S(2)}) collective-permute-start(bf16[384,4096]{0,1:T(8,128)(2,1)} %collective-permute-done.14), channel_id=1, source_target_pairs={{0,4},{4,0},{8,12},{12,8},{1,5},{5,1},{9,13},{13,9},{2,6},{6,2},{1... | collective-permute-start | bytes 9437192 | tf_op jit(solution)/shard_map/ppermute | solution.py:28
  344.4 75.7 %collective-permute-start.19 = (bf16[384,4096]{0,1:T(8,128)(2,1)}, bf16[384,4096]{0,1:T(8,128)(2,1)}, u32[]{:S(2)}, u32[]{:S(2)}) collective-permute-start(bf16[384,4096]{0,1:T(8,128)(2,1)} %bitcast.31), channel_id=1, source_target_pairs={{0,4},{4,0},{8,12},{12,8},{1,5},{5,1},{9,13},{13,9},{2,6},{6,2},{1... | collective-permute-start | bytes 9437192 | tf_op jit(solution)/shard_map/ppermute | solution.py:28
  713.1 266.6 %collective-permute-start.35 = (bf16[1,256,1536]{2,1,0:T(8,128)(2,1)}, bf16[1,256,1536]{2,1,0:T(8,128)(2,1)}, u32[]{:S(2)}, u32[]{:S(2)}) collective-permute-start(bf16[1,256,1536]{2,1,0:T(8,128)(2,1)} %get-tuple-element.155), channel_id=1, source_target_pairs={{0,2},{1,3},{2,0},{3,1},{4,6},{5,7},{6,4},{7,5},{8,10},{9,11},{10,... | collective-permute-start | bytes 2359304 | tf_op jit(solution)/shard_map/ppermute | solution.py:28
  713.8 269.3 %collective-permute-start.36 = (bf16[1,256,1536]{2,1,0:T(8,128)(2,1)}, bf16[1,256,1536]{2,1,0:T(8,128)(2,1)}, u32[]{:S(2)}, u32[]{:S(2)}) collective-permute-start(bf16[1,256,1536]{2,1,0:T(8,128)(2,1)} %get-tuple-element.154), channel_id=1, source_target_pairs={{0,3},{1,2},{2,1},{3,0},{4,7},{5,6},{6,5},{7,4},{8,11},{9,10},{10,... | collective-permute-start | bytes 2359304 | tf_op jit(solution)/shard_map/ppermute | solution.py:28
  1374.6 430.3 %reduce-scatter.7.cloned.1.call-start = ((), (), s32[]{:S(2)}) async-start(), calls=%async_computation.9 | async-start | bytes 1474560 | tf_op jit(solution)/shard_map/reduce_scatter | solution.py:274
  1407.9 399.0 %reduce-scatter.11.cloned.1.call-start = ((), (), s32[]{:S(2)}) async-start(), calls=%async_computation.12 | async-start | bytes 1474560 | tf_op jit(solution)/shard_map/reduce_scatter | solution.py:274
  1408.0 100.4 %collective-permute-start.61 = (bf16[384,4096]{1,0:T(8,128)(2,1)}, bf16[384,4096]{1,0:T(8,128)(2,1)}, u32[]{:S(2)}, u32[]{:S(2)}) collective-permute-start(bf16[384,4096]{1,0:T(8,128)(2,1)} %get-tuple-element.72), channel_id=1, source_target_pairs={{0,8},{4,12},{8,0},{12,4},{1,9},{5,13},{9,1},{13,5},{2,10},{6,14},... | collective-permute-start | bytes 9437192 | tf_op jit(solution)/shard_map/ppermute | solution.py:28
  1411.5 91.8 %collective-permute-start.58 = (bf16[384,1536]{1,0:T(8,128)(2,1)S(1)}, bf16[384,1536]{1,0:T(8,128)(2,1)S(1)}, u32[]{:S(2)}, u32[]{:S(2)}) collective-permute-start(bf16[384,1536]{1,0:T(8,128)(2,1)S(1)} %add_convert_fusion.15), channel_id=1, source_target_pairs={{0,8},{4,12},{8,0},{12,4},{1,9},{5,13},{9,1},{13,5},{2,10},{6,14},... | collective-permute-start | bytes 3538952 | tf_op jit(solution)/shard_map/ppermute | solution.py:28
  1508.4 300.4 %reduce-scatter.17.cloned.1.call-start = ((), (), s32[]{:S(2)}) async-start(), calls=%async_computation.15 | async-start | bytes 3932160 | tf_op jit(solution)/shard_map/reduce_scatter | solution.py:274
  1518.9 292.2 %all-gather.15.cloned.1.call-start = ((), (), s32[]{:S(2)}) async-start(), calls=%async_computation.11 | async-start | bytes 1474560 | tf_op jit(solution)/shard_map/all_gather | solution.py:444
  1519.0 69.2 %collective-permute-start.60 = (bf16[384,4096]{1,0:T(8,128)(2,1)}, bf16[384,4096]{1,0:T(8,128)(2,1)}, u32[]{:S(2)}, u32[]{:S(2)}) collective-permute-start(bf16[384,4096]{1,0:T(8,128)(2,1)} %get-tuple-element.70), channel_id=1, source_target_pairs={{0,8},{4,12},{8,0},{12,4},{1,9},{5,13},{9,1},{13,5},{2,10},{6,14},... | collective-permute-start | bytes 9437192 | tf_op jit(solution)/shard_map/ppermute | solution.py:28
  1520.6 301.0 %reduce-scatter.15.cloned.1.call-start = ((), (), s32[]{:S(2)}) async-start(), calls=%async_computation.14 | async-start | bytes 3932160 | tf_op jit(solution)/shard_map/reduce_scatter | solution.py:274
  1594.2 229.8 %reduce-scatter.13.cloned.1.call-start = ((), (), s32[]{:S(2)}) async-start(), calls=%async_computation.13 | async-start | bytes 3932160 | tf_op jit(solution)/shard_map/reduce_scatter | solution.py:274
  1594.3 68.2 %collective-permute-start.59 = (bf16[384,4096]{1,0:T(8,128)(2,1)}, bf16[384,4096]{1,0:T(8,128)(2,1)S(1)}, u32[]{:S(2)}, u32[]{:S(2)}) collective-permute-start(bf16[384,4096]{1,0:T(8,128)(2,1)} %get-tuple-element.68), channel_id=1, source_target_pairs={{0,8},{4,12},{8,0},{12,4},{1,9},{5,13},{9,1},{13,5},{2,10},{6,14},... | collective-permute-start | bytes 9437192 | tf_op jit(solution)/shard_map/ppermute | solution.py:28
  1709.1 95.6 %collective-permute-start.44 = (bf16[1,256,1536]{2,1,0:T(8,128)(2,1)S(1)}, bf16[1,256,1536]{2,1,0:T(8,128)(2,1)S(1)}, u32[]{:S(2)}, u32[]{:S(2)}) collective-permute-start(bf16[1,256,1536]{2,1,0:T(8,128)(2,1)S(1)} %get-tuple-element.148), channel_id=1, source_target_pairs={{0,2},{1,3},{2,0},{3,1},{4,6},{5,7},{6,4},{7,5},{8,10},{9,11},{10,... | collective-permute-start | bytes 2359304 | tf_op jit(solution)/shard_map/ppermute | solution.py:28
  1709.2 95.6 %collective-permute-start.45 = (bf16[1,256,1536]{2,1,0:T(8,128)(2,1)S(1)}, bf16[1,256,1536]{2,1,0:T(8,128)(2,1)S(1)}, u32[]{:S(2)}, u32[]{:S(2)}) collective-permute-start(bf16[1,256,1536]{2,1,0:T(8,128)(2,1)S(1)} %get-tuple-element.147), channel_id=1, source_target_pairs={{0,3},{1,2},{2,1},{3,0},{4,7},{5,6},{6,5},{7,4},{8,11},{9,10},{10,... | collective-permute-start | bytes 2359304 | tf_op jit(solution)/shard_map/ppermute | solution.py:28
  (160 other events, 4100.6 us)
Sparse Core Ops, SparseCore 0:
  9.6 59.7 all-gather.8
  71.6 29.4 all-gather.16
  102.6 62.6 all-gather.10
  166.7 62.1 all-gather.12
  230.3 62.1 all-gather.18
  1374.7 27.3 reduce-scatter.8
  1408.0 27.3 reduce-scatter.6
  1508.5 27.3 reduce-scatter.10
  1538.2 58.9 reduce-scatter.16
  1598.6 30.4 all-gather.14
  1631.4 69.1 reduce-scatter.14
  1702.7 107.1 reduce-scatter.12

commit v3 on v2

--- a/solution.py
+++ b/solution.py
@@ -221,6 +221,8 @@
     seg = t // micro
     copies = HEADS // KV_HEADS
     dims = KV_HEADS * HD
+    low_bits = bits_of(dsize)[:1]
+    high_bits = bits_of(dsize)[1:]
     same_seq = [[g + micro * r for r in range(ranks)] for g in range(micro)]
 
     def exchange(blocks):
@@ -237,21 +239,35 @@
             axis=axis,
         )
 
-    def spread_rows(block):
+    def swap_in(parts, bit):
+        parts = dict(parts)
+        for m in sorted(parts):
+            parts[m ^ bit] = swapped(parts[m], "dp", bit)
+        return parts
+
+    def spread_far(block):
         parts = {0: block}
-        for bit in reversed(bits_of(dsize)):
-            for m in sorted(parts):
-                parts[m ^ bit] = swapped(parts[m], "dp", bit)
+        for bit in reversed(high_bits):
+            parts = swap_in(parts, bit)
+        return parts
+
+    def spread_near(parts):
+        for bit in low_bits:
+            parts = swap_in(parts, bit)
         return jnp.concatenate([parts[m] for m in range(dsize)], axis=0)
 
-    def gather_weight(shard):
+    def gather_columns(shard):
         whole = lax.all_gather(shard, "tensor", axis=0)
-        whole = whole.transpose(1, 0, 2).reshape(share, tsize * shard.shape[1])
-        return spread_rows(whole)
-
-    def spread_inputs(array):
+        return whole.transpose(1, 0, 2).reshape(share, tsize * shard.shape[1])
+
+    def tied(*arrays):
+        return lax.optimization_barrier(arrays)
+
+    def exchange_half(array):
         side = lax.axis_index("section")
-        mine = exchange(lax.dynamic_slice_in_dim(array, side * (width // 2), width // 2, 2))
+        return exchange(lax.dynamic_slice_in_dim(array, side * (width // 2), width // 2, 2))
+
+    def join_halves(mine):
         other = swapped(mine, "section", 1)
         whole = jnp.concatenate(
             [jnp.where(first_section, mine, other), jnp.where(first_section, other, mine)], axis=2
@@ -261,33 +277,40 @@
     def split_rows(grad):
         return {m: grad[m * share : (m + 1) * share].astype(bf16) for m in range(dsize)}
 
-    def add_partner(parts, bit):
-        summed = {}
-        for m in sorted(parts):
-            if not m & bit:
-                got = swapped(parts[m ^ bit], "dp", bit)
-                summed[m] = (parts[m].astype(f32) + got.astype(f32)).astype(bf16)
-        return summed
+    def add_partner(parts, bits):
+        for bit in bits:
+            summed = {}
+            for m in sorted(parts):
+                if not m & bit:
+                    got = swapped(parts[m ^ bit], "dp", bit)
+                    summed[m] = (parts[m].astype(f32) + got.astype(f32)).astype(bf16)
+            parts = summed
+        return parts
 
     def scatter_columns(part):
         part = part.reshape(share, tsize, -1).transpose(1, 0, 2)
         return lax.psum_scatter(part, "tensor", scatter_dimension=0)
 
-    def finish_rows(parts, bits):
-        for bit in bits:
-            parts = add_partner(parts, bit)
-        return parts
-
-    rows_in = spread_inputs(inputs)
+    PIECES = 2
+    cols = w_gate.shape[2] // PIECES
+
+    def pieces_of(array):
+        return [array[:, i * cols : (i + 1) * cols] for i in range(PIECES)]
+
     attn_scale = reorder(attn_gain[0], 0)
     mlp_scale = reorder(mlp_gain[0], 0)
-
-    wq = gather_weight(w_query[0])
-    wkv = spread_rows(jnp.concatenate([w_key[0], w_value[0]], axis=1))
-    wo = gather_weight(w_out[0].T)
-    wg = gather_weight(w_gate[0])
-    wu = gather_weight(w_up[0])
-    wd = gather_weight(w_down[0].T)
+    mine = exchange_half(inputs)
+    far_kv = spread_far(jnp.concatenate([w_key[0], w_value[0]], axis=1))
+    mine, far_kv = tied(mine, far_kv)
+    rows_in = join_halves(mine)
+    wkv = spread_near(far_kv)
+    wq = spread_near(spread_far(gather_columns(w_query[0])))
+    wo = spread_near(spread_far(gather_columns(w_out[0].T)))
+    far_gate = [spread_far(gather_columns(part)) for part in pieces_of(w_gate[0])]
+    far_up = [spread_far(gather_columns(part)) for part in pieces_of(w_up[0])]
+    far_down = [spread_far(gather_columns(part)) for part in pieces_of(w_down[0].T)]
+    wg = [spread_near(part) for part in far_gate]
+    wu = [spread_near(part) for part in far_up]
 
     places = seg * n + jnp.arange(n)
     half = HD // 2
@@ -320,7 +343,7 @@
         step = n // count
         return [slice(i * step, (i + 1) * step) for i in range(count)]
 
-    def forward(rows_bf):
+    def forward(rows_bf, extra=None):
         rows = rows_bf.astype(f32)
         normed, inverse = norm_forward(rows, attn_scale)
         normed = normed.astype(bf16)
@@ -333,64 +356,82 @@
         values = all_keys(values.astype(bf16))
         mixed, lse = attention_forward(queries, keys, values.transpose(0, 2, 1), offset, single)
         mixed = mixed.transpose(2, 0, 1, 3).reshape(n, HEADS * HD)
+        if extra is not None:
+            mixed, extra = tied(mixed, extra)
         middle = rows + mm_nt(mixed, wo)
         normed_mlp, inverse_mlp = norm_forward(middle, mlp_scale)
         normed_mlp = normed_mlp.astype(bf16)
-        gate = mm(normed_mlp, wg)
-        upward = mm(normed_mlp, wu)
-        hidden = (jax.nn.silu(gate) * upward).astype(bf16)
+        gates, ups, hiddens = [], [], []
+        for w1, w2 in zip(wg, wu):
+            gate = mm(normed_mlp, w1)
+            upward = mm(normed_mlp, w2)
+            hiddens.append((jax.nn.silu(gate) * upward).astype(bf16))
+            gates.append(gate.astype(bf16))
+            ups.append(upward.astype(bf16))
         kept = (
             rows_bf, inverse, normed, queries, keys, values, lse, mixed,
-            middle, inverse_mlp, normed_mlp, gate.astype(bf16), upward.astype(bf16), hidden,
+            middle, inverse_mlp, normed_mlp, gates, ups, hiddens,
         )
-        return kept
+        return kept, extra
 
     def layer_output(kept, chunk):
-        middle, hidden = kept[8], kept[13]
-        return (middle[chunk] + mm_nt(hidden[chunk], wd)).astype(bf16)
-
-    def backward(grad, kept, weights_too):
+        middle, hiddens = kept[8], kept[13]
+        total = middle[chunk]
+        for hidden, w in zip(hiddens, wd):
+            total = total + mm_nt(hidden[chunk], w)
+        return total.astype(bf16)
+
+    def backward(grad, kept, weights_too, extra=None):
         (
             rows_bf, inverse, normed, queries, keys, values, lse, mixed,
-            middle, inverse_mlp, normed_mlp, gate, upward, hidden,
+            middle, inverse_mlp, normed_mlp, gates, ups, hiddens,
         ) = kept
         rows = rows_bf.astype(f32)
-        gate = gate.astype(f32)
-        upward = upward.astype(f32)
-        done = None
-        low_bits = bits_of(dsize)[:1]
-        high_bits = bits_of(dsize)[1:]
+        near_bits = low_bits
         if weights_too:
-            down = mm_tn(grad, hidden).astype(bf16)
-            grad, down = lax.optimization_barrier((grad, down))
-            down = split_rows(down)
-        hidden_grad = mm(grad, wd)
-        sigma = jax.nn.sigmoid(gate)
-        gate_grad = (hidden_grad * upward * (sigma * (1.0 + gate * (1.0 - sigma)))).astype(bf16)
-        up_grad = (hidden_grad * gate * sigma).astype(bf16)
+            downs = [mm_tn(grad, hidden).astype(bf16) for hidden in hiddens]
+            grad, downs = tied(grad, downs)
+            downs = [add_partner(split_rows(part), near_bits) for part in downs]
+        gate_grads, up_grads = [], []
+        for gate, upward, w in zip(gates, ups, wd):
+            gate = gate.astype(f32)
+            hidden_grad = mm(grad, w)
+            sigma = jax.nn.sigmoid(gate)
+            gate_grads.append(
+                (hidden_grad * upward.astype(f32) * (sigma * (1.0 + gate * (1.0 - sigma)))).astype(bf16)
+            )
+            up_grads.append((hidden_grad * gate * sigma).astype(bf16))
         if weights_too:
-            down = finish_rows(down, low_bits)
-            gate_up = mm_tn(normed_mlp, gate_grad).astype(bf16)
-            up_up = mm_tn(normed_mlp, up_grad).astype(bf16)
-            gate_grad, up_grad, gate_up, up_up, down = lax.optimization_barrier(
-                (gate_grad, up_grad, gate_up, up_up, down)
-            )
-            gate_up = split_rows(gate_up)
-            up_up = split_rows(up_up)
-        mlp_back = mm_nt(gate_grad, wg) + mm_nt(up_grad, wu)
+            gate_grads, up_grads, downs = tied(gate_grads, up_grads, downs)
+            downs = [add_partner(part, high_bits) for part in downs]
+            gate_ups = [mm_tn(normed_mlp, part).astype(bf16) for part in gate_grads]
+            gate_grads, up_grads, gate_ups = tied(gate_grads, up_grads, gate_ups)
+            up_ups = [mm_tn(normed_mlp, part).astype(bf16) for part in up_grads]
+            gate_ups = [add_partner(split_rows(part), near_bits) for part in gate_ups]
+            gate_grads, up_grads, gate_ups, up_ups = tied(gate_grads, up_grads, gate_ups, up_ups)
+            gate_ups = [add_partner(part, high_bits) for part in gate_ups]
+            up_ups = [add_partner(split_rows(part), near_bits) for part in up_ups]
+        mlp_back = 0.0
+        for gate_grad, up_grad, w1, w2 in zip(gate_grads, up_grads, wg, wu):
+            mlp_back = mlp_back + mm_nt(gate_grad, w1) + mm_nt(up_grad, w2)
         middle_grad = grad.astype(f32) + norm_backward(middle, inverse_mlp, mlp_scale, mlp_back)
         middle_bf = middle_grad.astype(bf16)
         if weights_too:
+            middle_bf, downs, up_ups = tied(middle_bf, downs, up_ups)
+            downs = [scatter_columns(part[0]) for part in downs]
+            up_ups = [add_partner(part, high_bits) for part in up_ups]
             out_up = mm_tn(middle_bf, mixed).astype(bf16)
-            gate_up = finish_rows(gate_up, low_bits)
-            up_up = finish_rows(up_up, low_bits)
-            middle_bf, out_up, gate_up, up_up = lax.optimization_barrier(
-                (middle_bf, out_up, gate_up, up_up)
-            )
-            out_up = split_rows(out_up)
+            middle_bf, out_up = tied(middle_bf, out_up)
+            out_up = add_partner(split_rows(out_up), near_bits)
         mixed_grad = mm(middle_bf, wo).astype(bf16)
         mixed_grad = mixed_grad.reshape(n, KV_HEADS, copies, HD).transpose(1, 2, 0, 3)
+        if extra is not None:
+            mixed_grad, extra = tied(mixed_grad, extra)
         dq, dk, dv = attention_backward(queries, keys, values, mixed_grad, lse, offset, single)
+        if weights_too:
+            dq, dk, dv, gate_ups, out_up = tied(dq, dk, dv, gate_ups, out_up)
+            gate_ups = [scatter_columns(part[0]) for part in gate_ups]
+            out_up = add_partner(out_up, high_bits)
         dk = own_keys(dk)
         dv = own_keys(dv)
         dq = rotate(dq.astype(f32), cosine, -sine)
@@ -403,41 +444,40 @@
                 attn_back = mm_nt(dq[chunk], wq) + mm_nt(dkv[chunk], wkv)
                 branch = norm_backward(rows[chunk], inverse[chunk], attn_scale, attn_back)
                 outgoing.append((middle_grad[chunk] + branch).astype(bf16))
-            return outgoing
+            return outgoing, extra
+        kv_up = mm_tn(normed, dkv).astype(bf16)
+        dq, dkv, kv_up = tied(dq, dkv, kv_up)
         query_up = mm_tn(normed, dq).astype(bf16)
-        kv_up = mm_tn(normed, dkv).astype(bf16)
-        dq, dkv, query_up, kv_up = lax.optimization_barrier((dq, dkv, query_up, kv_up))
+        dq, dkv, query_up = tied(dq, dkv, query_up)
         attn_back = mm_nt(dq, wq) + mm_nt(dkv, wkv)
         outgoing = middle_grad + norm_backward(rows, inverse, attn_scale, attn_back)
-        sums = [
-            scatter_columns(finish_rows(parts, bits)[0])
-            for parts, bits in (
-                (down, high_bits), (gate_up, high_bits), (up_up, high_bits),
-                (out_up, bits_of(dsize)),
-                (split_rows(query_up), bits_of(dsize)),
-                (split_rows(kv_up), bits_of(dsize)),
-            )
-        ]
+        all_bits = low_bits + high_bits
+        kv = scatter_columns(add_partner(split_rows(kv_up), all_bits)[0])
+        query = scatter_columns(add_partner(split_rows(query_up), all_bits)[0])
+        up_ups = [scatter_columns(part[0]) for part in up_ups]
+        out = scatter_columns(out_up[0])
         gains = jnp.stack(
             [gain_sum(rows, inverse, attn_back), gain_sum(middle, inverse_mlp, mlp_back)]
         )
-        return outgoing.astype(bf16), sums, gains
+        sums = [jnp.concatenate(parts, axis=1) for parts in (downs, gate_ups, up_ups)]
+        return outgoing.astype(bf16), sums + [out, query, kv], gains
 
     def to_places(rows):
         return exchange(reorder(rows, 1).reshape(micro, nloc, width))[None]
 
-    kept = forward(rows_in)
+    kept, _ = forward(rows_in)
+    hiddens, far_down = tied(kept[13][:1], far_down)
+    kept = kept[:13] + (hiddens + kept[13][1:],)
+    wd = [spread_near(part) for part in far_down]
     received = jnp.concatenate(
         [shifted(layer_output(kept, chunk), "section", 1) for chunk in token_chunks(4)], axis=0
     )
-    received, late_cotangent = lax.optimization_barrier((received, cotangent))
-    kept = forward(jnp.where(first_section, rows_in, received))
+    received, late_cotangent = tied(received, cotangent)
+    half_cot = exchange_half(late_cotangent)
+    kept, cot = forward(jnp.where(first_section, rows_in, received), join_halves(half_cot))
     second_out = layer_output(kept, slice(0, n))
-    cot = spread_inputs(late_cotangent)
-    first_grad = backward(cot, kept, False)
-    outputs = to_places(second_out)
+    first_grad, outputs = backward(cot, kept, False, to_places(second_out))
     returned = jnp.concatenate([shifted(part, "section", -1) for part in first_grad], axis=0)
-    returned, outputs = lax.optimization_barrier((returned, outputs))
     second_grad, sums, gains = backward(jnp.where(first_section, returned, cot), kept, True)
     input_grads = to_places(second_grad)
     down, gate, up, out, query, kv = sums

time: 1860 us -> 1990 us (1.070)
  waiting for transfers between devices: 736 us -> 856 us
    ppermute x54 -> x72, waiting for transfers between devices: 513 us -> 392 us  [swapped(): lax.ppermute(array, axis, [(i, i ^ bit) for i in range(lax.axis_size(axis...]
    all_gather x5 -> x8, waiting for transfers between devices: 121 us -> 232 us  [gather_columns(): whole = lax.all_gather(shard, 'tensor', axis=0)]
    reduce_scatter x6 -> x9, waiting for transfers between devices: 0.03 us -> 90.5 us  [scatter_columns(): return lax.psum_scatter(part, 'tensor', scatter_dimension=0)]
    all_gather x1, waiting for transfers between devices: 0.01 us -> 28.8 us  [local(): lax.all_gather(kv, 'tensor', axis=0).transpose(1, 0, 2)]
    ppermute x54 -> x72, starting transfers between devices: 54.4 us -> 67.8 us  [swapped(): lax.ppermute(array, axis, [(i, i ^ bit) for i in range(lax.axis_size(axis...]
    dot_general x21 -> x30, matrix products: 238 us -> 251 us  [mm_nt(): lax.dot_general(left, right, (((1,), (1,)), ((), ())), preferred_element_...]
    unnamed x240 -> x319, local copies, waits for them, and re-layouts: 37.9 us -> 48.7 us
    convert_element_type x12 -> x18, other arithmetic: 46.9 us -> 57.4 us  [add_partner(): summed[m] = (parts[m].astype(f32) + got.astype(f32)).astype(bf16)]
  transfers between devices with their start and end apart: 74 -> 98, of which waited for: 29 -> 36; matrix products, arithmetic and copies ran while one was open for 32% -> 26% of each run, Pallas kernels for 3% -> 4%
where the time goes in v3:
time: 1990 us; the launch traced here: 1980 us
  waiting for transfers between devices  856 us (43%)
  matrix products  517 us (26%)
  local copies, waits for them, and re-layouts  234 us (12%)
  other arithmetic  157 us (8%)
  Pallas kernels  116 us (6%)
  starting transfers between devices  81.9 us (4%)
    ppermute x72, waiting for transfers between devices, swapped(): lax.ppermute(array, axis, [(i, i ^ bit) for i in range(lax.axis_size(axis...  392 us
    dot_general x30, matrix products, mm_nt(): lax.dot_general(left, right, (((1,), (1,)), ((), ())), preferred_element_...  251 us
    all_gather x8, waiting for transfers between devices, gather_columns(): whole = lax.all_gather(shard, 'tensor', axis=0)  232 us
    dot_general x18, matrix products, mm(): return jnp.dot(left, right, preferred_element_type=f32)  194 us
    ppermute x8, waiting for transfers between devices, shifted(): return lax.ppermute(array, axis, pairs)  110 us
    reduce_scatter x9, waiting for transfers between devices, scatter_columns(): return lax.psum_scatter(part, 'tensor', scatter_dimension=0)  90.5 us
    pallas_call x2, Pallas kernels, attention_backward(): pl.pallas_call(functools.partial(attend_backward_kernel, single=single),...  75.2 us
    dot_general x9, matrix products, mm_tn(): lax.dot_general(left, right, (((0,), (0,)), ((), ())), preferred_element_...  71.8 us
  transfers between devices with their start and end apart: 98, of which 36 were waited for; matrix products, arithmetic and copies ran while one was open for 26% of the time, Pallas kernels for 4%

profile of v3, /device:TPU:0, one launch (start us, length us, event | category | flops | bytes accessed | tf_op | source)
XLA Modules:
  0.0 1979.2 jit_solution(17391011663946999674)
XLA Ops:
  28.9 29.4 %collective-permute-done = bf16[1,256,768]{2,1,0:T(8,128)(2,1)S(1)} collective-permute-done((bf16[1,256,768]{2,1,0:T(8,128)(2,1)S(1)}, bf16[1,256,768]{2,1,0:T(8,128)(2,1)S(1)}, u32[]{:S(2)}, u32[]{:S(2)}) %collective-permute-start) | collective-permute-done | bytes 393248 | tf_op jit(solution)/shard_map/ppermute | solution.py:28
  79.6 19.8 all-gather.21.cloned.1.call-done
  101.8 36.0 %all-gather.23.cloned.1.call-done = bf16[1536,512]{1,0:T(8,128)(2,1)} async-done(((bf16[384,512]{1,0:T(8,128)(2,1)}), bf16[1536,512]{1,0:T(8,128)(2,1)}) %all-gather.23.cloned.1.call-update) | async-done | bytes 1572880 | tf_op jit(solution)/shard_map/all_gather | solution.py:260
  140.3 34.8 %all-gather.25.cloned.1.call-done = bf16[1536,512]{1,0:T(8,128)(2,1)} async-done(((bf16[384,512]{1,0:T(8,128)(2,1)}), bf16[1536,512]{1,0:T(8,128)(2,1)}) %all-gather.25.cloned.1.call-update) | async-done | bytes 1572880 | tf_op jit(solution)/shard_map/all_gather | solution.py:260
  177.8 35.4 %all-gather.27.cloned.1.call-done = bf16[1536,512]{1,0:T(8,128)(2,1)} async-done(((bf16[384,512]{1,0:T(8,128)(2,1)}), bf16[1536,512]{1,0:T(8,128)(2,1)}) %all-gather.27.cloned.1.call-update) | async-done | bytes 1572880 | tf_op jit(solution)/shard_map/all_gather | solution.py:260
  215.7 35.4 %all-gather.29.cloned.1.call-done = bf16[1536,512]{1,0:T(8,128)(2,1)} async-done(((bf16[384,512]{1,0:T(8,128)(2,1)}), bf16[1536,512]{1,0:T(8,128)(2,1)}) %all-gather.29.cloned.1.call-update) | async-done | bytes 1572880 | tf_op jit(solution)/shard_map/all_gather | solution.py:260
  253.7 35.6 %all-gather.31.cloned.1.call-done = bf16[1536,512]{1,0:T(8,128)(2,1)} async-done(((bf16[384,512]{1,0:T(8,128)(2,1)}), bf16[1536,512]{1,0:T(8,128)(2,1)}) %all-gather.31.cloned.1.call-update) | async-done | bytes 1572880 | tf_op jit(solution)/shard_map/all_gather | solution.py:260
  291.8 35.5 %all-gather.33.cloned.1.call-done = bf16[1536,512]{1,0:T(8,128)(2,1)} async-done(((bf16[384,512]{1,0:T(8,128)(2,1)}), bf16[1536,512]{1,0:T(8,128)(2,1)}) %all-gather.33.cloned.1.call-update) | async-done | bytes 1572880 | tf_op jit(solution)/shard_map/all_gather | solution.py:260
  396.8 20.4 %attend_forward.2 = (bf16[8,2,1024,96]{3,2,1,0:T(8,128)(2,1)S(1)}, f32[8,4,1,512]{3,2,1,0:T(1,128)}) custom-call(s32[1]{0:T(128)} %bitcast.offset_ref, bf16[8,2,1024,96]{3,2,1,0:T(8,128)(2,1)S(1)} %pad_maximum_fusion.6.q_ref, bf16[8,1024,96]{2,1,0:T(8,128)(2,1)S(1)} %copy.189.k_ref, bf16[8,96,1024]{2,1,0:T(8,128)(2,1)S(1)} %bitcast.254), custom_call_target="tpu_custom_call" | custom-call | flops 12884901888 | bytes 16777216 | tf_op jit(solution)/shard_map/attend_forward/pallas_call | solution.py:166
  463.4 33.8 %collective-permute-done.24 = bf16[384,2048]{0,1:T(8,128)(2,1)} collective-permute-done((bf16[384,2048]{0,1:T(8,128)(2,1)}, bf16[384,2048]{0,1:T(8,128)(2,1)}, u32[]{:S(2)}, u32[]{:S(2)}) %collective-permute-start.24) | collective-permute-done | bytes 1572896 | tf_op jit(solution)/shard_map/ppermute | solution.py:28
  497.9 33.1 %collective-permute-done.27 = bf16[384,2048]{0,1:T(8,128)(2,1)} collective-permute-done((bf16[384,2048]{0,1:T(8,128)(2,1)}, bf16[384,2048]{0,1:T(8,128)(2,1)}, u32[]{:S(2)}, u32[]{:S(2)}) %collective-permute-start.27) | collective-permute-done | bytes 1572896 | tf_op jit(solution)/shard_map/ppermute | solution.py:28
  543.2 20.6 %collective-permute-done.20 = bf16[384,2048]{0,1:T(8,128)(2,1)} collective-permute-done((bf16[384,2048]{0,1:T(8,128)(2,1)S(1)}, bf16[384,2048]{0,1:T(8,128)(2,1)}, u32[]{:S(2)}, u32[]{:S(2)}) %collective-permute-start.20) | collective-permute-done | bytes 1572896 | tf_op jit(solution)/shard_map/ppermute | solution.py:28
  627.9 16.9 collective-permute-done.32
  747.5 20.7 %attend_forward.3 = (bf16[8,2,1024,96]{3,2,1,0:T(8,128)(2,1)S(1)}, f32[8,4,1,512]{3,2,1,0:T(1,128)S(1)}) custom-call(s32[1]{0:T(128)} %bitcast.offset_ref, bf16[8,2,1024,96]{3,2,1,0:T(8,128)(2,1)S(1)} %pad_maximum_fusion.7.q_ref, bf16[8,1024,96]{2,1,0:T(8,128)(2,1)S(1)} %copy-done.7, bf16[8,96,1024]{2,1,0:T(8,128)(2,1)S(1)} %bitcast.246), custom_call_target="tpu_custom_call" | custom-call | flops 12884901888 | bytes 16777216 | tf_op jit(solution)/shard_map/attend_forward/pallas_call | solution.py:166
  868.9 17.9 fusion.43
  902.1 18.5 fusion.41
  920.7 25.9 %multiply_reduce_fusion.2 = (f32[1024]{0:T(1024)S(1)}, f32[1024,1536]{1,0:T(8,128)}) fusion(f32[1024,1536]{1,0:T(8,128)} %copy-done.20, f32[1536]{0:T(1024)S(1)} %copy-done.97, bf16[384,2048]{0,1:T(8,128)(2,1)} %collective-permute-done.28, bf16[384,2048]{0,1:T(8,128)(2,1)} %collective-permute-done.27, bf16[384,2048]{0,1:T(8,128)(2,1)} %collective-permute-done.26, ...), kind=kOutput, calls=%fused_computation.92 | convolution fusion | flops 6491732992 | bytes 50341888 | tf_op jit(solution)/shard_map/dot_general | solution.py:49
  958.4 16.9 add_convert_fusion.4
  1015.1 19.4 collective-permute-done.40
  1040.0 37.5 %attend_backward.2 = (bf16[8,2,1024,96]{3,2,1,0:T(8,128)(2,1)S(1)}, bf16[8,1024,96]{2,1,0:T(8,128)(2,1)S(1)}, bf16[8,1024,96]{2,1,0:T(8,128)(2,1)S(1)}) custom-call(s32[1]{0:T(128)} %bitcast.offset_ref, bf16[8,2,1024,96]{3,2,1,0:T(8,128)(2,1)} %copy-done, bf16[8,1024,96]{2,1,0:T(8,128)(2,1)S(1)} %copy-done.8, bf16[8,96,1024]{2,1,0:T(8,128)(2,1)S(1)} %copy-done.18, ...), custom_call_target="tpu_custom_call" | custom-call | flops 32212254720 | bytes 33554432 | tf_op jit(solution)/shard_map/attend_backward/pallas_call | solution.py:191
  1350.5 17.4 multiply_reduce_fusion
  1422.5 37.7 %attend_backward.3 = (bf16[8,2,1024,96]{3,2,1,0:T(8,128)(2,1)S(1)}, bf16[8,1024,96]{2,1,0:T(8,128)(2,1)S(1)}, bf16[8,1024,96]{2,1,0:T(8,128)(2,1)S(1)}) custom-call(s32[1]{0:T(128)} %bitcast.offset_ref, bf16[8,2,1024,96]{3,2,1,0:T(8,128)(2,1)} %copy-done, bf16[8,1024,96]{2,1,0:T(8,128)(2,1)S(1)} %copy-done.9, bf16[8,96,1024]{2,1,0:T(8,128)(2,1)S(1)} %copy-done.19, ...), custom_call_target="tpu_custom_call" | custom-call | flops 32212254720 | bytes 33554432 | tf_op jit(solution)/shard_map/attend_backward/pallas_call | solution.py:191
  1516.3 27.5 %collective-permute-done.76 = bf16[384,1536]{1,0:T(8,128)(2,1)S(1)} collective-permute-done((bf16[384,1536]{1,0:T(8,128)(2,1)S(1)}, bf16[384,1536]{1,0:T(8,128)(2,1)S(1)}, u32[]{:S(2)}, u32[]{:S(2)}) %collective-permute-start.76) | collective-permute-done | bytes 1179680 | tf_op jit(solution)/shard_map/ppermute | solution.py:28
  1554.9 35.3 %collective-permute-done.78 = bf16[384,2048]{1,0:T(8,128)(2,1)S(1)} collective-permute-done((bf16[384,2048]{1,0:T(8,128)(2,1)}, bf16[384,2048]{1,0:T(8,128)(2,1)S(1)}, u32[]{:S(2)}, u32[]{:S(2)}) %collective-permute-start.78) | collective-permute-done | bytes 1572896 | tf_op jit(solution)/shard_map/ppermute | solution.py:28
  1594.3 35.4 %collective-permute-done.79 = bf16[384,2048]{1,0:T(8,128)(2,1)S(1)} collective-permute-done((bf16[384,2048]{1,0:T(8,128)(2,1)}, bf16[384,2048]{1,0:T(8,128)(2,1)S(1)}, u32[]{:S(2)}, u32[]{:S(2)}) %collective-permute-start.79) | collective-permute-done | bytes 1572896 | tf_op jit(solution)/shard_map/ppermute | solution.py:28
  1706.6 18.6 collective-permute-start.64
  1729.1 23.3 %collective-permute-done.69 = f32[2,1536]{1,0:T(2,128)S(1)} collective-permute-done((f32[2,1536]{1,0:T(2,128)S(1)}, f32[2,1536]{1,0:T(2,128)S(1)}, u32[]{:S(2)}, u32[]{:S(2)}) %collective-permute-start.69) | collective-permute-done | bytes 12320 | tf_op jit(solution)/shard_map/ppermute | solution.py:28
  1759.6 74.7 %collective-permute-done.65 = bf16[1,256,1536]{2,1,0:T(8,128)(2,1)} collective-permute-done((bf16[1,256,1536]{2,1,0:T(8,128)(2,1)}, bf16[1,256,1536]{2,1,0:T(8,128)(2,1)}, u32[]{:S(2)}, u32[]{:S(2)}) %collective-permute-start.65) | collective-permute-done | bytes 786464 | tf_op jit(solution)/shard_map/ppermute | solution.py:28
  1842.2 31.7 %reduce-scatter.22.cloned.1.call-done = bf16[1,384,512]{2,1,0:T(8,128)(2,1)} async-done(((bf16[4,384,512]{2,1,0:T(8,128)(2,1)}), bf16[1,384,512]{2,1,0:T(8,128)(2,1)}) %reduce-scatter.22.cloned.1.call-update) | async-done | bytes 393232 | tf_op jit(solution)/shard_map/reduce_scatter | solution.py:292
  1876.3 29.9 %reduce-scatter.14.cloned.1.call-done = bf16[1,384,384]{1,2,0:T(8,128)(2,1)} async-done(((bf16[4,384,384]{1,2,0:T(8,128)(2,1)}), bf16[1,384,384]{1,2,0:T(8,128)(2,1)}) %reduce-scatter.14.cloned.1.call-update) | async-done | bytes 294928 | tf_op jit(solution)/shard_map/reduce_scatter | solution.py:292
  1908.1 28.8 %reduce-scatter.10.cloned.1.call-done = bf16[1,384,384]{2,1,0:T(8,128)(2,1)} async-done(((bf16[4,384,384]{2,1,0:T(8,128)(2,1)}), bf16[1,384,384]{2,1,0:T(8,128)(2,1)}) %reduce-scatter.10.cloned.1.call-update) | async-done | bytes 294928 | tf_op jit(solution)/shard_map/reduce_scatter | solution.py:292
  1938.7 28.8 %all-gather.19.cloned.1.call-done = bf16[4,384,384]{2,1,0:T(8,128)(2,1)} async-done(((bf16[1,384,384]{2,1,0:T(8,128)(2,1)}), bf16[4,384,384]{2,1,0:T(8,128)(2,1)}) %all-gather.19.cloned.1.call-update) | async-done | bytes 1179664 | tf_op jit(solution)/shard_map/all_gather | solution.py:484
  (750 shorter events, 1029.5 us)
Async XLA Ops:
  7.9 91.4 %all-gather.21.cloned.1.call-start = ((), (), s32[]{:S(2)}) async-start(), calls=%async_computation.20 | async-start | bytes 1474560 | tf_op jit(solution)/shard_map/all_gather | solution.py:260
  9.9 127.9 %all-gather.23.cloned.1.call-start = ((), (), s32[]{:S(2)}) async-start(), calls=%async_computation.21 | async-start | bytes 1966080 | tf_op jit(solution)/shard_map/all_gather | solution.py:260
  12.1 163.1 %all-gather.25.cloned.1.call-start = ((), (), s32[]{:S(2)}) async-start(), calls=%async_computation.22 | async-start | bytes 1966080 | tf_op jit(solution)/shard_map/all_gather | solution.py:260
  14.2 198.9 %all-gather.27.cloned.1.call-start = ((), (), s32[]{:S(2)}) async-start(), calls=%async_computation.23 | async-start | bytes 1966080 | tf_op jit(solution)/shard_map/all_gather | solution.py:260
  15.5 235.6 %all-gather.29.cloned.1.call-start = ((), (), s32[]{:S(2)}) async-start(), calls=%async_computation.24 | async-start | bytes 1966080 | tf_op jit(solution)/shard_map/all_gather | solution.py:260
  16.1 273.1 %all-gather.31.cloned.1.call-start = ((), (), s32[]{:S(2)}) async-start(), calls=%async_computation.25 | async-start | bytes 1966080 | tf_op jit(solution)/shard_map/all_gather | solution.py:260
  16.9 310.5 %all-gather.33.cloned.1.call-start = ((), (), s32[]{:S(2)}) async-start(), calls=%async_computation.26 | async-start | bytes 1966080 | tf_op jit(solution)/shard_map/all_gather | solution.py:260
  21.0 1737.4 %reduce-scatter.12.cloned.1.call-start = ((), (), s32[]{:S(2)}) async-start(), calls=%async_computation.11 | async-start | bytes 1474560 | tf_op jit(solution)/shard_map/reduce_scatter | solution.py:292
  68.7 261.2 %collective-permute-start.8 = (bf16[384,1536]{1,0:T(8,128)(2,1)}, bf16[384,1536]{1,0:T(8,128)(2,1)}, u32[]{:S(2)}, u32[]{:S(2)}) collective-permute-start(bf16[384,1536]{1,0:T(8,128)(2,1)} %pad_maximum_fusion.20), channel_id=1, source_target_pairs={{0,4},{4,0},{8,12},{12,8},{1,5},{5,1},{9,13},{13,9},{2,6},{6,2},{1... | collective-permute-start | bytes 3538952 | tf_op jit(solution)/shard_map/ppermute | solution.py:28
  68.8 269.8 %collective-permute-start.4 = (bf16[4,256,768]{2,1,0:T(8,128)(2,1)S(1)}, bf16[4,256,768]{2,1,0:T(8,128)(2,1)}, u32[]{:S(2)}, u32[]{:S(2)}) collective-permute-start(bf16[4,256,768]{2,1,0:T(8,128)(2,1)S(1)} %constant_dynamic-update-slice_fusion.15), channel_id=1, source_target_pairs={{0,16},{16,0},{1,17},{17,1},{2,18},{18,2},{3,19},{19,3},{4,20},{20... | collective-permute-start | bytes 4718600 | tf_op jit(solution)/shard_map/ppermute | solution.py:28
  70.4 265.9 %collective-permute-start.9 = (bf16[384,1536]{1,0:T(8,128)(2,1)}, bf16[384,1536]{1,0:T(8,128)(2,1)}, u32[]{:S(2)}, u32[]{:S(2)}) collective-permute-start(bf16[384,1536]{1,0:T(8,128)(2,1)} %collective-permute-done.3), channel_id=1, source_target_pairs={{0,4},{4,0},{8,12},{12,8},{1,5},{5,1},{9,13},{13,9},{2,6},{6,2},{1... | collective-permute-start | bytes 3538952 | tf_op jit(solution)/shard_map/ppermute | solution.py:28
  78.1 264.2 %collective-permute-start.6 = (bf16[384,1536]{0,1:T(8,128)(2,1)}, bf16[384,1536]{0,1:T(8,128)(2,1)}, u32[]{:S(2)}, u32[]{:S(2)}) collective-permute-start(bf16[384,1536]{0,1:T(8,128)(2,1)} %bitcast.339), channel_id=1, source_target_pairs={{0,8},{4,12},{8,0},{12,4},{1,9},{5,13},{9,1},{13,5},{2,10},{6,14},... | collective-permute-start | bytes 3538952 | tf_op jit(solution)/shard_map/ppermute | solution.py:28
  79.5 286.1 %collective-permute-start.5 = (bf16[384,1536]{0,1:T(8,128)(2,1)}, bf16[384,1536]{0,1:T(8,128)(2,1)}, u32[]{:S(2)}, u32[]{:S(2)}) collective-permute-start(bf16[384,1536]{0,1:T(8,128)(2,1)} %bitcast.340), channel_id=1, source_target_pairs={{0,4},{4,0},{8,12},{12,8},{1,5},{5,1},{9,13},{13,9},{2,6},{6,2},{1... | collective-permute-start | bytes 3538952 | tf_op jit(solution)/shard_map/ppermute | solution.py:28
  336.2 89.2 %collective-permute-start.10 = (bf16[384,1536]{0,1:T(8,128)(2,1)}, bf16[384,1536]{0,1:T(8,128)(2,1)}, u32[]{:S(2)}, u32[]{:S(2)}) collective-permute-start(bf16[384,1536]{0,1:T(8,128)(2,1)} %bitcast.20), channel_id=1, source_target_pairs={{0,4},{4,0},{8,12},{12,8},{1,5},{5,1},{9,13},{13,9},{2,6},{6,2},{1... | collective-permute-start | bytes 3538952 | tf_op jit(solution)/shard_map/ppermute | solution.py:28
  338.6 87.3 %collective-permute-start.14 = (bf16[384,2048]{0,1:T(8,128)(2,1)}, bf16[384,2048]{0,1:T(8,128)(2,1)}, u32[]{:S(2)}, u32[]{:S(2)}) collective-permute-start(bf16[384,2048]{0,1:T(8,128)(2,1)} %bitcast.24), channel_id=1, source_target_pairs={{0,8},{4,12},{8,0},{12,4},{1,9},{5,13},{9,1},{13,5},{2,10},{6,14},... | collective-permute-start | bytes 4718600 | tf_op jit(solution)/shard_map/ppermute | solution.py:28
  438.7 92.2 %collective-permute-start.27 = (bf16[384,2048]{0,1:T(8,128)(2,1)}, bf16[384,2048]{0,1:T(8,128)(2,1)}, u32[]{:S(2)}, u32[]{:S(2)}) collective-permute-start(bf16[384,2048]{0,1:T(8,128)(2,1)} %bitcast.43), channel_id=1, source_target_pairs={{0,8},{4,12},{8,0},{12,4},{1,9},{5,13},{9,1},{13,5},{2,10},{6,14},... | collective-permute-start | bytes 4718600 | tf_op jit(solution)/shard_map/ppermute | solution.py:28
  439.3 91.6 %collective-permute-start.18 = (bf16[384,2048]{0,1:T(8,128)(2,1)}, bf16[384,2048]{0,1:T(8,128)(2,1)}, u32[]{:S(2)}, u32[]{:S(2)}) collective-permute-start(bf16[384,2048]{0,1:T(8,128)(2,1)} %collective-permute-done.17), channel_id=1, source_target_pairs={{0,4},{4,0},{8,12},{12,8},{1,5},{5,1},{9,13},{13,9},{2,6},{6,2},{1... | collective-permute-start | bytes 4718600 | tf_op jit(solution)/shard_map/ppermute | solution.py:28
  451.3 112.4 %collective-permute-start.23 = (bf16[384,2048]{0,1:T(8,128)(2,1)}, bf16[384,2048]{0,1:T(8,128)(2,1)}, u32[]{:S(2)}, u32[]{:S(2)}) collective-permute-start(bf16[384,2048]{0,1:T(8,128)(2,1)} %bitcast.40), channel_id=1, source_target_pairs={{0,4},{4,0},{8,12},{12,8},{1,5},{5,1},{9,13},{13,9},{2,6},{6,2},{1... | collective-permute-start | bytes 4718600 | tf_op jit(solution)/shard_map/ppermute | solution.py:28
  463.4 111.8 %collective-permute-start.26 = (bf16[384,2048]{0,1:T(8,128)(2,1)}, bf16[384,2048]{0,1:T(8,128)(2,1)}, u32[]{:S(2)}, u32[]{:S(2)}) collective-permute-start(bf16[384,2048]{0,1:T(8,128)(2,1)} %bitcast.43), channel_id=1, source_target_pairs={{0,4},{4,0},{8,12},{12,8},{1,5},{5,1},{9,13},{13,9},{2,6},{6,2},{1... | collective-permute-start | bytes 4718600 | tf_op jit(solution)/shard_map/ppermute | solution.py:28
  1374.4 86.0 %collective-permute-start.61 = (bf16[384,2048]{1,0:T(8,128)(2,1)}, bf16[384,2048]{1,0:T(8,128)(2,1)}, u32[]{:S(2)}, u32[]{:S(2)}) collective-permute-start(bf16[384,2048]{1,0:T(8,128)(2,1)} %get-tuple-element.134), channel_id=1, source_target_pairs={{0,8},{4,12},{8,0},{12,4},{1,9},{5,13},{9,1},{13,5},{2,10},{6,14},... | collective-permute-start | bytes 4718600 | tf_op jit(solution)/shard_map/ppermute | solution.py:28
  1382.7 82.2 %collective-permute-start.60 = (bf16[384,2048]{1,0:T(8,128)(2,1)}, bf16[384,2048]{1,0:T(8,128)(2,1)}, u32[]{:S(2)}, u32[]{:S(2)}) collective-permute-start(bf16[384,2048]{1,0:T(8,128)(2,1)} %get-tuple-element.132), channel_id=1, source_target_pairs={{0,8},{4,12},{8,0},{12,4},{1,9},{5,13},{9,1},{13,5},{2,10},{6,14},... | collective-permute-start | bytes 4718600 | tf_op jit(solution)/shard_map/ppermute | solution.py:28
  1546.6 290.1 %reduce-scatter.24.cloned.1.call-start = ((), (), s32[]{:S(2)}) async-start(), calls=%async_computation.18 | async-start | bytes 1966080 | tf_op jit(solution)/shard_map/reduce_scatter | solution.py:292
  1548.3 288.5 %reduce-scatter.26.cloned.1.call-start = ((), (), s32[]{:S(2)}) async-start(), calls=%async_computation.19 | async-start | bytes 1966080 | tf_op jit(solution)/shard_map/reduce_scatter | solution.py:292
  1549.9 289.8 %reduce-scatter.16.cloned.1.call-start = ((), (), s32[]{:S(2)}) async-start(), calls=%async_computation.14 | async-start | bytes 1966080 | tf_op jit(solution)/shard_map/reduce_scatter | solution.py:292
  1552.8 286.9 %reduce-scatter.18.cloned.1.call-start = ((), (), s32[]{:S(2)}) async-start(), calls=%async_computation.15 | async-start | bytes 1966080 | tf_op jit(solution)/shard_map/reduce_scatter | solution.py:292
  1554.2 288.0 %reduce-scatter.20.cloned.1.call-start = ((), (), s32[]{:S(2)}) async-start(), calls=%async_computation.16 | async-start | bytes 1966080 | tf_op jit(solution)/shard_map/reduce_scatter | solution.py:292
  1592.0 281.8 %reduce-scatter.22.cloned.1.call-start = ((), (), s32[]{:S(2)}) async-start(), calls=%async_computation.17 | async-start | bytes 1966080 | tf_op jit(solution)/shard_map/reduce_scatter | solution.py:292
  1633.0 273.2 %reduce-scatter.14.cloned.1.call-start = ((), (), s32[]{:S(2)}) async-start(), calls=%async_computation.13 | async-start | bytes 1474560 | tf_op jit(solution)/shard_map/reduce_scatter | solution.py:292
  1663.2 273.7 %reduce-scatter.10.cloned.1.call-start = ((), (), s32[]{:S(2)}) async-start(), calls=%async_computation.10 | async-start | bytes 1474560 | tf_op jit(solution)/shard_map/reduce_scatter | solution.py:292
  1694.4 273.1 %all-gather.19.cloned.1.call-start = ((), (), s32[]{:S(2)}) async-start(), calls=%async_computation.12 | async-start | bytes 1474560 | tf_op jit(solution)/shard_map/all_gather | solution.py:484
  1754.8 79.4 %collective-permute-start.65 = (bf16[1,256,1536]{2,1,0:T(8,128)(2,1)}, bf16[1,256,1536]{2,1,0:T(8,128)(2,1)}, u32[]{:S(2)}, u32[]{:S(2)}) collective-permute-start(bf16[1,256,1536]{2,1,0:T(8,128)(2,1)} %get-tuple-element.250), channel_id=1, source_target_pairs={{0,2},{1,3},{2,0},{3,1},{4,6},{5,7},{6,4},{7,5},{8,10},{9,11},{10,... | collective-permute-start | bytes 2359304 | tf_op jit(solution)/shard_map/ppermute | solution.py:28
  1755.4 80.1 %collective-permute-start.66 = (bf16[1,256,1536]{2,1,0:T(8,128)(2,1)}, bf16[1,256,1536]{2,1,0:T(8,128)(2,1)}, u32[]{:S(2)}, u32[]{:S(2)}) collective-permute-start(bf16[1,256,1536]{2,1,0:T(8,128)(2,1)} %get-tuple-element.249), channel_id=1, source_target_pairs={{0,3},{1,2},{2,1},{3,0},{4,7},{5,6},{6,5},{7,4},{8,11},{9,10},{10,... | collective-permute-start | bytes 2359304 | tf_op jit(solution)/shard_map/ppermute | solution.py:28
  (219 other events, 6176.3 us)
Sparse Core Ops, SparseCore 0:
  9.6 48.8 all-gather.16
  60.1 39.2 all-gather.20
  101.5 36.1 all-gather.22
  139.2 35.9 all-gather.24
  177.2 35.9 all-gather.26
  215.1 35.9 all-gather.28
  253.3 35.9 all-gather.30
  291.4 35.9 all-gather.32
  1546.7 43.5 reduce-scatter.11
  1592.4 33.9 reduce-scatter.23
  1629.3 34.2 reduce-scatter.25
  1665.8 34.2 reduce-scatter.15
  1703.0 43.3 reduce-scatter.17
  1748.5 77.8 reduce-scatter.19
  1828.5 45.3 reduce-scatter.21
  1876.1 30.1 reduce-scatter.13
  1909.0 27.8 reduce-scatter.9
  1938.3 29.1 all-gather.18

commit v4 on v3

--- a/solution.py
+++ b/solution.py
@@ -291,26 +291,42 @@
         part = part.reshape(share, tsize, -1).transpose(1, 0, 2)
         return lax.psum_scatter(part, "tensor", scatter_dimension=0)
 
-    PIECES = 2
-    cols = w_gate.shape[2] // PIECES
-
-    def pieces_of(array):
-        return [array[:, i * cols : (i + 1) * cols] for i in range(PIECES)]
-
     attn_scale = reorder(attn_gain[0], 0)
     mlp_scale = reorder(mlp_gain[0], 0)
     mine = exchange_half(inputs)
-    far_kv = spread_far(jnp.concatenate([w_key[0], w_value[0]], axis=1))
-    mine, far_kv = tied(mine, far_kv)
+    last = spread_far(jnp.concatenate([w_key[0], w_value[0]], axis=1))
+    mine, last = tied(mine, last)
+    wkv = spread_near(last)
     rows_in = join_halves(mine)
-    wkv = spread_near(far_kv)
-    wq = spread_near(spread_far(gather_columns(w_query[0])))
-    wo = spread_near(spread_far(gather_columns(w_out[0].T)))
-    far_gate = [spread_far(gather_columns(part)) for part in pieces_of(w_gate[0])]
-    far_up = [spread_far(gather_columns(part)) for part in pieces_of(w_up[0])]
-    far_down = [spread_far(gather_columns(part)) for part in pieces_of(w_down[0].T)]
-    wg = [spread_near(part) for part in far_gate]
-    wu = [spread_near(part) for part in far_up]
+
+    def spread_weight(shard, pieces, last):
+        rows = share // pieces
+        fars = []
+        for i in range(pieces):
+            whole = lax.all_gather(shard[i * rows : (i + 1) * rows], "tensor", axis=0)
+            whole, last = tied(whole, last)
+            if fars:
+                fars[-1] = last
+            whole = whole.transpose(1, 0, 2).reshape(rows, tsize * shard.shape[1])
+            last = spread_far(whole)
+            fars.append(last)
+        return fars, last
+
+    def settle(fars):
+        parts = [dict(far) for far in fars]
+        for bit in low_bits:
+            parts = [swap_in(part, bit) for part in parts]
+        return jnp.concatenate([part[m] for m in range(dsize) for part in parts], axis=0)
+
+    fars, last = spread_weight(w_query[0], 1, last)
+    wq = settle(fars)
+    fars, last = spread_weight(w_out[0].T, 1, last)
+    wo = settle(fars)
+    fars, last = spread_weight(w_gate[0], 2, last)
+    wg = settle(fars)
+    fars, last = spread_weight(w_up[0], 2, last)
+    wu = settle(fars)
+    far_down, last = spread_weight(w_down[0].T, 2, last)
 
     places = seg * n + jnp.arange(n)
     half = HD // 2
@@ -361,77 +377,66 @@
         middle = rows + mm_nt(mixed, wo)
         normed_mlp, inverse_mlp = norm_forward(middle, mlp_scale)
         normed_mlp = normed_mlp.astype(bf16)
-        gates, ups, hiddens = [], [], []
-        for w1, w2 in zip(wg, wu):
-            gate = mm(normed_mlp, w1)
-            upward = mm(normed_mlp, w2)
-            hiddens.append((jax.nn.silu(gate) * upward).astype(bf16))
-            gates.append(gate.astype(bf16))
-            ups.append(upward.astype(bf16))
+        gate = mm(normed_mlp, wg)
+        upward = mm(normed_mlp, wu)
+        hidden = (jax.nn.silu(gate) * upward).astype(bf16)
         kept = (
             rows_bf, inverse, normed, queries, keys, values, lse, mixed,
-            middle, inverse_mlp, normed_mlp, gates, ups, hiddens,
+            middle, inverse_mlp, normed_mlp, gate.astype(bf16), upward.astype(bf16), hidden,
         )
         return kept, extra
 
     def layer_output(kept, chunk):
-        middle, hiddens = kept[8], kept[13]
-        total = middle[chunk]
-        for hidden, w in zip(hiddens, wd):
-            total = total + mm_nt(hidden[chunk], w)
-        return total.astype(bf16)
+        middle, hidden = kept[8], kept[13]
+        return (middle[chunk] + mm_nt(hidden[chunk], wd)).astype(bf16)
 
     def backward(grad, kept, weights_too, extra=None):
         (
             rows_bf, inverse, normed, queries, keys, values, lse, mixed,
-            middle, inverse_mlp, normed_mlp, gates, ups, hiddens,
+            middle, inverse_mlp, normed_mlp, gate, upward, hidden,
         ) = kept
         rows = rows_bf.astype(f32)
-        near_bits = low_bits
         if weights_too:
-            downs = [mm_tn(grad, hidden).astype(bf16) for hidden in hiddens]
-            grad, downs = tied(grad, downs)
-            downs = [add_partner(split_rows(part), near_bits) for part in downs]
-        gate_grads, up_grads = [], []
-        for gate, upward, w in zip(gates, ups, wd):
-            gate = gate.astype(f32)
-            hidden_grad = mm(grad, w)
-            sigma = jax.nn.sigmoid(gate)
-            gate_grads.append(
-                (hidden_grad * upward.astype(f32) * (sigma * (1.0 + gate * (1.0 - sigma)))).astype(bf16)
-            )
-            up_grads.append((hidden_grad * gate * sigma).astype(bf16))
+            down = mm_tn(grad, hidden).astype(bf16)
+            grad, down = tied(grad, down)
+            down = add_partner(split_rows(down), low_bits)
+        gate = gate.astype(f32)
+        hidden_grad = mm(grad, wd)
+        sigma = jax.nn.sigmoid(gate)
+        gate_grad = (
+            hidden_grad * upward.astype(f32) * (sigma * (1.0 + gate * (1.0 - sigma)))
+        ).astype(bf16)
+        up_grad = (hidden_grad * gate * sigma).astype(bf16)
         if weights_too:
-            gate_grads, up_grads, downs = tied(gate_grads, up_grads, downs)
-            downs = [add_partner(part, high_bits) for part in downs]
-            gate_ups = [mm_tn(normed_mlp, part).astype(bf16) for part in gate_grads]
-            gate_grads, up_grads, gate_ups = tied(gate_grads, up_grads, gate_ups)
-            up_ups = [mm_tn(normed_mlp, part).astype(bf16) for part in up_grads]
-            gate_ups = [add_partner(split_rows(part), near_bits) for part in gate_ups]
-            gate_grads, up_grads, gate_ups, up_ups = tied(gate_grads, up_grads, gate_ups, up_ups)
-            gate_ups = [add_partner(part, high_bits) for part in gate_ups]
-            up_ups = [add_partner(split_rows(part), near_bits) for part in up_ups]
-        mlp_back = 0.0
-        for gate_grad, up_grad, w1, w2 in zip(gate_grads, up_grads, wg, wu):
-            mlp_back = mlp_back + mm_nt(gate_grad, w1) + mm_nt(up_grad, w2)
+            gate_grad, up_grad, down = tied(gate_grad, up_grad, down)
+            down = add_partner(down, high_bits)
+            gate_sum = mm_tn(normed_mlp, gate_grad).astype(bf16)
+            gate_grad, up_grad, gate_sum = tied(gate_grad, up_grad, gate_sum)
+            gate_sum = add_partner(split_rows(gate_sum), low_bits)
+            up_sum = mm_tn(normed_mlp, up_grad).astype(bf16)
+            gate_grad, up_grad, up_sum = tied(gate_grad, up_grad, up_sum)
+            up_sum = add_partner(split_rows(up_sum), low_bits)
+        mlp_back = mm_nt(gate_grad, wg)
+        if weights_too:
+            mlp_back, down, gate_sum = tied(mlp_back, down, gate_sum)
+            gate_sum = add_partner(gate_sum, high_bits)
+        mlp_back = mlp_back + mm_nt(up_grad, wu)
         middle_grad = grad.astype(f32) + norm_backward(middle, inverse_mlp, mlp_scale, mlp_back)
         middle_bf = middle_grad.astype(bf16)
         if weights_too:
-            middle_bf, downs, up_ups = tied(middle_bf, downs, up_ups)
-            downs = [scatter_columns(part[0]) for part in downs]
-            up_ups = [add_partner(part, high_bits) for part in up_ups]
-            out_up = mm_tn(middle_bf, mixed).astype(bf16)
-            middle_bf, out_up = tied(middle_bf, out_up)
-            out_up = add_partner(split_rows(out_up), near_bits)
+            down = scatter_columns(down[0])
+            out = mm_tn(middle_bf, mixed).astype(bf16)
+            middle_bf, out, up_sum = tied(middle_bf, out, up_sum)
+            out = add_partner(split_rows(out), low_bits)
         mixed_grad = mm(middle_bf, wo).astype(bf16)
         mixed_grad = mixed_grad.reshape(n, KV_HEADS, copies, HD).transpose(1, 2, 0, 3)
         if extra is not None:
             mixed_grad, extra = tied(mixed_grad, extra)
+        if weights_too:
+            mixed_grad, gate_sum, out = tied(mixed_grad, gate_sum, out)
+            gate_sum = scatter_columns(gate_sum[0])
+            up_sum = add_partner(up_sum, high_bits)
         dq, dk, dv = attention_backward(queries, keys, values, mixed_grad, lse, offset, single)
-        if weights_too:
-            dq, dk, dv, gate_ups, out_up = tied(dq, dk, dv, gate_ups, out_up)
-            gate_ups = [scatter_columns(part[0]) for part in gate_ups]
-            out_up = add_partner(out_up, high_bits)
         dk = own_keys(dk)
         dv = own_keys(dv)
         dq = rotate(dq.astype(f32), cosine, -sine)
@@ -445,30 +450,55 @@
                 branch = norm_backward(rows[chunk], inverse[chunk], attn_scale, attn_back)
                 outgoing.append((middle_grad[chunk] + branch).astype(bf16))
             return outgoing, extra
-        kv_up = mm_tn(normed, dkv).astype(bf16)
-        dq, dkv, kv_up = tied(dq, dkv, kv_up)
-        query_up = mm_tn(normed, dq).astype(bf16)
-        dq, dkv, query_up = tied(dq, dkv, query_up)
+        kv = mm_tn(normed, dkv).astype(bf16)
+        query = mm_tn(normed, dq).astype(bf16)
+        dq, dkv, kv, query, down, up_sum = tied(dq, dkv, kv, query, down, up_sum)
+        up_sum = scatter_columns(up_sum[0])
+        kv = add_partner(split_rows(kv), low_bits)
+        query = add_partner(split_rows(query), low_bits)
         attn_back = mm_nt(dq, wq) + mm_nt(dkv, wkv)
         outgoing = middle_grad + norm_backward(rows, inverse, attn_scale, attn_back)
-        all_bits = low_bits + high_bits
-        kv = scatter_columns(add_partner(split_rows(kv_up), all_bits)[0])
-        query = scatter_columns(add_partner(split_rows(query_up), all_bits)[0])
-        up_ups = [scatter_columns(part[0]) for part in up_ups]
-        out = scatter_columns(out_up[0])
+        outgoing = outgoing.astype(bf16)
+        outgoing, kv, query = tied(outgoing, kv, query)
+        kv = add_partner(kv, high_bits)[0]
+        out = add_partner(out, high_bits)[0]
+        query = add_partner(query, high_bits)[0]
+        pair = jnp.concatenate(
+            [out.reshape(share, tsize, -1), query.reshape(share, tsize, -1)], axis=2
+        )
+        pair, gate_sum = tied(pair, gate_sum)
+        pair = scatter_columns(pair)
         gains = jnp.stack(
             [gain_sum(rows, inverse, attn_back), gain_sum(middle, inverse_mlp, mlp_back)]
         )
-        sums = [jnp.concatenate(parts, axis=1) for parts in (downs, gate_ups, up_ups)]
-        return outgoing.astype(bf16), sums + [out, query, kv], gains
+        half_cols = pair.shape[1] // 2
+        sums = [down, gate_sum, up_sum, pair[:, :half_cols], pair[:, half_cols:]]
+        return outgoing, sums + [sum_over_tensor(kv)], gains
+
+    def sum_over_tensor(array):
+        bits = bits_of(tsize)
+        for bit in bits:
+            side = (t & bit) != 0
+            size = array.shape[1] // 2
+            low, high = array[:, :size], array[:, size:]
+            got = swapped(jnp.where(side, low, high), "tensor", bit)
+            kept_half = jnp.where(side, high, low)
+            array = (kept_half.astype(f32) + got.astype(f32)).astype(bf16)
+        for bit in reversed(bits):
+            side = (t & bit) != 0
+            got = swapped(array, "tensor", bit)
+            array = jnp.concatenate(
+                [jnp.where(side, got, array), jnp.where(side, array, got)], axis=1
+            )
+        return array
 
     def to_places(rows):
         return exchange(reorder(rows, 1).reshape(micro, nloc, width))[None]
 
     kept, _ = forward(rows_in)
-    hiddens, far_down = tied(kept[13][:1], far_down)
-    kept = kept[:13] + (hiddens + kept[13][1:],)
-    wd = [spread_near(part) for part in far_down]
+    far_down[-1], hidden = tied(far_down[-1], kept[13])
+    kept = kept[:13] + (hidden,)
+    wd = settle(far_down)
     received = jnp.concatenate(
         [shifted(layer_output(kept, chunk), "section", 1) for chunk in token_chunks(4)], axis=0
     )
@@ -481,7 +511,6 @@
     second_grad, sums, gains = backward(jnp.where(first_section, returned, cot), kept, True)
     input_grads = to_places(second_grad)
     down, gate, up, out, query, kv = sums
-    kv = lax.all_gather(kv, "tensor", axis=0).transpose(1, 0, 2).reshape(share, 2 * dims)
     gains = reorder(gains, 1)
     for axis, size in (("dp", dsize), ("tensor", tsize)):
         for bit in bits_of(size):

time: 1990 us -> 1630 us (0.82)
  waiting for transfers between devices: 856 us -> 506 us
  local copies, waits for them, and re-layouts: 234 us -> 285 us
  matrix products: 517 us -> 489 us
    all_gather x9 -> x8, waiting for transfers between devices: 261 us -> 0.56 us  [spread_weight(): whole = lax.all_gather(shard[i * rows:(i + 1) * rows], 'tensor', axis=0)]
    reduce_scatter x9 -> x4, waiting for transfers between devices: 90.5 us -> 0.01 us  [scatter_columns(): return lax.psum_scatter(part, 'tensor', scatter_dimension=0)]
    unnamed x319 -> x277, local copies, waits for them, and re-layouts: 48.7 us -> 91.2 us
    dot_general x30 -> x21, matrix products: 251 us -> 219 us  [mm_nt(): lax.dot_general(left, right, (((1,), (1,)), ((), ())), preferred_element_...]
    ppermute x72 -> x67, starting transfers between devices: 67.8 us -> 50.9 us  [swapped(): lax.ppermute(array, axis, [(i, i ^ bit) for i in range(lax.axis_size(axis...]
    ppermute x72 -> x67, waiting for transfers between devices: 392 us -> 377 us  [swapped(): lax.ppermute(array, axis, [(i, i ^ bit) for i in range(lax.axis_size(axis...]
    convert_element_type x18 -> x12, other arithmetic: 57.4 us -> 49.8 us  [add_partner(): summed[m] = (parts[m].astype(f32) + got.astype(f32)).astype(bf16)]
    dot_general x9 -> x6, matrix products: 71.8 us -> 76.5 us  [mm_tn(): lax.dot_general(left, right, (((0,), (0,)), ((), ())), preferred_element_...]
  transfers between devices with their start and end apart: 98 -> 87, of which waited for: 36 -> 29; matrix products, arithmetic and copies ran while one was open for 26% -> 38% of each run, Pallas kernels for 4% -> 5%
where the time goes in v4:
time: 1630 us
  waiting for transfers between devices  506 us (31%)
  matrix products  489 us (30%)
  local copies, waits for them, and re-layouts  285 us (17%)
  other arithmetic  151 us (9%)
  Pallas kernels  116 us (7%)
  starting transfers between devices  63.9 us (4%)
  between operations  16.7 us (1%)
    ppermute x67, waiting for transfers between devices, swapped(): lax.ppermute(array, axis, [(i, i ^ bit) for i in range(lax.axis_size(axis...  377 us
    dot_general x21, matrix products, mm_nt(): lax.dot_general(left, right, (((1,), (1,)), ((), ())), preferred_element_...  219 us
    dot_general x12, matrix products, mm(): return jnp.dot(left, right, preferred_element_type=f32)  194 us
    ppermute x8, waiting for transfers between devices, shifted(): return lax.ppermute(array, axis, pairs)  126 us
    unnamed x277, local copies, waits for them, and re-layouts  91.2 us
    dot_general x6, matrix products, mm_tn(): lax.dot_general(left, right, (((0,), (0,)), ((), ())), preferred_element_...  76.5 us
    pallas_call x2, Pallas kernels, attention_backward(): pl.pallas_call(functools.partial(attend_backward_kernel, single=single),...  75.1 us
    ppermute x67, starting transfers between devices, swapped(): lax.ppermute(array, axis, [(i, i ^ bit) for i in range(lax.axis_size(axis...  50.9 us
  transfers between devices with their start and end apart: 87, of which 29 were waited for; matrix products, arithmetic and copies ran while one was open for 38% of the time, Pallas kernels for 5%

profile of v4, /device:TPU:0, one launch (start us, length us, event | category | flops | bytes accessed | tf_op | source)
XLA Modules:
  0.0 1627.6 jit_solution(17629216759396287185)
XLA Ops:
  27.6 30.3 %collective-permute-done = bf16[1,256,768]{2,1,0:T(8,128)(2,1)S(1)} collective-permute-done((bf16[1,256,768]{2,1,0:T(8,128)(2,1)S(1)}, bf16[1,256,768]{2,1,0:T(8,128)(2,1)S(1)}, u32[]{:S(2)}, u32[]{:S(2)}) %collective-permute-start) | collective-permute-done | bytes 393248 | tf_op jit(solution)/shard_map/ppermute | solution.py:28
  87.1 18.8 %collective-permute-done.4 = bf16[4,256,768]{2,1,0:T(8,128)(2,1)} collective-permute-done((bf16[4,256,768]{2,1,0:T(8,128)(2,1)S(1)}, bf16[4,256,768]{2,1,0:T(8,128)(2,1)}, u32[]{:S(2)}, u32[]{:S(2)}) %collective-permute-start.4) | collective-permute-done | bytes 1572896 | tf_op jit(solution)/shard_map/ppermute | solution.py:28
  173.4 20.4 %attend_forward.2 = (bf16[8,2,1024,96]{3,2,1,0:T(8,128)(2,1)S(1)}, f32[8,4,1,512]{3,2,1,0:T(1,128)}) custom-call(s32[1]{0:T(128)} %bitcast.offset_ref, bf16[8,2,1024,96]{3,2,1,0:T(8,128)(2,1)S(1)} %pad_maximum_fusion.2.q_ref, bf16[8,1024,96]{2,1,0:T(8,128)(2,1)S(1)} %copy.139.k_ref, bf16[8,96,1024]{2,1,0:T(8,128)(2,1)S(1)} %bitcast.205), custom_call_target="tpu_custom_call" | custom-call | flops 12884901888 | bytes 16777216 | tf_op jit(solution)/shard_map/attend_forward/pallas_call | solution.py:166
  223.2 18.7 %collective-permute-done.14 = bf16[192,4096]{1,0:T(8,128)(2,1)} collective-permute-done((bf16[192,4096]{1,0:T(8,128)(2,1)}, bf16[192,4096]{1,0:T(8,128)(2,1)}, u32[]{:S(2)}, u32[]{:S(2)}) %collective-permute-start.14) | collective-permute-done | bytes 1572896 | tf_op jit(solution)/shard_map/ppermute | solution.py:28
  257.6 22.1 %collective-permute-done.15 = bf16[192,4096]{1,0:T(8,128)(2,1)} collective-permute-done((bf16[192,4096]{1,0:T(8,128)(2,1)S(1)}, bf16[192,4096]{1,0:T(8,128)(2,1)}, u32[]{:S(2)}, u32[]{:S(2)}) %collective-permute-start.15) | collective-permute-done | bytes 1572896 | tf_op jit(solution)/shard_map/ppermute | solution.py:28
  284.5 21.6 %fusion.94 = f32[1024,4096]{1,0:T(8,128)} fusion(bf16[1536,4096]{1,0:T(8,128)(2,1)} %constant_dynamic-update-slice_fusion.4, f32[1024,1536]{1,0:T(8,128)} %get-tuple-element.323, f32[1536]{0:T(1024)S(1)} %pad_maximum_fusion.23, f32[1024]{0:T(1024)S(1)} %add_rsqrt_fusion.2), kind=kOutput, calls=%fused_computation.327 | convolution fusion | flops 12889620480 | bytes 35661824 | tf_op jit(solution)/shard_map/dot_general | solution.py:45
  335.1 22.2 %collective-permute-done.17 = bf16[192,4096]{1,0:T(8,128)(2,1)} collective-permute-done((bf16[192,4096]{1,0:T(8,128)(2,1)S(1)}, bf16[192,4096]{1,0:T(8,128)(2,1)}, u32[]{:S(2)}, u32[]{:S(2)}) %collective-permute-start.17) | collective-permute-done | bytes 1572896 | tf_op jit(solution)/shard_map/ppermute | solution.py:28
  362.0 23.3 %multiply_convert_fusion.1 = bf16[1024,4096]{1,0:T(8,128)(2,1)} fusion(f32[1024,4096]{1,0:T(8,128)} %fusion.94, bf16[1536,4096]{1,0:T(8,128)(2,1)} %constant_dynamic-update-slice_fusion.12, f32[1024,1536]{1,0:T(8,128)} %get-tuple-element.323, f32[1536]{0:T(1024)S(1)} %pad_maximum_fusion.23, f32[1024]{0:T(1024)S(1)} %add_rsqrt_fusion.2), kind=kOutput, calls=%fused_computation.20 | convolution fusion | flops 12914786304 | bytes 44050432 | tf_op jit(solution)/shard_map/dot_general | solution.py:45
  481.5 16.9 %collective-permute-done.33 = bf16[256,1536]{1,0:T(8,128)(2,1)S(1)} collective-permute-done((bf16[256,1536]{1,0:T(8,128)(2,1)}, bf16[256,1536]{1,0:T(8,128)(2,1)S(1)}, u32[]{:S(2)}, u32[]{:S(2)}) %collective-permute-start.33) | collective-permute-done | bytes 786464 | tf_op jit(solution)/shard_map/ppermute | solution.py:24
  591.9 20.7 %attend_forward.3 = (bf16[8,2,1024,96]{3,2,1,0:T(8,128)(2,1)S(1)}, f32[8,4,1,512]{3,2,1,0:T(1,128)S(1)}) custom-call(s32[1]{0:T(128)} %bitcast.offset_ref, bf16[8,2,1024,96]{3,2,1,0:T(8,128)(2,1)S(1)} %pad_maximum_fusion.3.q_ref, bf16[8,1024,96]{2,1,0:T(8,128)(2,1)S(1)} %copy-done.5, bf16[8,96,1024]{2,1,0:T(8,128)(2,1)S(1)} %bitcast.197), custom_call_target="tpu_custom_call" | custom-call | flops 12884901888 | bytes 16777216 | tf_op jit(solution)/shard_map/attend_forward/pallas_call | solution.py:166
  641.2 20.6 %fusion.116 = f32[1024,4096]{1,0:T(8,128)} fusion(bf16[1024,1536]{1,0:T(8,128)(2,1)S(1)} %multiply_convert_fusion.2, bf16[1536,4096]{1,0:T(8,128)(2,1)} %constant_dynamic-update-slice_fusion.4), kind=kOutput, calls=%fused_computation.345 | convolution fusion | flops 12884901888 | bytes 32505856 | tf_op jit(solution)/shard_map/dot_general | solution.py:45
  661.8 29.2 %multiply_convert_fusion = (bf16[1024,4096]{1,0:T(8,128)(2,1)}, bf16[1024,4096]{1,0:T(8,128)(2,1)}, bf16[1024,4096]{1,0:T(8,128)(2,1)}) fusion(f32[1024,4096]{1,0:T(8,128)} %fusion.116, bf16[1024,1536]{1,0:T(8,128)(2,1)S(1)} %multiply_convert_fusion.2, bf16[1536,4096]{1,0:T(8,128)(2,1)} %constant_dynamic-update-slice_fusion.12), kind=kOutput, calls=%fused_computation.19 | convolution fusion | flops 12918456320 | bytes 57671680 | tf_op jit(solution)/shard_map/dot_general | solution.py:45
  691.0 18.9 %add_convert_fusion.13 = bf16[1024,1536]{1,0:T(8,128)(2,1)S(1)} fusion(f32[1024,1536]{1,0:T(8,128)} %copy-done.15, bf16[1024,4096]{1,0:T(8,128)(2,1)} %get-tuple-element.210, bf16[1536,4096]{1,0:T(8,128)(2,1)} %constant_dynamic-update-slice_fusion.20), kind=kOutput, calls=%fused_computation.72 | convolution fusion | flops 12888047616 | bytes 30408704 | tf_op jit(solution)/shard_map/dot_general | solution.py:49
  716.6 19.5 %fusion.115 = f32[1024,4096]{1,0:T(8,128)} fusion(bf16[1024,1536]{1,0:T(8,128)(2,1)S(1)} %copy-done.17, bf16[1536,4096]{1,0:T(8,128)(2,1)} %constant_dynamic-update-slice_fusion.20), kind=kOutput, calls=%fused_computation.344 | convolution fusion | flops 12884901888 | bytes 32505856 | tf_op jit(solution)/shard_map/dot_general | solution.py:45
  736.1 22.5 %fusion.15 = f32[1024,1536]{1,0:T(8,128)} fusion(bf16[1536,4096]{1,0:T(8,128)(2,1)} %constant_dynamic-update-slice_fusion.12, f32[1024,4096]{1,0:T(8,128)} %fusion.115, bf16[1024,4096]{1,0:T(8,128)(2,1)} %get-tuple-element.211), kind=kOutput, calls=%fused_computation.36 | convolution fusion | flops 12914262016 | bytes 44040192 | tf_op jit(solution)/shard_map/dot_general | solution.py:49
  758.6 30.9 %multiply_reduce_fusion.2 = (f32[1024]{0:T(1024)S(1)}, f32[1024,1536]{1,0:T(8,128)}) fusion(f32[1024,1536]{1,0:T(8,128)} %copy-done.15, f32[1536]{0:T(1024)S(1)} %copy-done.93, f32[1024,1536]{1,0:T(8,128)} %fusion.15, bf16[1536,4096]{1,0:T(8,128)(2,1)} %constant_dynamic-update-slice_fusion.4, f32[1024,4096]{1,0:T(8,128)} %fusion.115, ...), kind=kOutput, calls=%fused_computation.74 | convolution fusion | flops 12941523968 | bytes 65021952 | tf_op jit(solution)/shard_map/dot_general | solution.py:49
  824.4 37.6 %attend_backward.2 = (bf16[8,2,1024,96]{3,2,1,0:T(8,128)(2,1)S(1)}, bf16[8,1024,96]{2,1,0:T(8,128)(2,1)S(1)}, bf16[8,1024,96]{2,1,0:T(8,128)(2,1)S(1)}) custom-call(s32[1]{0:T(128)} %bitcast.offset_ref, bf16[8,2,1024,96]{3,2,1,0:T(8,128)(2,1)} %copy-done, bf16[8,1024,96]{2,1,0:T(8,128)(2,1)S(1)} %copy-done.6, bf16[8,96,1024]{2,1,0:T(8,128)(2,1)S(1)} %copy-done.13, ...), custom_call_target="tpu_custom_call" | custom-call | flops 32212254720 | bytes 33554432 | tf_op jit(solution)/shard_map/attend_backward/pallas_call | solution.py:191
  947.6 16.9 %collective-permute-done.42 = bf16[256,1536]{1,0:T(8,128)(2,1)S(1)} collective-permute-done((bf16[256,1536]{1,0:T(8,128)(2,1)S(1)}, bf16[256,1536]{1,0:T(8,128)(2,1)S(1)}, u32[]{:S(2)}, u32[]{:S(2)}) %collective-permute-start.42) | collective-permute-done | bytes 786464 | tf_op jit(solution)/shard_map/ppermute | solution.py:24
  964.4 16.9 %collective-permute-done.44 = bf16[256,1536]{1,0:T(8,128)(2,1)S(1)} collective-permute-done((bf16[256,1536]{1,0:T(8,128)(2,1)S(1)}, bf16[256,1536]{1,0:T(8,128)(2,1)S(1)}, u32[]{:S(2)}, u32[]{:S(2)}) %collective-permute-start.44) | collective-permute-done | bytes 786464 | tf_op jit(solution)/shard_map/ppermute | solution.py:24
  996.5 17.0 %convolution_convert_fusion.2 = bf16[1536,4096]{1,0:T(8,128)(2,1)S(1)} fusion(bf16[1024,1536]{1,0:T(8,128)(2,1)S(1)} %maximum_select_fusion, bf16[1024,4096]{1,0:T(8,128)(2,1)} %get-tuple-element.210), kind=kOutput, calls=%fused_computation.23 | convolution fusion | flops 12891193344 | bytes 24117248 | tf_op jit(solution)/shard_map/dot_general | solution.py:55
  1020.4 29.0 %fusion.12 = (bf16[1024,4096]{1,0:T(8,128)(2,1)}, bf16[1024,4096]{1,0:T(8,128)(2,1)}) fusion(bf16[1024,4096]{1,0:T(8,128)(2,1)} %get-tuple-element.211, bf16[1024,4096]{1,0:T(8,128)(2,1)} %get-tuple-element.326, bf16[1024,1536]{1,0:T(8,128)(2,1)} %copy-done.31, bf16[1536,4096]{1,0:T(8,128)(2,1)} %constant_dynamic-update-slice_fusion.20), kind=kOutput, calls=%fused_computation.18 | convolution fusion | flops 12947816448 | bytes 49283072 | tf_op jit(solution)/shard_map/dot_general | solution.py:45
  1056.6 19.1 %convolution_convert_fusion.1 = bf16[1536,4096]{1,0:T(8,128)(2,1)} fusion(bf16[1024,1536]{1,0:T(8,128)(2,1)S(1)} %copy-done.72, bf16[1024,4096]{1,0:T(8,128)(2,1)} %get-tuple-element.121), kind=kOutput, calls=%fused_computation.22 | convolution fusion | flops 12891193344 | bytes 24117248 | tf_op jit(solution)/shard_map/dot_general | solution.py:55
  1075.7 19.3 %convolution_convert_fusion = bf16[1536,4096]{1,0:T(8,128)(2,1)} fusion(bf16[1024,1536]{1,0:T(8,128)(2,1)S(1)} %copy-done.72, bf16[1024,4096]{1,0:T(8,128)(2,1)} %get-tuple-element.126), kind=kOutput, calls=%fused_computation.21 | convolution fusion | flops 12891193344 | bytes 24117248 | tf_op jit(solution)/shard_map/dot_general | solution.py:55
  1109.5 19.6 %fusion.117 = f32[1024,1536]{1,0:T(8,128)} fusion(bf16[1024,4096]{1,0:T(8,128)(2,1)} %get-tuple-element.121, bf16[1536,4096]{1,0:T(8,128)(2,1)} %constant_dynamic-update-slice_fusion.4), kind=kOutput, calls=%fused_computation.346 | convolution fusion | flops 12884901888 | bytes 27262976 | tf_op jit(solution)/shard_map/dot_general | solution.py:49
  1135.1 44.0 %collective-permute-done.48 = bf16[384,4096]{1,0:T(8,128)(2,1)} collective-permute-done((bf16[384,4096]{1,0:T(8,128)(2,1)S(1)}, bf16[384,4096]{1,0:T(8,128)(2,1)}, u32[]{:S(2)}, u32[]{:S(2)}) %collective-permute-start.48) | collective-permute-done | bytes 3145760 | tf_op jit(solution)/shard_map/ppermute | solution.py:28
  1184.4 21.8 %multiply_reduce_fusion = (f32[1536]{0:T(1024)S(1)}, f32[1024]{0:T(1024)S(1)}, f32[1024,1536]{1,0:T(8,128)}) fusion(f32[1024,1536]{1,0:T(8,128)S(1)} %bitcast.215, f32[1024]{0:T(1024)S(1)} %copy-done.97, f32[1024,1536]{1,0:T(8,128)} %fusion.117, f32[1536]{0:T(1024)S(1)} %copy-done.94, bf16[1024,4096]{1,0:T(8,128)(2,1)} %get-tuple-element.126, ...), kind=kOutput, calls=%fused_computation.60 | convolution fusion | flops 12895908864 | bytes 39866368 | tf_op jit(solution)/shard_map/dot_general | solution.py:49
  1267.4 37.5 %attend_backward.3 = (bf16[8,2,1024,96]{3,2,1,0:T(8,128)(2,1)S(1)}, bf16[8,1024,96]{2,1,0:T(8,128)(2,1)S(1)}, bf16[8,1024,96]{2,1,0:T(8,128)(2,1)S(1)}) custom-call(s32[1]{0:T(128)} %bitcast.offset_ref, bf16[8,2,1024,96]{3,2,1,0:T(8,128)(2,1)} %copy-done, bf16[8,1024,96]{2,1,0:T(8,128)(2,1)S(1)} %copy-done.7, bf16[8,96,1024]{2,1,0:T(8,128)(2,1)S(1)} %copy-done.14, ...), custom_call_target="tpu_custom_call" | custom-call | flops 32212254720 | bytes 33554432 | tf_op jit(solution)/shard_map/attend_backward/pallas_call | solution.py:191
  1407.6 18.3 %collective-permute-done.68 = bf16[384,1536]{1,0:T(8,128)(2,1)S(1)} collective-permute-done((bf16[384,1536]{1,0:T(8,128)(2,1)S(1)}, bf16[384,1536]{1,0:T(8,128)(2,1)S(1)}, u32[]{:S(2)}, u32[]{:S(2)}) %collective-permute-start.68) | collective-permute-done | bytes 1179680 | tf_op jit(solution)/shard_map/ppermute | solution.py:28
  1434.2 16.9 %collective-permute-done.69 = bf16[384,1536]{1,0:T(8,128)(2,1)S(1)} collective-permute-done((bf16[384,1536]{1,0:T(8,128)(2,1)S(1)}, bf16[384,1536]{1,0:T(8,128)(2,1)S(1)}, u32[]{:S(2)}, u32[]{:S(2)}) %collective-permute-start.69) | collective-permute-done | bytes 1179680 | tf_op jit(solution)/shard_map/ppermute | solution.py:28
  1453.2 22.3 %collective-permute-done.70 = bf16[384,1536]{1,0:T(8,128)(2,1)} collective-permute-done((bf16[384,1536]{1,0:T(8,128)(2,1)}, bf16[384,1536]{1,0:T(8,128)(2,1)}, u32[]{:S(2)}, u32[]{:S(2)}) %collective-permute-start.70) | collective-permute-done | bytes 1179680 | tf_op jit(solution)/shard_map/ppermute | solution.py:28
  1483.2 48.7 %collective-permute-done.71 = bf16[384,768]{1,0:T(8,128)(2,1)S(1)} collective-permute-done((bf16[384,768]{1,0:T(8,128)(2,1)S(1)}, bf16[384,768]{1,0:T(8,128)(2,1)S(1)}, u32[]{:S(2)}, u32[]{:S(2)}) %collective-permute-start.71) | collective-permute-done | bytes 589856 | tf_op jit(solution)/shard_map/ppermute | solution.py:28
  1548.7 34.6 %collective-permute-done.72 = bf16[384,384]{1,0:T(8,128)(2,1)S(1)} collective-permute-done((bf16[384,384]{1,0:T(8,128)(2,1)S(1)}, bf16[384,384]{1,0:T(8,128)(2,1)S(1)}, u32[]{:S(2)}, u32[]{:S(2)}) %collective-permute-start.72) | collective-permute-done | bytes 294944 | tf_op jit(solution)/shard_map/ppermute | solution.py:28
  (652 shorter events, 835.0 us)
Async XLA Ops:
  7.2 68.6 %all-gather.12.cloned.1.call-start = ((), (), s32[]{:S(2)}) async-start(), calls=%async_computation.4 | async-start | bytes 1474560 | tf_op jit(solution)/shard_map/all_gather | solution.py:306
  7.9 101.9 %all-gather.22.cloned.1.call-start = ((), (), s32[]{:S(2)}) async-start(), calls=%async_computation.13 | async-start | bytes 1474560 | tf_op jit(solution)/shard_map/all_gather | solution.py:306
  9.8 128.6 %all-gather.20.cloned.1.call-start = ((), (), s32[]{:S(2)}) async-start(), calls=%async_computation.8 | async-start | bytes 1966080 | tf_op jit(solution)/shard_map/all_gather | solution.py:306
  12.0 189.9 %all-gather.18.cloned.1.call-start = ((), (), s32[]{:S(2)}) async-start(), calls=%async_computation.7 | async-start | bytes 1966080 | tf_op jit(solution)/shard_map/all_gather | solution.py:306
  12.6 210.6 %all-gather.16.cloned.1.call-start = ((), (), s32[]{:S(2)}) async-start(), calls=%async_computation.6 | async-start | bytes 1966080 | tf_op jit(solution)/shard_map/all_gather | solution.py:306
  13.7 243.9 %all-gather.14.cloned.1.call-start = ((), (), s32[]{:S(2)}) async-start(), calls=%async_computation.5 | async-start | bytes 1966080 | tf_op jit(solution)/shard_map/all_gather | solution.py:306
  14.2 296.0 %all-gather.26.cloned.1.call-start = ((), (), s32[]{:S(2)}) async-start(), calls=%async_computation.15 | async-start | bytes 1966080 | tf_op jit(solution)/shard_map/all_gather | solution.py:306
  15.6 319.5 %all-gather.24.cloned.1.call-start = ((), (), s32[]{:S(2)}) async-start(), calls=%async_computation.14 | async-start | bytes 1966080 | tf_op jit(solution)/shard_map/all_gather | solution.py:306
  16.8 51.9 %collective-permute-start.3 = (bf16[384,1536]{1,0:T(8,128)(2,1)}, bf16[384,1536]{1,0:T(8,128)(2,1)}, u32[]{:S(2)}, u32[]{:S(2)}) collective-permute-start(bf16[384,1536]{1,0:T(8,128)(2,1)} %pad_maximum_fusion.17), channel_id=1, source_target_pairs={{0,8},{4,12},{8,0},{12,4},{1,9},{5,13},{9,1},{13,5},{2,10},{6,14},... | collective-permute-start | bytes 3538952 | tf_op jit(solution)/shard_map/ppermute | solution.py:28
  68.8 1292.7 %reduce-scatter.5.cloned.1.call-start = ((), (), s32[]{:S(2)}) async-start(), calls=%async_computation.9 | async-start | bytes 3932160 | tf_op jit(solution)/shard_map/reduce_scatter | solution.py:292
  79.8 64.5 %collective-permute-start.5 = (bf16[384,1536]{0,1:T(8,128)(2,1)}, bf16[384,1536]{0,1:T(8,128)(2,1)}, u32[]{:S(2)}, u32[]{:S(2)}) collective-permute-start(bf16[384,1536]{0,1:T(8,128)(2,1)} %bitcast.278), channel_id=1, source_target_pairs={{0,4},{4,0},{8,12},{12,8},{1,5},{5,1},{9,13},{13,9},{2,6},{6,2},{1... | collective-permute-start | bytes 3538952 | tf_op jit(solution)/shard_map/ppermute | solution.py:28
  137.5 67.9 %collective-permute-start.10 = (bf16[384,1536]{0,1:T(8,128)(2,1)}, bf16[384,1536]{0,1:T(8,128)(2,1)}, u32[]{:S(2)}, u32[]{:S(2)}) collective-permute-start(bf16[384,1536]{0,1:T(8,128)(2,1)} %bitcast.287), channel_id=1, source_target_pairs={{0,4},{4,0},{8,12},{12,8},{1,5},{5,1},{9,13},{13,9},{2,6},{6,2},{1... | collective-permute-start | bytes 3538952 | tf_op jit(solution)/shard_map/ppermute | solution.py:28
  142.9 59.1 %collective-permute-start.13 = (bf16[192,4096]{1,0:T(8,128)(2,1)}, bf16[192,4096]{1,0:T(8,128)(2,1)}, u32[]{:S(2)}, u32[]{:S(2)}) collective-permute-start(bf16[192,4096]{1,0:T(8,128)(2,1)} %bitcast.110), channel_id=1, source_target_pairs={{0,8},{4,12},{8,0},{12,4},{1,9},{5,13},{9,1},{13,5},{2,10},{6,14},... | collective-permute-start | bytes 4718600 | tf_op jit(solution)/shard_map/ppermute | solution.py:28
  449.2 65.6 %collective-permute-start.34 = (bf16[256,1536]{1,0:T(8,128)(2,1)}, bf16[256,1536]{1,0:T(8,128)(2,1)S(1)}, u32[]{:S(2)}, u32[]{:S(2)}) collective-permute-start(bf16[256,1536]{1,0:T(8,128)(2,1)} %get-tuple-element.236), channel_id=1, source_target_pairs={{0,16},{1,17},{2,18},{3,19},{4,20},{5,21},{6,22},{7,23},{8,24},{9,... | collective-permute-start | bytes 2359304 | tf_op jit(solution)/shard_map/ppermute | solution.py:24
  712.2 104.4 %collective-permute-start.39 = (bf16[1,256,1536]{2,1,0:T(8,128)(2,1)}, bf16[1,256,1536]{2,1,0:T(8,128)(2,1)}, u32[]{:S(2)}, u32[]{:S(2)}) collective-permute-start(bf16[1,256,1536]{2,1,0:T(8,128)(2,1)} %get-tuple-element.272), channel_id=1, source_target_pairs={{0,1},{1,0},{2,3},{3,2},{4,5},{5,4},{6,7},{7,6},{8,9},{9,8},{10,11... | collective-permute-start | bytes 2359304 | tf_op jit(solution)/shard_map/ppermute | solution.py:28
  713.4 105.5 %collective-permute-start.40 = (bf16[1,256,1536]{2,1,0:T(8,128)(2,1)}, bf16[1,256,1536]{2,1,0:T(8,128)(2,1)}, u32[]{:S(2)}, u32[]{:S(2)}) collective-permute-start(bf16[1,256,1536]{2,1,0:T(8,128)(2,1)} %get-tuple-element.271), channel_id=1, source_target_pairs={{0,2},{1,3},{2,0},{3,1},{4,6},{5,7},{6,4},{7,5},{8,10},{9,11},{10,... | collective-permute-start | bytes 2359304 | tf_op jit(solution)/shard_map/ppermute | solution.py:28
  714.3 106.7 %collective-permute-start.41 = (bf16[1,256,1536]{2,1,0:T(8,128)(2,1)}, bf16[1,256,1536]{2,1,0:T(8,128)(2,1)}, u32[]{:S(2)}, u32[]{:S(2)}) collective-permute-start(bf16[1,256,1536]{2,1,0:T(8,128)(2,1)} %get-tuple-element.270), channel_id=1, source_target_pairs={{0,3},{1,2},{2,1},{3,0},{4,7},{5,6},{6,5},{7,4},{8,11},{9,10},{10,... | collective-permute-start | bytes 2359304 | tf_op jit(solution)/shard_map/ppermute | solution.py:28
  929.3 51.9 %collective-permute-start.44 = (bf16[256,1536]{1,0:T(8,128)(2,1)S(1)}, bf16[256,1536]{1,0:T(8,128)(2,1)S(1)}, u32[]{:S(2)}, u32[]{:S(2)}) collective-permute-start(bf16[256,1536]{1,0:T(8,128)(2,1)S(1)} %get-tuple-element.226), channel_id=1, source_target_pairs={{16,0},{17,1},{18,2},{19,3},{20,4},{21,5},{22,6},{23,7},{24,8},{25... | collective-permute-start | bytes 2359304 | tf_op jit(solution)/shard_map/ppermute | solution.py:24
  930.6 64.5 %collective-permute-start.45 = (bf16[256,1536]{1,0:T(8,128)(2,1)S(1)}, bf16[256,1536]{1,0:T(8,128)(2,1)S(1)}, u32[]{:S(2)}, u32[]{:S(2)}) collective-permute-start(bf16[256,1536]{1,0:T(8,128)(2,1)S(1)} %get-tuple-element.225), channel_id=1, source_target_pairs={{16,0},{17,1},{18,2},{19,3},{20,4},{21,5},{22,6},{23,7},{24,8},{25... | collective-permute-start | bytes 2359304 | tf_op jit(solution)/shard_map/ppermute | solution.py:24
  1101.3 112.6 %collective-permute-start.51 = (bf16[384,4096]{1,0:T(8,128)(2,1)}, bf16[384,4096]{1,0:T(8,128)(2,1)S(1)}, u32[]{:S(2)}, u32[]{:S(2)}) collective-permute-start(bf16[384,4096]{1,0:T(8,128)(2,1)} %get-tuple-element.215), channel_id=1, source_target_pairs={{0,4},{4,0},{8,12},{12,8},{1,5},{5,1},{9,13},{13,9},{2,6},{6,2},{1... | collective-permute-start | bytes 9437192 | tf_op jit(solution)/shard_map/ppermute | solution.py:28
  1101.3 112.6 %collective-permute-start.52 = (bf16[384,4096]{1,0:T(8,128)(2,1)}, bf16[384,4096]{1,0:T(8,128)(2,1)}, u32[]{:S(2)}, u32[]{:S(2)}) collective-permute-start(bf16[384,4096]{1,0:T(8,128)(2,1)} %get-tuple-element.214), channel_id=1, source_target_pairs={{0,4},{4,0},{8,12},{12,8},{1,5},{5,1},{9,13},{13,9},{2,6},{6,2},{1... | collective-permute-start | bytes 9437192 | tf_op jit(solution)/shard_map/ppermute | solution.py:28
  1108.9 70.2 %collective-permute-start.48 = (bf16[384,4096]{1,0:T(8,128)(2,1)S(1)}, bf16[384,4096]{1,0:T(8,128)(2,1)}, u32[]{:S(2)}, u32[]{:S(2)}) collective-permute-start(bf16[384,4096]{1,0:T(8,128)(2,1)S(1)} %copy-done.75), channel_id=1, source_target_pairs={{0,8},{4,12},{8,0},{12,4},{1,9},{5,13},{9,1},{13,5},{2,10},{6,14},... | collective-permute-start | bytes 9437192 | tf_op jit(solution)/shard_map/ppermute | solution.py:28
  1183.8 78.4 %collective-permute-start.53 = (bf16[384,4096]{1,0:T(8,128)(2,1)}, bf16[384,4096]{1,0:T(8,128)(2,1)}, u32[]{:S(2)}, u32[]{:S(2)}) collective-permute-start(bf16[384,4096]{1,0:T(8,128)(2,1)} %get-tuple-element.130), channel_id=1, source_target_pairs={{0,8},{4,12},{8,0},{12,4},{1,9},{5,13},{9,1},{13,5},{2,10},{6,14},... | collective-permute-start | bytes 9437192 | tf_op jit(solution)/shard_map/ppermute | solution.py:28
  1231.5 117.1 %collective-permute-start.56 = (bf16[384,4096]{1,0:T(8,128)(2,1)}, bf16[384,4096]{1,0:T(8,128)(2,1)}, u32[]{:S(2)}, u32[]{:S(2)}) collective-permute-start(bf16[384,4096]{1,0:T(8,128)(2,1)} %get-tuple-element.138), channel_id=1, source_target_pairs={{0,8},{4,12},{8,0},{12,4},{1,9},{5,13},{9,1},{13,5},{2,10},{6,14},... | collective-permute-start | bytes 9437192 | tf_op jit(solution)/shard_map/ppermute | solution.py:28
  1237.7 215.4 %reduce-scatter.7.cloned.1.call-start = ((), (), s32[]{:S(2)}) async-start(), calls=%async_computation.10 | async-start | bytes 3932160 | tf_op jit(solution)/shard_map/reduce_scatter | solution.py:292
  1333.7 281.2 %reduce-scatter.11.cloned.1.call-start = ((), (), s32[]{:S(2)}) async-start(), calls=%async_computation.12 | async-start | bytes 3932160 | tf_op jit(solution)/shard_map/reduce_scatter | solution.py:292
  1379.5 237.8 %reduce-scatter.9.cloned.1.call-start = ((), (), s32[]{:S(2)}) async-start(), calls=%async_computation.11 | async-start | bytes 2949120 | tf_op jit(solution)/shard_map/reduce_scatter | solution.py:292
  1477.4 54.5 %collective-permute-start.71 = (bf16[384,768]{1,0:T(8,128)(2,1)S(1)}, bf16[384,768]{1,0:T(8,128)(2,1)S(1)}, u32[]{:S(2)}, u32[]{:S(2)}) collective-permute-start(bf16[384,768]{1,0:T(8,128)(2,1)S(1)} %broadcast_select_fusion.5), channel_id=1, source_target_pairs={{0,1},{1,0},{2,3},{3,2},{4,5},{5,4},{6,7},{7,6},{8,9},{9,8},{10,11... | collective-permute-start | bytes 1769480 | tf_op jit(solution)/shard_map/ppermute | solution.py:28
  1478.2 70.5 %collective-permute-start.61 = (bf16[1,256,1536]{2,1,0:T(8,128)(2,1)S(1)}, bf16[1,256,1536]{2,1,0:T(8,128)(2,1)S(1)}, u32[]{:S(2)}, u32[]{:S(2)}) collective-permute-start(bf16[1,256,1536]{2,1,0:T(8,128)(2,1)S(1)} %get-tuple-element.265), channel_id=1, source_target_pairs={{0,1},{1,0},{2,3},{3,2},{4,5},{5,4},{6,7},{7,6},{8,9},{9,8},{10,11... | collective-permute-start | bytes 2359304 | tf_op jit(solution)/shard_map/ppermute | solution.py:28
  1480.4 103.1 %collective-permute-start.62 = (bf16[1,256,1536]{2,1,0:T(8,128)(2,1)S(1)}, bf16[1,256,1536]{2,1,0:T(8,128)(2,1)S(1)}, u32[]{:S(2)}, u32[]{:S(2)}) collective-permute-start(bf16[1,256,1536]{2,1,0:T(8,128)(2,1)S(1)} %get-tuple-element.264), channel_id=1, source_target_pairs={{0,2},{1,3},{2,0},{3,1},{4,6},{5,7},{6,4},{7,5},{8,10},{9,11},{10,... | collective-permute-start | bytes 2359304 | tf_op jit(solution)/shard_map/ppermute | solution.py:28
  1481.0 117.1 %collective-permute-start.63 = (bf16[1,256,1536]{2,1,0:T(8,128)(2,1)S(1)}, bf16[1,256,1536]{2,1,0:T(8,128)(2,1)S(1)}, u32[]{:S(2)}, u32[]{:S(2)}) collective-permute-start(bf16[1,256,1536]{2,1,0:T(8,128)(2,1)S(1)} %get-tuple-element.263), channel_id=1, source_target_pairs={{0,3},{1,2},{2,1},{3,0},{4,7},{5,6},{6,5},{7,4},{8,11},{9,10},{10,... | collective-permute-start | bytes 2359304 | tf_op jit(solution)/shard_map/ppermute | solution.py:28
  1532.2 51.1 %collective-permute-start.72 = (bf16[384,384]{1,0:T(8,128)(2,1)S(1)}, bf16[384,384]{1,0:T(8,128)(2,1)S(1)}, u32[]{:S(2)}, u32[]{:S(2)}) collective-permute-start(bf16[384,384]{1,0:T(8,128)(2,1)S(1)} %broadcast_select_fusion.8), channel_id=1, source_target_pairs={{0,2},{1,3},{2,0},{3,1},{4,6},{5,7},{6,4},{7,5},{8,10},{9,11},{10,... | collective-permute-start | bytes 884744 | tf_op jit(solution)/shard_map/ppermute | solution.py:28
  (180 other events, 4196.8 us)
Sparse Core Ops, SparseCore 0:
  9.6 59.6 all-gather.11
  71.4 29.1 all-gather.21
  102.2 36.1 all-gather.19
  139.9 35.9 all-gather.17
  177.3 35.9 all-gather.15
  214.7 35.9 all-gather.13
  252.3 35.9 all-gather.25
  289.8 35.9 all-gather.23
  1237.8 57.4 reduce-scatter.4
  1333.8 57.4 reduce-scatter.6
  1393.6 60.5 reduce-scatter.10
  1456.4 74.4 reduce-scatter.8

commit v5 on v4

v5 whole, which is shorter than its diff:
```python
import functools

import jax
import jax.numpy as jnp
from jax import lax
from jax.experimental import pallas as pl
from jax.experimental.pallas import tpu as pltpu
from jax.sharding import PartitionSpec as P

HEADS = 16
KV_HEADS = 8
HD = 96
L = 1024

epsilon = 1e-05
rope_base = 100000.0
bf16 = jnp.bfloat16
f32 = jnp.float32


def shifted(array, axis, by):
    size = lax.axis_size(axis)
    pairs = [(i, i + by) for i in range(size) if 0 <= i + by < size]
    return lax.ppermute(array, axis, pairs)


def swapped(array, axis, bit):
    return lax.ppermute(array, axis, [(i, i ^ bit) for i in range(lax.axis_size(axis))])


def bits_of(size):
    return [1 << k for k in range(size.bit_length() - 1)]


def mm(left, right):
    return jnp.dot(left, right, preferred_element_type=f32)


def mm_nt(left, right):
    return lax.dot_general(
        left, right, (((1,), (1,)), ((), ())), preferred_element_type=f32
    )


def mm_tn(left, right):
    return lax.dot_general(
        left, right, (((0,), (0,)), ((), ())), preferred_element_type=f32
    )


QB = 256
HP = 128
LOG2E = 1.4426950408889634
MIB = 2**20


def whole(shape):
    rest = (0,) * len(shape)
    return pl.BlockSpec(tuple(shape), lambda *_: rest, pipeline_mode=pl.Buffered(1))


def rows_of(shape, first=0):
    return pl.BlockSpec(tuple(shape), lambda i: (first + i, 0))


def columns_of(shape, first=0):
    return pl.BlockSpec(tuple(shape), lambda i: (0, first + i))


def kernel_call(kernel, grid, in_specs, out_specs, out_shape, flops, name, scratch=(), trans=0):
    moved = sum(2 * shape.size for shape in out_shape)
    return pl.pallas_call(
        kernel,
        grid=grid,
        in_specs=in_specs,
        out_specs=out_specs,
        out_shape=out_shape,
        scratch_shapes=scratch,
        compiler_params=pltpu.CompilerParams(vmem_limit_bytes=56 * MIB),
        cost_estimate=pl.CostEstimate(
            flops=int(flops), bytes_accessed=int(moved + flops // 512), transcendentals=int(trans)
        ),
        name=name,
    )


def turned(values, cosine, sine):
    parts = []
    for at in range(0, values.shape[1], HP):
        head = values[:, at : at + HP]
        parts.append(head * cosine + pltpu.roll(head, HP // 2, 1) * sine)
    return parts[0] if len(parts) == 1 else jnp.concatenate(parts, axis=1)


def project_kernel(h_ref, gain_ref, w_ref, cos_ref, sin_ref, out_ref, normed_ref, *, turning):
    step = pl.program_id(0)

    @pl.when(step == 0)
    def _():
        rows = h_ref[...].astype(f32)
        inverse = lax.rsqrt(jnp.mean(rows * rows, axis=-1, keepdims=True) + epsilon)
        normed_ref[...] = (rows * inverse * gain_ref[...]).astype(bf16)

    values = mm(normed_ref[...], w_ref[...])

    @pl.when(step < turning)
    def _():
        out_ref[...] = turned(values, cos_ref[...], sin_ref[...]).astype(bf16)

    @pl.when(step >= turning)
    def _():
        out_ref[...] = values.astype(bf16)


def project(h, gain, w, cosine, sine, turned_columns):
    n, width = h.shape
    total = w.shape[1]
    block = 512
    out_shape = (
        jax.ShapeDtypeStruct((n, total), bf16),
        jax.ShapeDtypeStruct((n, width), bf16),
    )
    return kernel_call(
        functools.partial(project_kernel, turning=turned_columns // block),
        (total // block,),
        [
            whole(h.shape), whole(gain.shape), columns_of((width, block)),
            whole(cosine.shape), whole(sine.shape),
        ],
        [columns_of((n, block)), whole((n, width))],
        out_shape,
        2 * n * width * total,
        "project",
    )(h, gain, w, cosine, sine)


def join_kernel(mixed_ref, h_ref, w_ref, gain_ref, middle_ref, normed_ref):
    middle = h_ref[...].astype(f32) + mm_nt(mixed_ref[...], w_ref[...])
    middle_ref[...] = middle
    inverse = lax.rsqrt(jnp.mean(middle * middle, axis=-1, keepdims=True) + epsilon)
    normed_ref[...] = (middle * inverse * gain_ref[...]).astype(bf16)


def join(mixed, h, w, gain):
    n, width = h.shape
    block = min(QB, n)
    out_shape = (
        jax.ShapeDtypeStruct((n, width), f32),
        jax.ShapeDtypeStruct((n, width), bf16),
    )
    return kernel_call(
        join_kernel,
        (n // block,),
        [
            rows_of((block, mixed.shape[1])), rows_of((block, width)),
            whole(w.shape), whole(gain.shape),
        ],
        [rows_of((block, width))] * 2,
        out_shape,
        2 * n * width * mixed.shape[1],
        "join",
    )(mixed, h, w, gain)


def gate_up_kernel(x_ref, wg_ref, wu_ref, gate_ref, up_ref, hidden_ref):
    x = x_ref[...]
    gate = mm(x, wg_ref[...])
    upward = mm(x, wu_ref[...])
    gate_ref[...] = gate.astype(bf16)
    up_ref[...] = upward.astype(bf16)
    hidden_ref[...] = (gate * jax.nn.sigmoid(gate) * upward).astype(bf16)


def gate_up(x, wg, wu):
    n, width = x.shape
    total = wg.shape[1]
    block = 512
    return kernel_call(
        gate_up_kernel,
        (total // block,),
        [whole(x.shape), columns_of((width, block)), columns_of((width, block))],
        [columns_of((n, block))] * 3,
        (jax.ShapeDtypeStruct((n, total), bf16),) * 3,
        4 * n * width * total,
        "gate_up",
        trans=n * total,
    )(x, wg, wu)


def down_kernel(hidden_ref, middle_ref, w_ref, out_ref):
    out_ref[...] = (middle_ref[...] + mm_nt(hidden_ref[...], w_ref[...])).astype(bf16)


def down_rows(hidden, middle, w, first, count):
    n, width = middle.shape
    block = min(QB, n)
    return kernel_call(
        down_kernel,
        (count,),
        [
            rows_of((block, hidden.shape[1]), first), rows_of((block, width), first),
            whole(w.shape),
        ],
        [rows_of((block, width))],
        (jax.ShapeDtypeStruct((count * block, width), bf16),),
        2 * count * block * width * hidden.shape[1],
        "down_rows",
    )(hidden, middle, w)[0]


def feed_back_kernel(
    grad_ref, gate_ref, up_ref, wd_ref, wg_ref, wu_ref, middle_ref, gain_ref,
    total_ref, low_ref, sum_ref, *grad_refs
):
    step = pl.program_id(0)
    gate = gate_ref[...].astype(f32)
    hidden_grad = mm(grad_ref[...], wd_ref[...])
    sigma = jax.nn.sigmoid(gate)
    gate_grad = hidden_grad * up_ref[...].astype(f32) * (sigma * (1.0 + gate * (1.0 - sigma)))
    gate_grad = gate_grad.astype(bf16)
    up_grad = (hidden_grad * gate * sigma).astype(bf16)
    for ref, value in zip(grad_refs, (gate_grad, up_grad)):
        ref[...] = value
    part = mm_nt(gate_grad, wg_ref[...]) + mm_nt(up_grad, wu_ref[...])

    @pl.when(step == 0)
    def _():
        total_ref[...] = part

    @pl.when(step > 0)
    def _():
        total_ref[...] += part

    @pl.when(step == pl.num_programs(0) - 1)
    def _():
        n = total_ref.shape[0]
        size = min(QB, n)
        sums = 0.0
        for at in range(0, n, size):
            rows = slice(at, at + size)
            middle = middle_ref[rows]
            back = total_ref[rows]
            inverse = lax.rsqrt(jnp.mean(middle * middle, axis=-1, keepdims=True) + epsilon)
            sums = sums + jnp.sum(back * middle * inverse, axis=0, keepdims=True)
            scaled = back * gain_ref[...]
            mean_term = jnp.mean(scaled * middle, axis=-1, keepdims=True)
            branch = scaled * inverse - middle * (inverse * inverse * inverse * mean_term)
            result = grad_ref[rows].astype(f32) + branch
            total_ref[rows] = result
            low_ref[rows] = result.astype(bf16)
        sum_ref[...] = sums


def feed_back(grad, gate, upward, wd, wg, wu, middle, gain, with_grads):
    n, width = grad.shape
    total = wg.shape[1]
    block = 512
    out_shape = (
        jax.ShapeDtypeStruct((n, width), f32),
        jax.ShapeDtypeStruct((n, width), bf16),
        jax.ShapeDtypeStruct((1, width), f32),
    )
    out_specs = [whole((n, width)), whole((n, width)), whole((1, width))]
    if with_grads:
        out_shape += (jax.ShapeDtypeStruct((n, total), bf16),) * 2
        out_specs += [columns_of((n, block))] * 2
    return kernel_call(
        feed_back_kernel,
        (total // block,),
        [
            whole(grad.shape), columns_of((n, block)), columns_of((n, block)),
            columns_of((width, block)), columns_of((width, block)), columns_of((width, block)),
            whole(middle.shape), whole(gain.shape),
        ],
        out_specs,
        out_shape,
        6 * n * width * total,
        "feed_back",
        trans=n * total,
    )(grad, gate, upward, wd, wg, wu, middle, gain)


def heads_back_kernel(
    dq_ref, dk_ref, dv_ref, w_ref, h_ref, grad_ref, gain_ref, out_ref, sum_ref
):
    step = pl.program_id(0)
    back = 0.0
    at = 0
    for ref in (dq_ref, dk_ref, dv_ref):
        back = back + mm_nt(ref[...], w_ref[:, at : at + ref.shape[1]])
        at += ref.shape[1]
    rows = h_ref[...].astype(f32)
    inverse = lax.rsqrt(jnp.mean(rows * rows, axis=-1, keepdims=True) + epsilon)
    sums = jnp.sum(back * rows * inverse, axis=0, keepdims=True)
    scaled = back * gain_ref[...]
    mean_term = jnp.mean(scaled * rows, axis=-1, keepdims=True)
    branch = scaled * inverse - rows * (inverse * inverse * inverse * mean_term)
    out_ref[...] = (grad_ref[...] + branch).astype(bf16)

    @pl.when(step == 0)
    def _():
        sum_ref[...] = sums

    @pl.when(step > 0)
    def _():
        sum_ref[...] += sums


def heads_back(dq, dk, dv, w, h, grad, gain, first, count):
    n, width = h.shape
    block = min(QB, n)
    out_shape = (
        jax.ShapeDtypeStruct((count * block, width), bf16),
        jax.ShapeDtypeStruct((1, width), f32),
    )
    return kernel_call(
        heads_back_kernel,
        (count,),
        [rows_of((block, a.shape[1]), first) for a in (dq, dk, dv)]
        + [
            whole(w.shape), rows_of((block, width), first), rows_of((block, width), first),
            whole(gain.shape),
        ],
        [rows_of((block, width)), whole((1, width))],
        out_shape,
        2 * count * block * width * w.shape[1],
        "heads_back",
    )(dq, dk, dv, w, h, grad, gain)


def two_heads(ref, rows):
    return jnp.concatenate([ref[rows, :HP], ref[rows, HP:]], axis=0)


def score_parts(offset_ref, k_ref, q, i, size, single):
    cols = q.shape[0]
    first = i * size if single else 0
    count = size if single else k_ref.shape[0]
    parts = []
    if first:
        parts.append((0, first, mm_nt(k_ref[:first], q)))
    diagonal = mm_nt(k_ref[first : first + count], q)
    key_at = first + lax.broadcasted_iota(jnp.int32, (count, cols), 0)
    query_at = i * size + lax.rem(lax.broadcasted_iota(jnp.int32, (count, cols), 1), size)
    if not single:
        query_at = query_at + offset_ref[0]
    diagonal = jnp.where(key_at <= query_at, diagonal, -1e30)
    parts.append((first, count, diagonal))
    return parts


def attend_forward_kernel(offset_ref, q_ref, k_ref, v_ref, o_ref, lse_ref, *, single):
    n = q_ref.shape[0]
    size = min(QB, n)
    factor = HD ** (-0.5) * LOG2E
    vt = v_ref[...].T
    for i in range(n // size):
        rows = slice(i * size, (i + 1) * size)
        q = two_heads(q_ref, rows)
        parts = score_parts(offset_ref, k_ref, q, i, size, single)
        top = functools.reduce(
            jnp.maximum, [jnp.max(part, axis=0, keepdims=True) for _, _, part in parts]
        )
        total = 0.0
        mixed = 0.0
        for first, count, part in parts:
            weights = jnp.exp2((part - top) * factor)
            total = total + jnp.sum(weights, axis=0, keepdims=True)
            mixed = mixed + mm(vt[:, first : first + count], weights.astype(bf16))
        mixed = (mixed * (1.0 / total)).T.astype(bf16)
        o_ref[rows, :HP] = mixed[:size]
        o_ref[rows, HP:] = mixed[size:]
        lse_ref[0, i] = top * factor + jnp.log2(total)


def attend_backward_kernel(
    offset_ref, q_ref, k_ref, v_ref, g_ref, lse_ref, cosq_ref, sinq_ref, cosk_ref, sink_ref,
    dq_ref, dk_ref, dv_ref, dk_acc, dv_acc, *, single
):
    n = q_ref.shape[0]
    size = min(QB, n)
    scale = HD ** (-0.5)
    factor = scale * LOG2E
    kt = k_ref[...].T
    dk_acc[...] = jnp.zeros_like(dk_acc)
    dv_acc[...] = jnp.zeros_like(dv_acc)
    for i in range(n // size):
        rows = slice(i * size, (i + 1) * size)
        q = two_heads(q_ref, rows)
        g = two_heads(g_ref, rows)
        lse = lse_ref[0, i]
        kept = []
        centre = 0.0
        for first, count, part in score_parts(offset_ref, k_ref, q, i, size, single):
            keys = slice(first, first + count)
            probs = jnp.exp2(part * factor - lse)
            prob_grad = mm_nt(v_ref[keys], g)
            dv_acc[keys] += mm(probs.astype(bf16), g)
            centre = centre + jnp.sum(probs * prob_grad, axis=0, keepdims=True)
            kept.append((keys, probs, prob_grad))
        dqt = 0.0
        for keys, probs, prob_grad in kept:
            score_grad = (probs * (prob_grad - centre)).astype(bf16)
            dk_acc[keys] += mm(score_grad, q)
            dqt = dqt + mm(kt[:, keys], score_grad)
        dq = (dqt * scale).T
        for c in range(2):
            head = turned(dq[c * size : (c + 1) * size], cosq_ref[rows], sinq_ref[rows])
            dq_ref[rows, c * HP : (c + 1) * HP] = head.astype(bf16)
    dk_ref[...] = turned(dk_acc[...] * scale, cosk_ref[...], sink_ref[...]).astype(bf16)
    dv_ref[...] = dv_acc[...].astype(bf16)


SCALAR = pl.BlockSpec(memory_space=pltpu.SMEM)


def attention_forward(q, k, v, offset, single):
    n = q[0].shape[0]
    size = min(QB, n)
    count = k[0].shape[0]
    out_shape = (
        jax.ShapeDtypeStruct((n, HEADS * HP), bf16),
        jax.ShapeDtypeStruct((KV_HEADS, n // size, 1, 2 * size), f32),
    )
    return kernel_call(
        functools.partial(attend_forward_kernel, single=single),
        (KV_HEADS,),
        [
            SCALAR, columns_of((n, 2 * HP), q[1] // 2), columns_of((count, HP), k[1]),
            columns_of((count, HP), v[1]),
        ],
        [
            columns_of((n, 2 * HP)),
            pl.BlockSpec((1, n // size, 1, 2 * size), lambda h: (h, 0, 0, 0)),
        ],
        out_shape,
        4 * HEADS * n * count * HP,
        "attend_forward",
        trans=HEADS * n * count,
    )(offset, q[0], k[0], v[0])


def attention_backward(q, k, v, mixed_grad, lse, query_tables, key_tables, offset, single):
    n = q[0].shape[0]
    size = min(QB, n)
    count = k[0].shape[0]
    out_shape = (
        jax.ShapeDtypeStruct((n, HEADS * HP), bf16),
        jax.ShapeDtypeStruct((count, KV_HEADS * HP), bf16),
        jax.ShapeDtypeStruct((count, KV_HEADS * HP), bf16),
    )
    return kernel_call(
        functools.partial(attend_backward_kernel, single=single),
        (KV_HEADS,),
        [
            SCALAR, columns_of((n, 2 * HP), q[1] // 2), columns_of((count, HP), k[1]),
            columns_of((count, HP), v[1]), columns_of((n, 2 * HP)),
            pl.BlockSpec((1, n // size, 1, 2 * size), lambda h: (h, 0, 0, 0)),
        ]
        + [whole(table.shape) for table in query_tables + key_tables],
        [columns_of((n, 2 * HP)), columns_of((count, HP)), columns_of((count, HP))],
        out_shape,
        10 * HEADS * n * count * HP,
        "attend_backward",
        scratch=[pltpu.VMEM((count, HP), f32), pltpu.VMEM((count, HP), f32)],
        trans=HEADS * n * count,
    )(offset, q[0], k[0], v[0], mixed_grad, lse, *query_tables, *key_tables)


def padded(array):
    rows = array.shape[0]
    parts = array.reshape(rows, -1, HD // 2)
    parts = jnp.pad(parts, ((0, 0), (0, 0), (0, HP // 2 - HD // 2)))
    return parts.reshape(rows, -1)


def unpadded(array):
    rows = array.shape[0]
    return array.reshape(rows, -1, HP // 2)[:, :, : HD // 2].reshape(rows, -1)


def local(
    inputs, cotangent, attn_gain, w_query, w_key, w_value, w_out, mlp_gain, w_gate, w_up, w_down
):
    micro, nloc, width = inputs.shape
    tsize = lax.axis_size("tensor")
    dsize = lax.axis_size("dp")
    ranks = tsize // micro
    n = nloc * micro
    share = width // dsize
    first_section = lax.axis_index("section") == 0
    t = lax.axis_index("tensor")
    d = lax.axis_index("dp")
    seq = t % micro
    seg = t // micro
    copies = HEADS // KV_HEADS
    dims = KV_HEADS * HD
    low_bits = bits_of(dsize)[:1]
    high_bits = bits_of(dsize)[1:]
    same_seq = [[g + micro * r for r in range(ranks)] for g in range(micro)]

    def exchange(blocks):
        out = blocks
        for j in range(1, micro):
            sent = lax.dynamic_index_in_dim(blocks, seq ^ j, 0, keepdims=True)
            got = swapped(sent, "tensor", j)
            out = lax.dynamic_update_slice_in_dim(out, got, seq ^ j, 0)
        return out

    def reorder(array, axis):
        return jnp.concatenate(
            [lax.dynamic_slice_in_dim(array, (d ^ m) * share, share, axis) for m in range(dsize)],
            axis=axis,
        )

    def swap_in(parts, bit):
        parts = dict(parts)
        for m in sorted(parts):
            parts[m ^ bit] = swapped(parts[m], "dp", bit)
        return parts

    def spread_far(block):
        parts = {0: block}
        for bit in reversed(high_bits):
            parts = swap_in(parts, bit)
        return parts

    def spread_near(parts):
        for bit in low_bits:
            parts = swap_in(parts, bit)
        return jnp.concatenate([parts[m] for m in range(dsize)], axis=0)

    def gather_columns(shard):
        whole = lax.all_gather(shard, "tensor", axis=0)
        return whole.transpose(1, 0, 2).reshape(share, tsize * shard.shape[1])

    def tied(*arrays):
        return lax.optimization_barrier(arrays)

    def exchange_half(array):
        side = lax.axis_index("section")
        return exchange(lax.dynamic_slice_in_dim(array, side * (width // 2), width // 2, 2))

    def join_halves(mine):
        other = swapped(mine, "section", 1)
        whole = jnp.concatenate(
            [jnp.where(first_section, mine, other), jnp.where(first_section, other, mine)], axis=2
        )
        return reorder(whole.reshape(n, width), 1)

    def split_rows(grad):
        return {m: grad[m * share : (m + 1) * share].astype(bf16) for m in range(dsize)}

    def add_partner(parts, bits):
        for bit in bits:
            summed = {}
            for m in sorted(parts):
                if not m & bit:
                    got = swapped(parts[m ^ bit], "dp", bit)
                    summed[m] = (parts[m].astype(f32) + got.astype(f32)).astype(bf16)
            parts = summed
        return parts

    def rows_to_send(array):
        return jnp.concatenate(
            [array[:, m * share : (m + 1) * share] for m in range(dsize) if m & 1], axis=1
        )

    def rows_to_keep(array):
        return jnp.concatenate(
            [array[:, m * share : (m + 1) * share] for m in range(dsize) if not m & 1], axis=1
        )

    def swap_low(array):
        return swapped(array, "dp", 1)

    def add_low(mine, got):
        total = (mine.astype(f32) + got.astype(f32)).astype(bf16)
        return {2 * i: total[i * share : (i + 1) * share] for i in range(dsize // 2)}

    def send_far(parts):
        size = share // 2
        pairs = []
        for i in range(2):
            half = {m: part[i * size : (i + 1) * size] for m, part in parts.items()}
            bit = high_bits[0]
            kept = {m: part for m, part in half.items() if not m & bit}
            pairs.append([kept, {m: swapped(half[m ^ bit], "dp", bit) for m in kept}])
        return pairs

    def receive_far(pair):
        kept, got = pair
        parts = {m: (kept[m].astype(f32) + got[m].astype(f32)).astype(bf16) for m in kept}
        return add_partner(parts, high_bits[1:])[0]

    def scatter_columns(part):
        part = part.reshape(share, tsize, -1).transpose(1, 0, 2)
        return lax.psum_scatter(part, "tensor", scatter_dimension=0)

    attn_scale = reorder(attn_gain[0], 0)
    mlp_scale = reorder(mlp_gain[0], 0)
    mine = exchange_half(inputs)
    last = spread_far(jnp.concatenate([w_key[0], w_value[0]], axis=1))
    mine, last = tied(mine, last)
    wkv = spread_near(last)
    rows_in = join_halves(mine)

    def spread_weight(shard, pieces, last):
        rows = share // pieces
        fars = []
        for i in range(pieces):
            whole = lax.all_gather(shard[i * rows : (i + 1) * rows], "tensor", axis=0)
            whole, last = tied(whole, last)
            if fars:
                fars[-1] = last
            whole = whole.transpose(1, 0, 2).reshape(rows, tsize * shard.shape[1])
            last = spread_far(whole)
            fars.append(last)
        return fars, last

    def settle(fars):
        parts = [dict(far) for far in fars]
        for bit in low_bits:
            parts = [swap_in(part, bit) for part in parts]
        return jnp.concatenate([part[m] for m in range(dsize) for part in parts], axis=0)

    fars, last = spread_weight(w_query[0], 1, last)
    wqkv = jnp.concatenate([padded(settle(fars)), padded(wkv)], axis=1)
    fars, last = spread_weight(w_out[0].T, 1, last)
    wo = padded(settle(fars))
    fars, last = spread_weight(w_gate[0], 2, last)
    wg = settle(fars)
    fars, last = spread_weight(w_up[0], 2, last)
    wu = settle(fars)
    far_down, last = spread_weight(w_down[0].T, 2, last)

    def tables(positions):
        half = HD // 2
        freqs = rope_base ** (-jnp.arange(half, dtype=f32) / half)
        angles = positions.astype(f32)[:, None] * freqs[None, :]
        blank = ((0, 0), (0, HP // 2 - half))
        cosine = jnp.pad(jnp.cos(angles), blank)
        sine = jnp.pad(jnp.sin(angles), blank)
        return (
            jnp.concatenate([cosine, cosine], axis=1),
            jnp.concatenate([-sine, sine], axis=1),
        )

    query_tables = tables(seg * n + jnp.arange(n))
    single = ranks == 1
    offset = (seg * n).astype(jnp.int32).reshape(1)

    back_tables = (query_tables[0], -query_tables[1])
    if single:
        key_tables = back_tables
    else:
        key_tables = tables(jnp.arange(L))
        key_tables = (key_tables[0], -key_tables[1])
    q_lanes = HEADS * HP
    k_lanes = KV_HEADS * HP
    blocks = n // min(QB, n)
    attn_row = attn_scale[None]
    mlp_row = mlp_scale[None]

    def head_arrays(qkv):
        if single:
            return (qkv, 0), (qkv, HEADS), (qkv, HEADS + KV_HEADS)
        both = lax.all_gather(
            qkv[:, q_lanes:], "tensor", axis=0, tiled=True, axis_index_groups=same_seq
        )
        return (qkv, 0), (both, 0), (both, KV_HEADS)

    def own_rows(array):
        if single:
            return array
        return lax.psum_scatter(
            array, "tensor", scatter_dimension=0, tiled=True, axis_index_groups=same_seq
        )

    def forward(h, extra=None):
        qkv, normed = project(h, attn_row, wqkv, *query_tables, q_lanes + k_lanes)
        heads = head_arrays(qkv)
        mixed, lse = attention_forward(*heads, offset, single)
        if extra is not None:
            mixed, extra = tied(mixed, extra)
        middle, normed_mlp = join(mixed, h, wo, mlp_row)
        gate, upward, hidden = gate_up(normed_mlp, wg, wu)
        kept = (h, normed, heads, lse, mixed, middle, normed_mlp, gate, upward, hidden)
        return kept, extra

    def backward(grad, kept, weights_too, extra=None):
        h, normed, heads, lse, mixed, middle, normed_mlp, gate, upward, hidden = kept
        if weights_too:
            odd, even = rows_to_send(grad), rows_to_keep(grad)
            odd = mm_tn(odd, hidden).astype(bf16)
            even, odd = tied(even, odd)
            got = swap_low(odd)
            even = mm_tn(even, hidden).astype(bf16)
            even, grad = tied(even, grad)
            grad, down = tied(grad, add_low(even, got))
            first, second = send_far(down)
            down = receive_far(first)
        middle_grad, middle_bf, mlp_sum, *grads = feed_back(
            grad, gate, upward, wd, wg, wu, middle, mlp_row, weights_too
        )
        if weights_too:
            gate_grad, up_grad = grads
            gate_grad, up_grad, down, second[0] = tied(gate_grad, up_grad, down, second[0])
            down = [down, receive_far(second)]
            odd = mm_tn(rows_to_send(normed_mlp), gate_grad).astype(bf16)
            gate_grad, odd = tied(gate_grad, odd)
            got = swap_low(odd)
            even = mm_tn(rows_to_keep(normed_mlp), gate_grad).astype(bf16)
            even, up_grad = tied(even, up_grad)
            up_grad, gate_sum, down[1] = tied(up_grad, add_low(even, got), down[1])
            down = scatter_columns(jnp.concatenate(down, axis=0))
            first, second = send_far(gate_sum)
            gate_sum = receive_far(first)
            up_sum = mm_tn(normed_mlp, up_grad).astype(bf16)
            middle_bf, up_sum, gate_sum, second[0] = tied(middle_bf, up_sum, gate_sum, second[0])
            gate_sum = [gate_sum, receive_far(second)]
            up_sum = add_partner(split_rows(up_sum), low_bits)
            out = unpadded(mm_tn(middle_bf, mixed).astype(bf16))
            middle_bf, out = tied(middle_bf, out)
            out = add_partner(split_rows(out), low_bits)
        mixed_grad = mm(middle_bf, wo).astype(bf16)
        if extra is not None:
            mixed_grad, extra = tied(mixed_grad, extra)
        if weights_too:
            mixed_grad, gate_sum[1], up_sum, out = tied(mixed_grad, gate_sum[1], up_sum, out)
            gate_sum = scatter_columns(jnp.concatenate(gate_sum, axis=0))
            first, second = send_far(up_sum)
            up_sum = receive_far(first)
        dq, dk, dv = attention_backward(
            *heads, mixed_grad, lse, back_tables, key_tables, offset, single
        )
        dk = own_rows(dk)
        dv = own_rows(dv)
        if not weights_too:
            outgoing = [
                heads_back(dq, dk, dv, wqkv, h, middle_grad, attn_row, i, 1)[0]
                for i in range(blocks)
            ]
            return outgoing, extra
        dq, dk, dv, down, up_sum, second[0] = tied(dq, dk, dv, down, up_sum, second[0])
        up_sum = [up_sum, receive_far(second)]
        kv = jnp.concatenate(
            [unpadded(mm_tn(normed, dk).astype(bf16)), unpadded(mm_tn(normed, dv).astype(bf16))],
            axis=1,
        )
        query = unpadded(mm_tn(normed, dq).astype(bf16))
        dq, kv, query, up_sum[1] = tied(dq, kv, query, up_sum[1])
        up_sum = scatter_columns(jnp.concatenate(up_sum, axis=0))
        out = add_partner(out, high_bits)[0]
        kv = add_partner(split_rows(kv), low_bits)
        query = add_partner(split_rows(query), low_bits)
        outgoing, attn_sum = heads_back(dq, dk, dv, wqkv, h, middle_grad, attn_row, 0, blocks)
        outgoing, kv, query, out, gate_sum = tied(outgoing, kv, query, out, gate_sum)
        kv = add_partner(kv, high_bits)[0]
        query = add_partner(query, high_bits)[0]
        pair = jnp.concatenate(
            [out.reshape(share, tsize, -1), query.reshape(share, tsize, -1)], axis=2
        )
        pair, up_sum = tied(pair, up_sum)
        pair = scatter_columns(pair)
        gains = jnp.concatenate([attn_sum, mlp_sum], axis=0)
        half_cols = pair.shape[1] // 2
        sums = [down, gate_sum, up_sum, pair[:, :half_cols], pair[:, half_cols:]]
        return outgoing, sums + [sum_over_tensor(kv)], gains

    def sum_over_tensor(array):
        bits = bits_of(tsize)
        for bit in bits:
            side = (t & bit) != 0
            size = array.shape[1] // 2
            low, high = array[:, :size], array[:, size:]
            got = swapped(jnp.where(side, low, high), "tensor", bit)
            kept_half = jnp.where(side, high, low)
            array = (kept_half.astype(f32) + got.astype(f32)).astype(bf16)
        for bit in reversed(bits):
            side = (t & bit) != 0
            got = swapped(array, "tensor", bit)
            array = jnp.concatenate(
                [jnp.where(side, got, array), jnp.where(side, array, got)], axis=1
            )
        return array

    def to_places(rows):
        return exchange(reorder(rows, 1).reshape(micro, nloc, width))[None]

    kept, _ = forward(rows_in)
    far_down[-1], hidden = tied(far_down[-1], kept[-1])
    middle = kept[5]
    wd = settle(far_down)
    received = jnp.concatenate(
        [
            shifted(down_rows(hidden, middle, wd, i, 1), "section", 1)
            for i in range(blocks)
        ],
        axis=0,
    )
    received, late_cotangent = tied(received, cotangent)
    half_cot = exchange_half(late_cotangent)
    kept, cot = forward(jnp.where(first_section, rows_in, received), join_halves(half_cot))
    second_out = down_rows(kept[-1], kept[5], wd, 0, blocks)
    first_grad, outputs = backward(cot, kept, False, to_places(second_out))
    returned = jnp.concatenate([shifted(part, "section", -1) for part in first_grad], axis=0)
    second_grad, sums, gains = backward(jnp.where(first_section, returned, cot), kept, True)
    input_grads = to_places(second_grad)
    down, gate, up, out, query, kv = sums
    gains = reorder(gains, 1)
    for axis, size in (("dp", dsize), ("tensor", tsize)):
        for bit in bits_of(size):
            gains = gains + swapped(gains, axis, bit)
    return (
        outputs,
        input_grads,
        gains[:1],
        query.astype(f32)[None],
        kv[:, :dims].astype(f32)[None],
        kv[:, dims:].astype(f32)[None],
        out.astype(f32).T[None],
        gains[1:],
        gate.astype(f32)[None],
        up.astype(f32)[None],
        down.astype(f32).T[None],
    )


def solution(mesh):
    in_specs = (
        P(None, ("dp", "tensor"), None),
        P(None, ("dp", "tensor"), None),
        P("section", None),
        P("section", "dp", "tensor"),
        P("section", "dp", None),
        P("section", "dp", None),
        P("section", "tensor", "dp"),
        P("section", None),
        P("section", "dp", "tensor"),
        P("section", "dp", "tensor"),
        P("section", "tensor", "dp"),
    )
    out_specs = (
        P("section", None, ("dp", "tensor"), None),
        P("section", None, ("dp", "tensor"), None),
        P("section", None),
        P("section", "dp", "tensor"),
        P("section", "dp", None),
        P("section", "dp", None),
        P("section", "tensor", "dp"),
        P("section", None),
        P("section", "dp", "tensor"),
        P("section", "dp", "tensor"),
        P("section", "tensor", "dp"),
    )
    return jax.shard_map(local, mesh=mesh, in_specs=in_specs, out_specs=out_specs, check_vma=False)
```

time: 1630 us -> 1580 us (0.969)
  Pallas kernels: 116 us -> 511 us
  matrix products: 489 us -> 106 us
  local copies, waits for them, and re-layouts: 285 us -> 205 us
  other arithmetic: 151 us -> 103 us
  waiting for transfers between devices: 506 us -> 545 us
  starting transfers between devices: 63.9 us -> 89.4 us
    pallas_call x4 -> x22, Pallas kernels: 116 us -> 511 us  [the longest x2 126 us: feed_back(): kernel_call(feed_back_kernel, (total // block,), [whole(grad.shape), colu...]
    dot_general x21 -> x0, matrix products: 219 us -> none  [mm_nt(): lax.dot_general(left, right, (((1,), (1,)), ((), ())), preferred_element_...]
    dot_general x12 -> x2, matrix products: 194 us -> 20.6 us  [mm(): return jnp.dot(left, right, preferred_element_type=f32)]
    all_gather x8, waiting for transfers between devices: 0.56 us -> 33.9 us  [spread_weight(): whole = lax.all_gather(shard[i * rows:(i + 1) * rows], 'tensor', axis=0)]
    convert_element_type x12 -> x7, other arithmetic: 49.8 us -> 18 us  [add_partner(): summed[m] = (parts[m].astype(f32) + got.astype(f32)).astype(bf16)]
    another operation x9 -> x0, other arithmetic: 28.7 us -> none
    ppermute x67 -> x68, starting transfers between devices: 50.9 us -> 75.3 us  [swapped(): lax.ppermute(array, axis, [(i, i ^ bit) for i in range(lax.axis_size(axis...]
    unnamed x277 -> x140, local copies, waits for them, and re-layouts: 91.2 us -> 68.1 us
  transfers between devices with their start and end apart: 87 -> 88, of which waited for: 29 -> 32; matrix products, arithmetic and copies ran while one was open for 38% -> 22% of each run, Pallas kernels for 5% -> 21%
where the time goes in v5:
time: 1580 us
  waiting for transfers between devices  545 us (34%)
  Pallas kernels  511 us (32%)
  local copies, waits for them, and re-layouts  205 us (13%)
  matrix products  106 us (7%)
  other arithmetic  103 us (7%)
  starting transfers between devices  89.4 us (6%)
    ppermute x68, waiting for transfers between devices, swapped(): lax.ppermute(array, axis, [(i, i ^ bit) for i in range(lax.axis_size(axis...  382 us
    ppermute x8, waiting for transfers between devices, shifted(): return lax.ppermute(array, axis, pairs)  127 us
    pallas_call x2, Pallas kernels, feed_back(): kernel_call(feed_back_kernel, (total // block,), [whole(grad.shape), colu...  126 us
    dot_general x9, matrix products, mm_tn(): lax.dot_general(left, right, (((0,), (0,)), ((), ())), preferred_element_...  85.8 us
    ppermute x68, starting transfers between devices, swapped(): lax.ppermute(array, axis, [(i, i ^ bit) for i in range(lax.axis_size(axis...  75.3 us
    pallas_call x2, Pallas kernels, attention_backward(): kernel_call(functools.partial(attend_backward_kernel, single=single), (KV...  75.1 us
    unnamed x140, local copies, waits for them, and re-layouts  68.1 us
    pallas_call x5, Pallas kernels, heads_back(): kernel_call(heads_back_kernel, (count,), [rows_of((block, a.shape[1]), fi...  66.1 us
  transfers between devices with their start and end apart: 88, of which 32 were waited for; matrix products, arithmetic and copies ran while one was open for 22% of the time, Pallas kernels for 21%

profile of v5, /device:TPU:0, one launch (start us, length us, event | category | flops | bytes accessed | tf_op | source)
XLA Modules:
  0.0 1576.1 jit_solution(17069475484254161714)
XLA Ops:
  27.1 30.4 %collective-permute-done = bf16[1,256,768]{2,1,0:T(8,128)(2,1)S(1)} collective-permute-done((bf16[1,256,768]{2,1,0:T(8,128)(2,1)S(1)}, bf16[1,256,768]{2,1,0:T(8,128)(2,1)S(1)}, u32[]{:S(2)}, u32[]{:S(2)}) %collective-permute-start) | collective-permute-done | bytes 393248 | tf_op jit(solution)/shard_map/ppermute | solution.py:28
  111.3 27.9 %all-gather.18.cloned.1.call-done = bf16[4,192,1024]{2,1,0:T(8,128)(2,1)} async-done(((bf16[1,192,1024]{2,1,0:T(8,128)(2,1)}), bf16[4,192,1024]{2,1,0:T(8,128)(2,1)}) %all-gather.18.cloned.1.call-update) | async-done | bytes 1572880 | tf_op jit(solution)/shard_map/all_gather | solution.py:612
  168.3 24.6 %project.2 = (bf16[1024,4096]{1,0:T(8,128)(2,1)}, bf16[1024,1536]{1,0:T(8,128)(2,1)}) custom-call(bf16[1024,1536]{1,0:T(8,128)(2,1)} %pad_maximum_fusion.4.h_ref, f32[1,1536]{1,0:T(1,128)} %broadcast_in_dim.68.gain_ref, bf16[1536,4096]{1,0:T(8,128)(2,1)} %pad_maximum_fusion.w_ref, f32[1024,128]{1,0:T(8,128)} %get-tuple-element.364.cos_ref.cosq_ref.cosk_ref, ...), custom_call_target="tpu_custom_call" | custom-call | flops 12884901888 | bytes 36700160 | tf_op jit(solution)/shard_map/project/pallas_call | solution.py:123
  192.8 21.7 %attend_forward.2 = (bf16[1024,2048]{1,0:T(8,128)(2,1)}, f32[8,4,1,512]{3,2,1,0:T(1,128)}) custom-call(s32[1]{0:T(128)} %bitcast.offset_ref, bf16[1024,4096]{1,0:T(8,128)(2,1)} %get-tuple-element.131.q_ref.k_ref.v_ref, bf16[1024,4096]{1,0:T(8,128)(2,1)} %get-tuple-element.131.q_ref.k_ref.v_ref, bf16[1024,4096]{1,0:T(8,128)(2,1)} %get-tuple-element.131.q_ref.k_ref.v_ref), custom_call_target="tpu_custom_call" | custom-call | flops 8589934592 | bytes 21004288 | tf_op jit(solution)/shard_map/attend_forward/pallas_call | solution.py:425
  251.5 17.3 %collective-permute-done.8 = bf16[192,4096]{1,0:T(8,128)(2,1)} collective-permute-done((bf16[192,4096]{1,0:T(8,128)(2,1)}, bf16[192,4096]{1,0:T(8,128)(2,1)}, u32[]{:S(2)}, u32[]{:S(2)}) %collective-permute-start.8) | collective-permute-done | bytes 1572896 | tf_op jit(solution)/shard_map/ppermute | solution.py:28
  283.0 24.9 %collective-permute-done.9 = bf16[192,4096]{1,0:T(8,128)(2,1)} collective-permute-done((bf16[192,4096]{1,0:T(8,128)(2,1)}, bf16[192,4096]{1,0:T(8,128)(2,1)}, u32[]{:S(2)}, u32[]{:S(2)}) %collective-permute-start.9) | collective-permute-done | bytes 1572896 | tf_op jit(solution)/shard_map/ppermute | solution.py:28
  322.4 23.6 %collective-permute-done.10 = bf16[192,4096]{1,0:T(8,128)(2,1)} collective-permute-done((bf16[192,4096]{1,0:T(8,128)(2,1)}, bf16[192,4096]{1,0:T(8,128)(2,1)}, u32[]{:S(2)}, u32[]{:S(2)}) %collective-permute-start.10) | collective-permute-done | bytes 1572896 | tf_op jit(solution)/shard_map/ppermute | solution.py:28
  362.8 20.5 %collective-permute-done.11 = bf16[192,4096]{1,0:T(8,128)(2,1)} collective-permute-done((bf16[192,4096]{1,0:T(8,128)(2,1)}, bf16[192,4096]{1,0:T(8,128)(2,1)}, u32[]{:S(2)}, u32[]{:S(2)}) %collective-permute-start.11) | collective-permute-done | bytes 1572896 | tf_op jit(solution)/shard_map/ppermute | solution.py:28
  387.9 32.0 %gate_up.2 = (bf16[1024,4096]{1,0:T(8,128)(2,1)}, bf16[1024,4096]{1,0:T(8,128)(2,1)}, bf16[1024,4096]{1,0:T(8,128)(2,1)}) custom-call(bf16[1024,1536]{1,0:T(8,128)(2,1)} %get-tuple-element.133.x_ref, bf16[1536,4096]{1,0:T(8,128)(2,1)} %constant_dynamic-update-slice_fusion.wg_ref, bf16[1536,4096]{1,0:T(8,128)(2,1)} %constant_dynamic-update-slice_fusion.8.wu_ref), custom_call_target="tpu_custom_call" | custom-call | flops 25769803776 | bytes 75497472 | tf_op jit(solution)/shard_map/gate_up/pallas_call | solution.py:178
  496.3 16.7 %collective-permute-done.33 = bf16[256,1536]{1,0:T(8,128)(2,1)S(1)} collective-permute-done((bf16[256,1536]{1,0:T(8,128)(2,1)S(1)}, bf16[256,1536]{1,0:T(8,128)(2,1)S(1)}, u32[]{:S(2)}, u32[]{:S(2)}) %collective-permute-start.33) | collective-permute-done | bytes 786464 | tf_op jit(solution)/shard_map/ppermute | solution.py:24
  513.1 16.9 %collective-permute-done.32 = bf16[256,1536]{1,0:T(8,128)(2,1)S(1)} collective-permute-done((bf16[256,1536]{1,0:T(8,128)(2,1)S(1)}, bf16[256,1536]{1,0:T(8,128)(2,1)S(1)}, u32[]{:S(2)}, u32[]{:S(2)}) %collective-permute-start.32) | collective-permute-done | bytes 786464 | tf_op jit(solution)/shard_map/ppermute | solution.py:24
  529.9 16.1 %collective-permute-done.31 = bf16[256,1536]{1,0:T(8,128)(2,1)S(1)} collective-permute-done((bf16[256,1536]{1,0:T(8,128)(2,1)}, bf16[256,1536]{1,0:T(8,128)(2,1)S(1)}, u32[]{:S(2)}, u32[]{:S(2)}) %collective-permute-start.31) | collective-permute-done | bytes 786464 | tf_op jit(solution)/shard_map/ppermute | solution.py:24
  579.8 24.5 %project.3 = (bf16[1024,4096]{1,0:T(8,128)(2,1)}, bf16[1024,1536]{1,0:T(8,128)(2,1)}) custom-call(bf16[1024,1536]{1,0:T(8,128)(2,1)} %broadcast_select_fusion.h_ref, f32[1,1536]{1,0:T(1,128)} %broadcast_in_dim.68.gain_ref, bf16[1536,4096]{1,0:T(8,128)(2,1)} %pad_maximum_fusion.w_ref, f32[1024,128]{1,0:T(8,128)} %get-tuple-element.364.cos_ref.cosq_ref.cosk_ref, ...), custom_call_target="tpu_custom_call" | custom-call | flops 12884901888 | bytes 36700160 | tf_op jit(solution)/shard_map/project/pallas_call | solution.py:123
  604.3 21.7 %attend_forward.3 = (bf16[1024,2048]{1,0:T(8,128)(2,1)}, f32[8,4,1,512]{3,2,1,0:T(1,128)}) custom-call(s32[1]{0:T(128)} %bitcast.offset_ref, bf16[1024,4096]{1,0:T(8,128)(2,1)} %get-tuple-element.146.q_ref.k_ref.v_ref, bf16[1024,4096]{1,0:T(8,128)(2,1)} %get-tuple-element.146.q_ref.k_ref.v_ref, bf16[1024,4096]{1,0:T(8,128)(2,1)} %get-tuple-element.146.q_ref.k_ref.v_ref), custom_call_target="tpu_custom_call" | custom-call | flops 8589934592 | bytes 21004288 | tf_op jit(solution)/shard_map/attend_forward/pallas_call | solution.py:425
  641.7 31.9 %gate_up.3 = (bf16[1024,4096]{1,0:T(8,128)(2,1)}, bf16[1024,4096]{1,0:T(8,128)(2,1)}, bf16[1024,4096]{1,0:T(8,128)(2,1)}) custom-call(bf16[1024,1536]{1,0:T(8,128)(2,1)} %get-tuple-element.151.x_ref, bf16[1536,4096]{1,0:T(8,128)(2,1)} %constant_dynamic-update-slice_fusion.wg_ref, bf16[1536,4096]{1,0:T(8,128)(2,1)} %constant_dynamic-update-slice_fusion.8.wu_ref), custom_call_target="tpu_custom_call" | custom-call | flops 25769803776 | bytes 75497472 | tf_op jit(solution)/shard_map/gate_up/pallas_call | solution.py:178
  673.6 20.6 %down_rows.9 = bf16[1024,1536]{1,0:T(8,128)(2,1)} custom-call(bf16[1024,4096]{1,0:T(8,128)(2,1)} %get-tuple-element.156.hidden_ref, f32[1024,1536]{1,0:T(8,128)} %get-tuple-element.154.middle_ref, bf16[1536,4096]{1,0:T(8,128)(2,1)} %constant_dynamic-update-slice_fusion.16.w_ref.wd_ref), custom_call_target="tpu_custom_call" | custom-call | flops 12884901888 | bytes 28311552 | tf_op jit(solution)/shard_map/down_rows/pallas_call | solution.py:197
  709.5 62.4 %feed_back.2 = (f32[1024,1536]{1,0:T(8,128)}, bf16[1024,1536]{1,0:T(8,128)(2,1)}, f32[1,1536]{1,0:T(1,128)}) custom-call(bf16[1024,1536]{1,0:T(8,128)(2,1)} %pad_maximum_fusion.7.grad_ref, bf16[1024,4096]{1,0:T(8,128)(2,1)} %get-tuple-element.152.gate_ref, bf16[1024,4096]{1,0:T(8,128)(2,1)} %get-tuple-element.153.up_ref, ...), custom_call_target="tpu_custom_call" | custom-call | flops 38654705664 | bytes 81792000 | tf_op jit(solution)/shard_map/feed_back/pallas_call | solution.py:267
  785.7 15.4 collective-permute-done.41
  802.0 37.8 %attend_backward.2 = (bf16[1024,2048]{1,0:T(8,128)(2,1)}, bf16[1024,1024]{1,0:T(8,128)(2,1)}, bf16[1024,1024]{1,0:T(8,128)(2,1)}) custom-call(s32[1]{0:T(128)} %bitcast.offset_ref, bf16[1024,4096]{1,0:T(8,128)(2,1)} %get-tuple-element.146.q_ref.k_ref.v_ref, bf16[1024,4096]{1,0:T(8,128)(2,1)} %get-tuple-element.146.q_ref.k_ref.v_ref, ...), custom_call_target="tpu_custom_call" | custom-call | flops 21474836480 | bytes 50331648 | tf_op jit(solution)/shard_map/attend_backward/pallas_call | solution.py:452
  887.7 17.2 %collective-permute-done.45 = bf16[256,1536]{1,0:T(8,128)(2,1)S(1)} collective-permute-done((bf16[256,1536]{1,0:T(8,128)(2,1)S(1)}, bf16[256,1536]{1,0:T(8,128)(2,1)S(1)}, u32[]{:S(2)}, u32[]{:S(2)}) %collective-permute-start.45) | collective-permute-done | bytes 786464 | tf_op jit(solution)/shard_map/ppermute | solution.py:24
  904.9 16.9 %collective-permute-done.44 = bf16[256,1536]{1,0:T(8,128)(2,1)S(1)} collective-permute-done((bf16[256,1536]{1,0:T(8,128)(2,1)S(1)}, bf16[256,1536]{1,0:T(8,128)(2,1)S(1)}, u32[]{:S(2)}, u32[]{:S(2)}) %collective-permute-start.44) | collective-permute-done | bytes 786464 | tf_op jit(solution)/shard_map/ppermute | solution.py:24
  921.7 16.9 %collective-permute-done.43 = bf16[256,1536]{1,0:T(8,128)(2,1)S(1)} collective-permute-done((bf16[256,1536]{1,0:T(8,128)(2,1)S(1)}, bf16[256,1536]{1,0:T(8,128)(2,1)S(1)}, u32[]{:S(2)}, u32[]{:S(2)}) %collective-permute-start.43) | collective-permute-done | bytes 786464 | tf_op jit(solution)/shard_map/ppermute | solution.py:24
  985.6 63.9 %feed_back.3 = (f32[1024,1536]{1,0:T(8,128)}, bf16[1024,1536]{1,0:T(8,128)(2,1)}, f32[1,1536]{1,0:T(1,128)}, bf16[1024,4096]{1,0:T(8,128)(2,1)}, bf16[1024,4096]{1,0:T(8,128)(2,1)}) custom-call(bf16[1024,1536]{1,0:T(8,128)(2,1)} %copy-done.1, bf16[1024,4096]{1,0:T(8,128)(2,1)} %get-tuple-element.152.gate_ref, bf16[1024,4096]{1,0:T(8,128)(2,1)} %get-tuple-element.153.up_ref, ...), custom_call_target="tpu_custom_call" | custom-call | flops 38654705664 | bytes 98569216 | tf_op jit(solution)/shard_map/feed_back/pallas_call | solution.py:267
  1072.8 26.8 %collective-permute-done.49 = bf16[192,4096]{1,0:T(8,128)(2,1)S(1)} collective-permute-done((bf16[192,4096]{1,0:T(8,128)(2,1)S(1)}, bf16[192,4096]{1,0:T(8,128)(2,1)S(1)}, u32[]{:S(2)}, u32[]{:S(2)}) %collective-permute-start.49) | collective-permute-done | bytes 1572896 | tf_op jit(solution)/shard_map/ppermute | solution.py:28
  1117.4 20.4 %convolution_convert_fusion = bf16[1536,4096]{1,0:T(8,128)(2,1)} fusion(bf16[1024,1536]{1,0:T(8,128)(2,1)} %get-tuple-element.151.x_ref, bf16[1024,4096]{1,0:T(8,128)(2,1)} %get-tuple-element.185), kind=kOutput, calls=%fused_computation | convolution fusion | flops 12891193344 | bytes 24117248 | tf_op jit(solution)/shard_map/dot_general | solution.py:46
  1203.5 37.4 %attend_backward.3 = (bf16[1024,2048]{1,0:T(8,128)(2,1)}, bf16[1024,1024]{1,0:T(8,128)(2,1)}, bf16[1024,1024]{1,0:T(8,128)(2,1)}) custom-call(s32[1]{0:T(128)} %bitcast.offset_ref, bf16[1024,4096]{1,0:T(8,128)(2,1)} %get-tuple-element.146.q_ref.k_ref.v_ref, bf16[1024,4096]{1,0:T(8,128)(2,1)} %get-tuple-element.146.q_ref.k_ref.v_ref, ...), custom_call_target="tpu_custom_call" | custom-call | flops 21474836480 | bytes 50331648 | tf_op jit(solution)/shard_map/attend_backward/pallas_call | solution.py:452
  1302.4 23.3 %heads_back.9 = (bf16[1024,1536]{1,0:T(8,128)(2,1)}, f32[1,1536]{1,0:T(1,128)}) custom-call(bf16[1024,2048]{1,0:T(8,128)(2,1)} %get-tuple-element.206.dq_ref, bf16[1024,1024]{1,0:T(8,128)(2,1)} %get-tuple-element.203.dk_ref, bf16[1024,1024]{1,0:T(8,128)(2,1)} %get-tuple-element.204.dv_ref, bf16[1536,4096]{1,0:T(8,128)(2,1)} %pad_maximum_fusion.w_ref, ...), custom_call_target="tpu_custom_call" | custom-call | flops 12884901888 | bytes 28314624 | tf_op jit(solution)/shard_map/heads_back/pallas_call | solution.py:316
  1339.3 26.0 %collective-permute-done.67 = f32[2,1536]{1,0:T(2,128)S(1)} collective-permute-done((f32[2,1536]{1,0:T(2,128)S(1)}, f32[2,1536]{1,0:T(2,128)S(1)}, u32[]{:S(2)}, u32[]{:S(2)}) %collective-permute-start.67) | collective-permute-done | bytes 12320 | tf_op jit(solution)/shard_map/ppermute | solution.py:28
  1365.3 19.7 %collective-permute-start.68 = (f32[2,1536]{1,0:T(2,128)S(1)}, f32[2,1536]{1,0:T(2,128)}, u32[]{:S(2)}, u32[]{:S(2)}) collective-permute-start(f32[2,1536]{1,0:T(2,128)S(1)} %add.227), channel_id=1, source_target_pairs={{0,1},{1,0},{2,3},{3,2},{4,5},{5,4},{6,7},{7,6},{8,9},{9,8},{10,11... | collective-permute-start | bytes 36872 | tf_op jit(solution)/shard_map/ppermute | solution.py:28
  1427.9 51.2 %collective-permute-done.72 = bf16[384,768]{0,1:T(8,128)(2,1)S(1)} collective-permute-done((bf16[384,768]{0,1:T(8,128)(2,1)S(1)}, bf16[384,768]{0,1:T(8,128)(2,1)S(1)}, u32[]{:S(2)}, u32[]{:S(2)}) %collective-permute-start.72) | collective-permute-done | bytes 589856 | tf_op jit(solution)/shard_map/ppermute | solution.py:28
  1479.7 15.2 collective-permute-done.63
  1495.0 34.6 %collective-permute-done.73 = bf16[384,384]{0,1:T(8,128)(2,1)S(1)} collective-permute-done((bf16[384,384]{0,1:T(8,128)(2,1)S(1)}, bf16[384,384]{0,1:T(8,128)(2,1)S(1)}, u32[]{:S(2)}, u32[]{:S(2)}) %collective-permute-start.73) | collective-permute-done | bytes 294944 | tf_op jit(solution)/shard_map/ppermute | solution.py:28
  (465 shorter events, 704.4 us)
Async XLA Ops:
  7.2 65.3 %all-gather.20.cloned.1.call-start = ((), (), s32[]{:S(2)}) async-start(), calls=%async_computation.8 | async-start | bytes 1474560 | tf_op jit(solution)/shard_map/all_gather | solution.py:612
  7.9 92.9 %all-gather.26.cloned.1.call-start = ((), (), s32[]{:S(2)}) async-start(), calls=%async_computation.15 | async-start | bytes 1474560 | tf_op jit(solution)/shard_map/all_gather | solution.py:612
  9.8 129.4 %all-gather.18.cloned.1.call-start = ((), (), s32[]{:S(2)}) async-start(), calls=%async_computation.7 | async-start | bytes 1966080 | tf_op jit(solution)/shard_map/all_gather | solution.py:612
  12.0 216.9 %all-gather.16.cloned.1.call-start = ((), (), s32[]{:S(2)}) async-start(), calls=%async_computation.6 | async-start | bytes 1966080 | tf_op jit(solution)/shard_map/all_gather | solution.py:612
  12.5 238.9 %all-gather.14.cloned.1.call-start = ((), (), s32[]{:S(2)}) async-start(), calls=%async_computation.5 | async-start | bytes 1966080 | tf_op jit(solution)/shard_map/all_gather | solution.py:612
  13.6 269.4 %all-gather.12.cloned.1.call-start = ((), (), s32[]{:S(2)}) async-start(), calls=%async_computation.4 | async-start | bytes 1966080 | tf_op jit(solution)/shard_map/all_gather | solution.py:612
  14.1 308.2 %all-gather.24.cloned.1.call-start = ((), (), s32[]{:S(2)}) async-start(), calls=%async_computation.14 | async-start | bytes 1966080 | tf_op jit(solution)/shard_map/all_gather | solution.py:612
  15.5 347.3 %all-gather.22.cloned.1.call-start = ((), (), s32[]{:S(2)}) async-start(), calls=%async_computation.13 | async-start | bytes 1966080 | tf_op jit(solution)/shard_map/all_gather | solution.py:612
  16.3 52.4 %collective-permute-start.3 = (bf16[384,1536]{0,1:T(8,128)(2,1)S(1)}, bf16[384,1536]{0,1:T(8,128)(2,1)}, u32[]{:S(2)}, u32[]{:S(2)}) collective-permute-start(bf16[384,1536]{0,1:T(8,128)(2,1)S(1)} %pad_maximum_fusion.15), channel_id=1, source_target_pairs={{0,8},{4,12},{8,0},{12,4},{1,9},{5,13},{9,1},{13,5},{2,10},{6,14},... | collective-permute-start | bytes 3538952 | tf_op jit(solution)/shard_map/ppermute | solution.py:28
  69.3 1174.7 %reduce-scatter.5.cloned.1.call-start = ((), (), s32[]{:S(2)}) async-start(), calls=%async_computation.9 | async-start | bytes 3932160 | tf_op jit(solution)/shard_map/reduce_scatter | solution.py:598
  79.9 63.5 %collective-permute-start.13 = (bf16[384,1536]{0,1:T(8,128)(2,1)}, bf16[384,1536]{0,1:T(8,128)(2,1)}, u32[]{:S(2)}, u32[]{:S(2)}) collective-permute-start(bf16[384,1536]{0,1:T(8,128)(2,1)} %bitcast.13), channel_id=1, source_target_pairs={{0,4},{4,0},{8,12},{12,8},{1,5},{5,1},{9,13},{13,9},{2,6},{6,2},{1... | collective-permute-start | bytes 3538952 | tf_op jit(solution)/shard_map/ppermute | solution.py:28
  110.8 103.7 %collective-permute-start.17 = (bf16[384,1536]{0,1:T(8,128)(2,1)}, bf16[384,1536]{0,1:T(8,128)(2,1)}, u32[]{:S(2)}, u32[]{:S(2)}) collective-permute-start(bf16[384,1536]{0,1:T(8,128)(2,1)} %bitcast.16), channel_id=1, source_target_pairs={{0,4},{4,0},{8,12},{12,8},{1,5},{5,1},{9,13},{13,9},{2,6},{6,2},{1... | collective-permute-start | bytes 3538952 | tf_op jit(solution)/shard_map/ppermute | solution.py:28
  141.9 87.0 %collective-permute-start.7 = (bf16[192,4096]{1,0:T(8,128)(2,1)}, bf16[192,4096]{1,0:T(8,128)(2,1)}, u32[]{:S(2)}, u32[]{:S(2)}) collective-permute-start(bf16[192,4096]{1,0:T(8,128)(2,1)} %bitcast.89), channel_id=1, source_target_pairs={{0,8},{4,12},{8,0},{12,4},{1,9},{5,13},{9,1},{13,5},{2,10},{6,14},... | collective-permute-start | bytes 4718600 | tf_op jit(solution)/shard_map/ppermute | solution.py:28
  245.9 65.1 %collective-permute-start.21 = (bf16[192,4096]{1,0:T(8,128)(2,1)}, bf16[192,4096]{1,0:T(8,128)(2,1)}, u32[]{:S(2)}, u32[]{:S(2)}) collective-permute-start(bf16[192,4096]{1,0:T(8,128)(2,1)} %collective-permute-done.7), channel_id=1, source_target_pairs={{0,4},{4,0},{8,12},{12,8},{1,5},{5,1},{9,13},{13,9},{2,6},{6,2},{1... | collective-permute-start | bytes 4718600 | tf_op jit(solution)/shard_map/ppermute | solution.py:28
  481.3 64.7 %collective-permute-start.31 = (bf16[256,1536]{1,0:T(8,128)(2,1)}, bf16[256,1536]{1,0:T(8,128)(2,1)S(1)}, u32[]{:S(2)}, u32[]{:S(2)}) collective-permute-start(bf16[256,1536]{1,0:T(8,128)(2,1)} %down_rows.5), channel_id=1, source_target_pairs={{0,16},{1,17},{2,18},{3,19},{4,20},{5,21},{6,22},{7,23},{8,24},{9,... | collective-permute-start | bytes 2359304 | tf_op jit(solution)/shard_map/ppermute | solution.py:24
  701.8 82.0 %collective-permute-start.39 = (bf16[1,256,1536]{2,1,0:T(8,128)(2,1)}, bf16[1,256,1536]{2,1,0:T(8,128)(2,1)S(1)}, u32[]{:S(2)}, u32[]{:S(2)}) collective-permute-start(bf16[1,256,1536]{2,1,0:T(8,128)(2,1)} %get-tuple-element.315), channel_id=1, source_target_pairs={{0,1},{1,0},{2,3},{3,2},{4,5},{5,4},{6,7},{7,6},{8,9},{9,8},{10,11... | collective-permute-start | bytes 2359304 | tf_op jit(solution)/shard_map/ppermute | solution.py:28
  708.7 76.0 %collective-permute-start.40 = (bf16[1,256,1536]{2,1,0:T(8,128)(2,1)}, bf16[1,256,1536]{2,1,0:T(8,128)(2,1)S(1)}, u32[]{:S(2)}, u32[]{:S(2)}) collective-permute-start(bf16[1,256,1536]{2,1,0:T(8,128)(2,1)} %get-tuple-element.314), channel_id=1, source_target_pairs={{0,2},{1,3},{2,0},{3,1},{4,6},{5,7},{6,4},{7,5},{8,10},{9,11},{10,... | collective-permute-start | bytes 2359304 | tf_op jit(solution)/shard_map/ppermute | solution.py:28
  885.1 53.5 %collective-permute-start.43 = (bf16[256,1536]{1,0:T(8,128)(2,1)S(1)}, bf16[256,1536]{1,0:T(8,128)(2,1)S(1)}, u32[]{:S(2)}, u32[]{:S(2)}) collective-permute-start(bf16[256,1536]{1,0:T(8,128)(2,1)S(1)} %copy-done.40), channel_id=1, source_target_pairs={{16,0},{17,1},{18,2},{19,3},{20,4},{21,5},{22,6},{23,7},{24,8},{25... | collective-permute-start | bytes 2359304 | tf_op jit(solution)/shard_map/ppermute | solution.py:24
  886.4 64.6 %collective-permute-start.42 = (bf16[256,1536]{1,0:T(8,128)(2,1)}, bf16[256,1536]{1,0:T(8,128)(2,1)S(1)}, u32[]{:S(2)}, u32[]{:S(2)}) collective-permute-start(bf16[256,1536]{1,0:T(8,128)(2,1)} %get-tuple-element.164), channel_id=1, source_target_pairs={{16,0},{17,1},{18,2},{19,3},{20,4},{21,5},{22,6},{23,7},{24,8},{25... | collective-permute-start | bytes 2359304 | tf_op jit(solution)/shard_map/ppermute | solution.py:24
  983.9 65.8 %collective-permute-start.47 = (bf16[192,4096]{1,0:T(8,128)(2,1)S(1)}, bf16[192,4096]{1,0:T(8,128)(2,1)S(1)}, u32[]{:S(2)}, u32[]{:S(2)}) collective-permute-start(bf16[192,4096]{1,0:T(8,128)(2,1)S(1)} %get-tuple-element.304), channel_id=1, source_target_pairs={{0,8},{4,12},{8,0},{12,4},{1,9},{5,13},{9,1},{13,5},{2,10},{6,14},... | collective-permute-start | bytes 4718600 | tf_op jit(solution)/shard_map/ppermute | solution.py:28
  1113.0 74.1 %collective-permute-start.51 = (bf16[192,4096]{1,0:T(8,128)(2,1)}, bf16[192,4096]{1,0:T(8,128)(2,1)}, u32[]{:S(2)}, u32[]{:S(2)}) collective-permute-start(bf16[192,4096]{1,0:T(8,128)(2,1)} %get-tuple-element.301), channel_id=1, source_target_pairs={{0,8},{4,12},{8,0},{12,4},{1,9},{5,13},{9,1},{13,5},{2,10},{6,14},... | collective-permute-start | bytes 4718600 | tf_op jit(solution)/shard_map/ppermute | solution.py:28
  1117.3 219.1 %reduce-scatter.7.cloned.1.call-start = ((), (), s32[]{:S(2)}) async-start(), calls=%async_computation.10 | async-start | bytes 3932160 | tf_op jit(solution)/shard_map/reduce_scatter | solution.py:598
  1199.0 82.7 %collective-permute-start.57 = (bf16[192,4096]{1,0:T(8,128)(2,1)}, bf16[192,4096]{1,0:T(8,128)(2,1)}, u32[]{:S(2)}, u32[]{:S(2)}) collective-permute-start(bf16[192,4096]{1,0:T(8,128)(2,1)} %get-tuple-element.299), channel_id=1, source_target_pairs={{0,8},{4,12},{8,0},{12,4},{1,9},{5,13},{9,1},{13,5},{2,10},{6,14},... | collective-permute-start | bytes 4718600 | tf_op jit(solution)/shard_map/ppermute | solution.py:28
  1200.5 92.6 %collective-permute-start.62 = (bf16[384,1536]{0,1:T(8,128)(2,1)}, bf16[384,1536]{0,1:T(8,128)(2,1)}, u32[]{:S(2)}, u32[]{:S(2)}) collective-permute-start(bf16[384,1536]{0,1:T(8,128)(2,1)} %get-tuple-element.212), channel_id=1, source_target_pairs={{0,8},{4,12},{8,0},{12,4},{1,9},{5,13},{9,1},{13,5},{2,10},{6,14},... | collective-permute-start | bytes 3538952 | tf_op jit(solution)/shard_map/ppermute | solution.py:28
  1203.4 200.4 %reduce-scatter.9.cloned.1.call-start = ((), (), s32[]{:S(2)}) async-start(), calls=%async_computation.11 | async-start | bytes 3932160 | tf_op jit(solution)/shard_map/reduce_scatter | solution.py:598
  1288.6 277.5 %reduce-scatter.11.cloned.1.call-start = ((), (), s32[]{:S(2)}) async-start(), calls=%async_computation.12 | async-start | bytes 2949120 | tf_op jit(solution)/shard_map/reduce_scatter | solution.py:598
  1336.4 62.1 %collective-permute-start.70 = (bf16[384,1536]{0,1:T(8,128)(2,1)}, bf16[384,1536]{0,1:T(8,128)(2,1)}, u32[]{:S(2)}, u32[]{:S(2)}) collective-permute-start(bf16[384,1536]{0,1:T(8,128)(2,1)} %get-tuple-element.220), channel_id=1, source_target_pairs={{0,8},{4,12},{8,0},{12,4},{1,9},{5,13},{9,1},{13,5},{2,10},{6,14},... | collective-permute-start | bytes 3538952 | tf_op jit(solution)/shard_map/ppermute | solution.py:28
  1420.3 58.7 %collective-permute-start.72 = (bf16[384,768]{0,1:T(8,128)(2,1)S(1)}, bf16[384,768]{0,1:T(8,128)(2,1)S(1)}, u32[]{:S(2)}, u32[]{:S(2)}) collective-permute-start(bf16[384,768]{0,1:T(8,128)(2,1)S(1)} %broadcast_select_fusion.5), channel_id=1, source_target_pairs={{0,1},{1,0},{2,3},{3,2},{4,5},{5,4},{6,7},{7,6},{8,9},{9,8},{10,11... | collective-permute-start | bytes 1769480 | tf_op jit(solution)/shard_map/ppermute | solution.py:28
  1422.1 72.9 %collective-permute-start.63 = (bf16[1,256,1536]{2,1,0:T(8,128)(2,1)S(1)}, bf16[1,256,1536]{2,1,0:T(8,128)(2,1)S(1)}, u32[]{:S(2)}, u32[]{:S(2)}) collective-permute-start(bf16[1,256,1536]{2,1,0:T(8,128)(2,1)S(1)} %get-tuple-element.294), channel_id=1, source_target_pairs={{0,1},{1,0},{2,3},{3,2},{4,5},{5,4},{6,7},{7,6},{8,9},{9,8},{10,11... | collective-permute-start | bytes 2359304 | tf_op jit(solution)/shard_map/ppermute | solution.py:28
  1423.0 106.8 %collective-permute-start.64 = (bf16[1,256,1536]{2,1,0:T(8,128)(2,1)S(1)}, bf16[1,256,1536]{2,1,0:T(8,128)(2,1)S(1)}, u32[]{:S(2)}, u32[]{:S(2)}) collective-permute-start(bf16[1,256,1536]{2,1,0:T(8,128)(2,1)S(1)} %get-tuple-element.293), channel_id=1, source_target_pairs={{0,2},{1,3},{2,0},{3,1},{4,6},{5,7},{6,4},{7,5},{8,10},{9,11},{10,... | collective-permute-start | bytes 2359304 | tf_op jit(solution)/shard_map/ppermute | solution.py:28
  1424.3 119.7 %collective-permute-start.65 = (bf16[1,256,1536]{2,1,0:T(8,128)(2,1)S(1)}, bf16[1,256,1536]{2,1,0:T(8,128)(2,1)S(1)}, u32[]{:S(2)}, u32[]{:S(2)}) collective-permute-start(bf16[1,256,1536]{2,1,0:T(8,128)(2,1)S(1)} %get-tuple-element.292), channel_id=1, source_target_pairs={{0,3},{1,2},{2,1},{3,0},{4,7},{5,6},{6,5},{7,4},{8,11},{9,10},{10,... | collective-permute-start | bytes 2359304 | tf_op jit(solution)/shard_map/ppermute | solution.py:28
  1479.3 50.3 %collective-permute-start.73 = (bf16[384,384]{0,1:T(8,128)(2,1)S(1)}, bf16[384,384]{0,1:T(8,128)(2,1)S(1)}, u32[]{:S(2)}, u32[]{:S(2)}) collective-permute-start(bf16[384,384]{0,1:T(8,128)(2,1)S(1)} %broadcast_select_fusion.8), channel_id=1, source_target_pairs={{0,2},{1,3},{2,0},{3,1},{4,6},{5,7},{6,4},{7,5},{8,10},{9,11},{10,... | collective-permute-start | bytes 884744 | tf_op jit(solution)/shard_map/ppermute | solution.py:28
  (112 other events, 2613.7 us)
Sparse Core Ops, SparseCore 0:
  9.6 59.9 all-gather.19
  71.7 29.0 all-gather.25
  103.0 36.1 all-gather.17
  141.2 35.9 all-gather.15
  179.2 35.9 all-gather.13
  216.6 35.9 all-gather.11
  254.2 35.9 all-gather.23
  291.7 35.9 all-gather.21
  1117.4 75.8 reduce-scatter.4
  1203.5 76.4 reduce-scatter.6
  1288.7 76.3 reduce-scatter.8
  1403.9 75.6 reduce-scatter.10

commit v6 on v5

--- a/solution.py
+++ b/solution.py
@@ -629,8 +629,10 @@
     fars, last = spread_weight(w_out[0].T, 1, last)
     wo = padded(settle(fars))
     fars, last = spread_weight(w_gate[0], 2, last)
+    waits = list(fars)
     wg = settle(fars)
     fars, last = spread_weight(w_up[0], 2, last)
+    waits.append(fars[0])
     wu = settle(fars)
     far_down, last = spread_weight(w_down[0].T, 2, last)
 
@@ -677,16 +679,42 @@
             array, "tensor", scatter_dimension=0, tiled=True, axis_index_groups=same_seq
         )
 
-    def forward(h, extra=None):
+    def forward(h, extra=None, waits=None):
+        if waits:
+            h = tied(h, waits[0])[0]
         qkv, normed = project(h, attn_row, wqkv, *query_tables, q_lanes + k_lanes)
+        if waits:
+            qkv = tied(qkv, waits[1])[0]
         heads = head_arrays(qkv)
         mixed, lse = attention_forward(*heads, offset, single)
         if extra is not None:
             mixed, extra = tied(mixed, extra)
+        if waits:
+            mixed = tied(mixed, waits[2])[0]
         middle, normed_mlp = join(mixed, h, wo, mlp_row)
         gate, upward, hidden = gate_up(normed_mlp, wg, wu)
         kept = (h, normed, heads, lse, mixed, middle, normed_mlp, gate, upward, hidden)
         return kept, extra
+
+    def sum_over_tensor(array):
+        bits = bits_of(tsize)
+        for bit in bits:
+            side = (t & bit) != 0
+            size = array.shape[1] // 2
+            low, high = array[:, :size], array[:, size:]
+            got = swapped(jnp.where(side, low, high), "tensor", bit)
+            kept_half = jnp.where(side, high, low)
+            array = (kept_half.astype(f32) + got.astype(f32)).astype(bf16)
+        for bit in reversed(bits):
+            side = (t & bit) != 0
+            got = swapped(array, "tensor", bit)
+            array = jnp.concatenate(
+                [jnp.where(side, got, array), jnp.where(side, array, got)], axis=1
+            )
+        return array
+
+    def to_places(rows):
+        return exchange(reorder(rows, 1).reshape(micro, nloc, width))[None]
 
     def backward(grad, kept, weights_too, extra=None):
         h, normed, heads, lse, mixed, middle, normed_mlp, gate, upward, hidden = kept
@@ -698,22 +726,20 @@
             even = mm_tn(even, hidden).astype(bf16)
             even, grad = tied(even, grad)
             grad, down = tied(grad, add_low(even, got))
-            first, second = send_far(down)
-            down = receive_far(first)
+            down = add_partner(down, high_bits)[0]
         middle_grad, middle_bf, mlp_sum, *grads = feed_back(
             grad, gate, upward, wd, wg, wu, middle, mlp_row, weights_too
         )
         if weights_too:
             gate_grad, up_grad = grads
-            gate_grad, up_grad, down, second[0] = tied(gate_grad, up_grad, down, second[0])
-            down = [down, receive_far(second)]
+            gate_grad, up_grad, down = tied(gate_grad, up_grad, down)
+            down = scatter_columns(down)
             odd = mm_tn(rows_to_send(normed_mlp), gate_grad).astype(bf16)
             gate_grad, odd = tied(gate_grad, odd)
             got = swap_low(odd)
             even = mm_tn(rows_to_keep(normed_mlp), gate_grad).astype(bf16)
             even, up_grad = tied(even, up_grad)
-            up_grad, gate_sum, down[1] = tied(up_grad, add_low(even, got), down[1])
-            down = scatter_columns(jnp.concatenate(down, axis=0))
+            up_grad, gate_sum = tied(up_grad, add_low(even, got))
             first, second = send_far(gate_sum)
             gate_sum = receive_far(first)
             up_sum = mm_tn(normed_mlp, up_grad).astype(bf16)
@@ -737,76 +763,75 @@
         dk = own_rows(dk)
         dv = own_rows(dv)
         if not weights_too:
-            outgoing = [
-                heads_back(dq, dk, dv, wqkv, h, middle_grad, attn_row, i, 1)[0]
-                for i in range(blocks)
-            ]
-            return outgoing, extra
+            return (dq, dk, dv, middle_grad), extra
         dq, dk, dv, down, up_sum, second[0] = tied(dq, dk, dv, down, up_sum, second[0])
         up_sum = [up_sum, receive_far(second)]
         kv = jnp.concatenate(
             [unpadded(mm_tn(normed, dk).astype(bf16)), unpadded(mm_tn(normed, dv).astype(bf16))],
             axis=1,
         )
+        dq, kv = tied(dq, kv)
+        kv = add_partner(split_rows(kv), low_bits)
         query = unpadded(mm_tn(normed, dq).astype(bf16))
         dq, kv, query, up_sum[1] = tied(dq, kv, query, up_sum[1])
-        up_sum = scatter_columns(jnp.concatenate(up_sum, axis=0))
-        out = add_partner(out, high_bits)[0]
-        kv = add_partner(split_rows(kv), low_bits)
+        up_sum, dq = tied(jnp.concatenate(up_sum, axis=0), dq)
+        up_sum = scatter_columns(up_sum)
+        kv = add_partner(kv, high_bits)[0]
         query = add_partner(split_rows(query), low_bits)
         outgoing, attn_sum = heads_back(dq, dk, dv, wqkv, h, middle_grad, attn_row, 0, blocks)
-        outgoing, kv, query, out, gate_sum = tied(outgoing, kv, query, out, gate_sum)
-        kv = add_partner(kv, high_bits)[0]
+        outgoing, kv, query, gate_sum = tied(outgoing, kv, query, gate_sum)
+        out = add_partner(out, high_bits)[0]
         query = add_partner(query, high_bits)[0]
+        input_grads = to_places(outgoing)
+        kv = sum_over_tensor(kv)
         pair = jnp.concatenate(
             [out.reshape(share, tsize, -1), query.reshape(share, tsize, -1)], axis=2
         )
-        pair, up_sum = tied(pair, up_sum)
+        pair, up_sum, input_grads, kv, attn_sum = tied(pair, up_sum, input_grads, kv, attn_sum)
         pair = scatter_columns(pair)
         gains = jnp.concatenate([attn_sum, mlp_sum], axis=0)
         half_cols = pair.shape[1] // 2
         sums = [down, gate_sum, up_sum, pair[:, :half_cols], pair[:, half_cols:]]
-        return outgoing, sums + [sum_over_tensor(kv)], gains
-
-    def sum_over_tensor(array):
-        bits = bits_of(tsize)
-        for bit in bits:
-            side = (t & bit) != 0
-            size = array.shape[1] // 2
-            low, high = array[:, :size], array[:, size:]
-            got = swapped(jnp.where(side, low, high), "tensor", bit)
-            kept_half = jnp.where(side, high, low)
-            array = (kept_half.astype(f32) + got.astype(f32)).astype(bf16)
-        for bit in reversed(bits):
-            side = (t & bit) != 0
-            got = swapped(array, "tensor", bit)
-            array = jnp.concatenate(
-                [jnp.where(side, got, array), jnp.where(side, array, got)], axis=1
-            )
-        return array
-
-    def to_places(rows):
-        return exchange(reorder(rows, 1).reshape(micro, nloc, width))[None]
-
-    kept, _ = forward(rows_in)
-    far_down[-1], hidden = tied(far_down[-1], kept[-1])
+        return input_grads, sums + [kv], gains
+
+    def row_chunks():
+        if blocks < 2:
+            return [(0, blocks)]
+        return [(0, blocks // 2), (blocks // 2, blocks - blocks // 2)]
+
+    def send_chunks(make, by, source):
+        got = []
+        for first, count in row_chunks():
+            chunk, source = make(source, first, count)
+            if got:
+                chunk, got[-1] = tied(chunk, got[-1])
+            source, chunk = tied(source, chunk)
+            got.append(shifted(chunk, "section", by))
+        return jnp.concatenate(got, axis=0)
+
+    kept, _ = forward(rows_in, None, waits)
+    far_down[-1], hidden, late_cotangent = tied(far_down[-1], kept[-1], cotangent)
     middle = kept[5]
     wd = settle(far_down)
-    received = jnp.concatenate(
-        [
-            shifted(down_rows(hidden, middle, wd, i, 1), "section", 1)
-            for i in range(blocks)
-        ],
-        axis=0,
-    )
-    received, late_cotangent = tied(received, cotangent)
     half_cot = exchange_half(late_cotangent)
+    received = send_chunks(
+        lambda source, first, count: (down_rows(source, middle, wd, first, count), source),
+        1,
+        hidden,
+    )
+    received, half_cot = tied(received, half_cot)
     kept, cot = forward(jnp.where(first_section, rows_in, received), join_halves(half_cot))
     second_out = down_rows(kept[-1], kept[5], wd, 0, blocks)
-    first_grad, outputs = backward(cot, kept, False, to_places(second_out))
-    returned = jnp.concatenate([shifted(part, "section", -1) for part in first_grad], axis=0)
-    second_grad, sums, gains = backward(jnp.where(first_section, returned, cot), kept, True)
-    input_grads = to_places(second_grad)
+    (dq, dk, dv, middle_grad), outputs = backward(cot, kept, False, to_places(second_out))
+    returned = send_chunks(
+        lambda source, first, count: (
+            heads_back(source, dk, dv, wqkv, kept[0], middle_grad, attn_row, first, count)[0],
+            source,
+        ),
+        -1,
+        dq,
+    )
+    input_grads, sums, gains = backward(jnp.where(first_section, returned, cot), kept, True)
     down, gate, up, out, query, kv = sums
     gains = reorder(gains, 1)
     for axis, size in (("dp", dsize), ("tensor", tsize)):

time: 1580 us -> 1400 us (0.89)
  waiting for transfers between devices: 545 us -> 415 us
  starting transfers between devices: 89.4 us -> 62.9 us
  Pallas kernels: 511 us -> 487 us
    ppermute x68 -> x67, waiting for transfers between devices: 382 us -> 262 us  [swapped(): lax.ppermute(array, axis, [(i, i ^ bit) for i in range(lax.axis_size(axis...]
    ppermute x8 -> x4, waiting for transfers between devices: 127 us -> 74.4 us  [shifted(): return lax.ppermute(array, axis, pairs)]
    reduce_scatter x4, waiting for transfers between devices: 0.01 us -> 32.4 us  [scatter_columns(): return lax.psum_scatter(part, 'tensor', scatter_dimension=0)]
    ppermute x68 -> x67, starting transfers between devices: 75.3 us -> 51 us  [swapped(): lax.ppermute(array, axis, [(i, i ^ bit) for i in range(lax.axis_size(axis...]
    pallas_call x5 -> x3, Pallas kernels: 66.1 us -> 53.9 us  [heads_back(): kernel_call(heads_back_kernel, (count,), [rows_of((block, a.shape[1]), fi...]
    pallas_call x5 -> x3, Pallas kernels: 60.8 us -> 49 us  [down_rows(): kernel_call(down_kernel, (count,), [rows_of((block, hidden.shape[1]), fir...]
    unnamed x140 -> x116, local copies, waits for them, and re-layouts: 68.1 us -> 64.7 us
  transfers between devices with their start and end apart: 88 -> 83, of which waited for: 32 -> 28; matrix products, arithmetic and copies ran while one was open for 22% -> 25% of each run, Pallas kernels for 21% -> 25%
where the time goes in v6:
time: 1400 us
  Pallas kernels  487 us (35%)
  waiting for transfers between devices  415 us (30%)
  local copies, waits for them, and re-layouts  202 us (14%)
  matrix products  114 us (8%)
  other arithmetic  101 us (7%)
  starting transfers between devices  62.9 us (4%)
  between operations  15.6 us (1%)
    ppermute x67, waiting for transfers between devices, swapped(): lax.ppermute(array, axis, [(i, i ^ bit) for i in range(lax.axis_size(axis...  262 us
    pallas_call x2, Pallas kernels, feed_back(): kernel_call(feed_back_kernel, (total // block,), [whole(grad.shape), colu...  126 us
    dot_general x9, matrix products, mm_tn(): lax.dot_general(left, right, (((0,), (0,)), ((), ())), preferred_element_...  93.3 us
    pallas_call x2, Pallas kernels, attention_backward(): kernel_call(functools.partial(attend_backward_kernel, single=single), (KV...  74.9 us
    ppermute x4, waiting for transfers between devices, shifted(): return lax.ppermute(array, axis, pairs)  74.4 us
    unnamed x116, local copies, waits for them, and re-layouts  64.7 us
    pallas_call x2, Pallas kernels, gate_up(): kernel_call(gate_up_kernel, (total // block,), [whole(x.shape), columns_o...  63.8 us
    pallas_call x3, Pallas kernels, heads_back(): kernel_call(heads_back_kernel, (count,), [rows_of((block, a.shape[1]), fi...  53.9 us
  transfers between devices with their start and end apart: 83, of which 28 were waited for; matrix products, arithmetic and copies ran while one was open for 25% of the time, Pallas kernels for 25%

profile of v6, /device:TPU:0, one launch (start us, length us, event | category | flops | bytes accessed | tf_op | source)
XLA Modules:
  0.0 1397.6 jit_solution(3911802632104654214)
XLA Ops:
  27.1 30.4 %collective-permute-done = bf16[1,256,768]{2,1,0:T(8,128)(2,1)S(1)} collective-permute-done((bf16[1,256,768]{2,1,0:T(8,128)(2,1)S(1)}, bf16[1,256,768]{2,1,0:T(8,128)(2,1)S(1)}, u32[]{:S(2)}, u32[]{:S(2)}) %collective-permute-start) | collective-permute-done | bytes 393248 | tf_op jit(solution)/shard_map/ppermute | solution.py:28
  111.5 27.7 %all-gather.18.cloned.1.call-done = bf16[4,192,1024]{2,1,0:T(8,128)(2,1)} async-done(((bf16[1,192,1024]{2,1,0:T(8,128)(2,1)}), bf16[4,192,1024]{2,1,0:T(8,128)(2,1)}) %all-gather.18.cloned.1.call-update) | async-done | bytes 1572880 | tf_op jit(solution)/shard_map/all_gather | solution.py:612
  186.3 24.5 %project.2 = (bf16[1024,4096]{1,0:T(8,128)(2,1)}, bf16[1024,1536]{1,0:T(8,128)(2,1)}) custom-call(bf16[1024,1536]{1,0:T(8,128)(2,1)} %pad_maximum_fusion.4.h_ref, f32[1,1536]{1,0:T(1,128)} %broadcast_in_dim.68.gain_ref, bf16[1536,4096]{1,0:T(8,128)(2,1)} %pad_maximum_fusion.w_ref, f32[1024,128]{1,0:T(8,128)} %get-tuple-element.396.cos_ref.cosq_ref.cosk_ref, ...), custom_call_target="tpu_custom_call" | custom-call | flops 12884901888 | bytes 36700160 | tf_op jit(solution)/shard_map/project/pallas_call | solution.py:123
  225.4 21.9 %attend_forward.2 = (bf16[1024,2048]{1,0:T(8,128)(2,1)}, f32[8,4,1,512]{3,2,1,0:T(1,128)}) custom-call(s32[1]{0:T(128)} %bitcast.offset_ref, bf16[1024,4096]{1,0:T(8,128)(2,1)} %get-tuple-element.151.q_ref.k_ref.v_ref, bf16[1024,4096]{1,0:T(8,128)(2,1)} %get-tuple-element.151.q_ref.k_ref.v_ref, bf16[1024,4096]{1,0:T(8,128)(2,1)} %get-tuple-element.151.q_ref.k_ref.v_ref), custom_call_target="tpu_custom_call" | custom-call | flops 8589934592 | bytes 21004288 | tf_op jit(solution)/shard_map/attend_forward/pallas_call | solution.py:425
  274.5 13.1 join.2
  345.4 31.9 %gate_up.2 = (bf16[1024,4096]{1,0:T(8,128)(2,1)}, bf16[1024,4096]{1,0:T(8,128)(2,1)}, bf16[1024,4096]{1,0:T(8,128)(2,1)}) custom-call(bf16[1024,1536]{1,0:T(8,128)(2,1)} %get-tuple-element.156.x_ref, bf16[1536,4096]{1,0:T(8,128)(2,1)} %constant_dynamic-update-slice_fusion.wg_ref, bf16[1536,4096]{1,0:T(8,128)(2,1)} %constant_dynamic-update-slice_fusion.8.wu_ref), custom_call_target="tpu_custom_call" | custom-call | flops 25769803776 | bytes 75497472 | tf_op jit(solution)/shard_map/gate_up/pallas_call | solution.py:178
  391.5 14.3 %down_rows.3 = bf16[512,1536]{1,0:T(8,128)(2,1)} custom-call(bf16[1024,4096]{1,0:T(8,128)(2,1)} %get-tuple-element.164.hidden_ref, f32[1024,1536]{1,0:T(8,128)} %get-tuple-element.159.middle_ref, bf16[1536,4096]{1,0:T(8,128)(2,1)} %constant_dynamic-update-slice_fusion.16.w_ref.wd_ref), custom_call_target="tpu_custom_call" | custom-call | flops 6442450944 | bytes 14155776 | tf_op jit(solution)/shard_map/down_rows/pallas_call | solution.py:197
  409.5 14.1 %down_rows.4 = bf16[512,1536]{1,0:T(8,128)(2,1)} custom-call(bf16[1024,4096]{1,0:T(8,128)(2,1)} %get-tuple-element.164.hidden_ref, f32[1024,1536]{1,0:T(8,128)} %get-tuple-element.159.middle_ref, bf16[1536,4096]{1,0:T(8,128)(2,1)} %constant_dynamic-update-slice_fusion.16.w_ref.wd_ref), custom_call_target="tpu_custom_call" | custom-call | flops 6442450944 | bytes 14155776 | tf_op jit(solution)/shard_map/down_rows/pallas_call | solution.py:197
  423.6 20.0 %collective-permute-done.31 = bf16[512,1536]{1,0:T(8,128)(2,1)S(1)} collective-permute-done((bf16[512,1536]{1,0:T(8,128)(2,1)}, bf16[512,1536]{1,0:T(8,128)(2,1)S(1)}, u32[]{:S(2)}, u32[]{:S(2)}) %collective-permute-start.31) | collective-permute-done | bytes 1572896 | tf_op jit(solution)/shard_map/ppermute | solution.py:24
  465.5 13.5 collective-permute-done.34
  486.3 24.5 %project.3 = (bf16[1024,4096]{1,0:T(8,128)(2,1)}, bf16[1024,1536]{1,0:T(8,128)(2,1)}) custom-call(bf16[1024,1536]{1,0:T(8,128)(2,1)} %broadcast_select_fusion.h_ref, f32[1,1536]{1,0:T(1,128)} %broadcast_in_dim.68.gain_ref, bf16[1536,4096]{1,0:T(8,128)(2,1)} %pad_maximum_fusion.w_ref, f32[1024,128]{1,0:T(8,128)} %get-tuple-element.396.cos_ref.cosq_ref.cosk_ref, ...), custom_call_target="tpu_custom_call" | custom-call | flops 12884901888 | bytes 36700160 | tf_op jit(solution)/shard_map/project/pallas_call | solution.py:123
  510.8 21.7 %attend_forward.3 = (bf16[1024,2048]{1,0:T(8,128)(2,1)}, f32[8,4,1,512]{3,2,1,0:T(1,128)}) custom-call(s32[1]{0:T(128)} %bitcast.offset_ref, bf16[1024,4096]{1,0:T(8,128)(2,1)} %get-tuple-element.171.q_ref.k_ref.v_ref, bf16[1024,4096]{1,0:T(8,128)(2,1)} %get-tuple-element.171.q_ref.k_ref.v_ref, bf16[1024,4096]{1,0:T(8,128)(2,1)} %get-tuple-element.171.q_ref.k_ref.v_ref), custom_call_target="tpu_custom_call" | custom-call | flops 8589934592 | bytes 21004288 | tf_op jit(solution)/shard_map/attend_forward/pallas_call | solution.py:425
  535.2 13.1 join.3
  548.3 31.9 %gate_up.3 = (bf16[1024,4096]{1,0:T(8,128)(2,1)}, bf16[1024,4096]{1,0:T(8,128)(2,1)}, bf16[1024,4096]{1,0:T(8,128)(2,1)}) custom-call(bf16[1024,1536]{1,0:T(8,128)(2,1)} %get-tuple-element.176.x_ref, bf16[1536,4096]{1,0:T(8,128)(2,1)} %constant_dynamic-update-slice_fusion.wg_ref, bf16[1536,4096]{1,0:T(8,128)(2,1)} %constant_dynamic-update-slice_fusion.8.wu_ref), custom_call_target="tpu_custom_call" | custom-call | flops 25769803776 | bytes 75497472 | tf_op jit(solution)/shard_map/gate_up/pallas_call | solution.py:178
  580.1 20.6 %down_rows.5 = bf16[1024,1536]{1,0:T(8,128)(2,1)} custom-call(bf16[1024,4096]{1,0:T(8,128)(2,1)} %get-tuple-element.181.hidden_ref, f32[1024,1536]{1,0:T(8,128)} %get-tuple-element.179.middle_ref, bf16[1536,4096]{1,0:T(8,128)(2,1)} %constant_dynamic-update-slice_fusion.16.w_ref.wd_ref), custom_call_target="tpu_custom_call" | custom-call | flops 12884901888 | bytes 28311552 | tf_op jit(solution)/shard_map/down_rows/pallas_call | solution.py:197
  613.0 62.4 %feed_back.2 = (f32[1024,1536]{1,0:T(8,128)}, bf16[1024,1536]{1,0:T(8,128)(2,1)}, f32[1,1536]{1,0:T(1,128)}) custom-call(bf16[1024,1536]{1,0:T(8,128)(2,1)} %pad_maximum_fusion.7.grad_ref, bf16[1024,4096]{1,0:T(8,128)(2,1)} %get-tuple-element.177.gate_ref, bf16[1024,4096]{1,0:T(8,128)(2,1)} %get-tuple-element.178.up_ref, ...), custom_call_target="tpu_custom_call" | custom-call | flops 38654705664 | bytes 81792000 | tf_op jit(solution)/shard_map/feed_back/pallas_call | solution.py:267
  689.8 37.4 %attend_backward.2 = (bf16[1024,2048]{1,0:T(8,128)(2,1)}, bf16[1024,1024]{1,0:T(8,128)(2,1)}, bf16[1024,1024]{1,0:T(8,128)(2,1)}) custom-call(s32[1]{0:T(128)} %bitcast.offset_ref, bf16[1024,4096]{1,0:T(8,128)(2,1)} %get-tuple-element.171.q_ref.k_ref.v_ref, bf16[1024,4096]{1,0:T(8,128)(2,1)} %get-tuple-element.171.q_ref.k_ref.v_ref, ...), custom_call_target="tpu_custom_call" | custom-call | flops 21474836480 | bytes 50331648 | tf_op jit(solution)/shard_map/attend_backward/pallas_call | solution.py:452
  727.3 15.2 %heads_back.3 = (bf16[512,1536]{1,0:T(8,128)(2,1)}, f32[1,1536]{1,0:T(1,128)}) custom-call(bf16[1024,2048]{1,0:T(8,128)(2,1)} %get-tuple-element.190.dq_ref, bf16[1024,1024]{1,0:T(8,128)(2,1)} %get-tuple-element.186.dk_ref, bf16[1024,1024]{1,0:T(8,128)(2,1)} %get-tuple-element.187.dv_ref, bf16[1536,4096]{1,0:T(8,128)(2,1)} %pad_maximum_fusion.w_ref, ...), custom_call_target="tpu_custom_call" | custom-call | flops 6442450944 | bytes 14158848 | tf_op jit(solution)/shard_map/heads_back/pallas_call | solution.py:316
  744.0 15.6 %heads_back.4 = (bf16[512,1536]{1,0:T(8,128)(2,1)}, f32[1,1536]{1,0:T(1,128)}) custom-call(bf16[1024,2048]{1,0:T(8,128)(2,1)} %get-tuple-element.190.dq_ref, bf16[1024,1024]{1,0:T(8,128)(2,1)} %get-tuple-element.186.dk_ref, bf16[1024,1024]{1,0:T(8,128)(2,1)} %get-tuple-element.187.dv_ref, bf16[1536,4096]{1,0:T(8,128)(2,1)} %pad_maximum_fusion.w_ref, ...), custom_call_target="tpu_custom_call" | custom-call | flops 6442450944 | bytes 14158848 | tf_op jit(solution)/shard_map/heads_back/pallas_call | solution.py:316
  759.6 18.9 %collective-permute-done.40 = bf16[512,1536]{1,0:T(8,128)(2,1)S(1)} collective-permute-done((bf16[512,1536]{1,0:T(8,128)(2,1)}, bf16[512,1536]{1,0:T(8,128)(2,1)S(1)}, u32[]{:S(2)}, u32[]{:S(2)}) %collective-permute-start.40) | collective-permute-done | bytes 1572896 | tf_op jit(solution)/shard_map/ppermute | solution.py:24
  779.7 33.5 %collective-permute-done.41 = bf16[512,1536]{1,0:T(8,128)(2,1)S(1)} collective-permute-done((bf16[512,1536]{1,0:T(8,128)(2,1)}, bf16[512,1536]{1,0:T(8,128)(2,1)S(1)}, u32[]{:S(2)}, u32[]{:S(2)}) %collective-permute-start.41) | collective-permute-done | bytes 1572896 | tf_op jit(solution)/shard_map/ppermute | solution.py:24
  851.0 63.8 %feed_back.3 = (f32[1024,1536]{1,0:T(8,128)}, bf16[1024,1536]{1,0:T(8,128)(2,1)}, f32[1,1536]{1,0:T(1,128)}, bf16[1024,4096]{1,0:T(8,128)(2,1)}, bf16[1024,4096]{1,0:T(8,128)(2,1)}) custom-call(bf16[1024,1536]{1,0:T(8,128)(2,1)} %copy-done.3, bf16[1024,4096]{1,0:T(8,128)(2,1)} %get-tuple-element.177.gate_ref, bf16[1024,4096]{1,0:T(8,128)(2,1)} %get-tuple-element.178.up_ref, ...), custom_call_target="tpu_custom_call" | custom-call | flops 38654705664 | bytes 98569216 | tf_op jit(solution)/shard_map/feed_back/pallas_call | solution.py:267
  959.6 19.6 %convolution_convert_fusion = bf16[1536,4096]{1,0:T(8,128)(2,1)} fusion(bf16[1024,1536]{1,0:T(8,128)(2,1)S(1)} %copy-done.11, bf16[1024,4096]{1,0:T(8,128)(2,1)} %get-tuple-element.212), kind=kOutput, calls=%fused_computation | convolution fusion | flops 12891193344 | bytes 24117248 | tf_op jit(solution)/shard_map/dot_general | solution.py:46
  979.3 15.4 %collective-permute-done.45 = bf16[192,4096]{1,0:T(8,128)(2,1)S(1)} collective-permute-done((bf16[192,4096]{1,0:T(8,128)(2,1)S(1)}, bf16[192,4096]{1,0:T(8,128)(2,1)S(1)}, u32[]{:S(2)}, u32[]{:S(2)}) %collective-permute-start.45) | collective-permute-done | bytes 1572896 | tf_op jit(solution)/shard_map/ppermute | solution.py:28
  1054.4 37.4 %attend_backward.3 = (bf16[1024,2048]{1,0:T(8,128)(2,1)}, bf16[1024,1024]{1,0:T(8,128)(2,1)}, bf16[1024,1024]{1,0:T(8,128)(2,1)}) custom-call(s32[1]{0:T(128)} %bitcast.offset_ref, bf16[1024,4096]{1,0:T(8,128)(2,1)} %get-tuple-element.171.q_ref.k_ref.v_ref, bf16[1024,4096]{1,0:T(8,128)(2,1)} %get-tuple-element.171.q_ref.k_ref.v_ref, ...), custom_call_target="tpu_custom_call" | custom-call | flops 21474836480 | bytes 50331648 | tf_op jit(solution)/shard_map/attend_backward/pallas_call | solution.py:452
  1143.2 23.2 %heads_back.5 = (bf16[1024,1536]{1,0:T(8,128)(2,1)}, f32[1,1536]{1,0:T(1,128)}) custom-call(bf16[1024,2048]{1,0:T(8,128)(2,1)} %get-tuple-element.239.dq_ref, bf16[1024,1024]{1,0:T(8,128)(2,1)} %get-tuple-element.232.dk_ref, bf16[1024,1024]{1,0:T(8,128)(2,1)} %get-tuple-element.233.dv_ref, bf16[1536,4096]{1,0:T(8,128)(2,1)} %pad_maximum_fusion.w_ref, ...), custom_call_target="tpu_custom_call" | custom-call | flops 12884901888 | bytes 28314624 | tf_op jit(solution)/shard_map/heads_back/pallas_call | solution.py:316
  1190.7 43.3 %collective-permute-done.63 = bf16[384,768]{0,1:T(8,128)(2,1)} collective-permute-done((bf16[384,768]{0,1:T(8,128)(2,1)}, bf16[384,768]{0,1:T(8,128)(2,1)}, u32[]{:S(2)}, u32[]{:S(2)}) %collective-permute-start.63) | collective-permute-done | bytes 589856 | tf_op jit(solution)/shard_map/ppermute | solution.py:28
  1235.5 37.4 %collective-permute-done.60 = bf16[1,256,1536]{2,1,0:T(8,128)(2,1)} collective-permute-done((bf16[1,256,1536]{2,1,0:T(8,128)(2,1)}, bf16[1,256,1536]{2,1,0:T(8,128)(2,1)}, u32[]{:S(2)}, u32[]{:S(2)}) %collective-permute-start.60) | collective-permute-done | bytes 786464 | tf_op jit(solution)/shard_map/ppermute | solution.py:28
  1276.0 30.3 %collective-permute-done.64 = bf16[384,384]{0,1:T(8,128)(2,1)S(1)} collective-permute-done((bf16[384,384]{0,1:T(8,128)(2,1)S(1)}, bf16[384,384]{0,1:T(8,128)(2,1)S(1)}, u32[]{:S(2)}, u32[]{:S(2)}) %collective-permute-start.64) | collective-permute-done | bytes 294944 | tf_op jit(solution)/shard_map/ppermute | solution.py:28
  1307.4 13.4 collective-permute-done.65
  1324.7 12.7 collective-permute-done.66
  1355.1 32.4 %reduce-scatter.11.cloned.1.call-done = bf16[1,384,768]{2,1,0:T(8,128)(2,1)} async-done(((bf16[4,384,768]{2,1,0:T(8,128)(2,1)}), bf16[1,384,768]{2,1,0:T(8,128)(2,1)}) %reduce-scatter.11.cloned.1.call-update) | async-done | bytes 589840 | tf_op jit(solution)/shard_map/reduce_scatter | solution.py:598
  (424 shorter events, 546.8 us)
Async XLA Ops:
  7.2 65.6 %all-gather.20.cloned.1.call-start = ((), (), s32[]{:S(2)}) async-start(), calls=%async_computation.8 | async-start | bytes 1474560 | tf_op jit(solution)/shard_map/all_gather | solution.py:612
  7.9 92.9 %all-gather.26.cloned.1.call-start = ((), (), s32[]{:S(2)}) async-start(), calls=%async_computation.15 | async-start | bytes 1474560 | tf_op jit(solution)/shard_map/all_gather | solution.py:612
  9.8 129.4 %all-gather.18.cloned.1.call-start = ((), (), s32[]{:S(2)}) async-start(), calls=%async_computation.7 | async-start | bytes 1966080 | tf_op jit(solution)/shard_map/all_gather | solution.py:612
  12.0 170.3 %all-gather.16.cloned.1.call-start = ((), (), s32[]{:S(2)}) async-start(), calls=%async_computation.6 | async-start | bytes 1966080 | tf_op jit(solution)/shard_map/all_gather | solution.py:612
  12.5 203.7 %all-gather.14.cloned.1.call-start = ((), (), s32[]{:S(2)}) async-start(), calls=%async_computation.5 | async-start | bytes 1966080 | tf_op jit(solution)/shard_map/all_gather | solution.py:612
  13.6 247.4 %all-gather.12.cloned.1.call-start = ((), (), s32[]{:S(2)}) async-start(), calls=%async_computation.4 | async-start | bytes 1966080 | tf_op jit(solution)/shard_map/all_gather | solution.py:612
  14.1 276.0 %all-gather.24.cloned.1.call-start = ((), (), s32[]{:S(2)}) async-start(), calls=%async_computation.14 | async-start | bytes 1966080 | tf_op jit(solution)/shard_map/all_gather | solution.py:612
  15.5 312.2 %all-gather.22.cloned.1.call-start = ((), (), s32[]{:S(2)}) async-start(), calls=%async_computation.13 | async-start | bytes 1966080 | tf_op jit(solution)/shard_map/all_gather | solution.py:612
  16.3 52.4 %collective-permute-start.3 = (bf16[384,1536]{0,1:T(8,128)(2,1)S(1)}, bf16[384,1536]{0,1:T(8,128)(2,1)}, u32[]{:S(2)}, u32[]{:S(2)}) collective-permute-start(bf16[384,1536]{0,1:T(8,128)(2,1)S(1)} %pad_maximum_fusion.14), channel_id=1, source_target_pairs={{0,8},{4,12},{8,0},{12,4},{1,9},{5,13},{9,1},{13,5},{2,10},{6,14},... | collective-permute-start | bytes 3538952 | tf_op jit(solution)/shard_map/ppermute | solution.py:28
  69.3 1025.6 %reduce-scatter.5.cloned.1.call-start = ((), (), s32[]{:S(2)}) async-start(), calls=%async_computation.9 | async-start | bytes 3932160 | tf_op jit(solution)/shard_map/reduce_scatter | solution.py:598
  80.1 63.3 %collective-permute-start.13 = (bf16[384,1536]{0,1:T(8,128)(2,1)}, bf16[384,1536]{0,1:T(8,128)(2,1)}, u32[]{:S(2)}, u32[]{:S(2)}) collective-permute-start(bf16[384,1536]{0,1:T(8,128)(2,1)} %bitcast.13), channel_id=1, source_target_pairs={{0,4},{4,0},{8,12},{12,8},{1,5},{5,1},{9,13},{13,9},{2,6},{6,2},{1... | collective-permute-start | bytes 3538952 | tf_op jit(solution)/shard_map/ppermute | solution.py:28
  111.0 57.3 %collective-permute-start.17 = (bf16[384,1536]{0,1:T(8,128)(2,1)}, bf16[384,1536]{0,1:T(8,128)(2,1)}, u32[]{:S(2)}, u32[]{:S(2)}) collective-permute-start(bf16[384,1536]{0,1:T(8,128)(2,1)} %bitcast.16), channel_id=1, source_target_pairs={{0,4},{4,0},{8,12},{12,8},{1,5},{5,1},{9,13},{13,9},{2,6},{6,2},{1... | collective-permute-start | bytes 3538952 | tf_op jit(solution)/shard_map/ppermute | solution.py:28
  185.6 64.4 %collective-permute-start.20 = (bf16[192,4096]{1,0:T(8,128)(2,1)}, bf16[192,4096]{1,0:T(8,128)(2,1)}, u32[]{:S(2)}, u32[]{:S(2)}) collective-permute-start(bf16[192,4096]{1,0:T(8,128)(2,1)} %bitcast.91), channel_id=1, source_target_pairs={{0,4},{4,0},{8,12},{12,8},{1,5},{5,1},{9,13},{13,9},{2,6},{6,2},{1... | collective-permute-start | bytes 4718600 | tf_op jit(solution)/shard_map/ppermute | solution.py:28
  185.7 61.5 %collective-permute-start.19 = (bf16[192,4096]{1,0:T(8,128)(2,1)}, bf16[192,4096]{1,0:T(8,128)(2,1)}, u32[]{:S(2)}, u32[]{:S(2)}) collective-permute-start(bf16[192,4096]{1,0:T(8,128)(2,1)} %bitcast.89), channel_id=1, source_target_pairs={{0,4},{4,0},{8,12},{12,8},{1,5},{5,1},{9,13},{13,9},{2,6},{6,2},{1... | collective-permute-start | bytes 4718600 | tf_op jit(solution)/shard_map/ppermute | solution.py:28
  186.1 72.1 %collective-permute-start.21 = (bf16[192,4096]{1,0:T(8,128)(2,1)}, bf16[192,4096]{1,0:T(8,128)(2,1)}, u32[]{:S(2)}, u32[]{:S(2)}) collective-permute-start(bf16[192,4096]{1,0:T(8,128)(2,1)} %collective-permute-done.7), channel_id=1, source_target_pairs={{0,4},{4,0},{8,12},{12,8},{1,5},{5,1},{9,13},{13,9},{2,6},{6,2},{1... | collective-permute-start | bytes 4718600 | tf_op jit(solution)/shard_map/ppermute | solution.py:28
  481.4 51.1 %collective-permute-start.36 = (bf16[4,256,768]{2,1,0:T(8,128)(2,1)S(1)}, bf16[4,256,768]{2,1,0:T(8,128)(2,1)S(1)}, u32[]{:S(2)}, u32[]{:S(2)}) collective-permute-start(bf16[4,256,768]{2,1,0:T(8,128)(2,1)S(1)} %constant_dynamic-update-slice_fusion.24), channel_id=1, source_target_pairs={{0,16},{16,0},{1,17},{17,1},{2,18},{18,2},{3,19},{19,3},{4,20},{20... | collective-permute-start | bytes 4718600 | tf_op jit(solution)/shard_map/ppermute | solution.py:28
  608.4 77.5 %collective-permute-start.37 = (bf16[1,256,1536]{2,1,0:T(8,128)(2,1)}, bf16[1,256,1536]{2,1,0:T(8,128)(2,1)}, u32[]{:S(2)}, u32[]{:S(2)}) collective-permute-start(bf16[1,256,1536]{2,1,0:T(8,128)(2,1)} %get-tuple-element.345), channel_id=1, source_target_pairs={{0,1},{1,0},{2,3},{3,2},{4,5},{5,4},{6,7},{7,6},{8,9},{9,8},{10,11... | collective-permute-start | bytes 2359304 | tf_op jit(solution)/shard_map/ppermute | solution.py:28
  610.7 77.3 %collective-permute-start.38 = (bf16[1,256,1536]{2,1,0:T(8,128)(2,1)}, bf16[1,256,1536]{2,1,0:T(8,128)(2,1)S(1)}, u32[]{:S(2)}, u32[]{:S(2)}) collective-permute-start(bf16[1,256,1536]{2,1,0:T(8,128)(2,1)} %get-tuple-element.344), channel_id=1, source_target_pairs={{0,2},{1,3},{2,0},{3,1},{4,6},{5,7},{6,4},{7,5},{8,10},{9,11},{10,... | collective-permute-start | bytes 2359304 | tf_op jit(solution)/shard_map/ppermute | solution.py:28
  611.2 77.7 %collective-permute-start.39 = (bf16[1,256,1536]{2,1,0:T(8,128)(2,1)}, bf16[1,256,1536]{2,1,0:T(8,128)(2,1)S(1)}, u32[]{:S(2)}, u32[]{:S(2)}) collective-permute-start(bf16[1,256,1536]{2,1,0:T(8,128)(2,1)} %get-tuple-element.343), channel_id=1, source_target_pairs={{0,3},{1,2},{2,1},{3,0},{4,7},{5,6},{6,5},{7,4},{8,11},{9,10},{10,... | collective-permute-start | bytes 2359304 | tf_op jit(solution)/shard_map/ppermute | solution.py:28
  850.2 69.2 %collective-permute-start.43 = (bf16[384,4096]{1,0:T(8,128)(2,1)}, bf16[384,4096]{1,0:T(8,128)(2,1)}, u32[]{:S(2)}, u32[]{:S(2)}) collective-permute-start(bf16[384,4096]{1,0:T(8,128)(2,1)} %get-tuple-element.205), channel_id=1, source_target_pairs={{0,8},{4,12},{8,0},{12,4},{1,9},{5,13},{9,1},{13,5},{2,10},{6,14},... | collective-permute-start | bytes 9437192 | tf_op jit(solution)/shard_map/ppermute | solution.py:28
  948.9 225.2 %reduce-scatter.7.cloned.1.call-start = ((), (), s32[]{:S(2)}) async-start(), calls=%async_computation.10 | async-start | bytes 3932160 | tf_op jit(solution)/shard_map/reduce_scatter | solution.py:598
  958.2 78.3 %collective-permute-start.46 = (bf16[192,4096]{1,0:T(8,128)(2,1)S(1)}, bf16[192,4096]{1,0:T(8,128)(2,1)}, u32[]{:S(2)}, u32[]{:S(2)}) collective-permute-start(bf16[192,4096]{1,0:T(8,128)(2,1)S(1)} %get-tuple-element.333), channel_id=1, source_target_pairs={{0,8},{4,12},{8,0},{12,4},{1,9},{5,13},{9,1},{13,5},{2,10},{6,14},... | collective-permute-start | bytes 4718600 | tf_op jit(solution)/shard_map/ppermute | solution.py:28
  1052.3 80.4 %collective-permute-start.55 = (bf16[192,4096]{1,0:T(8,128)(2,1)}, bf16[192,4096]{1,0:T(8,128)(2,1)}, u32[]{:S(2)}, u32[]{:S(2)}) collective-permute-start(bf16[192,4096]{1,0:T(8,128)(2,1)} %get-tuple-element.331), channel_id=1, source_target_pairs={{0,8},{4,12},{8,0},{12,4},{1,9},{5,13},{9,1},{13,5},{2,10},{6,14},... | collective-permute-start | bytes 4718600 | tf_op jit(solution)/shard_map/ppermute | solution.py:28
  1053.7 130.7 %collective-permute-start.51 = (bf16[384,1536]{0,1:T(8,128)(2,1)}, bf16[384,1536]{0,1:T(8,128)(2,1)}, u32[]{:S(2)}, u32[]{:S(2)}) collective-permute-start(bf16[384,1536]{0,1:T(8,128)(2,1)} %get-tuple-element.221), channel_id=1, source_target_pairs={{0,8},{4,12},{8,0},{12,4},{1,9},{5,13},{9,1},{13,5},{2,10},{6,14},... | collective-permute-start | bytes 3538952 | tf_op jit(solution)/shard_map/ppermute | solution.py:28
  1054.3 284.5 %reduce-scatter.9.cloned.1.call-start = ((), (), s32[]{:S(2)}) async-start(), calls=%async_computation.11 | async-start | bytes 3932160 | tf_op jit(solution)/shard_map/reduce_scatter | solution.py:598
  1168.5 218.9 %reduce-scatter.11.cloned.1.call-start = ((), (), s32[]{:S(2)}) async-start(), calls=%async_computation.12 | async-start | bytes 2949120 | tf_op jit(solution)/shard_map/reduce_scatter | solution.py:598
  1175.0 59.1 %collective-permute-start.63 = (bf16[384,768]{0,1:T(8,128)(2,1)}, bf16[384,768]{0,1:T(8,128)(2,1)}, u32[]{:S(2)}, u32[]{:S(2)}) collective-permute-start(bf16[384,768]{0,1:T(8,128)(2,1)} %broadcast_select_fusion.7), channel_id=1, source_target_pairs={{0,1},{1,0},{2,3},{3,2},{4,5},{5,4},{6,7},{7,6},{8,9},{9,8},{10,11... | collective-permute-start | bytes 1769480 | tf_op jit(solution)/shard_map/ppermute | solution.py:28
  1182.4 90.5 %collective-permute-start.60 = (bf16[1,256,1536]{2,1,0:T(8,128)(2,1)}, bf16[1,256,1536]{2,1,0:T(8,128)(2,1)}, u32[]{:S(2)}, u32[]{:S(2)}) collective-permute-start(bf16[1,256,1536]{2,1,0:T(8,128)(2,1)} %get-tuple-element.326), channel_id=1, source_target_pairs={{0,1},{1,0},{2,3},{3,2},{4,5},{5,4},{6,7},{7,6},{8,9},{9,8},{10,11... | collective-permute-start | bytes 2359304 | tf_op jit(solution)/shard_map/ppermute | solution.py:28
  1187.5 87.6 %collective-permute-start.61 = (bf16[1,256,1536]{2,1,0:T(8,128)(2,1)}, bf16[1,256,1536]{2,1,0:T(8,128)(2,1)S(1)}, u32[]{:S(2)}, u32[]{:S(2)}) collective-permute-start(bf16[1,256,1536]{2,1,0:T(8,128)(2,1)} %get-tuple-element.325), channel_id=1, source_target_pairs={{0,2},{1,3},{2,0},{3,1},{4,6},{5,7},{6,4},{7,5},{8,10},{9,11},{10,... | collective-permute-start | bytes 2359304 | tf_op jit(solution)/shard_map/ppermute | solution.py:28
  1187.9 118.5 %collective-permute-start.62 = (bf16[1,256,1536]{2,1,0:T(8,128)(2,1)}, bf16[1,256,1536]{2,1,0:T(8,128)(2,1)S(1)}, u32[]{:S(2)}, u32[]{:S(2)}) collective-permute-start(bf16[1,256,1536]{2,1,0:T(8,128)(2,1)} %get-tuple-element.324), channel_id=1, source_target_pairs={{0,3},{1,2},{2,1},{3,0},{4,7},{5,6},{6,5},{7,4},{8,11},{9,10},{10,... | collective-permute-start | bytes 2359304 | tf_op jit(solution)/shard_map/ppermute | solution.py:28
  1189.9 132.0 %collective-permute-start.59 = (bf16[384,1536]{0,1:T(8,128)(2,1)}, bf16[384,1536]{0,1:T(8,128)(2,1)S(1)}, u32[]{:S(2)}, u32[]{:S(2)}) collective-permute-start(bf16[384,1536]{0,1:T(8,128)(2,1)} %get-tuple-element.248), channel_id=1, source_target_pairs={{0,8},{4,12},{8,0},{12,4},{1,9},{5,13},{9,1},{13,5},{2,10},{6,14},... | collective-permute-start | bytes 3538952 | tf_op jit(solution)/shard_map/ppermute | solution.py:28
  1235.3 70.9 %collective-permute-start.64 = (bf16[384,384]{0,1:T(8,128)(2,1)S(1)}, bf16[384,384]{0,1:T(8,128)(2,1)S(1)}, u32[]{:S(2)}, u32[]{:S(2)}) collective-permute-start(bf16[384,384]{0,1:T(8,128)(2,1)S(1)} %broadcast_select_fusion.10), channel_id=1, source_target_pairs={{0,2},{1,3},{2,0},{3,1},{4,6},{5,7},{6,4},{7,5},{8,10},{9,11},{10,... | collective-permute-start | bytes 884744 | tf_op jit(solution)/shard_map/ppermute | solution.py:28
  (95 other events, 2064.0 us)
Sparse Core Ops, SparseCore 0:
  9.6 59.8 all-gather.19
  71.7 29.1 all-gather.25
  103.0 36.1 all-gather.17
  141.2 35.9 all-gather.15
  179.2 35.9 all-gather.13
  216.6 35.9 all-gather.11
  254.2 35.9 all-gather.23
  291.7 35.9 all-gather.21
  949.0 58.5 reduce-scatter.4
  1054.5 58.6 reduce-scatter.6
  1168.6 105.3 reduce-scatter.8
  1339.0 48.4 reduce-scatter.10

commit v7 on v6

--- a/solution.py
+++ b/solution.py
@@ -49,6 +49,7 @@
 
 
 QB = 256
+ROWS = 512
 HP = 128
 LOG2E = 1.4426950408889634
 MIB = 2**20
@@ -143,7 +144,7 @@
 
 def join(mixed, h, w, gain):
     n, width = h.shape
-    block = min(QB, n)
+    block = min(ROWS, n)
     out_shape = (
         jax.ShapeDtypeStruct((n, width), f32),
         jax.ShapeDtypeStruct((n, width), bf16),
@@ -193,7 +194,7 @@
 
 def down_rows(hidden, middle, w, first, count):
     n, width = middle.shape
-    block = min(QB, n)
+    block = min(ROWS, n)
     return kernel_call(
         down_kernel,
         (count,),
@@ -208,20 +209,101 @@
     )(hidden, middle, w)[0]
 
 
-def feed_back_kernel(
-    grad_ref, gate_ref, up_ref, wd_ref, wg_ref, wu_ref, middle_ref, gain_ref,
-    total_ref, low_ref, sum_ref, *grad_refs
-):
-    step = pl.program_id(0)
+def hidden_back(grad_ref, gate_ref, up_ref, wd_ref):
     gate = gate_ref[...].astype(f32)
     hidden_grad = mm(grad_ref[...], wd_ref[...])
     sigma = jax.nn.sigmoid(gate)
     gate_grad = hidden_grad * up_ref[...].astype(f32) * (sigma * (1.0 + gate * (1.0 - sigma)))
-    gate_grad = gate_grad.astype(bf16)
-    up_grad = (hidden_grad * gate * sigma).astype(bf16)
-    for ref, value in zip(grad_refs, (gate_grad, up_grad)):
-        ref[...] = value
-    part = mm_nt(gate_grad, wg_ref[...]) + mm_nt(up_grad, wu_ref[...])
+    return gate_grad.astype(bf16), (hidden_grad * gate * sigma).astype(bf16)
+
+
+def feed_back_kernel(
+    grad_ref, gate_ref, up_ref, wd_ref, wg_ref, wu_ref, middle_ref, gain_ref,
+    total_ref, low_ref, sum_ref
+):
+    step = pl.program_id(0)
+    gate_grad, up_grad = hidden_back(grad_ref, gate_ref, up_ref, wd_ref)
+    accumulate_back(step, gate_grad, up_grad, wg_ref, wu_ref, total_ref)
+    finish_back(step, grad_ref, middle_ref, gain_ref, total_ref, low_ref, sum_ref)
+
+
+def feed_grads_kernel(
+    grad_ref, gate_ref, up_ref, wd_ref, normed_ref,
+    gate_grad_ref, up_grad_ref, gate_sum_ref, up_sum_ref, turned_ref
+):
+    @pl.when(pl.program_id(0) == 0)
+    def _():
+        turned_ref[...] = normed_ref[...].T
+
+    gate_grad, up_grad = hidden_back(grad_ref, gate_ref, up_ref, wd_ref)
+    gate_grad_ref[...] = gate_grad
+    up_grad_ref[...] = up_grad
+    gate_sum_ref[...] = mm(turned_ref[...], gate_grad).astype(bf16)
+    up_sum_ref[...] = mm(turned_ref[...], up_grad).astype(bf16)
+
+
+def feed_grads(grad, gate, upward, wd, normed):
+    n, width = grad.shape
+    total = gate.shape[1]
+    block = 512
+    return kernel_call(
+        feed_grads_kernel,
+        (total // block,),
+        [
+            whole(grad.shape), columns_of((n, block)), columns_of((n, block)),
+            columns_of((width, block)), whole(normed.shape),
+        ],
+        [columns_of((n, block))] * 2 + [columns_of((width, block))] * 2,
+        (jax.ShapeDtypeStruct((n, total), bf16),) * 2
+        + (jax.ShapeDtypeStruct((width, total), bf16),) * 2,
+        6 * n * width * total,
+        "feed_grads",
+        scratch=[pltpu.VMEM((width, n), bf16)],
+        trans=n * total,
+    )(grad, gate, upward, wd, normed)
+
+
+def rows_back_kernel(
+    gate_grad_ref, up_grad_ref, wg_ref, wu_ref, grad_ref, middle_ref, gain_ref,
+    total_ref, low_ref, sum_ref
+):
+    step = pl.program_id(0)
+    accumulate_back(step, gate_grad_ref[...], up_grad_ref[...], wg_ref, wu_ref, total_ref)
+    finish_back(step, grad_ref, middle_ref, gain_ref, total_ref, low_ref, sum_ref)
+
+
+def back_outputs(n, width):
+    return (
+        jax.ShapeDtypeStruct((n, width), f32),
+        jax.ShapeDtypeStruct((n, width), bf16),
+        jax.ShapeDtypeStruct((1, width), f32),
+    )
+
+
+def rows_back(gate_grad, up_grad, wg, wu, grad, middle, gain):
+    n, width = grad.shape
+    total = wg.shape[1]
+    block = 512
+    return kernel_call(
+        rows_back_kernel,
+        (total // block,),
+        [
+            columns_of((n, block)), columns_of((n, block)),
+            columns_of((width, block)), columns_of((width, block)),
+            whole(grad.shape), whole(middle.shape), whole(gain.shape),
+        ],
+        [whole((n, width)), whole((n, width)), whole((1, width))],
+        back_outputs(n, width),
+        4 * n * width * total,
+        "rows_back",
+    )(gate_grad, up_grad, wg, wu, grad, middle, gain)
+
+
+def accumulate_back(step, gate_grad, up_grad, wg_ref, wu_ref, total_ref):
+    part = mm_nt(
+        jnp.concatenate([gate_grad, up_grad], axis=1),
+        jnp.concatenate([wg_ref[...], wu_ref[...]], axis=1),
+    )
 
     @pl.when(step == 0)
     def _():
@@ -231,6 +313,8 @@
     def _():
         total_ref[...] += part
 
+
+def finish_back(step, grad_ref, middle_ref, gain_ref, total_ref, low_ref, sum_ref):
     @pl.when(step == pl.num_programs(0) - 1)
     def _():
         n = total_ref.shape[0]
@@ -251,19 +335,10 @@
         sum_ref[...] = sums
 
 
-def feed_back(grad, gate, upward, wd, wg, wu, middle, gain, with_grads):
+def feed_back(grad, gate, upward, wd, wg, wu, middle, gain):
     n, width = grad.shape
     total = wg.shape[1]
     block = 512
-    out_shape = (
-        jax.ShapeDtypeStruct((n, width), f32),
-        jax.ShapeDtypeStruct((n, width), bf16),
-        jax.ShapeDtypeStruct((1, width), f32),
-    )
-    out_specs = [whole((n, width)), whole((n, width)), whole((1, width))]
-    if with_grads:
-        out_shape += (jax.ShapeDtypeStruct((n, total), bf16),) * 2
-        out_specs += [columns_of((n, block))] * 2
     return kernel_call(
         feed_back_kernel,
         (total // block,),
@@ -272,8 +347,8 @@
             columns_of((width, block)), columns_of((width, block)), columns_of((width, block)),
             whole(middle.shape), whole(gain.shape),
         ],
-        out_specs,
-        out_shape,
+        [whole((n, width)), whole((n, width)), whole((1, width))],
+        back_outputs(n, width),
         6 * n * width * total,
         "feed_back",
         trans=n * total,
@@ -308,7 +383,7 @@
 
 def heads_back(dq, dk, dv, w, h, grad, gain, first, count):
     n, width = h.shape
-    block = min(QB, n)
+    block = min(ROWS, n)
     out_shape = (
         jax.ShapeDtypeStruct((count * block, width), bf16),
         jax.ShapeDtypeStruct((1, width), f32),
@@ -599,11 +674,8 @@
 
     attn_scale = reorder(attn_gain[0], 0)
     mlp_scale = reorder(mlp_gain[0], 0)
-    mine = exchange_half(inputs)
     last = spread_far(jnp.concatenate([w_key[0], w_value[0]], axis=1))
-    mine, last = tied(mine, last)
     wkv = spread_near(last)
-    rows_in = join_halves(mine)
 
     def spread_weight(shard, pieces, last):
         rows = share // pieces
@@ -628,11 +700,13 @@
     wqkv = jnp.concatenate([padded(settle(fars)), padded(wkv)], axis=1)
     fars, last = spread_weight(w_out[0].T, 1, last)
     wo = padded(settle(fars))
+    late_inputs, last = tied(inputs, last)
+    rows_in = join_halves(exchange_half(late_inputs))
     fars, last = spread_weight(w_gate[0], 2, last)
-    waits = list(fars)
+    waits = [fars[1]]
     wg = settle(fars)
     fars, last = spread_weight(w_up[0], 2, last)
-    waits.append(fars[0])
+    waits += fars
     wu = settle(fars)
     far_down, last = spread_weight(w_down[0].T, 2, last)
 
@@ -660,7 +734,7 @@
         key_tables = (key_tables[0], -key_tables[1])
     q_lanes = HEADS * HP
     k_lanes = KV_HEADS * HP
-    blocks = n // min(QB, n)
+    blocks = n // min(ROWS, n)
     attn_row = attn_scale[None]
     mlp_row = mlp_scale[None]
 
@@ -716,74 +790,69 @@
     def to_places(rows):
         return exchange(reorder(rows, 1).reshape(micro, nloc, width))[None]
 
-    def backward(grad, kept, weights_too, extra=None):
+    def backward(grad, kept, extra):
         h, normed, heads, lse, mixed, middle, normed_mlp, gate, upward, hidden = kept
-        if weights_too:
-            odd, even = rows_to_send(grad), rows_to_keep(grad)
-            odd = mm_tn(odd, hidden).astype(bf16)
-            even, odd = tied(even, odd)
-            got = swap_low(odd)
-            even = mm_tn(even, hidden).astype(bf16)
-            even, grad = tied(even, grad)
-            grad, down = tied(grad, add_low(even, got))
-            down = add_partner(down, high_bits)[0]
-        middle_grad, middle_bf, mlp_sum, *grads = feed_back(
-            grad, gate, upward, wd, wg, wu, middle, mlp_row, weights_too
-        )
-        if weights_too:
-            gate_grad, up_grad = grads
-            gate_grad, up_grad, down = tied(gate_grad, up_grad, down)
-            down = scatter_columns(down)
-            odd = mm_tn(rows_to_send(normed_mlp), gate_grad).astype(bf16)
-            gate_grad, odd = tied(gate_grad, odd)
-            got = swap_low(odd)
-            even = mm_tn(rows_to_keep(normed_mlp), gate_grad).astype(bf16)
-            even, up_grad = tied(even, up_grad)
-            up_grad, gate_sum = tied(up_grad, add_low(even, got))
-            first, second = send_far(gate_sum)
-            gate_sum = receive_far(first)
-            up_sum = mm_tn(normed_mlp, up_grad).astype(bf16)
-            middle_bf, up_sum, gate_sum, second[0] = tied(middle_bf, up_sum, gate_sum, second[0])
-            gate_sum = [gate_sum, receive_far(second)]
-            up_sum = add_partner(split_rows(up_sum), low_bits)
-            out = unpadded(mm_tn(middle_bf, mixed).astype(bf16))
-            middle_bf, out = tied(middle_bf, out)
-            out = add_partner(split_rows(out), low_bits)
+        middle_grad, middle_bf, _ = feed_back(grad, gate, upward, wd, wg, wu, middle, mlp_row)
         mixed_grad = mm(middle_bf, wo).astype(bf16)
-        if extra is not None:
-            mixed_grad, extra = tied(mixed_grad, extra)
-        if weights_too:
-            mixed_grad, gate_sum[1], up_sum, out = tied(mixed_grad, gate_sum[1], up_sum, out)
-            gate_sum = scatter_columns(jnp.concatenate(gate_sum, axis=0))
-            first, second = send_far(up_sum)
-            up_sum = receive_far(first)
+        mixed_grad, extra = tied(mixed_grad, extra)
         dq, dk, dv = attention_backward(
             *heads, mixed_grad, lse, back_tables, key_tables, offset, single
         )
+        return dq, own_rows(dk), own_rows(dv), middle_grad, extra
+
+    def backward_all(grad, kept):
+        h, normed, heads, lse, mixed, middle, normed_mlp, gate, upward, hidden = kept
+        odd, even = rows_to_send(grad), rows_to_keep(grad)
+        odd = mm_tn(odd, hidden).astype(bf16)
+        even, odd = tied(even, odd)
+        got = swap_low(odd)
+        even = mm_tn(even, hidden).astype(bf16)
+        even, grad = tied(even, grad)
+        grad, down = tied(grad, add_low(even, got))
+        down = add_partner(down, high_bits)[0]
+        gate_grad, up_grad, gate_sum, up_sum = feed_grads(grad, gate, upward, wd, normed_mlp)
+        gate_sum = add_partner(split_rows(gate_sum), low_bits)
+        gate_grad, up_grad, gate_sum, down = tied(gate_grad, up_grad, gate_sum, down)
+        down = scatter_columns(down)
+        first, second = send_far(gate_sum)
+        gate_sum = receive_far(first)
+        up_sum = add_partner(split_rows(up_sum), low_bits)
+        middle_grad, middle_bf, mlp_sum = rows_back(
+            gate_grad, up_grad, wg, wu, grad, middle, mlp_row
+        )
+        middle_bf, gate_sum, second[0], up_sum = tied(middle_bf, gate_sum, second[0], up_sum)
+        gate_sum = [gate_sum, receive_far(second)]
+        mixed_grad = mm(middle_bf, wo).astype(bf16)
+        mixed_grad, gate_sum[1], up_sum = tied(mixed_grad, gate_sum[1], up_sum)
+        gate_sum = scatter_columns(jnp.concatenate(gate_sum, axis=0))
+        first, second = send_far(up_sum)
+        up_sum = receive_far(first)
+        dq, dk, dv = attention_backward(
+            *heads, mixed_grad, lse, back_tables, key_tables, offset, single
+        )
         dk = own_rows(dk)
         dv = own_rows(dv)
-        if not weights_too:
-            return (dq, dk, dv, middle_grad), extra
         dq, dk, dv, down, up_sum, second[0] = tied(dq, dk, dv, down, up_sum, second[0])
         up_sum = [up_sum, receive_far(second)]
+        outgoing, attn_sum = heads_back(dq, dk, dv, wqkv, h, middle_grad, attn_row, 0, blocks)
+        outgoing, dk, dv, dq, middle_bf = tied(outgoing, dk, dv, dq, middle_bf)
+        input_grads = to_places(outgoing)
         kv = jnp.concatenate(
             [unpadded(mm_tn(normed, dk).astype(bf16)), unpadded(mm_tn(normed, dv).astype(bf16))],
             axis=1,
         )
-        dq, kv = tied(dq, kv)
+        dq, kv, up_sum[1] = tied(dq, kv, up_sum[1])
+        up_sum = scatter_columns(jnp.concatenate(up_sum, axis=0))
         kv = add_partner(split_rows(kv), low_bits)
         query = unpadded(mm_tn(normed, dq).astype(bf16))
-        dq, kv, query, up_sum[1] = tied(dq, kv, query, up_sum[1])
-        up_sum, dq = tied(jnp.concatenate(up_sum, axis=0), dq)
-        up_sum = scatter_columns(up_sum)
+        middle_bf, kv, query = tied(middle_bf, kv, query)
         kv = add_partner(kv, high_bits)[0]
         query = add_partner(split_rows(query), low_bits)
-        outgoing, attn_sum = heads_back(dq, dk, dv, wqkv, h, middle_grad, attn_row, 0, blocks)
-        outgoing, kv, query, gate_sum = tied(outgoing, kv, query, gate_sum)
-        out = add_partner(out, high_bits)[0]
+        out = unpadded(mm_tn(middle_bf, mixed).astype(bf16))
+        out, kv, query, gate_sum = tied(out, kv, query, gate_sum)
+        kv = sum_over_tensor(kv)
         query = add_partner(query, high_bits)[0]
-        input_grads = to_places(outgoing)
-        kv = sum_over_tensor(kv)
+        out = add_partner(split_rows(out), low_bits + high_bits)[0]
         pair = jnp.concatenate(
             [out.reshape(share, tsize, -1), query.reshape(share, tsize, -1)], axis=2
         )
@@ -822,7 +891,7 @@
     received, half_cot = tied(received, half_cot)
     kept, cot = forward(jnp.where(first_section, rows_in, received), join_halves(half_cot))
     second_out = down_rows(kept[-1], kept[5], wd, 0, blocks)
-    (dq, dk, dv, middle_grad), outputs = backward(cot, kept, False, to_places(second_out))
+    dq, dk, dv, middle_grad, outputs = backward(cot, kept, to_places(second_out))
     returned = send_chunks(
         lambda source, first, count: (
             heads_back(source, dk, dv, wqkv, kept[0], middle_grad, attn_row, first, count)[0],
@@ -831,7 +900,7 @@
         -1,
         dq,
     )
-    input_grads, sums, gains = backward(jnp.where(first_section, returned, cot), kept, True)
+    input_grads, sums, gains = backward_all(jnp.where(first_section, returned, cot), kept)
     down, gate, up, out, query, kv = sums
     gains = reorder(gains, 1)
     for axis, size in (("dp", dsize), ("tensor", tsize)):

time: 1400 us -> 1460 us (1.043)
  matrix products: 114 us -> 60.8 us
  Pallas kernels: 487 us -> 530 us
  waiting for transfers between devices: 415 us -> 449 us
  local copies, waits for them, and re-layouts: 202 us -> 218 us
    pallas_call x0 -> x2, Pallas kernels: none -> 98.1 us  [the longest x1 52.2 us: feed_grads(): kernel_call(feed_grads_kernel, (total // block,), [whole(grad.shape), col...]
    pallas_call x2 -> x1, Pallas kernels: 126 us -> 63.5 us  [feed_back(): kernel_call(feed_back_kernel, (total // block,), [whole(grad.shape), colu...]
    dot_general x9 -> x6, matrix products: 93.3 us -> 42.4 us  [mm_tn(): lax.dot_general(left, right, (((0,), (0,)), ((), ())), preferred_element_...]
    all_gather x8, waiting for transfers between devices: 44.8 us -> 67.9 us  [spread_weight(): whole = lax.all_gather(shard[i * rows:(i + 1) * rows], 'tensor', axis=0)]
    ppermute x67 -> x68, starting transfers between devices: 51 us -> 63.7 us  [swapped(): lax.ppermute(array, axis, [(i, i ^ bit) for i in range(lax.axis_size(axis...]
    ppermute x67 -> x68, waiting for transfers between devices: 262 us -> 274 us  [swapped(): lax.ppermute(array, axis, [(i, i ^ bit) for i in range(lax.axis_size(axis...]
    convert_element_type x8 -> x9, other arithmetic: 20.9 us -> 30.1 us  [add_partner(): summed[m] = (parts[m].astype(f32) + got.astype(f32)).astype(bf16)]
    unnamed x116 -> x108, local copies, waits for them, and re-layouts: 64.7 us -> 62.5 us
  transfers between devices with their start and end apart: 83 -> 84, of which waited for: 28 -> 30; matrix products, arithmetic and copies ran while one was open for 25% -> 23% of each run, Pallas kernels for 25% -> 27%
where the time goes in v7:
time: 1460 us; the launch traced here: 1450 us
  Pallas kernels  530 us (36%)
  waiting for transfers between devices  449 us (31%)
  local copies, waits for them, and re-layouts  218 us (15%)
  other arithmetic  105 us (7%)
  starting transfers between devices  75.9 us (5%)
  matrix products  60.8 us (4%)
  between operations  15.7 us (1%)
    ppermute x68, waiting for transfers between devices, swapped(): lax.ppermute(array, axis, [(i, i ^ bit) for i in range(lax.axis_size(axis...  274 us
    pallas_call x2, Pallas kernels, attention_backward(): kernel_call(functools.partial(attend_backward_kernel, single=single), (KV...  75.4 us
    ppermute x4, waiting for transfers between devices, shifted(): return lax.ppermute(array, axis, pairs)  72.8 us
    all_gather x8, waiting for transfers between devices, spread_weight(): whole = lax.all_gather(shard[i * rows:(i + 1) * rows], 'tensor', axis=0)  67.9 us
    pallas_call x2, Pallas kernels, gate_up(): kernel_call(gate_up_kernel, (total // block,), [whole(x.shape), columns_o...  64 us
    ppermute x68, starting transfers between devices, swapped(): lax.ppermute(array, axis, [(i, i ^ bit) for i in range(lax.axis_size(axis...  63.7 us
    pallas_call x1, Pallas kernels, feed_back(): kernel_call(feed_back_kernel, (total // block,), [whole(grad.shape), colu...  63.5 us
    unnamed x108, local copies, waits for them, and re-layouts  62.5 us
  transfers between devices with their start and end apart: 84, of which 30 were waited for; matrix products, arithmetic and copies ran while one was open for 23% of the time, Pallas kernels for 27%

profile of v7, /device:TPU:0, one launch (start us, length us, event | category | flops | bytes accessed | tf_op | source)
XLA Modules:
  0.0 1454.9 jit_solution(3439929812617251223)
XLA Ops:
  20.3 26.3 %collective-permute-done = bf16[384,1536]{0,1:T(8,128)(2,1)} collective-permute-done((bf16[384,1536]{0,1:T(8,128)(2,1)}, bf16[384,1536]{0,1:T(8,128)(2,1)}, u32[]{:S(2)}, u32[]{:S(2)}) %collective-permute-start) | collective-permute-done | bytes 1179680 | tf_op jit(solution)/shard_map/ppermute | solution.py:28
  52.7 28.5 %all-gather.20.cloned.1.call-done = bf16[4,192,1024]{2,1,0:T(8,128)(2,1)} async-done(((bf16[1,192,1024]{2,1,0:T(8,128)(2,1)}), bf16[4,192,1024]{2,1,0:T(8,128)(2,1)}) %all-gather.20.cloned.1.call-update) | async-done | bytes 1572880 | tf_op jit(solution)/shard_map/all_gather | solution.py:684
  88.5 24.2 %all-gather.22.cloned.1.call-done = bf16[1536,384]{1,0:T(8,128)(2,1)} async-done(((bf16[384,384]{1,0:T(8,128)(2,1)}), bf16[1536,384]{1,0:T(8,128)(2,1)}) %all-gather.22.cloned.1.call-update) | async-done | bytes 1179664 | tf_op jit(solution)/shard_map/all_gather | solution.py:684
  135.7 15.2 %all-gather.18.cloned.1.call-done = bf16[4,192,1024]{2,1,0:T(8,128)(2,1)} async-done(((bf16[1,192,1024]{2,1,0:T(8,128)(2,1)}), bf16[4,192,1024]{2,1,0:T(8,128)(2,1)}) %all-gather.18.cloned.1.call-update) | async-done | bytes 1572880 | tf_op jit(solution)/shard_map/all_gather | solution.py:684
  188.5 15.8 %collective-permute-done.3 = bf16[1,256,768]{2,1,0:T(8,128)(2,1)} collective-permute-done((bf16[1,256,768]{2,1,0:T(8,128)(2,1)}, bf16[1,256,768]{2,1,0:T(8,128)(2,1)}, u32[]{:S(2)}, u32[]{:S(2)}) %collective-permute-start.3) | collective-permute-done | bytes 393248 | tf_op jit(solution)/shard_map/ppermute | solution.py:28
  239.1 15.2 %collective-permute-done.8 = bf16[192,4096]{1,0:T(8,128)(2,1)} collective-permute-done((bf16[192,4096]{1,0:T(8,128)(2,1)S(1)}, bf16[192,4096]{1,0:T(8,128)(2,1)}, u32[]{:S(2)}, u32[]{:S(2)}) %collective-permute-start.8) | collective-permute-done | bytes 1572896 | tf_op jit(solution)/shard_map/ppermute | solution.py:28
  276.8 24.6 %project.2 = (bf16[1024,4096]{1,0:T(8,128)(2,1)}, bf16[1024,1536]{1,0:T(8,128)(2,1)}) custom-call(bf16[1024,1536]{1,0:T(8,128)(2,1)} %pad_maximum_fusion.4.h_ref, f32[1,1536]{1,0:T(1,128)} %broadcast_in_dim.68.gain_ref, bf16[1536,4096]{1,0:T(8,128)(2,1)} %pad_maximum_fusion.w_ref, f32[1024,128]{1,0:T(8,128)} %pad_maximum_fusion.17.cos_ref.cosq_ref.cosk_ref, ...), custom_call_target="tpu_custom_call" | custom-call | flops 12884901888 | bytes 36700160 | tf_op jit(solution)/shard_map/project/pallas_call | solution.py:124
  313.9 22.1 %attend_forward.2 = (bf16[1024,2048]{1,0:T(8,128)(2,1)}, f32[8,4,1,512]{3,2,1,0:T(1,128)}) custom-call(s32[1]{0:T(128)} %bitcast.offset_ref, bf16[1024,4096]{1,0:T(8,128)(2,1)} %get-tuple-element.142.q_ref.k_ref.v_ref, bf16[1024,4096]{1,0:T(8,128)(2,1)} %get-tuple-element.142.q_ref.k_ref.v_ref, bf16[1024,4096]{1,0:T(8,128)(2,1)} %get-tuple-element.142.q_ref.k_ref.v_ref), custom_call_target="tpu_custom_call" | custom-call | flops 8589934592 | bytes 21004288 | tf_op jit(solution)/shard_map/attend_forward/pallas_call | solution.py:500
  358.2 13.4 join.2
  384.7 32.0 %gate_up.2 = (bf16[1024,4096]{1,0:T(8,128)(2,1)}, bf16[1024,4096]{1,0:T(8,128)(2,1)}, bf16[1024,4096]{1,0:T(8,128)(2,1)}) custom-call(bf16[1024,1536]{1,0:T(8,128)(2,1)} %get-tuple-element.145.x_ref, bf16[1536,4096]{1,0:T(8,128)(2,1)} %constant_dynamic-update-slice_fusion.wg_ref, bf16[1536,4096]{1,0:T(8,128)(2,1)} %constant_dynamic-update-slice_fusion.8.wu_ref), custom_call_target="tpu_custom_call" | custom-call | flops 25769803776 | bytes 75497472 | tf_op jit(solution)/shard_map/gate_up/pallas_call | solution.py:179
  431.1 14.5 down_rows.3
  449.3 14.5 %down_rows.4 = bf16[512,1536]{1,0:T(8,128)(2,1)} custom-call(bf16[1024,4096]{1,0:T(8,128)(2,1)} %get-tuple-element.155.hidden_ref, f32[1024,1536]{1,0:T(8,128)} %get-tuple-element.150.middle_ref, bf16[1536,4096]{1,0:T(8,128)(2,1)} %constant_dynamic-update-slice_fusion.16.w_ref.wd_ref), custom_call_target="tpu_custom_call" | custom-call | flops 6442450944 | bytes 14155776 | tf_op jit(solution)/shard_map/down_rows/pallas_call | solution.py:198
  463.8 19.5 %collective-permute-done.31 = bf16[512,1536]{1,0:T(8,128)(2,1)S(1)} collective-permute-done((bf16[512,1536]{1,0:T(8,128)(2,1)}, bf16[512,1536]{1,0:T(8,128)(2,1)S(1)}, u32[]{:S(2)}, u32[]{:S(2)}) %collective-permute-start.31) | collective-permute-done | bytes 1572896 | tf_op jit(solution)/shard_map/ppermute | solution.py:24
  525.7 24.6 %project.3 = (bf16[1024,4096]{1,0:T(8,128)(2,1)}, bf16[1024,1536]{1,0:T(8,128)(2,1)}) custom-call(bf16[1024,1536]{1,0:T(8,128)(2,1)} %broadcast_select_fusion.h_ref, f32[1,1536]{1,0:T(1,128)} %broadcast_in_dim.68.gain_ref, bf16[1536,4096]{1,0:T(8,128)(2,1)} %pad_maximum_fusion.w_ref, f32[1024,128]{1,0:T(8,128)} %pad_maximum_fusion.17.cos_ref.cosq_ref.cosk_ref, ...), custom_call_target="tpu_custom_call" | custom-call | flops 12884901888 | bytes 36700160 | tf_op jit(solution)/shard_map/project/pallas_call | solution.py:124
  550.3 21.7 %attend_forward.3 = (bf16[1024,2048]{1,0:T(8,128)(2,1)}, f32[8,4,1,512]{3,2,1,0:T(1,128)}) custom-call(s32[1]{0:T(128)} %bitcast.offset_ref, bf16[1024,4096]{1,0:T(8,128)(2,1)} %get-tuple-element.162.q_ref.k_ref.v_ref, bf16[1024,4096]{1,0:T(8,128)(2,1)} %get-tuple-element.162.q_ref.k_ref.v_ref, bf16[1024,4096]{1,0:T(8,128)(2,1)} %get-tuple-element.162.q_ref.k_ref.v_ref), custom_call_target="tpu_custom_call" | custom-call | flops 8589934592 | bytes 21004288 | tf_op jit(solution)/shard_map/attend_forward/pallas_call | solution.py:500
  574.7 13.4 join.3
  588.1 32.0 %gate_up.3 = (bf16[1024,4096]{1,0:T(8,128)(2,1)}, bf16[1024,4096]{1,0:T(8,128)(2,1)}, bf16[1024,4096]{1,0:T(8,128)(2,1)}) custom-call(bf16[1024,1536]{1,0:T(8,128)(2,1)} %get-tuple-element.167.x_ref.normed_ref, bf16[1536,4096]{1,0:T(8,128)(2,1)} %constant_dynamic-update-slice_fusion.wg_ref, bf16[1536,4096]{1,0:T(8,128)(2,1)} %constant_dynamic-update-slice_fusion.8.wu_ref), custom_call_target="tpu_custom_call" | custom-call | flops 25769803776 | bytes 75497472 | tf_op jit(solution)/shard_map/gate_up/pallas_call | solution.py:179
  620.1 22.8 %down_rows.5 = bf16[1024,1536]{1,0:T(8,128)(2,1)} custom-call(bf16[1024,4096]{1,0:T(8,128)(2,1)} %get-tuple-element.172.hidden_ref, f32[1024,1536]{1,0:T(8,128)} %get-tuple-element.170.middle_ref, bf16[1536,4096]{1,0:T(8,128)(2,1)} %constant_dynamic-update-slice_fusion.16.w_ref.wd_ref), custom_call_target="tpu_custom_call" | custom-call | flops 12884901888 | bytes 28311552 | tf_op jit(solution)/shard_map/down_rows/pallas_call | solution.py:198
  654.9 63.5 %feed_back.1 = (f32[1024,1536]{1,0:T(8,128)}, bf16[1024,1536]{1,0:T(8,128)(2,1)}, f32[1,1536]{1,0:T(1,128)}) custom-call(bf16[1024,1536]{1,0:T(8,128)(2,1)} %pad_maximum_fusion.7.grad_ref, bf16[1024,4096]{1,0:T(8,128)(2,1)} %get-tuple-element.168.gate_ref, bf16[1024,4096]{1,0:T(8,128)(2,1)} %get-tuple-element.169.up_ref, ...), custom_call_target="tpu_custom_call" | custom-call | flops 38654705664 | bytes 81792000 | tf_op jit(solution)/shard_map/feed_back/pallas_call | solution.py:342
  732.5 37.6 %attend_backward.2 = (bf16[1024,2048]{1,0:T(8,128)(2,1)}, bf16[1024,1024]{1,0:T(8,128)(2,1)}, bf16[1024,1024]{1,0:T(8,128)(2,1)}) custom-call(s32[1]{0:T(128)} %bitcast.offset_ref, bf16[1024,4096]{1,0:T(8,128)(2,1)} %get-tuple-element.162.q_ref.k_ref.v_ref, bf16[1024,4096]{1,0:T(8,128)(2,1)} %get-tuple-element.162.q_ref.k_ref.v_ref, ...), custom_call_target="tpu_custom_call" | custom-call | flops 21474836480 | bytes 50331648 | tf_op jit(solution)/shard_map/attend_backward/pallas_call | solution.py:527
  770.1 16.1 %heads_back.3 = (bf16[512,1536]{1,0:T(8,128)(2,1)}, f32[1,1536]{1,0:T(1,128)}) custom-call(bf16[1024,2048]{1,0:T(8,128)(2,1)} %get-tuple-element.181.dq_ref, bf16[1024,1024]{1,0:T(8,128)(2,1)} %get-tuple-element.177.dk_ref, bf16[1024,1024]{1,0:T(8,128)(2,1)} %get-tuple-element.178.dv_ref, bf16[1536,4096]{1,0:T(8,128)(2,1)} %pad_maximum_fusion.w_ref, ...), custom_call_target="tpu_custom_call" | custom-call | flops 6442450944 | bytes 14158848 | tf_op jit(solution)/shard_map/heads_back/pallas_call | solution.py:391
  788.1 16.2 %heads_back.4 = (bf16[512,1536]{1,0:T(8,128)(2,1)}, f32[1,1536]{1,0:T(1,128)}) custom-call(bf16[1024,2048]{1,0:T(8,128)(2,1)} %get-tuple-element.181.dq_ref, bf16[1024,1024]{1,0:T(8,128)(2,1)} %get-tuple-element.177.dk_ref, bf16[1024,1024]{1,0:T(8,128)(2,1)} %get-tuple-element.178.dv_ref, bf16[1536,4096]{1,0:T(8,128)(2,1)} %pad_maximum_fusion.w_ref, ...), custom_call_target="tpu_custom_call" | custom-call | flops 6442450944 | bytes 14158848 | tf_op jit(solution)/shard_map/heads_back/pallas_call | solution.py:391
  804.3 18.0 %collective-permute-done.40 = bf16[512,1536]{1,0:T(8,128)(2,1)S(1)} collective-permute-done((bf16[512,1536]{1,0:T(8,128)(2,1)}, bf16[512,1536]{1,0:T(8,128)(2,1)S(1)}, u32[]{:S(2)}, u32[]{:S(2)}) %collective-permute-start.40) | collective-permute-done | bytes 1572896 | tf_op jit(solution)/shard_map/ppermute | solution.py:24
  823.7 33.4 %collective-permute-done.41 = bf16[512,1536]{1,0:T(8,128)(2,1)S(1)} collective-permute-done((bf16[512,1536]{1,0:T(8,128)(2,1)}, bf16[512,1536]{1,0:T(8,128)(2,1)S(1)}, u32[]{:S(2)}, u32[]{:S(2)}) %collective-permute-start.41) | collective-permute-done | bytes 1572896 | tf_op jit(solution)/shard_map/ppermute | solution.py:24
  891.7 52.2 %feed_grads.1 = (bf16[1024,4096]{1,0:T(8,128)(2,1)}, bf16[1024,4096]{1,0:T(8,128)(2,1)}, bf16[1536,4096]{1,0:T(8,128)(2,1)}, bf16[1536,4096]{1,0:T(8,128)(2,1)}) custom-call(bf16[1024,1536]{1,0:T(8,128)(2,1)} %copy-done.3, bf16[1024,4096]{1,0:T(8,128)(2,1)} %get-tuple-element.168.gate_ref, bf16[1024,4096]{1,0:T(8,128)(2,1)} %get-tuple-element.169.up_ref, ...), custom_call_target="tpu_custom_call" | custom-call | flops 38654705664 | bytes 117440512 | tf_op jit(solution)/shard_map/feed_grads/pallas_call | solution.py:249
  978.1 45.9 %rows_back.1 = (f32[1024,1536]{1,0:T(8,128)}, bf16[1024,1536]{1,0:T(8,128)(2,1)}, f32[1,1536]{1,0:T(1,128)}) custom-call(bf16[1024,4096]{1,0:T(8,128)(2,1)} %get-tuple-element.197.gate_grad_ref, bf16[1024,4096]{1,0:T(8,128)(2,1)} %get-tuple-element.198.up_grad_ref, bf16[1536,4096]{1,0:T(8,128)(2,1)} %constant_dynamic-update-slice_fusion.wg_ref, ...), custom_call_target="tpu_custom_call" | custom-call | flops 25769803776 | bytes 56626176 | tf_op jit(solution)/shard_map/rows_back/pallas_call | solution.py:287
  1030.1 15.3 %collective-permute-done.46 = bf16[192,4096]{1,0:T(8,128)(2,1)} collective-permute-done((bf16[192,4096]{1,0:T(8,128)(2,1)S(1)}, bf16[192,4096]{1,0:T(8,128)(2,1)}, u32[]{:S(2)}, u32[]{:S(2)}) %collective-permute-start.46) | collective-permute-done | bytes 1572896 | tf_op jit(solution)/shard_map/ppermute | solution.py:28
  1065.3 37.7 %attend_backward.3 = (bf16[1024,2048]{1,0:T(8,128)(2,1)}, bf16[1024,1024]{1,0:T(8,128)(2,1)}, bf16[1024,1024]{1,0:T(8,128)(2,1)}) custom-call(s32[1]{0:T(128)} %bitcast.offset_ref, bf16[1024,4096]{1,0:T(8,128)(2,1)} %get-tuple-element.162.q_ref.k_ref.v_ref, bf16[1024,4096]{1,0:T(8,128)(2,1)} %get-tuple-element.162.q_ref.k_ref.v_ref, ...), custom_call_target="tpu_custom_call" | custom-call | flops 21474836480 | bytes 50331648 | tf_op jit(solution)/shard_map/attend_backward/pallas_call | solution.py:527
  1103.0 28.8 %collective-permute-done.50 = bf16[192,4096]{1,0:T(8,128)(2,1)} collective-permute-done((bf16[192,4096]{1,0:T(8,128)(2,1)}, bf16[192,4096]{1,0:T(8,128)(2,1)}, u32[]{:S(2)}, u32[]{:S(2)}) %collective-permute-start.50) | collective-permute-done | bytes 1572896 | tf_op jit(solution)/shard_map/ppermute | solution.py:28
  1134.9 25.0 %heads_back.5 = (bf16[1024,1536]{1,0:T(8,128)(2,1)}, f32[1,1536]{1,0:T(1,128)}) custom-call(bf16[1024,2048]{1,0:T(8,128)(2,1)} %get-tuple-element.226.dq_ref, bf16[1024,1024]{1,0:T(8,128)(2,1)} %get-tuple-element.222.dk_ref, bf16[1024,1024]{1,0:T(8,128)(2,1)} %get-tuple-element.223.dv_ref, bf16[1536,4096]{1,0:T(8,128)(2,1)} %pad_maximum_fusion.w_ref, ...), custom_call_target="tpu_custom_call" | custom-call | flops 12884901888 | bytes 28314624 | tf_op jit(solution)/shard_map/heads_back/pallas_call | solution.py:391
  1251.1 57.0 %collective-permute-done.61 = bf16[1,256,1536]{2,1,0:T(8,128)(2,1)} collective-permute-done((bf16[1,256,1536]{2,1,0:T(8,128)(2,1)}, bf16[1,256,1536]{2,1,0:T(8,128)(2,1)}, u32[]{:S(2)}, u32[]{:S(2)}) %collective-permute-start.61) | collective-permute-done | bytes 786464 | tf_op jit(solution)/shard_map/ppermute | solution.py:28
  1412.8 31.8 %reduce-scatter.11.cloned.1.call-done = bf16[1,384,768]{2,1,0:T(8,128)(2,1)} async-done(((bf16[4,384,768]{2,1,0:T(8,128)(2,1)}), bf16[1,384,768]{2,1,0:T(8,128)(2,1)}) %reduce-scatter.11.cloned.1.call-update) | async-done | bytes 589840 | tf_op jit(solution)/shard_map/reduce_scatter | solution.py:673
  (415 shorter events, 580.3 us)
Async XLA Ops:
  7.9 73.2 %all-gather.20.cloned.1.call-start = ((), (), s32[]{:S(2)}) async-start(), calls=%async_computation.8 | async-start | bytes 1966080 | tf_op jit(solution)/shard_map/all_gather | solution.py:684
  10.0 102.6 %all-gather.22.cloned.1.call-start = ((), (), s32[]{:S(2)}) async-start(), calls=%async_computation.13 | async-start | bytes 1474560 | tf_op jit(solution)/shard_map/all_gather | solution.py:684
  12.0 138.9 %all-gather.18.cloned.1.call-start = ((), (), s32[]{:S(2)}) async-start(), calls=%async_computation.7 | async-start | bytes 1966080 | tf_op jit(solution)/shard_map/all_gather | solution.py:684
  12.5 226.5 %all-gather.16.cloned.1.call-start = ((), (), s32[]{:S(2)}) async-start(), calls=%async_computation.6 | async-start | bytes 1966080 | tf_op jit(solution)/shard_map/all_gather | solution.py:684
  13.6 287.8 %all-gather.14.cloned.1.call-start = ((), (), s32[]{:S(2)}) async-start(), calls=%async_computation.5 | async-start | bytes 1966080 | tf_op jit(solution)/shard_map/all_gather | solution.py:684
  14.1 321.8 %all-gather.26.cloned.1.call-start = ((), (), s32[]{:S(2)}) async-start(), calls=%async_computation.15 | async-start | bytes 1966080 | tf_op jit(solution)/shard_map/all_gather | solution.py:684
  15.5 356.1 %all-gather.24.cloned.1.call-start = ((), (), s32[]{:S(2)}) async-start(), calls=%async_computation.14 | async-start | bytes 1966080 | tf_op jit(solution)/shard_map/all_gather | solution.py:684
  48.9 63.7 %collective-permute-start.1 = (bf16[384,1536]{0,1:T(8,128)(2,1)}, bf16[384,1536]{0,1:T(8,128)(2,1)}, u32[]{:S(2)}, u32[]{:S(2)}) collective-permute-start(bf16[384,1536]{0,1:T(8,128)(2,1)} %bitcast.7), channel_id=1, source_target_pairs={{0,8},{4,12},{8,0},{12,4},{1,9},{5,13},{9,1},{13,5},{2,10},{6,14},... | collective-permute-start | bytes 3538952 | tf_op jit(solution)/shard_map/ppermute | solution.py:28
  50.7 66.0 %collective-permute-start.15 = (bf16[384,1536]{0,1:T(8,128)(2,1)}, bf16[384,1536]{0,1:T(8,128)(2,1)}, u32[]{:S(2)}, u32[]{:S(2)}) collective-permute-start(bf16[384,1536]{0,1:T(8,128)(2,1)} %pad_maximum_fusion.14), channel_id=1, source_target_pairs={{0,4},{4,0},{8,12},{12,8},{1,5},{5,1},{9,13},{13,9},{2,6},{6,2},{1... | collective-permute-start | bytes 3538952 | tf_op jit(solution)/shard_map/ppermute | solution.py:28
  50.7 66.0 %collective-permute-start.16 = (bf16[384,1536]{0,1:T(8,128)(2,1)}, bf16[384,1536]{0,1:T(8,128)(2,1)}, u32[]{:S(2)}, u32[]{:S(2)}) collective-permute-start(bf16[384,1536]{0,1:T(8,128)(2,1)} %collective-permute-done), channel_id=1, source_target_pairs={{0,4},{4,0},{8,12},{12,8},{1,5},{5,1},{9,13},{13,9},{2,6},{6,2},{1... | collective-permute-start | bytes 3538952 | tf_op jit(solution)/shard_map/ppermute | solution.py:28
  51.2 1083.7 %reduce-scatter.5.cloned.1.call-start = ((), (), s32[]{:S(2)}) async-start(), calls=%async_computation.9 | async-start | bytes 3932160 | tf_op jit(solution)/shard_map/reduce_scatter | solution.py:673
  82.7 68.2 %collective-permute-start.7 = (bf16[192,4096]{1,0:T(8,128)(2,1)S(1)}, bf16[192,4096]{1,0:T(8,128)(2,1)}, u32[]{:S(2)}, u32[]{:S(2)}) collective-permute-start(bf16[192,4096]{1,0:T(8,128)(2,1)S(1)} %bitcast.165), channel_id=1, source_target_pairs={{0,8},{4,12},{8,0},{12,4},{1,9},{5,13},{9,1},{13,5},{2,10},{6,14},... | collective-permute-start | bytes 4718600 | tf_op jit(solution)/shard_map/ppermute | solution.py:28
  88.4 71.3 %collective-permute-start.13 = (bf16[384,1536]{0,1:T(8,128)(2,1)}, bf16[384,1536]{0,1:T(8,128)(2,1)}, u32[]{:S(2)}, u32[]{:S(2)}) collective-permute-start(bf16[384,1536]{0,1:T(8,128)(2,1)} %bitcast.7), channel_id=1, source_target_pairs={{0,4},{4,0},{8,12},{12,8},{1,5},{5,1},{9,13},{13,9},{2,6},{6,2},{1... | collective-permute-start | bytes 3538952 | tf_op jit(solution)/shard_map/ppermute | solution.py:28
  135.2 88.1 %collective-permute-start.17 = (bf16[384,1536]{0,1:T(8,128)(2,1)}, bf16[384,1536]{0,1:T(8,128)(2,1)}, u32[]{:S(2)}, u32[]{:S(2)}) collective-permute-start(bf16[384,1536]{0,1:T(8,128)(2,1)} %bitcast.10), channel_id=1, source_target_pairs={{0,4},{4,0},{8,12},{12,8},{1,5},{5,1},{9,13},{13,9},{2,6},{6,2},{1... | collective-permute-start | bytes 3538952 | tf_op jit(solution)/shard_map/ppermute | solution.py:28
  157.8 64.7 %collective-permute-start.5 = (bf16[1,256,768]{2,1,0:T(8,128)(2,1)}, bf16[1,256,768]{2,1,0:T(8,128)(2,1)S(1)}, u32[]{:S(2)}, u32[]{:S(2)}) collective-permute-start(bf16[1,256,768]{2,1,0:T(8,128)(2,1)} %get-tuple-element.349), channel_id=1, source_target_pairs={{0,3},{1,2},{2,1},{3,0},{4,7},{5,6},{6,5},{7,4},{8,11},{9,10},{10,... | collective-permute-start | bytes 1179656 | tf_op jit(solution)/shard_map/ppermute | solution.py:28
  650.5 81.1 %collective-permute-start.39 = (bf16[1,256,1536]{2,1,0:T(8,128)(2,1)}, bf16[1,256,1536]{2,1,0:T(8,128)(2,1)S(1)}, u32[]{:S(2)}, u32[]{:S(2)}) collective-permute-start(bf16[1,256,1536]{2,1,0:T(8,128)(2,1)} %get-tuple-element.327), channel_id=1, source_target_pairs={{0,3},{1,2},{2,1},{3,0},{4,7},{5,6},{6,5},{7,4},{8,11},{9,10},{10,... | collective-permute-start | bytes 2359304 | tf_op jit(solution)/shard_map/ppermute | solution.py:28
  653.3 77.3 %collective-permute-start.38 = (bf16[1,256,1536]{2,1,0:T(8,128)(2,1)}, bf16[1,256,1536]{2,1,0:T(8,128)(2,1)S(1)}, u32[]{:S(2)}, u32[]{:S(2)}) collective-permute-start(bf16[1,256,1536]{2,1,0:T(8,128)(2,1)} %get-tuple-element.328), channel_id=1, source_target_pairs={{0,2},{1,3},{2,0},{3,1},{4,6},{5,7},{6,4},{7,5},{8,10},{9,11},{10,... | collective-permute-start | bytes 2359304 | tf_op jit(solution)/shard_map/ppermute | solution.py:28
  654.7 73.8 %collective-permute-start.37 = (bf16[1,256,1536]{2,1,0:T(8,128)(2,1)}, bf16[1,256,1536]{2,1,0:T(8,128)(2,1)}, u32[]{:S(2)}, u32[]{:S(2)}) collective-permute-start(bf16[1,256,1536]{2,1,0:T(8,128)(2,1)} %get-tuple-element.329), channel_id=1, source_target_pairs={{0,1},{1,0},{2,3},{3,2},{4,5},{5,4},{6,7},{7,6},{8,9},{9,8},{10,11... | collective-permute-start | bytes 2359304 | tf_op jit(solution)/shard_map/ppermute | solution.py:28
  890.4 70.5 %collective-permute-start.45 = (bf16[384,4096]{1,0:T(8,128)(2,1)}, bf16[384,4096]{1,0:T(8,128)(2,1)}, u32[]{:S(2)}, u32[]{:S(2)}) collective-permute-start(bf16[384,4096]{1,0:T(8,128)(2,1)} %get-tuple-element.196), channel_id=1, source_target_pairs={{0,8},{4,12},{8,0},{12,4},{1,9},{5,13},{9,1},{13,5},{2,10},{6,14},... | collective-permute-start | bytes 9437192 | tf_op jit(solution)/shard_map/ppermute | solution.py:28
  957.9 66.1 %collective-permute-start.48 = (bf16[384,4096]{1,0:T(8,128)(2,1)}, bf16[384,4096]{1,0:T(8,128)(2,1)}, u32[]{:S(2)}, u32[]{:S(2)}) collective-permute-start(bf16[384,4096]{1,0:T(8,128)(2,1)} %get-tuple-element.294), channel_id=1, source_target_pairs={{0,4},{4,0},{8,12},{12,8},{1,5},{5,1},{9,13},{13,9},{2,6},{6,2},{1... | collective-permute-start | bytes 9437192 | tf_op jit(solution)/shard_map/ppermute | solution.py:28
  957.9 66.1 %collective-permute-start.47 = (bf16[384,4096]{1,0:T(8,128)(2,1)}, bf16[384,4096]{1,0:T(8,128)(2,1)}, u32[]{:S(2)}, u32[]{:S(2)}) collective-permute-start(bf16[384,4096]{1,0:T(8,128)(2,1)} %get-tuple-element.295), channel_id=1, source_target_pairs={{0,4},{4,0},{8,12},{12,8},{1,5},{5,1},{9,13},{13,9},{2,6},{6,2},{1... | collective-permute-start | bytes 9437192 | tf_op jit(solution)/shard_map/ppermute | solution.py:28
  975.7 274.2 %reduce-scatter.7.cloned.1.call-start = ((), (), s32[]{:S(2)}) async-start(), calls=%async_computation.10 | async-start | bytes 3932160 | tf_op jit(solution)/shard_map/reduce_scatter | solution.py:673
  976.0 71.4 %collective-permute-start.49 = (bf16[192,4096]{1,0:T(8,128)(2,1)S(1)}, bf16[192,4096]{1,0:T(8,128)(2,1)S(1)}, u32[]{:S(2)}, u32[]{:S(2)}) collective-permute-start(bf16[192,4096]{1,0:T(8,128)(2,1)S(1)} %get-tuple-element.321), channel_id=1, source_target_pairs={{0,8},{4,12},{8,0},{12,4},{1,9},{5,13},{9,1},{13,5},{2,10},{6,14},... | collective-permute-start | bytes 4718600 | tf_op jit(solution)/shard_map/ppermute | solution.py:28
  977.4 68.1 %collective-permute-start.46 = (bf16[192,4096]{1,0:T(8,128)(2,1)S(1)}, bf16[192,4096]{1,0:T(8,128)(2,1)}, u32[]{:S(2)}, u32[]{:S(2)}) collective-permute-start(bf16[192,4096]{1,0:T(8,128)(2,1)S(1)} %get-tuple-element.322), channel_id=1, source_target_pairs={{0,8},{4,12},{8,0},{12,4},{1,9},{5,13},{9,1},{13,5},{2,10},{6,14},... | collective-permute-start | bytes 4718600 | tf_op jit(solution)/shard_map/ppermute | solution.py:28
  1063.2 108.7 %collective-permute-start.51 = (bf16[192,4096]{1,0:T(8,128)(2,1)}, bf16[192,4096]{1,0:T(8,128)(2,1)}, u32[]{:S(2)}, u32[]{:S(2)}) collective-permute-start(bf16[192,4096]{1,0:T(8,128)(2,1)} %get-tuple-element.319), channel_id=1, source_target_pairs={{0,8},{4,12},{8,0},{12,4},{1,9},{5,13},{9,1},{13,5},{2,10},{6,14},... | collective-permute-start | bytes 4718600 | tf_op jit(solution)/shard_map/ppermute | solution.py:28
  1064.5 67.3 %collective-permute-start.50 = (bf16[192,4096]{1,0:T(8,128)(2,1)}, bf16[192,4096]{1,0:T(8,128)(2,1)}, u32[]{:S(2)}, u32[]{:S(2)}) collective-permute-start(bf16[192,4096]{1,0:T(8,128)(2,1)} %get-tuple-element.320), channel_id=1, source_target_pairs={{0,8},{4,12},{8,0},{12,4},{1,9},{5,13},{9,1},{13,5},{2,10},{6,14},... | collective-permute-start | bytes 4718600 | tf_op jit(solution)/shard_map/ppermute | solution.py:28
  1065.2 325.4 %reduce-scatter.9.cloned.1.call-start = ((), (), s32[]{:S(2)}) async-start(), calls=%async_computation.11 | async-start | bytes 3932160 | tf_op jit(solution)/shard_map/reduce_scatter | solution.py:673
  1207.5 150.6 %collective-permute-start.63 = (bf16[1,256,1536]{2,1,0:T(8,128)(2,1)}, bf16[1,256,1536]{2,1,0:T(8,128)(2,1)}, u32[]{:S(2)}, u32[]{:S(2)}) collective-permute-start(bf16[1,256,1536]{2,1,0:T(8,128)(2,1)} %get-tuple-element.312), channel_id=1, source_target_pairs={{0,3},{1,2},{2,1},{3,0},{4,7},{5,6},{6,5},{7,4},{8,11},{9,10},{10,... | collective-permute-start | bytes 2359304 | tf_op jit(solution)/shard_map/ppermute | solution.py:28
  1209.9 126.6 %collective-permute-start.62 = (bf16[1,256,1536]{2,1,0:T(8,128)(2,1)}, bf16[1,256,1536]{2,1,0:T(8,128)(2,1)}, u32[]{:S(2)}, u32[]{:S(2)}) collective-permute-start(bf16[1,256,1536]{2,1,0:T(8,128)(2,1)} %get-tuple-element.313), channel_id=1, source_target_pairs={{0,2},{1,3},{2,0},{3,1},{4,6},{5,7},{6,4},{7,5},{8,10},{9,11},{10,... | collective-permute-start | bytes 2359304 | tf_op jit(solution)/shard_map/ppermute | solution.py:28
  1210.5 234.1 %reduce-scatter.11.cloned.1.call-start = ((), (), s32[]{:S(2)}) async-start(), calls=%async_computation.12 | async-start | bytes 2949120 | tf_op jit(solution)/shard_map/reduce_scatter | solution.py:673
  1242.9 65.1 %collective-permute-start.61 = (bf16[1,256,1536]{2,1,0:T(8,128)(2,1)}, bf16[1,256,1536]{2,1,0:T(8,128)(2,1)}, u32[]{:S(2)}, u32[]{:S(2)}) collective-permute-start(bf16[1,256,1536]{2,1,0:T(8,128)(2,1)} %get-tuple-element.314), channel_id=1, source_target_pairs={{0,1},{1,0},{2,3},{3,2},{4,5},{5,4},{6,7},{7,6},{8,9},{9,8},{10,11... | collective-permute-start | bytes 2359304 | tf_op jit(solution)/shard_map/ppermute | solution.py:28
  1250.0 74.1 %collective-permute-start.64 = (bf16[384,768]{0,1:T(8,128)(2,1)S(1)}, bf16[384,768]{0,1:T(8,128)(2,1)S(1)}, u32[]{:S(2)}, u32[]{:S(2)}) collective-permute-start(bf16[384,768]{0,1:T(8,128)(2,1)S(1)} %broadcast_select_fusion.7), channel_id=1, source_target_pairs={{0,1},{1,0},{2,3},{3,2},{4,5},{5,4},{6,7},{7,6},{8,9},{9,8},{10,11... | collective-permute-start | bytes 1769480 | tf_op jit(solution)/shard_map/ppermute | solution.py:28
  (92 other events, 2196.9 us)
Sparse Core Ops, SparseCore 0:
  9.6 33.1 all-gather.11
  44.9 36.1 all-gather.19
  83.3 29.2 all-gather.21
  114.6 36.2 all-gather.17
  152.9 64.5 all-gather.15
  218.9 35.9 all-gather.13
  256.5 35.9 all-gather.25
  294.1 35.9 all-gather.23
  975.8 59.3 reduce-scatter.4
  1065.3 59.3 reduce-scatter.6
  1210.6 107.4 reduce-scatter.8
  1390.8 53.7 reduce-scatter.10

commit v8 on v7

--- a/solution.py
+++ b/solution.py
@@ -49,7 +49,7 @@
 
 
 QB = 256
-ROWS = 512
+ROWS = 256
 HP = 128
 LOG2E = 1.4426950408889634
 MIB = 2**20
@@ -300,10 +300,7 @@
 
 
 def accumulate_back(step, gate_grad, up_grad, wg_ref, wu_ref, total_ref):
-    part = mm_nt(
-        jnp.concatenate([gate_grad, up_grad], axis=1),
-        jnp.concatenate([wg_ref[...], wu_ref[...]], axis=1),
-    )
+    part = mm_nt(gate_grad, wg_ref[...]) + mm_nt(up_grad, wu_ref[...])
 
     @pl.when(step == 0)
     def _():
@@ -574,13 +571,19 @@
     high_bits = bits_of(dsize)[1:]
     same_seq = [[g + micro * r for r in range(ranks)] for g in range(micro)]
 
+    def arrivals(blocks):
+        return [
+            swapped(lax.dynamic_index_in_dim(blocks, seq ^ j, 0, keepdims=True), "tensor", j)
+            for j in range(1, micro)
+        ]
+
+    def settled(blocks, got):
+        for j in range(1, micro):
+            blocks = lax.dynamic_update_slice_in_dim(blocks, got[j - 1], seq ^ j, 0)
+        return blocks
+
     def exchange(blocks):
-        out = blocks
-        for j in range(1, micro):
-            sent = lax.dynamic_index_in_dim(blocks, seq ^ j, 0, keepdims=True)
-            got = swapped(sent, "tensor", j)
-            out = lax.dynamic_update_slice_in_dim(out, got, seq ^ j, 0)
-        return out
+        return settled(blocks, arrivals(blocks))
 
     def reorder(array, axis):
         return jnp.concatenate(
@@ -653,11 +656,10 @@
         total = (mine.astype(f32) + got.astype(f32)).astype(bf16)
         return {2 * i: total[i * share : (i + 1) * share] for i in range(dsize // 2)}
 
-    def send_far(parts):
-        size = share // 2
+    def send_far(parts, size):
         pairs = []
-        for i in range(2):
-            half = {m: part[i * size : (i + 1) * size] for m, part in parts.items()}
+        for rows in (slice(0, size), slice(size, share)):
+            half = {m: part[rows] for m, part in parts.items()}
             bit = high_bits[0]
             kept = {m: part for m, part in half.items() if not m & bit}
             pairs.append([kept, {m: swapped(half[m ^ bit], "dp", bit) for m in kept}])
@@ -674,8 +676,11 @@
 
     attn_scale = reorder(attn_gain[0], 0)
     mlp_scale = reorder(mlp_gain[0], 0)
+    mine = exchange_half(inputs)
     last = spread_far(jnp.concatenate([w_key[0], w_value[0]], axis=1))
+    mine, last = tied(mine, last)
     wkv = spread_near(last)
+    rows_in = join_halves(mine)
 
     def spread_weight(shard, pieces, last):
         rows = share // pieces
@@ -700,13 +705,11 @@
     wqkv = jnp.concatenate([padded(settle(fars)), padded(wkv)], axis=1)
     fars, last = spread_weight(w_out[0].T, 1, last)
     wo = padded(settle(fars))
-    late_inputs, last = tied(inputs, last)
-    rows_in = join_halves(exchange_half(late_inputs))
     fars, last = spread_weight(w_gate[0], 2, last)
-    waits = [fars[1]]
+    waits = list(fars)
     wg = settle(fars)
     fars, last = spread_weight(w_up[0], 2, last)
-    waits += fars
+    waits.append(fars[0])
     wu = settle(fars)
     far_down, last = spread_weight(w_down[0].T, 2, last)
 
@@ -814,7 +817,7 @@
         gate_sum = add_partner(split_rows(gate_sum), low_bits)
         gate_grad, up_grad, gate_sum, down = tied(gate_grad, up_grad, gate_sum, down)
         down = scatter_columns(down)
-        first, second = send_far(gate_sum)
+        first, second = send_far(gate_sum, share // 2)
         gate_sum = receive_far(first)
         up_sum = add_partner(split_rows(up_sum), low_bits)
         middle_grad, middle_bf, mlp_sum = rows_back(
@@ -825,7 +828,7 @@
         mixed_grad = mm(middle_bf, wo).astype(bf16)
         mixed_grad, gate_sum[1], up_sum = tied(mixed_grad, gate_sum[1], up_sum)
         gate_sum = scatter_columns(jnp.concatenate(gate_sum, axis=0))
-        first, second = send_far(up_sum)
+        first, second = send_far(up_sum, share // 4)
         up_sum = receive_far(first)
         dq, dk, dv = attention_backward(
             *heads, mixed_grad, lse, back_tables, key_tables, offset, single
@@ -835,28 +838,33 @@
         dq, dk, dv, down, up_sum, second[0] = tied(dq, dk, dv, down, up_sum, second[0])
         up_sum = [up_sum, receive_far(second)]
         outgoing, attn_sum = heads_back(dq, dk, dv, wqkv, h, middle_grad, attn_row, 0, blocks)
-        outgoing, dk, dv, dq, middle_bf = tied(outgoing, dk, dv, dq, middle_bf)
-        input_grads = to_places(outgoing)
+        outgoing, dk, dv, dq, middle_bf, up_sum[1] = tied(
+            outgoing, dk, dv, dq, middle_bf, up_sum[1]
+        )
+        blocks_out = reorder(outgoing, 1).reshape(micro, nloc, width)
+        got = arrivals(blocks_out)
+        up_sum = scatter_columns(jnp.concatenate(up_sum, axis=0))
         kv = jnp.concatenate(
             [unpadded(mm_tn(normed, dk).astype(bf16)), unpadded(mm_tn(normed, dv).astype(bf16))],
             axis=1,
         )
-        dq, kv, up_sum[1] = tied(dq, kv, up_sum[1])
-        up_sum = scatter_columns(jnp.concatenate(up_sum, axis=0))
+        dq, kv = tied(dq, kv)
         kv = add_partner(split_rows(kv), low_bits)
         query = unpadded(mm_tn(normed, dq).astype(bf16))
-        middle_bf, kv, query = tied(middle_bf, kv, query)
+        middle_bf, kv, query, got[0] = tied(middle_bf, kv, query, got[0])
         kv = add_partner(kv, high_bits)[0]
         query = add_partner(split_rows(query), low_bits)
         out = unpadded(mm_tn(middle_bf, mixed).astype(bf16))
-        out, kv, query, gate_sum = tied(out, kv, query, gate_sum)
-        kv = sum_over_tensor(kv)
+        out, kv, query, gate_sum, got[1:-1] = tied(out, kv, query, gate_sum, got[1:-1])
         query = add_partner(query, high_bits)[0]
         out = add_partner(split_rows(out), low_bits + high_bits)[0]
+        out, query, got[-1:] = tied(out, query, got[-1:])
+        input_grads = settled(blocks_out, got)[None]
+        kv = sum_over_tensor(kv)
         pair = jnp.concatenate(
             [out.reshape(share, tsize, -1), query.reshape(share, tsize, -1)], axis=2
         )
-        pair, up_sum, input_grads, kv, attn_sum = tied(pair, up_sum, input_grads, kv, attn_sum)
+        pair, up_sum, attn_sum = tied(pair, up_sum, attn_sum)
         pair = scatter_columns(pair)
         gains = jnp.concatenate([attn_sum, mlp_sum], axis=0)
         half_cols = pair.shape[1] // 2

time: 1460 us -> 1380 us (0.945)
  waiting for transfers between devices: 449 us -> 383 us
    all_gather x8, waiting for transfers between devices: 67.9 us -> 34.2 us  [spread_weight(): whole = lax.all_gather(shard[i * rows:(i + 1) * rows], 'tensor', axis=0)]
    reduce_scatter x4, waiting for transfers between devices: 31.8 us -> 0.01 us  [scatter_columns(): return lax.psum_scatter(part, 'tensor', scatter_dimension=0)]
    unnamed x108 -> x118, local copies, waits for them, and re-layouts: 62.5 us -> 70.9 us
  transfers between devices with their start and end apart: 84 -> 84, of which waited for: 30 -> 27; matrix products, arithmetic and copies ran while one was open for 23% -> 25% of each run, Pallas kernels for 27% -> 28%
where the time goes in v8:
time: 1380 us; the launch traced here: 1370 us
  Pallas kernels  522 us (38%)
  waiting for transfers between devices  383 us (28%)
  local copies, waits for them, and re-layouts  223 us (16%)
  other arithmetic  102 us (7%)
  starting transfers between devices  63.9 us (5%)
  matrix products  62.9 us (5%)
  between operations  15.4 us (1%)
    ppermute x68, waiting for transfers between devices, swapped(): lax.ppermute(array, axis, [(i, i ^ bit) for i in range(lax.axis_size(axis...  272 us
    pallas_call x2, Pallas kernels, attention_backward(): kernel_call(functools.partial(attend_backward_kernel, single=single), (KV...  74.8 us
    ppermute x4, waiting for transfers between devices, shifted(): return lax.ppermute(array, axis, pairs)  74.7 us
    unnamed x118, local copies, waits for them, and re-layouts  70.9 us
    pallas_call x2, Pallas kernels, gate_up(): kernel_call(gate_up_kernel, (total // block,), [whole(x.shape), columns_o...  63.9 us
    pallas_call x1, Pallas kernels, feed_back(): kernel_call(feed_back_kernel, (total // block,), [whole(grad.shape), colu...  62.4 us
    pallas_call x3, Pallas kernels, heads_back(): kernel_call(heads_back_kernel, (count,), [rows_of((block, a.shape[1]), fi...  54.5 us
    ppermute x68, starting transfers between devices, swapped(): lax.ppermute(array, axis, [(i, i ^ bit) for i in range(lax.axis_size(axis...  52.4 us
  transfers between devices with their start and end apart: 84, of which 27 were waited for; matrix products, arithmetic and copies ran while one was open for 25% of the time, Pallas kernels for 28%

profile of v8, /device:TPU:0, one launch (start us, length us, event | category | flops | bytes accessed | tf_op | source)
XLA Modules:
  0.0 1372.0 jit_solution(9495003846723532244)
XLA Ops:
  27.2 30.4 %collective-permute-done = bf16[1,256,768]{2,1,0:T(8,128)(2,1)S(1)} collective-permute-done((bf16[1,256,768]{2,1,0:T(8,128)(2,1)S(1)}, bf16[1,256,768]{2,1,0:T(8,128)(2,1)S(1)}, u32[]{:S(2)}, u32[]{:S(2)}) %collective-permute-start) | collective-permute-done | bytes 393248 | tf_op jit(solution)/shard_map/ppermute | solution.py:28
  111.2 28.1 %all-gather.18.cloned.1.call-done = bf16[4,192,1024]{2,1,0:T(8,128)(2,1)} async-done(((bf16[1,192,1024]{2,1,0:T(8,128)(2,1)}), bf16[4,192,1024]{2,1,0:T(8,128)(2,1)}) %all-gather.18.cloned.1.call-update) | async-done | bytes 1572880 | tf_op jit(solution)/shard_map/all_gather | solution.py:689
  197.4 24.6 %project.2 = (bf16[1024,4096]{1,0:T(8,128)(2,1)}, bf16[1024,1536]{1,0:T(8,128)(2,1)}) custom-call(bf16[1024,1536]{1,0:T(8,128)(2,1)} %pad_maximum_fusion.4.h_ref, f32[1,1536]{1,0:T(1,128)} %broadcast_in_dim.68.gain_ref, bf16[1536,4096]{1,0:T(8,128)(2,1)} %pad_maximum_fusion.w_ref, f32[1024,128]{1,0:T(8,128)} %get-tuple-element.388.cos_ref.cosq_ref.cosk_ref, ...), custom_call_target="tpu_custom_call" | custom-call | flops 12884901888 | bytes 36700160 | tf_op jit(solution)/shard_map/project/pallas_call | solution.py:124
  236.7 21.9 %attend_forward.2 = (bf16[1024,2048]{1,0:T(8,128)(2,1)}, f32[8,4,1,512]{3,2,1,0:T(1,128)}) custom-call(s32[1]{0:T(128)} %bitcast.offset_ref, bf16[1024,4096]{1,0:T(8,128)(2,1)} %get-tuple-element.151.q_ref.k_ref.v_ref, bf16[1024,4096]{1,0:T(8,128)(2,1)} %get-tuple-element.151.q_ref.k_ref.v_ref, bf16[1024,4096]{1,0:T(8,128)(2,1)} %get-tuple-element.151.q_ref.k_ref.v_ref), custom_call_target="tpu_custom_call" | custom-call | flops 8589934592 | bytes 21004288 | tf_op jit(solution)/shard_map/attend_forward/pallas_call | solution.py:497
  284.7 13.1 join.2
  297.8 14.3 %collective-permute-done.10 = bf16[192,4096]{1,0:T(8,128)(2,1)} collective-permute-done((bf16[192,4096]{1,0:T(8,128)(2,1)}, bf16[192,4096]{1,0:T(8,128)(2,1)}, u32[]{:S(2)}, u32[]{:S(2)}) %collective-permute-start.10) | collective-permute-done | bytes 1572896 | tf_op jit(solution)/shard_map/ppermute | solution.py:28
  329.4 21.2 %collective-permute-done.11 = bf16[192,4096]{1,0:T(8,128)(2,1)} collective-permute-done((bf16[192,4096]{1,0:T(8,128)(2,1)}, bf16[192,4096]{1,0:T(8,128)(2,1)}, u32[]{:S(2)}, u32[]{:S(2)}) %collective-permute-start.11) | collective-permute-done | bytes 1572896 | tf_op jit(solution)/shard_map/ppermute | solution.py:28
  356.0 31.9 %gate_up.2 = (bf16[1024,4096]{1,0:T(8,128)(2,1)}, bf16[1024,4096]{1,0:T(8,128)(2,1)}, bf16[1024,4096]{1,0:T(8,128)(2,1)}) custom-call(bf16[1024,1536]{1,0:T(8,128)(2,1)} %get-tuple-element.156.x_ref, bf16[1536,4096]{1,0:T(8,128)(2,1)} %constant_dynamic-update-slice_fusion.wg_ref, bf16[1536,4096]{1,0:T(8,128)(2,1)} %constant_dynamic-update-slice_fusion.8.wu_ref), custom_call_target="tpu_custom_call" | custom-call | flops 25769803776 | bytes 75497472 | tf_op jit(solution)/shard_map/gate_up/pallas_call | solution.py:179
  402.3 14.5 %down_rows.3 = bf16[512,1536]{1,0:T(8,128)(2,1)} custom-call(bf16[1024,4096]{1,0:T(8,128)(2,1)} %get-tuple-element.164.hidden_ref, f32[1024,1536]{1,0:T(8,128)} %get-tuple-element.159.middle_ref, bf16[1536,4096]{1,0:T(8,128)(2,1)} %constant_dynamic-update-slice_fusion.16.w_ref.wd_ref), custom_call_target="tpu_custom_call" | custom-call | flops 6442450944 | bytes 14155776 | tf_op jit(solution)/shard_map/down_rows/pallas_call | solution.py:198
  420.5 14.1 %down_rows.4 = bf16[512,1536]{1,0:T(8,128)(2,1)} custom-call(bf16[1024,4096]{1,0:T(8,128)(2,1)} %get-tuple-element.164.hidden_ref, f32[1024,1536]{1,0:T(8,128)} %get-tuple-element.159.middle_ref, bf16[1536,4096]{1,0:T(8,128)(2,1)} %constant_dynamic-update-slice_fusion.16.w_ref.wd_ref), custom_call_target="tpu_custom_call" | custom-call | flops 6442450944 | bytes 14155776 | tf_op jit(solution)/shard_map/down_rows/pallas_call | solution.py:198
  434.7 20.0 %collective-permute-done.31 = bf16[512,1536]{1,0:T(8,128)(2,1)S(1)} collective-permute-done((bf16[512,1536]{1,0:T(8,128)(2,1)}, bf16[512,1536]{1,0:T(8,128)(2,1)S(1)}, u32[]{:S(2)}, u32[]{:S(2)}) %collective-permute-start.31) | collective-permute-done | bytes 1572896 | tf_op jit(solution)/shard_map/ppermute | solution.py:24
  497.1 24.7 %project.3 = (bf16[1024,4096]{1,0:T(8,128)(2,1)}, bf16[1024,1536]{1,0:T(8,128)(2,1)}) custom-call(bf16[1024,1536]{1,0:T(8,128)(2,1)} %broadcast_select_fusion.h_ref, f32[1,1536]{1,0:T(1,128)} %broadcast_in_dim.68.gain_ref, bf16[1536,4096]{1,0:T(8,128)(2,1)} %pad_maximum_fusion.w_ref, f32[1024,128]{1,0:T(8,128)} %get-tuple-element.388.cos_ref.cosq_ref.cosk_ref, ...), custom_call_target="tpu_custom_call" | custom-call | flops 12884901888 | bytes 36700160 | tf_op jit(solution)/shard_map/project/pallas_call | solution.py:124
  521.8 21.7 %attend_forward.3 = (bf16[1024,2048]{1,0:T(8,128)(2,1)}, f32[8,4,1,512]{3,2,1,0:T(1,128)}) custom-call(s32[1]{0:T(128)} %bitcast.offset_ref, bf16[1024,4096]{1,0:T(8,128)(2,1)} %get-tuple-element.171.q_ref.k_ref.v_ref, bf16[1024,4096]{1,0:T(8,128)(2,1)} %get-tuple-element.171.q_ref.k_ref.v_ref, bf16[1024,4096]{1,0:T(8,128)(2,1)} %get-tuple-element.171.q_ref.k_ref.v_ref), custom_call_target="tpu_custom_call" | custom-call | flops 8589934592 | bytes 21004288 | tf_op jit(solution)/shard_map/attend_forward/pallas_call | solution.py:497
  546.1 13.1 join.3
  559.3 32.0 %gate_up.3 = (bf16[1024,4096]{1,0:T(8,128)(2,1)}, bf16[1024,4096]{1,0:T(8,128)(2,1)}, bf16[1024,4096]{1,0:T(8,128)(2,1)}) custom-call(bf16[1024,1536]{1,0:T(8,128)(2,1)} %get-tuple-element.176.x_ref.normed_ref, bf16[1536,4096]{1,0:T(8,128)(2,1)} %constant_dynamic-update-slice_fusion.wg_ref, bf16[1536,4096]{1,0:T(8,128)(2,1)} %constant_dynamic-update-slice_fusion.8.wu_ref), custom_call_target="tpu_custom_call" | custom-call | flops 25769803776 | bytes 75497472 | tf_op jit(solution)/shard_map/gate_up/pallas_call | solution.py:179
  591.2 20.6 %down_rows.5 = bf16[1024,1536]{1,0:T(8,128)(2,1)} custom-call(bf16[1024,4096]{1,0:T(8,128)(2,1)} %get-tuple-element.181.hidden_ref, f32[1024,1536]{1,0:T(8,128)} %get-tuple-element.179.middle_ref, bf16[1536,4096]{1,0:T(8,128)(2,1)} %constant_dynamic-update-slice_fusion.16.w_ref.wd_ref), custom_call_target="tpu_custom_call" | custom-call | flops 12884901888 | bytes 28311552 | tf_op jit(solution)/shard_map/down_rows/pallas_call | solution.py:198
  623.9 62.4 %feed_back.1 = (f32[1024,1536]{1,0:T(8,128)}, bf16[1024,1536]{1,0:T(8,128)(2,1)}, f32[1,1536]{1,0:T(1,128)}) custom-call(bf16[1024,1536]{1,0:T(8,128)(2,1)} %pad_maximum_fusion.7.grad_ref, bf16[1024,4096]{1,0:T(8,128)(2,1)} %get-tuple-element.177.gate_ref, bf16[1024,4096]{1,0:T(8,128)(2,1)} %get-tuple-element.178.up_ref, ...), custom_call_target="tpu_custom_call" | custom-call | flops 38654705664 | bytes 81792000 | tf_op jit(solution)/shard_map/feed_back/pallas_call | solution.py:339
  700.9 37.3 %attend_backward.2 = (bf16[1024,2048]{1,0:T(8,128)(2,1)}, bf16[1024,1024]{1,0:T(8,128)(2,1)}, bf16[1024,1024]{1,0:T(8,128)(2,1)}) custom-call(s32[1]{0:T(128)} %bitcast.offset_ref, bf16[1024,4096]{1,0:T(8,128)(2,1)} %get-tuple-element.171.q_ref.k_ref.v_ref, bf16[1024,4096]{1,0:T(8,128)(2,1)} %get-tuple-element.171.q_ref.k_ref.v_ref, ...), custom_call_target="tpu_custom_call" | custom-call | flops 21474836480 | bytes 50331648 | tf_op jit(solution)/shard_map/attend_backward/pallas_call | solution.py:524
  738.2 15.2 %heads_back.3 = (bf16[512,1536]{1,0:T(8,128)(2,1)}, f32[1,1536]{1,0:T(1,128)}) custom-call(bf16[1024,2048]{1,0:T(8,128)(2,1)} %get-tuple-element.190.dq_ref, bf16[1024,1024]{1,0:T(8,128)(2,1)} %get-tuple-element.186.dk_ref, bf16[1024,1024]{1,0:T(8,128)(2,1)} %get-tuple-element.187.dv_ref, bf16[1536,4096]{1,0:T(8,128)(2,1)} %pad_maximum_fusion.w_ref, ...), custom_call_target="tpu_custom_call" | custom-call | flops 6442450944 | bytes 14158848 | tf_op jit(solution)/shard_map/heads_back/pallas_call | solution.py:388
  754.9 15.4 %heads_back.4 = (bf16[512,1536]{1,0:T(8,128)(2,1)}, f32[1,1536]{1,0:T(1,128)}) custom-call(bf16[1024,2048]{1,0:T(8,128)(2,1)} %get-tuple-element.190.dq_ref, bf16[1024,1024]{1,0:T(8,128)(2,1)} %get-tuple-element.186.dk_ref, bf16[1024,1024]{1,0:T(8,128)(2,1)} %get-tuple-element.187.dv_ref, bf16[1536,4096]{1,0:T(8,128)(2,1)} %pad_maximum_fusion.w_ref, ...), custom_call_target="tpu_custom_call" | custom-call | flops 6442450944 | bytes 14158848 | tf_op jit(solution)/shard_map/heads_back/pallas_call | solution.py:388
  770.3 18.9 %collective-permute-done.40 = bf16[512,1536]{1,0:T(8,128)(2,1)S(1)} collective-permute-done((bf16[512,1536]{1,0:T(8,128)(2,1)}, bf16[512,1536]{1,0:T(8,128)(2,1)S(1)}, u32[]{:S(2)}, u32[]{:S(2)}) %collective-permute-start.40) | collective-permute-done | bytes 1572896 | tf_op jit(solution)/shard_map/ppermute | solution.py:24
  790.5 33.4 %collective-permute-done.41 = bf16[512,1536]{1,0:T(8,128)(2,1)S(1)} collective-permute-done((bf16[512,1536]{1,0:T(8,128)(2,1)}, bf16[512,1536]{1,0:T(8,128)(2,1)S(1)}, u32[]{:S(2)}, u32[]{:S(2)}) %collective-permute-start.41) | collective-permute-done | bytes 1572896 | tf_op jit(solution)/shard_map/ppermute | solution.py:24
  858.2 52.2 %feed_grads.1 = (bf16[1024,4096]{1,0:T(8,128)(2,1)}, bf16[1024,4096]{1,0:T(8,128)(2,1)}, bf16[1536,4096]{1,0:T(8,128)(2,1)}, bf16[1536,4096]{1,0:T(8,128)(2,1)}) custom-call(bf16[1024,1536]{1,0:T(8,128)(2,1)} %copy-done.8, bf16[1024,4096]{1,0:T(8,128)(2,1)} %get-tuple-element.177.gate_ref, bf16[1024,4096]{1,0:T(8,128)(2,1)} %get-tuple-element.178.up_ref, ...), custom_call_target="tpu_custom_call" | custom-call | flops 38654705664 | bytes 117440512 | tf_op jit(solution)/shard_map/feed_grads/pallas_call | solution.py:249
  946.0 45.6 %rows_back.1 = (f32[1024,1536]{1,0:T(8,128)}, bf16[1024,1536]{1,0:T(8,128)(2,1)}, f32[1,1536]{1,0:T(1,128)}) custom-call(bf16[1024,4096]{1,0:T(8,128)(2,1)} %get-tuple-element.206.gate_grad_ref, bf16[1024,4096]{1,0:T(8,128)(2,1)} %get-tuple-element.207.up_grad_ref, bf16[1536,4096]{1,0:T(8,128)(2,1)} %constant_dynamic-update-slice_fusion.wg_ref, ...), custom_call_target="tpu_custom_call" | custom-call | flops 25769803776 | bytes 56626176 | tf_op jit(solution)/shard_map/rows_back/pallas_call | solution.py:287
  998.7 14.9 %collective-permute-done.46 = bf16[192,4096]{1,0:T(8,128)(2,1)} collective-permute-done((bf16[192,4096]{1,0:T(8,128)(2,1)}, bf16[192,4096]{1,0:T(8,128)(2,1)}, u32[]{:S(2)}, u32[]{:S(2)}) %collective-permute-start.46) | collective-permute-done | bytes 1572896 | tf_op jit(solution)/shard_map/ppermute | solution.py:28
  1029.5 37.5 %attend_backward.3 = (bf16[1024,2048]{1,0:T(8,128)(2,1)}, bf16[1024,1024]{1,0:T(8,128)(2,1)}, bf16[1024,1024]{1,0:T(8,128)(2,1)}) custom-call(s32[1]{0:T(128)} %bitcast.offset_ref, bf16[1024,4096]{1,0:T(8,128)(2,1)} %get-tuple-element.171.q_ref.k_ref.v_ref, bf16[1024,4096]{1,0:T(8,128)(2,1)} %get-tuple-element.171.q_ref.k_ref.v_ref, ...), custom_call_target="tpu_custom_call" | custom-call | flops 21474836480 | bytes 50331648 | tf_op jit(solution)/shard_map/attend_backward/pallas_call | solution.py:524
  1076.7 23.9 %heads_back.5 = (bf16[1024,1536]{1,0:T(8,128)(2,1)}, f32[1,1536]{1,0:T(1,128)}) custom-call(bf16[1024,2048]{1,0:T(8,128)(2,1)} %get-tuple-element.236.dq_ref, bf16[1024,1024]{1,0:T(8,128)(2,1)} %get-tuple-element.233.dk_ref, bf16[1024,1024]{1,0:T(8,128)(2,1)} %get-tuple-element.234.dv_ref, bf16[1536,4096]{1,0:T(8,128)(2,1)} %pad_maximum_fusion.w_ref, ...), custom_call_target="tpu_custom_call" | custom-call | flops 12884901888 | bytes 28314624 | tf_op jit(solution)/shard_map/heads_back/pallas_call | solution.py:388
  1100.6 19.8 %collective-permute-done.51 = bf16[288,4096]{1,0:T(8,128)(2,1)} collective-permute-done((bf16[288,4096]{1,0:T(8,128)(2,1)}, bf16[288,4096]{1,0:T(8,128)(2,1)}, u32[]{:S(2)}, u32[]{:S(2)}) %collective-permute-start.51) | collective-permute-done | bytes 2359328 | tf_op jit(solution)/shard_map/ppermute | solution.py:28
  1221.5 17.2 %collective-permute-done.62 = bf16[384,1536]{0,1:T(8,128)(2,1)} collective-permute-done((bf16[384,1536]{0,1:T(8,128)(2,1)}, bf16[384,1536]{0,1:T(8,128)(2,1)}, u32[]{:S(2)}, u32[]{:S(2)}) %collective-permute-start.62) | collective-permute-done | bytes 1179680 | tf_op jit(solution)/shard_map/ppermute | solution.py:28
  1241.3 22.3 %collective-permute-done.61 = bf16[384,1536]{0,1:T(8,128)(2,1)} collective-permute-done((bf16[384,1536]{0,1:T(8,128)(2,1)}, bf16[384,1536]{0,1:T(8,128)(2,1)}, u32[]{:S(2)}, u32[]{:S(2)}) %collective-permute-start.61) | collective-permute-done | bytes 1179680 | tf_op jit(solution)/shard_map/ppermute | solution.py:28
  1278.1 32.5 %collective-permute-done.69 = bf16[384,384]{0,1:T(8,128)(2,1)S(1)} collective-permute-done((bf16[384,384]{0,1:T(8,128)(2,1)S(1)}, bf16[384,384]{0,1:T(8,128)(2,1)S(1)}, u32[]{:S(2)}, u32[]{:S(2)}) %collective-permute-start.69) | collective-permute-done | bytes 294944 | tf_op jit(solution)/shard_map/ppermute | solution.py:28
  1312.9 22.7 %collective-permute-done.70 = bf16[384,384]{0,1:T(8,128)(2,1)S(1)} collective-permute-done((bf16[384,384]{0,1:T(8,128)(2,1)S(1)}, bf16[384,384]{0,1:T(8,128)(2,1)S(1)}, u32[]{:S(2)}, u32[]{:S(2)}) %collective-permute-start.70) | collective-permute-done | bytes 294944 | tf_op jit(solution)/shard_map/ppermute | solution.py:28
  (424 shorter events, 539.2 us)
Async XLA Ops:
  7.2 65.2 %all-gather.20.cloned.1.call-start = ((), (), s32[]{:S(2)}) async-start(), calls=%async_computation.8 | async-start | bytes 1474560 | tf_op jit(solution)/shard_map/all_gather | solution.py:689
  7.9 92.9 %all-gather.26.cloned.1.call-start = ((), (), s32[]{:S(2)}) async-start(), calls=%async_computation.15 | async-start | bytes 1474560 | tf_op jit(solution)/shard_map/all_gather | solution.py:689
  9.8 129.4 %all-gather.18.cloned.1.call-start = ((), (), s32[]{:S(2)}) async-start(), calls=%async_computation.7 | async-start | bytes 1966080 | tf_op jit(solution)/shard_map/all_gather | solution.py:689
  12.0 170.2 %all-gather.16.cloned.1.call-start = ((), (), s32[]{:S(2)}) async-start(), calls=%async_computation.6 | async-start | bytes 1966080 | tf_op jit(solution)/shard_map/all_gather | solution.py:689
  12.5 214.9 %all-gather.14.cloned.1.call-start = ((), (), s32[]{:S(2)}) async-start(), calls=%async_computation.5 | async-start | bytes 1966080 | tf_op jit(solution)/shard_map/all_gather | solution.py:689
  13.6 258.7 %all-gather.12.cloned.1.call-start = ((), (), s32[]{:S(2)}) async-start(), calls=%async_computation.4 | async-start | bytes 1966080 | tf_op jit(solution)/shard_map/all_gather | solution.py:689
  14.2 283.6 %all-gather.24.cloned.1.call-start = ((), (), s32[]{:S(2)}) async-start(), calls=%async_computation.14 | async-start | bytes 1966080 | tf_op jit(solution)/shard_map/all_gather | solution.py:689
  15.5 313.9 %all-gather.22.cloned.1.call-start = ((), (), s32[]{:S(2)}) async-start(), calls=%async_computation.13 | async-start | bytes 1966080 | tf_op jit(solution)/shard_map/all_gather | solution.py:689
  16.3 52.4 %collective-permute-start.3 = (bf16[384,1536]{0,1:T(8,128)(2,1)S(1)}, bf16[384,1536]{0,1:T(8,128)(2,1)}, u32[]{:S(2)}, u32[]{:S(2)}) collective-permute-start(bf16[384,1536]{0,1:T(8,128)(2,1)S(1)} %pad_maximum_fusion.14), channel_id=1, source_target_pairs={{0,8},{4,12},{8,0},{12,4},{1,9},{5,13},{9,1},{13,5},{2,10},{6,14},... | collective-permute-start | bytes 3538952 | tf_op jit(solution)/shard_map/ppermute | solution.py:28
  69.3 1007.4 %reduce-scatter.5.cloned.1.call-start = ((), (), s32[]{:S(2)}) async-start(), calls=%async_computation.9 | async-start | bytes 3932160 | tf_op jit(solution)/shard_map/reduce_scatter | solution.py:675
  79.7 62.2 %collective-permute-start.13 = (bf16[384,1536]{0,1:T(8,128)(2,1)}, bf16[384,1536]{0,1:T(8,128)(2,1)}, u32[]{:S(2)}, u32[]{:S(2)}) collective-permute-start(bf16[384,1536]{0,1:T(8,128)(2,1)} %bitcast.13), channel_id=1, source_target_pairs={{0,4},{4,0},{8,12},{12,8},{1,5},{5,1},{9,13},{13,9},{2,6},{6,2},{1... | collective-permute-start | bytes 3538952 | tf_op jit(solution)/shard_map/ppermute | solution.py:28
  110.7 57.7 %collective-permute-start.17 = (bf16[384,1536]{0,1:T(8,128)(2,1)}, bf16[384,1536]{0,1:T(8,128)(2,1)}, u32[]{:S(2)}, u32[]{:S(2)}) collective-permute-start(bf16[384,1536]{0,1:T(8,128)(2,1)} %bitcast.16), channel_id=1, source_target_pairs={{0,4},{4,0},{8,12},{12,8},{1,5},{5,1},{9,13},{13,9},{2,6},{6,2},{1... | collective-permute-start | bytes 3538952 | tf_op jit(solution)/shard_map/ppermute | solution.py:28
  195.4 66.0 %collective-permute-start.20 = (bf16[192,4096]{1,0:T(8,128)(2,1)}, bf16[192,4096]{1,0:T(8,128)(2,1)}, u32[]{:S(2)}, u32[]{:S(2)}) collective-permute-start(bf16[192,4096]{1,0:T(8,128)(2,1)} %bitcast.91), channel_id=1, source_target_pairs={{0,4},{4,0},{8,12},{12,8},{1,5},{5,1},{9,13},{13,9},{2,6},{6,2},{1... | collective-permute-start | bytes 4718600 | tf_op jit(solution)/shard_map/ppermute | solution.py:28
  196.8 61.7 %collective-permute-start.19 = (bf16[192,4096]{1,0:T(8,128)(2,1)}, bf16[192,4096]{1,0:T(8,128)(2,1)}, u32[]{:S(2)}, u32[]{:S(2)}) collective-permute-start(bf16[192,4096]{1,0:T(8,128)(2,1)} %bitcast.89), channel_id=1, source_target_pairs={{0,4},{4,0},{8,12},{12,8},{1,5},{5,1},{9,13},{13,9},{2,6},{6,2},{1... | collective-permute-start | bytes 4718600 | tf_op jit(solution)/shard_map/ppermute | solution.py:28
  197.1 72.5 %collective-permute-start.21 = (bf16[192,4096]{1,0:T(8,128)(2,1)}, bf16[192,4096]{1,0:T(8,128)(2,1)}, u32[]{:S(2)}, u32[]{:S(2)}) collective-permute-start(bf16[192,4096]{1,0:T(8,128)(2,1)} %collective-permute-done.7), channel_id=1, source_target_pairs={{0,4},{4,0},{8,12},{12,8},{1,5},{5,1},{9,13},{13,9},{2,6},{6,2},{1... | collective-permute-start | bytes 4718600 | tf_op jit(solution)/shard_map/ppermute | solution.py:28
  276.0 50.6 %collective-permute-start.25 = (bf16[192,4096]{1,0:T(8,128)(2,1)}, bf16[192,4096]{1,0:T(8,128)(2,1)}, u32[]{:S(2)}, u32[]{:S(2)}) collective-permute-start(bf16[192,4096]{1,0:T(8,128)(2,1)} %collective-permute-done.9), channel_id=1, source_target_pairs={{0,4},{4,0},{8,12},{12,8},{1,5},{5,1},{9,13},{13,9},{2,6},{6,2},{1... | collective-permute-start | bytes 4718600 | tf_op jit(solution)/shard_map/ppermute | solution.py:28
  494.7 48.7 %collective-permute-start.36 = (bf16[4,256,768]{2,1,0:T(8,128)(2,1)S(1)}, bf16[4,256,768]{2,1,0:T(8,128)(2,1)S(1)}, u32[]{:S(2)}, u32[]{:S(2)}) collective-permute-start(bf16[4,256,768]{2,1,0:T(8,128)(2,1)S(1)} %constant_dynamic-update-slice_fusion.24), channel_id=1, source_target_pairs={{0,16},{16,0},{1,17},{17,1},{2,18},{18,2},{3,19},{19,3},{4,20},{20... | collective-permute-start | bytes 4718600 | tf_op jit(solution)/shard_map/ppermute | solution.py:28
  619.5 80.5 %collective-permute-start.39 = (bf16[1,256,1536]{2,1,0:T(8,128)(2,1)}, bf16[1,256,1536]{2,1,0:T(8,128)(2,1)S(1)}, u32[]{:S(2)}, u32[]{:S(2)}) collective-permute-start(bf16[1,256,1536]{2,1,0:T(8,128)(2,1)} %get-tuple-element.337), channel_id=1, source_target_pairs={{0,3},{1,2},{2,1},{3,0},{4,7},{5,6},{6,5},{7,4},{8,11},{9,10},{10,... | collective-permute-start | bytes 2359304 | tf_op jit(solution)/shard_map/ppermute | solution.py:28
  621.0 78.0 %collective-permute-start.38 = (bf16[1,256,1536]{2,1,0:T(8,128)(2,1)}, bf16[1,256,1536]{2,1,0:T(8,128)(2,1)S(1)}, u32[]{:S(2)}, u32[]{:S(2)}) collective-permute-start(bf16[1,256,1536]{2,1,0:T(8,128)(2,1)} %get-tuple-element.338), channel_id=1, source_target_pairs={{0,2},{1,3},{2,0},{3,1},{4,6},{5,7},{6,4},{7,5},{8,10},{9,11},{10,... | collective-permute-start | bytes 2359304 | tf_op jit(solution)/shard_map/ppermute | solution.py:28
  622.9 74.1 %collective-permute-start.37 = (bf16[1,256,1536]{2,1,0:T(8,128)(2,1)}, bf16[1,256,1536]{2,1,0:T(8,128)(2,1)}, u32[]{:S(2)}, u32[]{:S(2)}) collective-permute-start(bf16[1,256,1536]{2,1,0:T(8,128)(2,1)} %get-tuple-element.339), channel_id=1, source_target_pairs={{0,1},{1,0},{2,3},{3,2},{4,5},{5,4},{6,7},{7,6},{8,9},{9,8},{10,11... | collective-permute-start | bytes 2359304 | tf_op jit(solution)/shard_map/ppermute | solution.py:28
  857.1 70.4 %collective-permute-start.45 = (bf16[384,4096]{1,0:T(8,128)(2,1)}, bf16[384,4096]{1,0:T(8,128)(2,1)S(1)}, u32[]{:S(2)}, u32[]{:S(2)}) collective-permute-start(bf16[384,4096]{1,0:T(8,128)(2,1)} %get-tuple-element.205), channel_id=1, source_target_pairs={{0,8},{4,12},{8,0},{12,4},{1,9},{5,13},{9,1},{13,5},{2,10},{6,14},... | collective-permute-start | bytes 9437192 | tf_op jit(solution)/shard_map/ppermute | solution.py:28
  922.4 69.2 %collective-permute-start.48 = (bf16[384,4096]{1,0:T(8,128)(2,1)}, bf16[384,4096]{1,0:T(8,128)(2,1)}, u32[]{:S(2)}, u32[]{:S(2)}) collective-permute-start(bf16[384,4096]{1,0:T(8,128)(2,1)} %get-tuple-element.306), channel_id=1, source_target_pairs={{0,4},{4,0},{8,12},{12,8},{1,5},{5,1},{9,13},{13,9},{2,6},{6,2},{1... | collective-permute-start | bytes 9437192 | tf_op jit(solution)/shard_map/ppermute | solution.py:28
  922.4 69.2 %collective-permute-start.47 = (bf16[384,4096]{1,0:T(8,128)(2,1)}, bf16[384,4096]{1,0:T(8,128)(2,1)}, u32[]{:S(2)}, u32[]{:S(2)}) collective-permute-start(bf16[384,4096]{1,0:T(8,128)(2,1)} %get-tuple-element.307), channel_id=1, source_target_pairs={{0,4},{4,0},{8,12},{12,8},{1,5},{5,1},{9,13},{13,9},{2,6},{6,2},{1... | collective-permute-start | bytes 9437192 | tf_op jit(solution)/shard_map/ppermute | solution.py:28
  942.0 264.8 %reduce-scatter.7.cloned.1.call-start = ((), (), s32[]{:S(2)}) async-start(), calls=%async_computation.10 | async-start | bytes 3932160 | tf_op jit(solution)/shard_map/reduce_scatter | solution.py:675
  943.9 72.8 %collective-permute-start.49 = (bf16[192,4096]{1,0:T(8,128)(2,1)}, bf16[192,4096]{1,0:T(8,128)(2,1)S(1)}, u32[]{:S(2)}, u32[]{:S(2)}) collective-permute-start(bf16[192,4096]{1,0:T(8,128)(2,1)} %get-tuple-element.331), channel_id=1, source_target_pairs={{0,8},{4,12},{8,0},{12,4},{1,9},{5,13},{9,1},{13,5},{2,10},{6,14},... | collective-permute-start | bytes 4718600 | tf_op jit(solution)/shard_map/ppermute | solution.py:28
  945.1 68.5 %collective-permute-start.46 = (bf16[192,4096]{1,0:T(8,128)(2,1)}, bf16[192,4096]{1,0:T(8,128)(2,1)}, u32[]{:S(2)}, u32[]{:S(2)}) collective-permute-start(bf16[192,4096]{1,0:T(8,128)(2,1)} %get-tuple-element.332), channel_id=1, source_target_pairs={{0,8},{4,12},{8,0},{12,4},{1,9},{5,13},{9,1},{13,5},{2,10},{6,14},... | collective-permute-start | bytes 4718600 | tf_op jit(solution)/shard_map/ppermute | solution.py:28
  1068.7 51.6 %collective-permute-start.51 = (bf16[288,4096]{1,0:T(8,128)(2,1)}, bf16[288,4096]{1,0:T(8,128)(2,1)}, u32[]{:S(2)}, u32[]{:S(2)}) collective-permute-start(bf16[288,4096]{1,0:T(8,128)(2,1)} %slice.187), channel_id=1, source_target_pairs={{0,8},{4,12},{8,0},{12,4},{1,9},{5,13},{9,1},{13,5},{2,10},{6,14},... | collective-permute-start | bytes 7077896 | tf_op jit(solution)/shard_map/ppermute | solution.py:28
  1074.4 199.8 %reduce-scatter.9.cloned.1.call-start = ((), (), s32[]{:S(2)}) async-start(), calls=%async_computation.11 | async-start | bytes 3932160 | tf_op jit(solution)/shard_map/reduce_scatter | solution.py:675
  1131.7 75.0 %collective-permute-start.58 = (bf16[1,256,1536]{2,1,0:T(8,128)(2,1)}, bf16[1,256,1536]{2,1,0:T(8,128)(2,1)}, u32[]{:S(2)}, u32[]{:S(2)}) collective-permute-start(bf16[1,256,1536]{2,1,0:T(8,128)(2,1)} %get-tuple-element.325), channel_id=1, source_target_pairs={{0,2},{1,3},{2,0},{3,1},{4,6},{5,7},{6,4},{7,5},{8,10},{9,11},{10,... | collective-permute-start | bytes 2359304 | tf_op jit(solution)/shard_map/ppermute | solution.py:28
  1170.3 191.6 %reduce-scatter.11.cloned.1.call-start = ((), (), s32[]{:S(2)}) async-start(), calls=%async_computation.12 | async-start | bytes 2949120 | tf_op jit(solution)/shard_map/reduce_scatter | solution.py:675
  1216.1 51.0 %collective-permute-start.63 = (bf16[1,256,1536]{2,1,0:T(8,128)(2,1)}, bf16[1,256,1536]{2,1,0:T(8,128)(2,1)}, u32[]{:S(2)}, u32[]{:S(2)}) collective-permute-start(bf16[1,256,1536]{2,1,0:T(8,128)(2,1)} %get-tuple-element.324), channel_id=1, source_target_pairs={{0,3},{1,2},{2,1},{3,0},{4,7},{5,6},{6,5},{7,4},{8,11},{9,10},{10,... | collective-permute-start | bytes 2359304 | tf_op jit(solution)/shard_map/ppermute | solution.py:28
  1221.5 52.7 %collective-permute-start.68 = (bf16[384,768]{0,1:T(8,128)(2,1)}, bf16[384,768]{0,1:T(8,128)(2,1)S(1)}, u32[]{:S(2)}, u32[]{:S(2)}) collective-permute-start(bf16[384,768]{0,1:T(8,128)(2,1)} %broadcast_select_fusion.5), channel_id=1, source_target_pairs={{0,1},{1,0},{2,3},{3,2},{4,5},{5,4},{6,7},{7,6},{8,9},{9,8},{10,11... | collective-permute-start | bytes 1769480 | tf_op jit(solution)/shard_map/ppermute | solution.py:28
  (97 other events, 2444.2 us)
Sparse Core Ops, SparseCore 0:
  9.6 60.0 all-gather.19
  71.8 28.9 all-gather.25
  103.0 36.1 all-gather.17
  141.2 35.9 all-gather.15
  179.2 35.9 all-gather.13
  216.6 35.9 all-gather.11
  254.2 35.9 all-gather.23
  291.7 35.9 all-gather.21
  942.1 58.1 reduce-scatter.4
  1074.5 58.0 reduce-scatter.6
  1170.4 68.1 reduce-scatter.8
  1274.3 65.3 reduce-scatter.10
